TPU v7x, 32 devices: a whole 2x2x4 slice. The times are simulated.
32 devices in a mesh: unit: 8 (over z, x), day: 4 (over y, core).
Axes of the slice: x: 2, y: 2, z: 4, core: 2. Of those that a mesh axis runs over, the one named last changes fastest.
Arguments:
- outcomes: float32 [32768, 1024], P('unit', 'day'), may hold values from -6 to 6
- cohort: int32 [32768], P('unit'), may hold values from 0 to 8
- pre_end: int32 [8], replicated, may hold values from 256 to 511
- post_start: int32 [8], replicated, may hold values from 512 to 767
- unit_logit: float32 [8, 32768], P(None, 'unit'), may hold values from -4 to 4
- time_logit: float32 [8, 1024], P(None, 'day'), may hold values from -4 to 4
Outputs:
- unit_weights: float32 [8, 32768], P(None, 'unit')
- time_weights: float32 [8, 1024], P(None, 'day')
All inputs are finite; a program needn't handle non-finite values.
Results may differ from a plain program's by a relative error of at most 0.0003.
Values sent between devices are 32-bit elements; how exact they have to be, the bound alone decides.
No kernel may reach another device: no remote copies, remote signals or barrier semaphores. Data moves between devices by JAX's collectives and lax.ppermute only.
A program may use at most 64 MiB of HBM per device.

v0:
```python
import functools

import jax
import jax.numpy as jnp
from jax import lax
from jax.experimental import pallas as pl
from jax.experimental.pallas import tpu as pltpu
from jax.sharding import PartitionSpec as P

step_rate = 16.0
f32 = jnp.float32
bf16 = jnp.bfloat16
lanes = 128
params = pltpu.CompilerParams(vmem_limit_bytes=24 * 1024 * 1024)


def split_left(value):
    first = value.astype(bf16).astype(f32)
    rest = value - first
    second = rest.astype(bf16).astype(f32)
    return [first, second, rest - second]


def left_of(value, other=None):
    other = jnp.zeros_like(value) if other is None else other
    return jnp.concatenate(split_left(value) + [other], axis=0).astype(bf16)


def split_panel(value):
    high = value.astype(bf16)
    return high, (value - high.astype(f32)).astype(bf16)


def rows_dot(left, high, low):
    return jnp.dot(left, high, preferred_element_type=f32) + jnp.dot(left, low, preferred_element_type=f32)


def days_dot(left, high, low):
    dims = (((1,), (1,)), ((), ()))
    return lax.dot_general(left, high, dims, preferred_element_type=f32) + lax.dot_general(
        left, low, dims, preferred_element_type=f32
    )


def add_terms(stack, groups):
    return stack[:groups] + stack[groups : 2 * groups] + stack[2 * groups : 3 * groups]


def tree_sum(values):
    values = list(values)
    while len(values) > 1:
        values = [values[i] + values[i + 1] for i in range(0, len(values), 2)]
    return values[0]


def column(row_ref):
    count = row_ref.shape[1]
    wide = jnp.broadcast_to(row_ref[...].astype(f32), (count, count))
    row = lax.broadcasted_iota(jnp.int32, (count, count), 0)
    lane = lax.broadcasted_iota(jnp.int32, (count, count), 1)
    return jnp.sum(jnp.where(row == lane, wide, 0.0), axis=1, keepdims=True).astype(jnp.int32)


def days_of(device, shape):
    return device * shape[1] + lax.broadcasted_iota(jnp.int32, shape, 1)


def first_kernel(all_count, copies_out, chunks, *refs):
    arguments, refs = refs[:6], refs[6:]
    sums, cross, raised_units, raised_days, ends, high_ref, low_ref, *held, small_sems, sems = refs
    panel, held_panel = arguments[0], held[0]
    groups, day_cols = held[5].shape
    unit_rows = panel.shape[0]
    rows = unit_rows // chunks
    small = [
        pltpu.make_async_copy(source, target, small_sems.at[i])
        for i, (source, target) in enumerate(zip(arguments[1:], held[1:]))
    ]
    for copy in small:
        copy.start()
    copies = []
    for chunk in range(chunks):
        here = pl.ds(chunk * rows, rows)
        copies.append(pltpu.make_async_copy(panel.at[here], held_panel.at[here], sems.at[chunk]))
        copies[-1].start()
    for copy in small:
        copy.wait()
    cohort, pre_row, post_row, unit_logit, time_logit = held[1:]
    pre_end, post_start = column(pre_row), column(post_row)
    ends[...] = jnp.broadcast_to(pre_end.astype(f32), ends.shape)
    days = days_of(lax.axis_index("day"), (groups, day_cols))
    raised_time = jnp.where(days < pre_end, jnp.exp(time_logit[...]), 0.0)
    raised_days[...] = raised_time
    after_len = (all_count - post_start).astype(f32)
    coef = left_of(raised_time - jnp.where(days >= post_start, 1.0, 0.0) / after_len)
    fitted = jnp.zeros((groups, day_cols), f32)
    treat_sum = jnp.zeros((groups, day_cols), f32)
    norm = jnp.zeros((groups, 1), f32)
    treat_count = jnp.zeros((groups, 1), f32)
    ctrl_count = jnp.zeros((groups, 1), f32)
    label = lax.broadcasted_iota(jnp.int32, (groups, rows), 0)
    for chunk in range(chunks):
        here = pl.ds(chunk * rows, rows)
        treated = jnp.where(cohort[:, here] == label, 1.0, 0.0)
        control = jnp.where(cohort[:, here] > label, 1.0, 0.0)
        raised = jnp.exp(unit_logit[:, here]) * control
        raised_units[:, here] = raised
        left = left_of(raised, treated)
        norm += jnp.sum(raised, axis=1, keepdims=True)
        treat_count += jnp.sum(treated, axis=1, keepdims=True)
        ctrl_count += jnp.sum(control, axis=1, keepdims=True)
        copies[chunk].wait()
        high, low = split_panel(held_panel[here, :])
        high_ref[here, :] = high
        low_ref[here, :] = low
        product = rows_dot(left, high, low)
        fitted += add_terms(product, groups)
        treat_sum += product[3 * groups :]
        cross[:, here] = add_terms(days_dot(coef, high, low), groups)
    lane = lax.broadcasted_iota(jnp.int32, (groups, lanes), 1)
    norms = jnp.where(lane == 0, norm, jnp.where(lane == 1, treat_count, ctrl_count))
    for i in range(copies_out):
        here = pl.ds(i * groups, groups)
        sums[here, :day_cols] = fitted
        sums[here, day_cols : 2 * day_cols] = treat_sum
        sums[here, 2 * day_cols :] = norms


def second_kernel(unit_devices, chunks, sums, high_ref, low_ref, cross, post, raised_days, ends, pack, norms):
    groups, day_cols = raised_days.shape
    unit_rows = cross.shape[1]
    rows = unit_rows // chunks
    total = tree_sum(sums[pl.ds(u * groups, groups), :] for u in range(unit_devices))
    unit_norm = total[:, 2 * day_cols : 2 * day_cols + 1]
    treat_count = jnp.maximum(total[:, 2 * day_cols + 1 : 2 * day_cols + 2], 1.0)
    norms[...] = total[:, 2 * day_cols :]
    gap = total[:, :day_cols] / unit_norm - total[:, day_cols : 2 * day_cols] / treat_count
    days = days_of(lax.axis_index("day"), (groups, day_cols)).astype(f32)
    left = left_of(jnp.where(days < ends[:, 0:1], gap, 0.0))
    for chunk in range(chunks):
        here = pl.ds(chunk * rows, rows)
        pack[:groups, here] = add_terms(days_dot(left, high_ref[here, :], low_ref[here, :]), groups)
    pack[groups : 2 * groups, :unit_rows] = cross[...]
    pack[2 * groups :, :unit_rows] = post[...]
    time_norm = jnp.sum(raised_days[...], axis=1, keepdims=True)
    pack[:, unit_rows:] = jnp.broadcast_to(jnp.concatenate([time_norm] * 3, axis=0), (3 * groups, lanes))


def third_kernel(half, copies_out, chunks, *refs):
    parts, refs = refs[:half], refs[half:]
    high_ref, low_ref, norms, raised_units, raised_days, ends, scaled, lam, grads = refs
    groups, unit_rows = raised_units.shape
    day_cols = raised_days.shape[1]
    rows = unit_rows // chunks
    unit_norm, ctrl_count = norms[:, 0:1], norms[:, 2:3]
    factor = -step_rate / jnp.sqrt(ends[:, 0:1])
    time_norm = tree_sum(ref[:groups, unit_rows : unit_rows + 1] for ref in parts)
    lam[...] = raised_days[...] / time_norm
    time_grad = jnp.zeros((groups, day_cols), f32)
    new_sum = jnp.zeros((groups, 1), f32)
    for chunk in range(chunks):
        here = pl.ds(chunk * rows, rows)
        whole = tree_sum(ref[:, here] for ref in parts)
        raised = raised_units[:, here]
        new = raised / unit_norm * jnp.exp(whole[:groups] * factor)
        new_sum += jnp.sum(new, axis=1, keepdims=True)
        scaled[:, here] = new * ctrl_count
        shortfall = whole[groups : 2 * groups] / time_norm + whole[2 * groups :]
        left = left_of(jnp.where(raised > 0.0, shortfall, 0.0))
        time_grad += add_terms(rows_dot(left, high_ref[here, :], low_ref[here, :]), groups)
    for i in range(copies_out):
        here = pl.ds(i * groups, groups)
        grads[here, :day_cols] = time_grad
        grads[here, day_cols:] = jnp.broadcast_to(new_sum, (groups, lanes))


def fourth_kernel(unit_devices, grads, lam, norms, moved, totals):
    groups, day_cols = lam.shape
    total = tree_sum(grads[pl.ds(u * groups, groups), :] for u in range(unit_devices))
    root = jnp.sqrt(jnp.maximum(norms[:, 2:3], 1.0))
    new = lam[...] * jnp.exp(total[:, :day_cols] * (-step_rate / root))
    moved[...] = new
    lane = lax.broadcasted_iota(jnp.int32, (groups, lanes), 1)
    totals[...] = jnp.where(lane == 0, total[:, day_cols:], jnp.sum(new, axis=1, keepdims=True))


def fifth_kernel(half, *refs):
    totals, refs = refs[:half], refs[half:]
    sent_totals, scaled, sent_scaled, moved, ends, unit_weights, time_weights = refs
    first = lax.axis_index("day") < half
    own = jnp.where(first, totals[0][:, 0:1], sent_totals[:, 0:1])
    unit_weights[...] = jnp.where(first, scaled[...], sent_scaled[...]) / own
    day_total = tree_sum(ref[:, 1:2] for ref in totals)
    time_weights[...] = jnp.where(first, moved[...] / day_total * ends[:, 0:1], 0.0)


def local(outcomes, cohort, pre_end, post_start, unit_logit, time_logit):
    groups = pre_end.shape[0]
    unit_rows, day_cols = outcomes.shape
    day_devices = lax.axis_size("day")
    unit_devices = lax.axis_size("unit")
    half = day_devices // 2
    assert half * 2 == day_devices and half & (half - 1) == 0
    assert unit_devices & (unit_devices - 1) == 0
    chunks = 8
    vmem = pl.BlockSpec(memory_space=pltpu.VMEM)
    hbm = pl.BlockSpec(memory_space=pltpu.HBM)

    def spread(value, day_xor, up):
        pairs = [
            (u * day_devices + d, u * day_devices + (d ^ day_xor) + up) for u in range(unit_devices) for d in range(half)
        ]
        return lax.ppermute(value, ("unit", "day"), pairs)

    def over_days(value):
        return [value] + [spread(value, k, 0) for k in range(1, half)]

    def over_units(value):
        return lax.all_to_all(value, "unit", split_axis=0, concat_axis=0, tiled=True)

    def call(kernel, shapes, name, args, in_spec=vmem, **more):
        return pl.pallas_call(
            kernel,
            in_specs=[in_spec] * len(args),
            out_specs=[vmem] * len(shapes),
            out_shape=[jax.ShapeDtypeStruct(shape, kind) for shape, kind in shapes],
            compiler_params=params,
            name=name,
            **more,
        )(*args)

    arguments = (outcomes, cohort[None, :], pre_end[None, :], post_start[None, :], unit_logit, time_logit)
    sums, cross, raised_units, raised_days, ends, high, low = call(
        functools.partial(first_kernel, day_devices * day_cols, unit_devices, chunks),
        [
            ((unit_devices * groups, 2 * day_cols + lanes), f32),
            ((groups, unit_rows), f32),
            ((groups, unit_rows), f32),
            ((groups, day_cols), f32),
            ((groups, lanes), f32),
            ((unit_rows, day_cols), bf16),
            ((unit_rows, day_cols), bf16),
        ],
        "first_products",
        [pltpu.with_memory_space_constraint(argument, pltpu.HBM) for argument in arguments],
        in_spec=hbm,
        scratch_shapes=[pltpu.VMEM(argument.shape, argument.dtype) for argument in arguments]
        + [pltpu.SemaphoreType.DMA((5,)), pltpu.SemaphoreType.DMA((chunks,))],
    )
    downward = [
        (u * day_devices + d + half, u * day_devices + d) for u in range(unit_devices) for d in range(half)
    ]
    post = lax.ppermute(cross, ("unit", "day"), downward)
    all_sums = over_units(sums)
    pack, norms = call(
        functools.partial(second_kernel, unit_devices, chunks),
        [((3 * groups, unit_rows + lanes), f32), ((groups, lanes), f32)],
        "unit_gradient",
        (all_sums, high, low, cross, post, raised_days, ends),
    )
    scaled, lam, grads = call(
        functools.partial(third_kernel, half, unit_devices, chunks),
        [
            ((groups, unit_rows), f32),
            ((groups, day_cols), f32),
            ((unit_devices * groups, day_cols + lanes), f32),
        ],
        "time_gradient",
        (*over_days(pack), high, low, norms, raised_units, raised_days, ends),
    )
    sent_scaled = spread(scaled, 0, half)
    moved, totals = call(
        functools.partial(fourth_kernel, unit_devices),
        [((groups, day_cols), f32), ((groups, lanes), f32)],
        "new_time_weights",
        (over_units(grads), lam, norms),
    )
    sent_totals = spread(totals, 0, half)
    return call(
        functools.partial(fifth_kernel, half),
        [((groups, unit_rows), f32), ((groups, day_cols), f32)],
        "scale_weights",
        (*over_days(totals), sent_totals, scaled, sent_scaled, moved, ends),
    )


def solution(mesh):
    return jax.shard_map(
        local,
        mesh=mesh,
        in_specs=(P("unit", "day"), P("unit"), P(), P(), P(None, "unit"), P(None, "day")),
        out_specs=(P(None, "unit"), P(None, "day")),
        check_vma=False,
    )
```

profile of v0, /device:TPU:0, one launch (start us, length us, event | category | flops | bytes accessed | tf_op | source)
XLA Modules:
  0.0 48.6 jit_solution(15436342664849998393)
XLA Ops:
  0.6 6.0 %first_products.1 = (f32[64,640]{1,0:T(8,128)}, f32[8,4096]{1,0:T(8,128)S(1)}, f32[8,4096]{1,0:T(8,128)S(1)}, f32[8,256]{1,0:T(8,128)S(1)}, f32[8,128]{1,0:T(8,1...) custom-call(f32[4096,256]{1,0:T(8,128)} %refs_0_.1, s32[1,4096]{1,0:T(1,128)} %bitcast.9, ...), custom_call_target="tpu_custom_call" | custom-call | tf_op jit(solution)/shard_map/first_products/pallas_call | solution.py:222
  6.6 0.0 copy-start
  6.6 1.3 %copy-done = bf16[4096,256]{1,0:T(8,128)(2,1)} copy-done((bf16[4096,256]{1,0:T(8,128)(2,1)}, bf16[4096,256]{1,0:T(8,128)(2,1)S(1)}, u32[]{:S(2)}) %copy-start) | copy-done | bytes 2097176
  8.0 7.3 %all-to-all-start = ((f32[8,8,640]{2,1,0:T(8,128)}), f32[8,8,640]{2,1,0:T(8,128)S(1)}, u32[]{:S(2)}, u32[]{:S(2)}) async-start(f32[8,8,640]{2,1,0:T(8,128)} %bitcast.3), calls=%async_computation | async-start | bytes 327680 | tf_op jit(solution)/shard_map/all_to_all | solution.py:219
  15.2 1.3 %collective-permute-start = (f32[8,4096]{1,0:T(8,128)S(1)}, f32[8,4096]{1,0:T(8,128)S(1)}, u32[]{:S(2)}, u32[]{:S(2)}) collective-permute-start(f32[8,4096]{1,0:T(8,128)S(1)} %get-tuple-element.19.cross), channel_id=1, source_target_pairs={{2,0},{3,1},{6,4},{7,5},{10,8},{11,9},{14,12},{15,13},{18,16},{19,... | collective-permute-start | bytes 393224 | tf_op jit(solution)/shard_map/ppermute | solution.py:253
  16.5 5.6 %collective-permute-done.post = f32[8,4096]{1,0:T(8,128)S(1)} collective-permute-done((f32[8,4096]{1,0:T(8,128)S(1)}, f32[8,4096]{1,0:T(8,128)S(1)}, u32[]{:S(2)}, u32[]{:S(2)}) %collective-permute-start) | collective-permute-done | bytes 131104 | tf_op jit(solution)/shard_map/ppermute | solution.py:253
  22.1 0.7 %all-to-all-done = f32[8,8,640]{2,1,0:T(8,128)S(1)} async-done(((f32[8,8,640]{2,1,0:T(8,128)}), f32[8,8,640]{2,1,0:T(8,128)S(1)}, u32[]{:S(2)}, u32[]{:S(2)}) %all-to-all-start) | async-done | bytes 163872 | tf_op jit(solution)/shard_map/all_to_all | solution.py:219
  22.8 0.0 copy-start.1
  22.8 1.6 %copy-done.1 = bf16[4096,256]{1,0:T(8,128)(2,1)S(1)} copy-done((bf16[4096,256]{1,0:T(8,128)(2,1)S(1)}, bf16[4096,256]{1,0:T(8,128)(2,1)}, u32[]{:S(2)}) %copy-start.1) | copy-done | bytes 2097176
  24.4 1.3 %unit_gradient.1 = (f32[24,4224]{1,0:T(8,128)S(1)}, f32[8,128]{1,0:T(8,128)S(1)}) custom-call(f32[64,640]{1,0:T(8,128)S(1)} %bitcast.7, bf16[4096,256]{1,0:T(8,128)(2,1)S(1)} %get-tuple-element.17.high_ref.refs_2_, bf16[4096,256]{1,0:T(8,128)(2,1)S(1)} %copy-done.1, f32[8,4096]{1,0:T(8,128)S(1)} %get-tuple-element.19.cross, ...), custom_call_target="tpu_custom_call" | custom-call | tf_op jit(solution)/shard_map/unit_gradient/pallas_call | solution.py:222
  25.7 1.9 %collective-permute-start.1 = (f32[24,4224]{1,0:T(8,128)S(1)}, f32[24,4224]{1,0:T(8,128)S(1)}, u32[]{:S(2)}, u32[]{:S(2)}) collective-permute-start(f32[24,4224]{1,0:T(8,128)S(1)} %get-tuple-element.22.refs_0_), channel_id=1, source_target_pairs={{0,1},{1,0},{4,5},{5,4},{8,9},{9,8},{12,13},{13,12},{16,17},{17,16... | collective-permute-start | bytes 1216520 | tf_op jit(solution)/shard_map/ppermute | solution.py:213
  27.7 1.7 %collective-permute-done.1.refs_1_ = f32[24,4224]{1,0:T(8,128)S(1)} collective-permute-done((f32[24,4224]{1,0:T(8,128)S(1)}, f32[24,4224]{1,0:T(8,128)S(1)}, u32[]{:S(2)}, u32[]{:S(2)}) %collective-permute-start.1) | collective-permute-done | bytes 405536 | tf_op jit(solution)/shard_map/ppermute | solution.py:213
  29.4 1.6 %time_gradient.1 = (f32[8,4096]{1,0:T(8,128)S(1)}, f32[8,256]{1,0:T(8,128)S(1)}, f32[64,384]{1,0:T(8,128)}) custom-call(f32[24,4224]{1,0:T(8,128)S(1)} %get-tuple-element.22.refs_0_, f32[24,4224]{1,0:T(8,128)S(1)} %collective-permute-done.1.refs_1_, bf16[4096,256]{1,0:T(8,128)(2,1)S(1)} %get-tuple-element.17.high_ref.refs_2_, ...), custom_call_target="tpu_custom_call" | custom-call | tf_op jit(solution)/shard_map/time_gradient/pallas_call | solution.py:222
  30.9 5.3 %all-to-all-start.1 = ((f32[8,8,384]{2,1,0:T(8,128)}), f32[8,8,384]{2,1,0:T(8,128)S(1)}, u32[]{:S(2)}, u32[]{:S(2)}) async-start(f32[8,8,384]{2,1,0:T(8,128)} %bitcast.5), calls=%async_computation.1 | async-start | bytes 196608 | tf_op jit(solution)/shard_map/all_to_all | solution.py:219
  36.2 1.3 %collective-permute-start.4 = (f32[8,4096]{1,0:T(8,128)S(1)}, f32[8,4096]{1,0:T(8,128)S(1)}, u32[]{:S(2)}, u32[]{:S(2)}) collective-permute-start(f32[8,4096]{1,0:T(8,128)S(1)} %get-tuple-element.28.refs_3_), channel_id=1, source_target_pairs={{0,2},{1,3},{4,6},{5,7},{8,10},{9,11},{12,14},{13,15},{16,18},{17,... | collective-permute-start | bytes 393224 | tf_op jit(solution)/shard_map/ppermute | solution.py:213
  37.5 5.8 %all-to-all-done.1 = f32[8,8,384]{2,1,0:T(8,128)S(1)} async-done(((f32[8,8,384]{2,1,0:T(8,128)}), f32[8,8,384]{2,1,0:T(8,128)S(1)}, u32[]{:S(2)}, u32[]{:S(2)}) %all-to-all-start.1) | async-done | bytes 98336 | tf_op jit(solution)/shard_map/all_to_all | solution.py:219
  43.3 0.2 new_time_weights.1
  43.5 1.3 %collective-permute-start.3 = (f32[8,128]{1,0:T(8,128)S(1)}, f32[8,128]{1,0:T(8,128)S(1)}, u32[]{:S(2)}, u32[]{:S(2)}) collective-permute-start(f32[8,128]{1,0:T(8,128)S(1)} %get-tuple-element.27.refs_0_), channel_id=1, source_target_pairs={{0,2},{1,3},{4,6},{5,7},{8,10},{9,11},{12,14},{13,15},{16,18},{17,... | collective-permute-start | bytes 12296 | tf_op jit(solution)/shard_map/ppermute | solution.py:213
  44.8 1.9 %collective-permute-start.2 = (f32[8,128]{1,0:T(8,128)S(1)}, f32[8,128]{1,0:T(8,128)S(1)}, u32[]{:S(2)}, u32[]{:S(2)}) collective-permute-start(f32[8,128]{1,0:T(8,128)S(1)} %get-tuple-element.27.refs_0_), channel_id=1, source_target_pairs={{0,1},{1,0},{4,5},{5,4},{8,9},{9,8},{12,13},{13,12},{16,17},{17,16... | collective-permute-start | bytes 12296 | tf_op jit(solution)/shard_map/ppermute | solution.py:213
  46.7 0.0 collective-permute-done.4.refs_4_
  46.7 0.0 collective-permute-done.3.refs_2_
  46.7 1.1 %collective-permute-done.2.refs_1_ = f32[8,128]{1,0:T(8,128)S(1)} collective-permute-done((f32[8,128]{1,0:T(8,128)S(1)}, f32[8,128]{1,0:T(8,128)S(1)}, u32[]{:S(2)}, u32[]{:S(2)}) %collective-permute-start.2) | collective-permute-done | bytes 4128 | tf_op jit(solution)/shard_map/ppermute | solution.py:213
  47.8 0.8 %scale_weights.1 = (f32[8,4096]{1,0:T(8,128)}, f32[8,256]{1,0:T(8,128)}) custom-call(f32[8,128]{1,0:T(8,128)S(1)} %get-tuple-element.27.refs_0_, f32[8,128]{1,0:T(8,128)S(1)} %collective-permute-done.2.refs_1_, f32[8,128]{1,0:T(8,128)S(1)} %collective-permute-done.3.refs_2_, f32[8,4096]{1,0:T(8,128)S(1)} %get-tuple-element.28.refs_3_, ...), custom_call_target="tpu_custom_call" | custom-call | tf_op jit(solution)/shard_map/scale_weights/pallas_call | solution.py:222
Async XLA Ops:
  6.6 1.3 %copy-start = (bf16[4096,256]{1,0:T(8,128)(2,1)}, bf16[4096,256]{1,0:T(8,128)(2,1)S(1)}, u32[]{:S(2)}) copy-start(bf16[4096,256]{1,0:T(8,128)(2,1)S(1)} %get-tuple-element.18.low_ref.refs_3_) | copy-start | bytes 6291460
  8.0 14.8 %all-to-all-start = ((f32[8,8,640]{2,1,0:T(8,128)}), f32[8,8,640]{2,1,0:T(8,128)S(1)}, u32[]{:S(2)}, u32[]{:S(2)}) async-start(f32[8,8,640]{2,1,0:T(8,128)} %bitcast.3), calls=%async_computation | async-start | bytes 327680 | tf_op jit(solution)/shard_map/all_to_all | solution.py:219
  15.2 6.8 %collective-permute-start = (f32[8,4096]{1,0:T(8,128)S(1)}, f32[8,4096]{1,0:T(8,128)S(1)}, u32[]{:S(2)}, u32[]{:S(2)}) collective-permute-start(f32[8,4096]{1,0:T(8,128)S(1)} %get-tuple-element.19.cross), channel_id=1, source_target_pairs={{2,0},{3,1},{6,4},{7,5},{10,8},{11,9},{14,12},{15,13},{18,16},{19,... | collective-permute-start | bytes 393224 | tf_op jit(solution)/shard_map/ppermute | solution.py:253
  22.8 1.6 %copy-start.1 = (bf16[4096,256]{1,0:T(8,128)(2,1)S(1)}, bf16[4096,256]{1,0:T(8,128)(2,1)}, u32[]{:S(2)}) copy-start(bf16[4096,256]{1,0:T(8,128)(2,1)} %copy-done) | copy-start | bytes 6291460
  25.7 3.6 %collective-permute-start.1 = (f32[24,4224]{1,0:T(8,128)S(1)}, f32[24,4224]{1,0:T(8,128)S(1)}, u32[]{:S(2)}, u32[]{:S(2)}) collective-permute-start(f32[24,4224]{1,0:T(8,128)S(1)} %get-tuple-element.22.refs_0_), channel_id=1, source_target_pairs={{0,1},{1,0},{4,5},{5,4},{8,9},{9,8},{12,13},{13,12},{16,17},{17,16... | collective-permute-start | bytes 1216520 | tf_op jit(solution)/shard_map/ppermute | solution.py:213
  30.9 12.4 %all-to-all-start.1 = ((f32[8,8,384]{2,1,0:T(8,128)}), f32[8,8,384]{2,1,0:T(8,128)S(1)}, u32[]{:S(2)}, u32[]{:S(2)}) async-start(f32[8,8,384]{2,1,0:T(8,128)} %bitcast.5), calls=%async_computation.1 | async-start | bytes 196608 | tf_op jit(solution)/shard_map/all_to_all | solution.py:219
  36.2 10.5 %collective-permute-start.4 = (f32[8,4096]{1,0:T(8,128)S(1)}, f32[8,4096]{1,0:T(8,128)S(1)}, u32[]{:S(2)}, u32[]{:S(2)}) collective-permute-start(f32[8,4096]{1,0:T(8,128)S(1)} %get-tuple-element.28.refs_3_), channel_id=1, source_target_pairs={{0,2},{1,3},{4,6},{5,7},{8,10},{9,11},{12,14},{13,15},{16,18},{17,... | collective-permute-start | bytes 393224 | tf_op jit(solution)/shard_map/ppermute | solution.py:213
  43.5 3.2 %collective-permute-start.3 = (f32[8,128]{1,0:T(8,128)S(1)}, f32[8,128]{1,0:T(8,128)S(1)}, u32[]{:S(2)}, u32[]{:S(2)}) collective-permute-start(f32[8,128]{1,0:T(8,128)S(1)} %get-tuple-element.27.refs_0_), channel_id=1, source_target_pairs={{0,2},{1,3},{4,6},{5,7},{8,10},{9,11},{12,14},{13,15},{16,18},{17,... | collective-permute-start | bytes 12296 | tf_op jit(solution)/shard_map/ppermute | solution.py:213
  44.8 3.1 %collective-permute-start.2 = (f32[8,128]{1,0:T(8,128)S(1)}, f32[8,128]{1,0:T(8,128)S(1)}, u32[]{:S(2)}, u32[]{:S(2)}) collective-permute-start(f32[8,128]{1,0:T(8,128)S(1)} %get-tuple-element.27.refs_0_), channel_id=1, source_target_pairs={{0,1},{1,0},{4,5},{5,4},{8,9},{9,8},{12,13},{13,12},{16,17},{17,16... | collective-permute-start | bytes 12296 | tf_op jit(solution)/shard_map/ppermute | solution.py:213
where the time goes:
time: 49 us; the launch traced here: 48.6 us
  starting transfers between devices  20.2 us (41%)
  waiting for transfers between devices  14.9 us (30%)
  Pallas kernels  9.78 us (20%)
  local copies, waits for them, and re-layouts  2.92 us (6%)
  between operations  0.71 us (1%)
    all_to_all x2, starting transfers between devices, over_units(): lax.all_to_all(value, 'unit', split_axis=0, concat_axis=0, tiled=True)  12.5 us
    pallas_call x5, Pallas kernels, call(): pl.pallas_call(kernel, in_specs=[in_spec] * len(args), out_specs=[vmem] *...  9.78 us
    all_to_all x2, waiting for transfers between devices, over_units(): lax.all_to_all(value, 'unit', split_axis=0, concat_axis=0, tiled=True)  6.55 us
    ppermute x4, starting transfers between devices, spread(): return lax.ppermute(value, ('unit', 'day'), pairs)  6.43 us
    ppermute x1, waiting for transfers between devices, local(): post = lax.ppermute(cross, ('unit', 'day'), downward)  5.56 us
    unnamed x4, local copies, waits for them, and re-layouts  2.92 us
    ppermute x4, waiting for transfers between devices, spread(): return lax.ppermute(value, ('unit', 'day'), pairs)  2.82 us
    ppermute x1, starting transfers between devices, local(): post = lax.ppermute(cross, ('unit', 'day'), downward)  1.28 us
  transfers between devices with their start and end apart: 7, of which 5 were waited for; matrix products, arithmetic and copies ran while one was open for 0% of the time, Pallas kernels for 0%

commit v1 on v0

--- a/solution.py
+++ b/solution.py
@@ -65,7 +65,7 @@
     return device * shape[1] + lax.broadcasted_iota(jnp.int32, shape, 1)
 
 
-def first_kernel(all_count, copies_out, chunks, *refs):
+def first_kernel(all_count, chunks, *refs):
     arguments, refs = refs[:6], refs[6:]
     sums, cross, raised_units, raised_days, ends, high_ref, low_ref, *held, small_sems, sems = refs
     panel, held_panel = arguments[0], held[0]
@@ -119,18 +119,18 @@
         cross[:, here] = add_terms(days_dot(coef, high, low), groups)
     lane = lax.broadcasted_iota(jnp.int32, (groups, lanes), 1)
     norms = jnp.where(lane == 0, norm, jnp.where(lane == 1, treat_count, ctrl_count))
-    for i in range(copies_out):
-        here = pl.ds(i * groups, groups)
-        sums[here, :day_cols] = fitted
-        sums[here, day_cols : 2 * day_cols] = treat_sum
-        sums[here, 2 * day_cols :] = norms
-
-
-def second_kernel(unit_devices, chunks, sums, high_ref, low_ref, cross, post, raised_days, ends, pack, norms):
+    sums[:, :day_cols] = fitted
+    sums[:, day_cols : 2 * day_cols] = treat_sum
+    sums[:, 2 * day_cols :] = norms
+
+
+def second_kernel(chunks, sums, high_ref, low_ref, cross, post, raised_days, ends, pack, norms):
     groups, day_cols = raised_days.shape
     unit_rows = cross.shape[1]
     rows = unit_rows // chunks
-    total = tree_sum(sums[pl.ds(u * groups, groups), :] for u in range(unit_devices))
+    total = sums[0]
+    for other in range(1, sums.shape[0]):
+        total = total + sums[other]
     unit_norm = total[:, 2 * day_cols : 2 * day_cols + 1]
     treat_count = jnp.maximum(total[:, 2 * day_cols + 1 : 2 * day_cols + 2], 1.0)
     norms[...] = total[:, 2 * day_cols :]
@@ -146,7 +146,7 @@
     pack[:, unit_rows:] = jnp.broadcast_to(jnp.concatenate([time_norm] * 3, axis=0), (3 * groups, lanes))
 
 
-def third_kernel(half, copies_out, chunks, *refs):
+def third_kernel(half, chunks, *refs):
     parts, refs = refs[:half], refs[half:]
     high_ref, low_ref, norms, raised_units, raised_days, ends, scaled, lam, grads = refs
     groups, unit_rows = raised_units.shape
@@ -168,15 +168,15 @@
         shortfall = whole[groups : 2 * groups] / time_norm + whole[2 * groups :]
         left = left_of(jnp.where(raised > 0.0, shortfall, 0.0))
         time_grad += add_terms(rows_dot(left, high_ref[here, :], low_ref[here, :]), groups)
-    for i in range(copies_out):
-        here = pl.ds(i * groups, groups)
-        grads[here, :day_cols] = time_grad
-        grads[here, day_cols:] = jnp.broadcast_to(new_sum, (groups, lanes))
-
-
-def fourth_kernel(unit_devices, grads, lam, norms, moved, totals):
+    grads[:, :day_cols] = time_grad
+    grads[:, day_cols:] = jnp.broadcast_to(new_sum, (groups, lanes))
+
+
+def fourth_kernel(grads, lam, norms, moved, totals):
     groups, day_cols = lam.shape
-    total = tree_sum(grads[pl.ds(u * groups, groups), :] for u in range(unit_devices))
+    total = grads[0]
+    for other in range(1, grads.shape[0]):
+        total = total + grads[other]
     root = jnp.sqrt(jnp.maximum(norms[:, 2:3], 1.0))
     new = lam[...] * jnp.exp(total[:, :day_cols] * (-step_rate / root))
     moved[...] = new
@@ -215,8 +215,19 @@
     def over_days(value):
         return [value] + [spread(value, k, 0) for k in range(1, half)]
 
-    def over_units(value):
-        return lax.all_to_all(value, "unit", split_axis=0, concat_axis=0, tiled=True)
+    def gather_step(value, low, count):
+        starts = [u for u in range(unit_devices) if u // low % count == 0]
+        members = [[u + low * i for i in range(count)] for u in starts]
+        return lax.all_gather(value, "unit", axis_index_groups=members)
+
+    def over_units(value, digits):
+        low = 1
+        for count in digits:
+            if low > 1:
+                value = jnp.sum(value, axis=0)
+            value = gather_step(value, low, count)
+            low *= count
+        return value
 
     def call(kernel, shapes, name, args, in_spec=vmem, **more):
         return pl.pallas_call(
@@ -231,9 +242,9 @@
 
     arguments = (outcomes, cohort[None, :], pre_end[None, :], post_start[None, :], unit_logit, time_logit)
     sums, cross, raised_units, raised_days, ends, high, low = call(
-        functools.partial(first_kernel, day_devices * day_cols, unit_devices, chunks),
+        functools.partial(first_kernel, day_devices * day_cols, chunks),
         [
-            ((unit_devices * groups, 2 * day_cols + lanes), f32),
+            ((groups, 2 * day_cols + lanes), f32),
             ((groups, unit_rows), f32),
             ((groups, unit_rows), f32),
             ((groups, day_cols), f32),
@@ -251,29 +262,29 @@
         (u * day_devices + d + half, u * day_devices + d) for u in range(unit_devices) for d in range(half)
     ]
     post = lax.ppermute(cross, ("unit", "day"), downward)
-    all_sums = over_units(sums)
+    all_sums = over_units(sums, [2] * (unit_devices.bit_length() - 1))
     pack, norms = call(
-        functools.partial(second_kernel, unit_devices, chunks),
+        functools.partial(second_kernel, chunks),
         [((3 * groups, unit_rows + lanes), f32), ((groups, lanes), f32)],
         "unit_gradient",
         (all_sums, high, low, cross, post, raised_days, ends),
     )
     scaled, lam, grads = call(
-        functools.partial(third_kernel, half, unit_devices, chunks),
+        functools.partial(third_kernel, half, chunks),
         [
             ((groups, unit_rows), f32),
             ((groups, day_cols), f32),
-            ((unit_devices * groups, day_cols + lanes), f32),
+            ((groups, day_cols + lanes), f32),
         ],
         "time_gradient",
         (*over_days(pack), high, low, norms, raised_units, raised_days, ends),
     )
     sent_scaled = spread(scaled, 0, half)
     moved, totals = call(
-        functools.partial(fourth_kernel, unit_devices),
+        fourth_kernel,
         [((groups, day_cols), f32), ((groups, lanes), f32)],
         "new_time_weights",
-        (over_units(grads), lam, norms),
+        (over_units(grads, [2, unit_devices // 2]), lam, norms),
     )
     sent_totals = spread(totals, 0, half)
     return call(

time: 49 us -> 53.9 us (1.100)
  blocking collectives: 0 us -> 33.4 us
  starting transfers between devices: 20.2 us -> 8.06 us
  waiting for transfers between devices: 14.9 us -> 2.83 us
  local copies, waits for them, and re-layouts: 2.92 us -> 0 us
  Pallas kernels: 9.78 us -> 8.59 us
    all_gather x0 -> x5, blocking collectives: none -> 33.4 us  [gather_step(): return lax.all_gather(value, 'unit', axis_index_groups=members)]
    all_to_all x2 -> x0, starting transfers between devices: 12.5 us -> none  [over_units(): lax.all_to_all(value, 'unit', split_axis=0, concat_axis=0, tiled=True)]
    all_to_all x2 -> x0, waiting for transfers between devices: 6.55 us -> none  [over_units(): lax.all_to_all(value, 'unit', split_axis=0, concat_axis=0, tiled=True)]
    ppermute x1, waiting for transfers between devices: 5.56 us -> 0.01 us  [local(): post = lax.ppermute(cross, ('unit', 'day'), downward)]
    unnamed x4 -> x0, local copies, waits for them, and re-layouts: 2.92 us -> none
    pallas_call x5, Pallas kernels: 9.78 us -> 8.59 us  [call(): pl.pallas_call(kernel, in_specs=[in_spec] * len(args), out_specs=[vmem] *...]
  transfers between devices with their start and end apart: 7 -> 5, of which waited for: 5 -> 2; matrix products, arithmetic and copies ran while one was open for 0% -> 0% of each run, Pallas kernels for 0% -> 0%
where the time goes in v1:
time: 53.9 us; the launch traced here: 53.6 us
  blocking collectives  33.4 us (62%)
  Pallas kernels  8.59 us (16%)
  starting transfers between devices  8.06 us (15%)
  waiting for transfers between devices  2.83 us (5%)
  between operations  0.71 us (1%)
    all_gather x5, blocking collectives, gather_step(): return lax.all_gather(value, 'unit', axis_index_groups=members)  33.4 us
    pallas_call x5, Pallas kernels, call(): pl.pallas_call(kernel, in_specs=[in_spec] * len(args), out_specs=[vmem] *...  8.59 us
    ppermute x4, starting transfers between devices, spread(): return lax.ppermute(value, ('unit', 'day'), pairs)  6.76 us
    ppermute x4, waiting for transfers between devices, spread(): return lax.ppermute(value, ('unit', 'day'), pairs)  2.83 us
    ppermute x1, starting transfers between devices, local(): post = lax.ppermute(cross, ('unit', 'day'), downward)  1.29 us
  transfers between devices with their start and end apart: 5, of which 2 were waited for; matrix products, arithmetic and copies ran while one was open for 0% of the time, Pallas kernels for 0%

profile of v1, /device:TPU:0, one launch (start us, length us, event | category | flops | bytes accessed | tf_op | source)
XLA Modules:
  0.0 53.6 jit_solution(12076543376570661334)
XLA Ops:
  0.6 5.5 %first_products.1 = (f32[8,640]{1,0:T(8,128)S(1)}, f32[8,4096]{1,0:T(8,128)S(1)}, f32[8,4096]{1,0:T(8,128)S(1)}, f32[8,256]{1,0:T(8,128)S(1)}, f32[8,128]{1,0:T(...) custom-call(f32[4096,256]{1,0:T(8,128)} %refs_0_.1, s32[1,4096]{1,0:T(1,128)} %bitcast.13, ...), custom_call_target="tpu_custom_call" | custom-call | tf_op jit(solution)/shard_map/first_products/pallas_call | solution.py:233
  6.1 1.3 %collective-permute-start = (f32[8,4096]{1,0:T(8,128)S(1)}, f32[8,4096]{1,0:T(8,128)S(1)}, u32[]{:S(2)}, u32[]{:S(2)}) collective-permute-start(f32[8,4096]{1,0:T(8,128)S(1)} %get-tuple-element.19.cross), channel_id=1, source_target_pairs={{2,0},{3,1},{6,4},{7,5},{10,8},{11,9},{14,12},{15,13},{18,16},{19,... | collective-permute-start | bytes 393224 | tf_op jit(solution)/shard_map/ppermute | solution.py:264
  7.4 5.4 %all-gather = f32[16,640]{1,0:T(8,128)S(1)} all-gather(f32[8,640]{1,0:T(8,128)S(1)} %get-tuple-element.16), channel_id=2, replica_groups={{0,4},{8,12},{16,20},{24,28},{1,5},{9,13},{17,21},{25,29},{2,6},{10,14}..., dimensions={0}, use_global_device_ids=true | all-gather | bytes 61440 | tf_op jit(solution)/shard_map/all_gather | solution.py:221
  12.8 4.5 %all-gather.1 = f32[16,640]{1,0:T(8,128)S(1)} all-gather(f32[8,640]{1,0:T(8,128)S(1)} %bitcast_reduce_fusion.1), channel_id=3, replica_groups={{0,8},{4,12},{16,24},{20,28},{1,9},{5,13},{17,25},{21,29},{2,10},{6,14}..., dimensions={0}, use_global_device_ids=true | all-gather | bytes 61440 | tf_op jit(solution)/shard_map/all_gather | solution.py:221
  17.3 5.5 %all-gather.2 = f32[16,640]{1,0:T(8,128)S(1)} all-gather(f32[8,640]{1,0:T(8,128)S(1)} %bitcast_reduce_fusion), channel_id=4, replica_groups={{0,16},{4,20},{8,24},{12,28},{1,17},{5,21},{9,25},{13,29},{2,18},{6,22}..., dimensions={0}, use_global_device_ids=true | all-gather | bytes 61440 | tf_op jit(solution)/shard_map/all_gather | solution.py:221
  22.8 0.0 collective-permute-done.post
  22.8 1.3 %unit_gradient.1 = (f32[24,4224]{1,0:T(8,128)S(1)}, f32[8,128]{1,0:T(8,128)S(1)}) custom-call(f32[2,8,640]{2,1,0:T(8,128)S(1)} %bitcast.12, bf16[4096,256]{1,0:T(8,128)(2,1)S(1)} %get-tuple-element.17.high_ref.refs_2_, bf16[4096,256]{1,0:T(8,128)(2,1)S(1)} %get-tuple-element.18.low_ref.refs_3_, f32[8,4096]{1,0:T(8,128)S(1)} %get-tuple-element.19.cross, ...), custom_call_target="tpu_custom_call" | custom-call | tf_op jit(solution)/shard_map/unit_gradient/pallas_call | solution.py:233
  24.1 1.9 %collective-permute-start.1 = (f32[24,4224]{1,0:T(8,128)S(1)}, f32[24,4224]{1,0:T(8,128)S(1)}, u32[]{:S(2)}, u32[]{:S(2)}) collective-permute-start(f32[24,4224]{1,0:T(8,128)S(1)} %get-tuple-element.22.refs_0_), channel_id=1, source_target_pairs={{0,1},{1,0},{4,5},{5,4},{8,9},{9,8},{12,13},{13,12},{16,17},{17,16... | collective-permute-start | bytes 1216520 | tf_op jit(solution)/shard_map/ppermute | solution.py:213
  26.0 1.7 %collective-permute-done.1.refs_1_ = f32[24,4224]{1,0:T(8,128)S(1)} collective-permute-done((f32[24,4224]{1,0:T(8,128)S(1)}, f32[24,4224]{1,0:T(8,128)S(1)}, u32[]{:S(2)}, u32[]{:S(2)}) %collective-permute-start.1) | collective-permute-done | bytes 405536 | tf_op jit(solution)/shard_map/ppermute | solution.py:213
  27.7 0.9 %time_gradient.1 = (f32[8,4096]{1,0:T(8,128)S(1)}, f32[8,256]{1,0:T(8,128)S(1)}, f32[8,384]{1,0:T(8,128)S(1)}) custom-call(f32[24,4224]{1,0:T(8,128)S(1)} %get-tuple-element.22.refs_0_, f32[24,4224]{1,0:T(8,128)S(1)} %collective-permute-done.1.refs_1_, bf16[4096,256]{1,0:T(8,128)(2,1)S(1)} %get-tuple-element.17.high_ref.refs_2_, ...), custom_call_target="tpu_custom_call" | custom-call | tf_op jit(solution)/shard_map/time_gradient/pallas_call | solution.py:233
  28.6 4.4 %all-gather.3 = f32[16,384]{1,0:T(8,128)S(1)} all-gather(f32[8,384]{1,0:T(8,128)S(1)} %get-tuple-element.25), channel_id=5, replica_groups={{0,4},{8,12},{16,20},{24,28},{1,5},{9,13},{17,21},{25,29},{2,6},{10,14}..., dimensions={0}, use_global_device_ids=true | all-gather | bytes 36864 | tf_op jit(solution)/shard_map/all_gather | solution.py:221
  33.0 1.6 %collective-permute-start.4 = (f32[8,4096]{1,0:T(8,128)S(1)}, f32[8,4096]{1,0:T(8,128)S(1)}, u32[]{:S(2)}, u32[]{:S(2)}) collective-permute-start(f32[8,4096]{1,0:T(8,128)S(1)} %get-tuple-element.28.refs_3_), channel_id=1, source_target_pairs={{0,2},{1,3},{4,6},{5,7},{8,10},{9,11},{12,14},{13,15},{16,18},{17,... | collective-permute-start | bytes 393224 | tf_op jit(solution)/shard_map/ppermute | solution.py:213
  34.7 13.7 %all-gather.4 = f32[32,384]{1,0:T(8,128)S(1)} all-gather(f32[8,384]{1,0:T(8,128)S(1)} %bitcast_reduce_fusion.2), channel_id=6, replica_groups={{0,8,16,24},{4,12,20,28},{1,9,17,25},{5,13,21,29},{2,10,18,26},{6,14,22..., dimensions={0}, use_global_device_ids=true | all-gather | bytes 61440 | tf_op jit(solution)/shard_map/all_gather | solution.py:221
  48.3 0.2 new_time_weights.1
  48.5 1.3 %collective-permute-start.3 = (f32[8,128]{1,0:T(8,128)S(1)}, f32[8,128]{1,0:T(8,128)S(1)}, u32[]{:S(2)}, u32[]{:S(2)}) collective-permute-start(f32[8,128]{1,0:T(8,128)S(1)} %get-tuple-element.27.refs_0_), channel_id=1, source_target_pairs={{0,2},{1,3},{4,6},{5,7},{8,10},{9,11},{12,14},{13,15},{16,18},{17,... | collective-permute-start | bytes 12296 | tf_op jit(solution)/shard_map/ppermute | solution.py:213
  49.8 1.9 %collective-permute-start.2 = (f32[8,128]{1,0:T(8,128)S(1)}, f32[8,128]{1,0:T(8,128)S(1)}, u32[]{:S(2)}, u32[]{:S(2)}) collective-permute-start(f32[8,128]{1,0:T(8,128)S(1)} %get-tuple-element.27.refs_0_), channel_id=1, source_target_pairs={{0,1},{1,0},{4,5},{5,4},{8,9},{9,8},{12,13},{13,12},{16,17},{17,16... | collective-permute-start | bytes 12296 | tf_op jit(solution)/shard_map/ppermute | solution.py:213
  51.7 0.0 collective-permute-done.3.refs_2_
  51.7 1.1 %collective-permute-done.2.refs_1_ = f32[8,128]{1,0:T(8,128)S(1)} collective-permute-done((f32[8,128]{1,0:T(8,128)S(1)}, f32[8,128]{1,0:T(8,128)S(1)}, u32[]{:S(2)}, u32[]{:S(2)}) %collective-permute-start.2) | collective-permute-done | bytes 4128 | tf_op jit(solution)/shard_map/ppermute | solution.py:213
  52.8 0.0 collective-permute-done.4.refs_4_
  52.8 0.8 %scale_weights.1 = (f32[8,4096]{1,0:T(8,128)}, f32[8,256]{1,0:T(8,128)}) custom-call(f32[8,128]{1,0:T(8,128)S(1)} %get-tuple-element.27.refs_0_, f32[8,128]{1,0:T(8,128)S(1)} %collective-permute-done.2.refs_1_, f32[8,128]{1,0:T(8,128)S(1)} %collective-permute-done.3.refs_2_, f32[8,4096]{1,0:T(8,128)S(1)} %get-tuple-element.28.refs_3_, ...), custom_call_target="tpu_custom_call" | custom-call | tf_op jit(solution)/shard_map/scale_weights/pallas_call | solution.py:233
  (3 shorter events, 0.0 us)
Async XLA Ops:
  6.1 16.7 %collective-permute-start = (f32[8,4096]{1,0:T(8,128)S(1)}, f32[8,4096]{1,0:T(8,128)S(1)}, u32[]{:S(2)}, u32[]{:S(2)}) collective-permute-start(f32[8,4096]{1,0:T(8,128)S(1)} %get-tuple-element.19.cross), channel_id=1, source_target_pairs={{2,0},{3,1},{6,4},{7,5},{10,8},{11,9},{14,12},{15,13},{18,16},{19,... | collective-permute-start | bytes 393224 | tf_op jit(solution)/shard_map/ppermute | solution.py:264
  24.1 3.6 %collective-permute-start.1 = (f32[24,4224]{1,0:T(8,128)S(1)}, f32[24,4224]{1,0:T(8,128)S(1)}, u32[]{:S(2)}, u32[]{:S(2)}) collective-permute-start(f32[24,4224]{1,0:T(8,128)S(1)} %get-tuple-element.22.refs_0_), channel_id=1, source_target_pairs={{0,1},{1,0},{4,5},{5,4},{8,9},{9,8},{12,13},{13,12},{16,17},{17,16... | collective-permute-start | bytes 1216520 | tf_op jit(solution)/shard_map/ppermute | solution.py:213
  33.0 19.8 %collective-permute-start.4 = (f32[8,4096]{1,0:T(8,128)S(1)}, f32[8,4096]{1,0:T(8,128)S(1)}, u32[]{:S(2)}, u32[]{:S(2)}) collective-permute-start(f32[8,4096]{1,0:T(8,128)S(1)} %get-tuple-element.28.refs_3_), channel_id=1, source_target_pairs={{0,2},{1,3},{4,6},{5,7},{8,10},{9,11},{12,14},{13,15},{16,18},{17,... | collective-permute-start | bytes 393224 | tf_op jit(solution)/shard_map/ppermute | solution.py:213
  48.5 3.2 %collective-permute-start.3 = (f32[8,128]{1,0:T(8,128)S(1)}, f32[8,128]{1,0:T(8,128)S(1)}, u32[]{:S(2)}, u32[]{:S(2)}) collective-permute-start(f32[8,128]{1,0:T(8,128)S(1)} %get-tuple-element.27.refs_0_), channel_id=1, source_target_pairs={{0,2},{1,3},{4,6},{5,7},{8,10},{9,11},{12,14},{13,15},{16,18},{17,... | collective-permute-start | bytes 12296 | tf_op jit(solution)/shard_map/ppermute | solution.py:213
  49.8 3.1 %collective-permute-start.2 = (f32[8,128]{1,0:T(8,128)S(1)}, f32[8,128]{1,0:T(8,128)S(1)}, u32[]{:S(2)}, u32[]{:S(2)}) collective-permute-start(f32[8,128]{1,0:T(8,128)S(1)} %get-tuple-element.27.refs_0_), channel_id=1, source_target_pairs={{0,1},{1,0},{4,5},{5,4},{8,9},{9,8},{12,13},{13,12},{16,17},{17,16... | collective-permute-start | bytes 12296 | tf_op jit(solution)/shard_map/ppermute | solution.py:213

commit v2 on v1

--- a/solution.py
+++ b/solution.py
@@ -67,7 +67,7 @@
 
 def first_kernel(all_count, chunks, *refs):
     arguments, refs = refs[:6], refs[6:]
-    sums, cross, raised_units, raised_days, ends, high_ref, low_ref, *held, small_sems, sems = refs
+    sums, raised_units, raised_days, coef, ends, high_ref, low_ref, *held, left_ref, small_sems, sems = refs
     panel, held_panel = arguments[0], held[0]
     groups, day_cols = held[5].shape
     unit_rows = panel.shape[0]
@@ -86,51 +86,56 @@
     for copy in small:
         copy.wait()
     cohort, pre_row, post_row, unit_logit, time_logit = held[1:]
+    label = lax.broadcasted_iota(jnp.int32, (groups, unit_rows), 0)
+    treated = jnp.where(cohort[...] == label, 1.0, 0.0)
+    control = jnp.where(cohort[...] > label, 1.0, 0.0)
+    raised = jnp.exp(unit_logit[...]) * control
+    raised_units[...] = raised
+    left_ref[...] = left_of(raised, treated)
+    lane = lax.broadcasted_iota(jnp.int32, (groups, lanes), 1)
+    sums[:, 2 * day_cols :] = jnp.where(
+        lane == 0,
+        jnp.sum(raised, axis=1, keepdims=True),
+        jnp.where(
+            lane == 1, jnp.sum(treated, axis=1, keepdims=True), jnp.sum(control, axis=1, keepdims=True)
+        ),
+    )
     pre_end, post_start = column(pre_row), column(post_row)
     ends[...] = jnp.broadcast_to(pre_end.astype(f32), ends.shape)
     days = days_of(lax.axis_index("day"), (groups, day_cols))
     raised_time = jnp.where(days < pre_end, jnp.exp(time_logit[...]), 0.0)
     raised_days[...] = raised_time
     after_len = (all_count - post_start).astype(f32)
-    coef = left_of(raised_time - jnp.where(days >= post_start, 1.0, 0.0) / after_len)
-    fitted = jnp.zeros((groups, day_cols), f32)
-    treat_sum = jnp.zeros((groups, day_cols), f32)
-    norm = jnp.zeros((groups, 1), f32)
-    treat_count = jnp.zeros((groups, 1), f32)
-    ctrl_count = jnp.zeros((groups, 1), f32)
-    label = lax.broadcasted_iota(jnp.int32, (groups, rows), 0)
-    for chunk in range(chunks):
-        here = pl.ds(chunk * rows, rows)
-        treated = jnp.where(cohort[:, here] == label, 1.0, 0.0)
-        control = jnp.where(cohort[:, here] > label, 1.0, 0.0)
-        raised = jnp.exp(unit_logit[:, here]) * control
-        raised_units[:, here] = raised
-        left = left_of(raised, treated)
-        norm += jnp.sum(raised, axis=1, keepdims=True)
-        treat_count += jnp.sum(treated, axis=1, keepdims=True)
-        ctrl_count += jnp.sum(control, axis=1, keepdims=True)
+    coef[...] = left_of(raised_time - jnp.where(days >= post_start, 1.0, 0.0) / after_len)
+    product = jnp.zeros((4 * groups, day_cols), f32)
+    for chunk in range(chunks):
+        here = pl.ds(chunk * rows, rows)
         copies[chunk].wait()
         high, low = split_panel(held_panel[here, :])
         high_ref[here, :] = high
         low_ref[here, :] = low
-        product = rows_dot(left, high, low)
-        fitted += add_terms(product, groups)
-        treat_sum += product[3 * groups :]
-        cross[:, here] = add_terms(days_dot(coef, high, low), groups)
-    lane = lax.broadcasted_iota(jnp.int32, (groups, lanes), 1)
-    norms = jnp.where(lane == 0, norm, jnp.where(lane == 1, treat_count, ctrl_count))
-    sums[:, :day_cols] = fitted
-    sums[:, day_cols : 2 * day_cols] = treat_sum
-    sums[:, 2 * day_cols :] = norms
-
-
-def second_kernel(chunks, sums, high_ref, low_ref, cross, post, raised_days, ends, pack, norms):
+        product += rows_dot(left_ref[:, here], high, low)
+    sums[:, :day_cols] = add_terms(product, groups)
+    sums[:, day_cols : 2 * day_cols] = product[3 * groups :]
+
+
+def cross_kernel(chunks, coef, high_ref, low_ref, cross):
+    groups, unit_rows = cross.shape
+    rows = unit_rows // chunks
+    for chunk in range(chunks):
+        here = pl.ds(chunk * rows, rows)
+        cross[:, here] = add_terms(days_dot(coef[...], high_ref[here, :], low_ref[here, :]), groups)
+
+
+def add_kernel(left, right, *refs):
+    refs[-1][...] = left[...] + right[...]
+
+
+def second_kernel(chunks, sums, other_sums, high_ref, low_ref, cross, post, raised_days, ends, pack, norms):
     groups, day_cols = raised_days.shape
     unit_rows = cross.shape[1]
     rows = unit_rows // chunks
-    total = sums[0]
-    for other in range(1, sums.shape[0]):
-        total = total + sums[other]
+    total = sums[...] + other_sums[...]
     unit_norm = total[:, 2 * day_cols : 2 * day_cols + 1]
     treat_count = jnp.maximum(total[:, 2 * day_cols + 1 : 2 * day_cols + 2], 1.0)
     norms[...] = total[:, 2 * day_cols :]
@@ -172,11 +177,9 @@
     grads[:, day_cols:] = jnp.broadcast_to(new_sum, (groups, lanes))
 
 
-def fourth_kernel(grads, lam, norms, moved, totals):
+def fourth_kernel(grads, other_grads, lam, norms, moved, totals):
     groups, day_cols = lam.shape
-    total = grads[0]
-    for other in range(1, grads.shape[0]):
-        total = total + grads[other]
+    total = grads[...] + other_grads[...]
     root = jnp.sqrt(jnp.maximum(norms[:, 2:3], 1.0))
     new = lam[...] * jnp.exp(total[:, :day_cols] * (-step_rate / root))
     moved[...] = new
@@ -203,36 +206,40 @@
     assert half * 2 == day_devices and half & (half - 1) == 0
     assert unit_devices & (unit_devices - 1) == 0
     chunks = 8
+    beside = pl.CostEstimate(flops=10**10, bytes_accessed=0, transcendentals=0)
     vmem = pl.BlockSpec(memory_space=pltpu.VMEM)
     hbm = pl.BlockSpec(memory_space=pltpu.HBM)
 
-    def spread(value, day_xor, up):
+    def spread(value, unit_xor, day_xor, up):
         pairs = [
-            (u * day_devices + d, u * day_devices + (d ^ day_xor) + up) for u in range(unit_devices) for d in range(half)
+            (u * day_devices + d, (u ^ unit_xor) * day_devices + (d ^ day_xor) + up)
+            for u in range(unit_devices)
+            for d in range(half)
         ]
         return lax.ppermute(value, ("unit", "day"), pairs)
 
     def over_days(value):
-        return [value] + [spread(value, k, 0) for k in range(1, half)]
-
-    def gather_step(value, low, count):
-        starts = [u for u in range(unit_devices) if u // low % count == 0]
-        members = [[u + low * i for i in range(count)] for u in starts]
-        return lax.all_gather(value, "unit", axis_index_groups=members)
-
-    def over_units(value, digits):
-        low = 1
-        for count in digits:
-            if low > 1:
-                value = jnp.sum(value, axis=0)
-            value = gather_step(value, low, count)
-            low *= count
-        return value
-
-    def call(kernel, shapes, name, args, in_spec=vmem, **more):
+        return [value] + [spread(value, 0, k, 0) for k in range(1, half)]
+
+    def over_units(value, after=()):
+        weight = 1
+        while 2 * weight < unit_devices:
+            args = (value, spread(value, weight, 0, 0), *after)
+            (value,) = call(
+                add_kernel,
+                [(value.shape, f32)],
+                "add_halves",
+                args,
+                in_specs=[vmem, vmem] + [pl.BlockSpec(memory_space=pl.ANY)] * len(after),
+                cost_estimate=beside,
+            )
+            weight, after = 2 * weight, ()
+        return value, spread(value, weight, 0, 0)
+
+    def call(kernel, shapes, name, args, in_specs=None, **more):
         return pl.pallas_call(
             kernel,
-            in_specs=[in_spec] * len(args),
+            in_specs=in_specs or [vmem] * len(args),
             out_specs=[vmem] * len(shapes),
             out_shape=[jax.ShapeDtypeStruct(shape, kind) for shape, kind in shapes],
             compiler_params=params,
@@ -241,33 +248,46 @@
         )(*args)
 
     arguments = (outcomes, cohort[None, :], pre_end[None, :], post_start[None, :], unit_logit, time_logit)
-    sums, cross, raised_units, raised_days, ends, high, low = call(
-        functools.partial(first_kernel, day_devices * day_cols, chunks),
+    sums, raised_units, raised_days, coef, ends, high, low = call(
+        functools.partial(first_kernel, day_devices * day_cols, 4),
         [
             ((groups, 2 * day_cols + lanes), f32),
             ((groups, unit_rows), f32),
-            ((groups, unit_rows), f32),
             ((groups, day_cols), f32),
+            ((4 * groups, day_cols), bf16),
             ((groups, lanes), f32),
             ((unit_rows, day_cols), bf16),
             ((unit_rows, day_cols), bf16),
         ],
-        "first_products",
+        "first_product",
         [pltpu.with_memory_space_constraint(argument, pltpu.HBM) for argument in arguments],
-        in_spec=hbm,
+        in_specs=[hbm] * len(arguments),
         scratch_shapes=[pltpu.VMEM(argument.shape, argument.dtype) for argument in arguments]
-        + [pltpu.SemaphoreType.DMA((5,)), pltpu.SemaphoreType.DMA((chunks,))],
+        + [
+            pltpu.VMEM((4 * groups, unit_rows), bf16),
+            pltpu.SemaphoreType.DMA((5,)),
+            pltpu.SemaphoreType.DMA((4,)),
+        ],
+    )
+    (cross,) = call(
+        functools.partial(cross_kernel, chunks),
+        [((groups, unit_rows), f32)],
+        "time_product",
+        (coef, high, low),
+        cost_estimate=pl.CostEstimate(
+            flops=4 * 32 * unit_rows * day_cols, bytes_accessed=4 * unit_rows * day_cols, transcendentals=0
+        ),
     )
     downward = [
         (u * day_devices + d + half, u * day_devices + d) for u in range(unit_devices) for d in range(half)
     ]
     post = lax.ppermute(cross, ("unit", "day"), downward)
-    all_sums = over_units(sums, [2] * (unit_devices.bit_length() - 1))
+    all_sums = over_units(sums, (cross,))
     pack, norms = call(
         functools.partial(second_kernel, chunks),
         [((3 * groups, unit_rows + lanes), f32), ((groups, lanes), f32)],
         "unit_gradient",
-        (all_sums, high, low, cross, post, raised_days, ends),
+        (*all_sums, high, low, cross, post, raised_days, ends),
     )
     scaled, lam, grads = call(
         functools.partial(third_kernel, half, chunks),
@@ -279,19 +299,20 @@
         "time_gradient",
         (*over_days(pack), high, low, norms, raised_units, raised_days, ends),
     )
-    sent_scaled = spread(scaled, 0, half)
+    sent_scaled = spread(scaled, 0, 0, half)
     moved, totals = call(
         fourth_kernel,
         [((groups, day_cols), f32), ((groups, lanes), f32)],
         "new_time_weights",
-        (over_units(grads, [2, unit_devices // 2]), lam, norms),
-    )
-    sent_totals = spread(totals, 0, half)
+        (*over_units(grads), lam, norms),
+    )
+    all_totals = over_days(totals)
+    sent_totals = spread(totals, 0, 0, half)
     return call(
         functools.partial(fifth_kernel, half),
         [((groups, unit_rows), f32), ((groups, day_cols), f32)],
         "scale_weights",
-        (*over_days(totals), sent_totals, scaled, sent_scaled, moved, ends),
+        (*all_totals, sent_totals, scaled, sent_scaled, moved, ends),
     )
 
 

time: 53.9 us -> 52.3 us (0.970)
  blocking collectives: 33.4 us -> 0 us
  starting transfers between devices: 8.06 us -> 33.8 us
  waiting for transfers between devices: 2.83 us -> 9.47 us
  Pallas kernels: 8.59 us -> 7.78 us
    all_gather x5 -> x0, blocking collectives: 33.4 us -> none  [gather_step(): return lax.all_gather(value, 'unit', axis_index_groups=members)]
    ppermute x4 -> x10, starting transfers between devices: 6.76 us -> 32.6 us  [spread(): return lax.ppermute(value, ('unit', 'day'), pairs)]
    ppermute x4 -> x10, waiting for transfers between devices: 2.83 us -> 9.47 us  [spread(): return lax.ppermute(value, ('unit', 'day'), pairs)]
    pallas_call x5 -> x10, Pallas kernels: 8.59 us -> 7.78 us  [call(): pl.pallas_call(kernel, in_specs=in_specs or [vmem] * len(args), out_specs...]
  transfers between devices with their start and end apart: 5 -> 11, of which waited for: 2 -> 8; matrix products, arithmetic and copies ran while one was open for 0% -> 0% of each run, Pallas kernels for 0% -> 3%
where the time goes in v2:
time: 52.3 us; the launch traced here: 51.8 us
  starting transfers between devices  33.8 us (65%)
  waiting for transfers between devices  9.47 us (18%)
  Pallas kernels  7.78 us (15%)
  between operations  0.75 us (1%)
    ppermute x10, starting transfers between devices, spread(): return lax.ppermute(value, ('unit', 'day'), pairs)  32.6 us
    ppermute x10, waiting for transfers between devices, spread(): return lax.ppermute(value, ('unit', 'day'), pairs)  9.47 us
    pallas_call x10, Pallas kernels, call(): pl.pallas_call(kernel, in_specs=in_specs or [vmem] * len(args), out_specs...  7.78 us
    ppermute x1, starting transfers between devices, local(): post = lax.ppermute(cross, ('unit', 'day'), downward)  1.29 us
  transfers between devices with their start and end apart: 11, of which 8 were waited for; matrix products, arithmetic and copies ran while one was open for 0% of the time, Pallas kernels for 3%

profile of v2, /device:TPU:0, one launch (start us, length us, event | category | flops | bytes accessed | tf_op | source)
XLA Modules:
  0.0 51.8 jit_solution(797427895446549992)
XLA Ops:
  0.6 3.4 %first_product.1 = (f32[8,640]{1,0:T(8,128)S(1)}, f32[8,4096]{1,0:T(8,128)S(1)}, f32[8,256]{1,0:T(8,128)S(1)}, bf16[32,256]{1,0:T(8,128)(2,1)S(1)}, f32[8,128]{1...) custom-call(f32[4096,256]{1,0:T(8,128)} %refs_0_.1, s32[1,4096]{1,0:T(1,128)} %bitcast.3, ...), custom_call_target="tpu_custom_call" | custom-call | tf_op jit(solution)/shard_map/first_product/pallas_call | solution.py:240
  4.0 4.8 %collective-permute-start = (f32[8,640]{1,0:T(8,128)S(1)}, f32[8,640]{1,0:T(8,128)S(1)}, u32[]{:S(2)}, u32[]{:S(2)}) collective-permute-start(f32[8,640]{1,0:T(8,128)S(1)} %get-tuple-element.16.left), channel_id=1, source_target_pairs={{0,4},{1,5},{4,0},{5,1},{8,12},{9,13},{12,8},{13,9},{16,20},{17,21... | collective-permute-start | bytes 61448 | tf_op jit(solution)/shard_map/ppermute | solution.py:219
  8.9 1.3 %time_product.1.refs_0_.cross = f32[8,4096]{1,0:T(8,128)S(1)} custom-call(bf16[32,256]{1,0:T(8,128)(2,1)S(1)} %get-tuple-element.17.coef, bf16[4096,256]{1,0:T(8,128)(2,1)S(1)} %get-tuple-element.18.high_ref.refs_2_, bf16[4096,256]{1,0:T(8,128)(2,1)S(1)} %get-tuple-element.19.low_ref.refs_3_), custom_call_target="tpu_custom_call" | custom-call | flops 134217728 | bytes 4194304 | tf_op jit(solution)/shard_map/time_product/pallas_call | solution.py:240
  10.1 0.5 collective-permute-done.right
  10.6 4.0 %collective-permute-start.1 = (f32[8,640]{1,0:T(8,128)S(1)}, f32[8,640]{1,0:T(8,128)S(1)}, u32[]{:S(2)}, u32[]{:S(2)}) collective-permute-start(f32[8,640]{1,0:T(8,128)S(1)} %add_halves.4.left), channel_id=1, source_target_pairs={{0,8},{1,9},{4,12},{5,13},{8,0},{9,1},{12,4},{13,5},{16,24},{17,25... | collective-permute-start | bytes 61448 | tf_op jit(solution)/shard_map/ppermute | solution.py:219
  14.6 1.3 %collective-permute-start.3 = (f32[8,4096]{1,0:T(8,128)S(1)}, f32[8,4096]{1,0:T(8,128)S(1)}, u32[]{:S(2)}, u32[]{:S(2)}) collective-permute-start(f32[8,4096]{1,0:T(8,128)S(1)} %time_product.1.refs_0_.cross), channel_id=1, source_target_pairs={{2,0},{3,1},{6,4},{7,5},{10,8},{11,9},{14,12},{15,13},{18,16},{19,... | collective-permute-start | bytes 393224 | tf_op jit(solution)/shard_map/ppermute | solution.py:284
  15.9 0.4 collective-permute-done.1.right
  16.4 4.9 %collective-permute-start.2 = (f32[8,640]{1,0:T(8,128)S(1)}, f32[8,640]{1,0:T(8,128)S(1)}, u32[]{:S(2)}, u32[]{:S(2)}) collective-permute-start(f32[8,640]{1,0:T(8,128)S(1)} %add_halves.5.sums), channel_id=1, source_target_pairs={{0,16},{1,17},{4,20},{5,21},{8,24},{9,25},{12,28},{13,29},{16,0},{... | collective-permute-start | bytes 61448 | tf_op jit(solution)/shard_map/ppermute | solution.py:219
  21.3 1.7 %collective-permute-done.2.other_sums = f32[8,640]{1,0:T(8,128)S(1)} collective-permute-done((f32[8,640]{1,0:T(8,128)S(1)}, f32[8,640]{1,0:T(8,128)S(1)}, u32[]{:S(2)}, u32[]{:S(2)}) %collective-permute-start.2) | collective-permute-done | bytes 20512 | tf_op jit(solution)/shard_map/ppermute | solution.py:219
  23.0 0.0 collective-permute-done.3.post
  23.0 1.3 %unit_gradient.1 = (f32[24,4224]{1,0:T(8,128)S(1)}, f32[8,128]{1,0:T(8,128)S(1)}) custom-call(f32[8,640]{1,0:T(8,128)S(1)} %add_halves.5.sums, f32[8,640]{1,0:T(8,128)S(1)} %collective-permute-done.2.other_sums, bf16[4096,256]{1,0:T(8,128)(2,1)S(1)} %get-tuple-element.18.high_ref.refs_2_, bf16[4096,256]{1,0:T(8,128)(2,1)S(1)} %get-tuple-element.19.low_ref.refs_3_, ...), custom_call_target="tpu_custom_call" | custom-call | tf_op jit(solution)/shard_map/unit_gradient/pallas_call | solution.py:240
  24.4 1.9 %collective-permute-start.4 = (f32[24,4224]{1,0:T(8,128)S(1)}, f32[24,4224]{1,0:T(8,128)S(1)}, u32[]{:S(2)}, u32[]{:S(2)}) collective-permute-start(f32[24,4224]{1,0:T(8,128)S(1)} %get-tuple-element.22.refs_0_), channel_id=1, source_target_pairs={{0,1},{1,0},{4,5},{5,4},{8,9},{9,8},{12,13},{13,12},{16,17},{17,16... | collective-permute-start | bytes 1216520 | tf_op jit(solution)/shard_map/ppermute | solution.py:219
  26.3 1.7 %collective-permute-done.4.refs_1_ = f32[24,4224]{1,0:T(8,128)S(1)} collective-permute-done((f32[24,4224]{1,0:T(8,128)S(1)}, f32[24,4224]{1,0:T(8,128)S(1)}, u32[]{:S(2)}, u32[]{:S(2)}) %collective-permute-start.4) | collective-permute-done | bytes 405536 | tf_op jit(solution)/shard_map/ppermute | solution.py:219
  28.0 0.9 %time_gradient.1 = (f32[8,4096]{1,0:T(8,128)S(1)}, f32[8,256]{1,0:T(8,128)S(1)}, f32[8,384]{1,0:T(8,128)S(1)}) custom-call(f32[24,4224]{1,0:T(8,128)S(1)} %get-tuple-element.22.refs_0_, f32[24,4224]{1,0:T(8,128)S(1)} %collective-permute-done.4.refs_1_, bf16[4096,256]{1,0:T(8,128)(2,1)S(1)} %get-tuple-element.18.high_ref.refs_2_, ...), custom_call_target="tpu_custom_call" | custom-call | tf_op jit(solution)/shard_map/time_gradient/pallas_call | solution.py:240
  28.9 3.7 %collective-permute-start.5 = (f32[8,384]{1,0:T(8,128)S(1)}, f32[8,384]{1,0:T(8,128)S(1)}, u32[]{:S(2)}, u32[]{:S(2)}) collective-permute-start(f32[8,384]{1,0:T(8,128)S(1)} %get-tuple-element.25.left), channel_id=1, source_target_pairs={{0,4},{1,5},{4,0},{5,1},{8,12},{9,13},{12,8},{13,9},{16,20},{17,21... | collective-permute-start | bytes 36872 | tf_op jit(solution)/shard_map/ppermute | solution.py:219
  32.6 1.9 %collective-permute-done.5.right = f32[8,384]{1,0:T(8,128)S(1)} collective-permute-done((f32[8,384]{1,0:T(8,128)S(1)}, f32[8,384]{1,0:T(8,128)S(1)}, u32[]{:S(2)}, u32[]{:S(2)}) %collective-permute-start.5) | collective-permute-done | bytes 12320 | tf_op jit(solution)/shard_map/ppermute | solution.py:219
  34.5 3.8 %collective-permute-start.6 = (f32[8,384]{1,0:T(8,128)S(1)}, f32[8,384]{1,0:T(8,128)S(1)}, u32[]{:S(2)}, u32[]{:S(2)}) collective-permute-start(f32[8,384]{1,0:T(8,128)S(1)} %add_halves.6.left), channel_id=1, source_target_pairs={{0,8},{1,9},{4,12},{5,13},{8,0},{9,1},{12,4},{13,5},{16,24},{17,25... | collective-permute-start | bytes 36872 | tf_op jit(solution)/shard_map/ppermute | solution.py:219
  38.3 1.3 %collective-permute-start.10 = (f32[8,4096]{1,0:T(8,128)S(1)}, f32[8,4096]{1,0:T(8,128)S(1)}, u32[]{:S(2)}, u32[]{:S(2)}) collective-permute-start(f32[8,4096]{1,0:T(8,128)S(1)} %get-tuple-element.28.refs_3_), channel_id=1, source_target_pairs={{0,2},{1,3},{4,6},{5,7},{8,10},{9,11},{12,14},{13,15},{16,18},{17,... | collective-permute-start | bytes 393224 | tf_op jit(solution)/shard_map/ppermute | solution.py:219
  39.6 0.5 collective-permute-done.6.right
  40.1 4.8 %collective-permute-start.7 = (f32[8,384]{1,0:T(8,128)S(1)}, f32[8,384]{1,0:T(8,128)S(1)}, u32[]{:S(2)}, u32[]{:S(2)}) collective-permute-start(f32[8,384]{1,0:T(8,128)S(1)} %add_halves.7.grads), channel_id=1, source_target_pairs={{0,16},{1,17},{4,20},{5,21},{8,24},{9,25},{12,28},{13,29},{16,0},{... | collective-permute-start | bytes 36872 | tf_op jit(solution)/shard_map/ppermute | solution.py:219
  44.9 1.7 %collective-permute-done.7.other_grads = f32[8,384]{1,0:T(8,128)S(1)} collective-permute-done((f32[8,384]{1,0:T(8,128)S(1)}, f32[8,384]{1,0:T(8,128)S(1)}, u32[]{:S(2)}, u32[]{:S(2)}) %collective-permute-start.7) | collective-permute-done | bytes 12320 | tf_op jit(solution)/shard_map/ppermute | solution.py:219
  46.6 0.2 new_time_weights.1
  46.7 1.3 %collective-permute-start.9 = (f32[8,128]{1,0:T(8,128)S(1)}, f32[8,128]{1,0:T(8,128)S(1)}, u32[]{:S(2)}, u32[]{:S(2)}) collective-permute-start(f32[8,128]{1,0:T(8,128)S(1)} %get-tuple-element.27.refs_0_), channel_id=1, source_target_pairs={{0,2},{1,3},{4,6},{5,7},{8,10},{9,11},{12,14},{13,15},{16,18},{17,... | collective-permute-start | bytes 12296 | tf_op jit(solution)/shard_map/ppermute | solution.py:219
  48.0 1.9 %collective-permute-start.8 = (f32[8,128]{1,0:T(8,128)S(1)}, f32[8,128]{1,0:T(8,128)S(1)}, u32[]{:S(2)}, u32[]{:S(2)}) collective-permute-start(f32[8,128]{1,0:T(8,128)S(1)} %get-tuple-element.27.refs_0_), channel_id=1, source_target_pairs={{0,1},{1,0},{4,5},{5,4},{8,9},{9,8},{12,13},{13,12},{16,17},{17,16... | collective-permute-start | bytes 12296 | tf_op jit(solution)/shard_map/ppermute | solution.py:219
  50.0 0.0 collective-permute-done.9.refs_2_
  50.0 1.1 %collective-permute-done.8.refs_1_ = f32[8,128]{1,0:T(8,128)S(1)} collective-permute-done((f32[8,128]{1,0:T(8,128)S(1)}, f32[8,128]{1,0:T(8,128)S(1)}, u32[]{:S(2)}, u32[]{:S(2)}) %collective-permute-start.8) | collective-permute-done | bytes 4128 | tf_op jit(solution)/shard_map/ppermute | solution.py:219
  51.1 0.0 collective-permute-done.10.refs_4_
  51.1 0.8 %scale_weights.1 = (f32[8,4096]{1,0:T(8,128)}, f32[8,256]{1,0:T(8,128)}) custom-call(f32[8,128]{1,0:T(8,128)S(1)} %get-tuple-element.27.refs_0_, f32[8,128]{1,0:T(8,128)S(1)} %collective-permute-done.8.refs_1_, f32[8,128]{1,0:T(8,128)S(1)} %collective-permute-done.9.refs_2_, f32[8,4096]{1,0:T(8,128)S(1)} %get-tuple-element.28.refs_3_, ...), custom_call_target="tpu_custom_call" | custom-call | tf_op jit(solution)/shard_map/scale_weights/pallas_call | solution.py:240
  (4 shorter events, 0.0 us)
Async XLA Ops:
  4.0 6.6 %collective-permute-start = (f32[8,640]{1,0:T(8,128)S(1)}, f32[8,640]{1,0:T(8,128)S(1)}, u32[]{:S(2)}, u32[]{:S(2)}) collective-permute-start(f32[8,640]{1,0:T(8,128)S(1)} %get-tuple-element.16.left), channel_id=1, source_target_pairs={{0,4},{1,5},{4,0},{5,1},{8,12},{9,13},{12,8},{13,9},{16,20},{17,21... | collective-permute-start | bytes 61448 | tf_op jit(solution)/shard_map/ppermute | solution.py:219
  10.6 5.8 %collective-permute-start.1 = (f32[8,640]{1,0:T(8,128)S(1)}, f32[8,640]{1,0:T(8,128)S(1)}, u32[]{:S(2)}, u32[]{:S(2)}) collective-permute-start(f32[8,640]{1,0:T(8,128)S(1)} %add_halves.4.left), channel_id=1, source_target_pairs={{0,8},{1,9},{4,12},{5,13},{8,0},{9,1},{12,4},{13,5},{16,24},{17,25... | collective-permute-start | bytes 61448 | tf_op jit(solution)/shard_map/ppermute | solution.py:219
  14.6 8.4 %collective-permute-start.3 = (f32[8,4096]{1,0:T(8,128)S(1)}, f32[8,4096]{1,0:T(8,128)S(1)}, u32[]{:S(2)}, u32[]{:S(2)}) collective-permute-start(f32[8,4096]{1,0:T(8,128)S(1)} %time_product.1.refs_0_.cross), channel_id=1, source_target_pairs={{2,0},{3,1},{6,4},{7,5},{10,8},{11,9},{14,12},{15,13},{18,16},{19,... | collective-permute-start | bytes 393224 | tf_op jit(solution)/shard_map/ppermute | solution.py:284
  16.4 6.7 %collective-permute-start.2 = (f32[8,640]{1,0:T(8,128)S(1)}, f32[8,640]{1,0:T(8,128)S(1)}, u32[]{:S(2)}, u32[]{:S(2)}) collective-permute-start(f32[8,640]{1,0:T(8,128)S(1)} %add_halves.5.sums), channel_id=1, source_target_pairs={{0,16},{1,17},{4,20},{5,21},{8,24},{9,25},{12,28},{13,29},{16,0},{... | collective-permute-start | bytes 61448 | tf_op jit(solution)/shard_map/ppermute | solution.py:219
  24.4 3.6 %collective-permute-start.4 = (f32[24,4224]{1,0:T(8,128)S(1)}, f32[24,4224]{1,0:T(8,128)S(1)}, u32[]{:S(2)}, u32[]{:S(2)}) collective-permute-start(f32[24,4224]{1,0:T(8,128)S(1)} %get-tuple-element.22.refs_0_), channel_id=1, source_target_pairs={{0,1},{1,0},{4,5},{5,4},{8,9},{9,8},{12,13},{13,12},{16,17},{17,16... | collective-permute-start | bytes 1216520 | tf_op jit(solution)/shard_map/ppermute | solution.py:219
  28.9 5.6 %collective-permute-start.5 = (f32[8,384]{1,0:T(8,128)S(1)}, f32[8,384]{1,0:T(8,128)S(1)}, u32[]{:S(2)}, u32[]{:S(2)}) collective-permute-start(f32[8,384]{1,0:T(8,128)S(1)} %get-tuple-element.25.left), channel_id=1, source_target_pairs={{0,4},{1,5},{4,0},{5,1},{8,12},{9,13},{12,8},{13,9},{16,20},{17,21... | collective-permute-start | bytes 36872 | tf_op jit(solution)/shard_map/ppermute | solution.py:219
  34.5 5.6 %collective-permute-start.6 = (f32[8,384]{1,0:T(8,128)S(1)}, f32[8,384]{1,0:T(8,128)S(1)}, u32[]{:S(2)}, u32[]{:S(2)}) collective-permute-start(f32[8,384]{1,0:T(8,128)S(1)} %add_halves.6.left), channel_id=1, source_target_pairs={{0,8},{1,9},{4,12},{5,13},{8,0},{9,1},{12,4},{13,5},{16,24},{17,25... | collective-permute-start | bytes 36872 | tf_op jit(solution)/shard_map/ppermute | solution.py:219
  38.3 12.8 %collective-permute-start.10 = (f32[8,4096]{1,0:T(8,128)S(1)}, f32[8,4096]{1,0:T(8,128)S(1)}, u32[]{:S(2)}, u32[]{:S(2)}) collective-permute-start(f32[8,4096]{1,0:T(8,128)S(1)} %get-tuple-element.28.refs_3_), channel_id=1, source_target_pairs={{0,2},{1,3},{4,6},{5,7},{8,10},{9,11},{12,14},{13,15},{16,18},{17,... | collective-permute-start | bytes 393224 | tf_op jit(solution)/shard_map/ppermute | solution.py:219
  40.1 6.5 %collective-permute-start.7 = (f32[8,384]{1,0:T(8,128)S(1)}, f32[8,384]{1,0:T(8,128)S(1)}, u32[]{:S(2)}, u32[]{:S(2)}) collective-permute-start(f32[8,384]{1,0:T(8,128)S(1)} %add_halves.7.grads), channel_id=1, source_target_pairs={{0,16},{1,17},{4,20},{5,21},{8,24},{9,25},{12,28},{13,29},{16,0},{... | collective-permute-start | bytes 36872 | tf_op jit(solution)/shard_map/ppermute | solution.py:219
  46.7 3.2 %collective-permute-start.9 = (f32[8,128]{1,0:T(8,128)S(1)}, f32[8,128]{1,0:T(8,128)S(1)}, u32[]{:S(2)}, u32[]{:S(2)}) collective-permute-start(f32[8,128]{1,0:T(8,128)S(1)} %get-tuple-element.27.refs_0_), channel_id=1, source_target_pairs={{0,2},{1,3},{4,6},{5,7},{8,10},{9,11},{12,14},{13,15},{16,18},{17,... | collective-permute-start | bytes 12296 | tf_op jit(solution)/shard_map/ppermute | solution.py:219
  48.0 3.1 %collective-permute-start.8 = (f32[8,128]{1,0:T(8,128)S(1)}, f32[8,128]{1,0:T(8,128)S(1)}, u32[]{:S(2)}, u32[]{:S(2)}) collective-permute-start(f32[8,128]{1,0:T(8,128)S(1)} %get-tuple-element.27.refs_0_), channel_id=1, source_target_pairs={{0,1},{1,0},{4,5},{5,4},{8,9},{9,8},{12,13},{13,12},{16,17},{17,16... | collective-permute-start | bytes 12296 | tf_op jit(solution)/shard_map/ppermute | solution.py:219

commit v3 on v0

v3 whole, which is shorter than its diff:
```python
import functools

import jax
import jax.numpy as jnp
from jax import lax
from jax.experimental import pallas as pl
from jax.experimental.pallas import tpu as pltpu
from jax.sharding import PartitionSpec as P

step_rate = 16.0
f32 = jnp.float32
bf16 = jnp.bfloat16
lanes = 128
params = pltpu.CompilerParams(vmem_limit_bytes=24 * 1024 * 1024)
vmem = pl.BlockSpec(memory_space=pltpu.VMEM)
hbm = pl.BlockSpec(memory_space=pltpu.HBM)
any_space = pl.BlockSpec(memory_space=pl.ANY)


def split_left(value):
    first = value.astype(bf16).astype(f32)
    rest = value - first
    second = rest.astype(bf16).astype(f32)
    return [first, second, rest - second]


def left_of(value, other=None):
    other = jnp.zeros_like(value) if other is None else other
    return jnp.concatenate(split_left(value) + [other], axis=0).astype(bf16)


def split_panel(value):
    high = value.astype(bf16)
    return high, (value - high.astype(f32)).astype(bf16)


def rows_dot(left, high, low):
    return jnp.dot(left, high, preferred_element_type=f32) + jnp.dot(left, low, preferred_element_type=f32)


def days_dot(left, high, low):
    dims = (((1,), (1,)), ((), ()))
    return lax.dot_general(left, high, dims, preferred_element_type=f32) + lax.dot_general(
        left, low, dims, preferred_element_type=f32
    )


def add_terms(stack, groups):
    return stack[:groups] + stack[groups : 2 * groups] + stack[2 * groups : 3 * groups]


def tree_sum(values):
    values = list(values)
    while len(values) > 1:
        values = [values[i] + values[i + 1] for i in range(0, len(values), 2)]
    return values[0]


def column(row_ref):
    count = row_ref.shape[1]
    wide = jnp.broadcast_to(row_ref[...].astype(f32), (count, count))
    row = lax.broadcasted_iota(jnp.int32, (count, count), 0)
    lane = lax.broadcasted_iota(jnp.int32, (count, count), 1)
    return jnp.sum(jnp.where(row == lane, wide, 0.0), axis=1, keepdims=True).astype(jnp.int32)


def days_of(device, shape):
    return device * shape[1] + lax.broadcasted_iota(jnp.int32, shape, 1)


def fetch(sources, targets, sems):
    copies = [pltpu.make_async_copy(*pair, sems.at[i]) for i, pair in enumerate(zip(sources, targets))]
    for copy in copies:
        copy.start()
    return copies


def fetch_rows(source, target, sems, chunks):
    rows = source.shape[0] // chunks
    parts = [pl.ds(chunk * rows, rows) for chunk in range(chunks)]
    copies = fetch([source.at[here] for here in parts], [target.at[here] for here in parts], sems)
    return list(zip(parts, copies))


def wait_all(copies):
    for copy in copies:
        copy.wait()


def repeat_out(block, out, sems):
    rows = block.shape[0]
    places = [out.at[pl.ds(i * rows, rows)] for i in range(out.shape[0] // rows)]
    wait_all(fetch([block] * len(places), places, sems))


def first_kernel(all_count, half, chunks, *refs):
    arguments, refs = refs[:6], refs[6:]
    out, cross, *held, block, left_ref, small_sems, panel_sems, out_sems = refs
    groups, day_cols = held[5].shape
    unit_rows = held[0].shape[0]
    small = fetch(arguments[1:], held[1:], small_sems)
    parts = fetch_rows(arguments[0], held[0], panel_sems, chunks)
    panel, cohort, _, post_row, unit_logit, _ = held
    wait_all(small)
    me = lax.axis_index("day")

    @pl.when(me < half)
    def _():
        label = lax.broadcasted_iota(jnp.int32, (groups, unit_rows), 0)
        treated = jnp.where(cohort[...] == label, 1.0, 0.0)
        control = jnp.where(cohort[...] > label, 1.0, 0.0)
        raised = jnp.exp(unit_logit[...]) * control
        left_ref[...] = left_of(raised, treated)
        lane = lax.broadcasted_iota(jnp.int32, (groups, lanes), 1)
        block[:, 2 * day_cols :] = jnp.where(
            lane == 0,
            jnp.sum(raised, axis=1, keepdims=True),
            jnp.where(
                lane == 1, jnp.sum(treated, axis=1, keepdims=True), jnp.sum(control, axis=1, keepdims=True)
            ),
        )
        product = jnp.zeros((4 * groups, day_cols), f32)
        for here, copy in parts:
            copy.wait()
            product += rows_dot(left_ref[:, here], *split_panel(panel[here, :]))
        block[:, :day_cols] = add_terms(product, groups)
        block[:, day_cols : 2 * day_cols] = product[3 * groups :]
        repeat_out(block, out, out_sems)

    @pl.when(me >= half)
    def _():
        post_start = column(post_row)
        after = jnp.where(days_of(me, (groups, day_cols)) >= post_start, 1.0, 0.0)
        left = left_of(after / (all_count - post_start).astype(f32))
        for here, copy in parts:
            copy.wait()
            cross[:, here] = add_terms(days_dot(left, *split_panel(panel[here, :])), groups)


def token_kernel(value, token):
    token[...] = value[:, : token.shape[1]]


def second_kernel(chunks, unit_devices, half, *refs):
    arguments, refs = refs[:6], refs[6:]
    sums, post, _, pack, norms, raised_units, raised_days, ends, high_ref, low_ref, *refs = refs
    held, small_sems, panel_sems = refs[:6], refs[6], refs[7]
    groups, day_cols = raised_days.shape
    unit_rows = raised_units.shape[1]
    small = fetch(arguments[1:], held[1:], small_sems)
    parts = fetch_rows(arguments[0], held[0], panel_sems, chunks)
    panel, cohort, pre_row, _, unit_logit, time_logit = held
    total = tree_sum(sums[pl.ds(u * groups, groups), :] for u in range(unit_devices))
    unit_norm = total[:, 2 * day_cols : 2 * day_cols + 1]
    treat_count = jnp.maximum(total[:, 2 * day_cols + 1 : 2 * day_cols + 2], 1.0)
    norms[...] = total[:, 2 * day_cols :]
    pack[2 * groups :, :unit_rows] = post[...]
    wait_all(small)
    pre_end = column(pre_row)
    ends[...] = jnp.broadcast_to(pre_end.astype(f32), ends.shape)
    before = days_of(lax.axis_index("day"), (groups, day_cols)) < pre_end
    gap = total[:, :day_cols] / unit_norm - total[:, day_cols : 2 * day_cols] / treat_count
    raised_time = jnp.where(before, jnp.exp(time_logit[...]), 0.0)
    raised_days[...] = raised_time
    time_norm = jnp.sum(raised_time, axis=1, keepdims=True)
    pack[:, unit_rows:] = jnp.broadcast_to(jnp.concatenate([time_norm] * 3, axis=0), (3 * groups, lanes))
    left = split_left(jnp.where(before, gap, 0.0)) + split_left(raised_time)
    left = jnp.concatenate(left, axis=0).astype(bf16)
    label = lax.broadcasted_iota(jnp.int32, (groups, unit_rows), 0)
    raised_units[...] = jnp.where(cohort[...] > label, jnp.exp(unit_logit[...]), 0.0)
    for here, copy in parts:
        copy.wait()
        high, low = split_panel(panel[here, :])
        high_ref[here, :] = high
        low_ref[here, :] = low
        product = days_dot(left, high, low)
        pack[:groups, here] = add_terms(product, groups)
        pack[groups : 2 * groups, here] = add_terms(product[3 * groups :], groups)


def third_kernel(half, chunks, *refs):
    parts, refs = refs[:half], refs[half:]
    high_ref, low_ref, norms, raised_units, raised_days, ends, scaled, lam, out, block, out_sems = refs
    groups, unit_rows = raised_units.shape
    day_cols = raised_days.shape[1]
    rows = unit_rows // chunks
    unit_norm, ctrl_count = norms[:, 0:1], norms[:, 2:3]
    factor = -step_rate / jnp.sqrt(ends[:, 0:1])
    time_norm = tree_sum(ref[:groups, unit_rows : unit_rows + 1] for ref in parts)
    lam[...] = raised_days[...] / time_norm
    time_grad = jnp.zeros((groups, day_cols), f32)
    new_sum = jnp.zeros((groups, 1), f32)
    for chunk in range(chunks):
        here = pl.ds(chunk * rows, rows)
        whole = tree_sum(ref[:, here] for ref in parts)
        raised = raised_units[:, here]
        new = raised / unit_norm * jnp.exp(whole[:groups] * factor)
        new_sum += jnp.sum(new, axis=1, keepdims=True)
        scaled[:, here] = new * ctrl_count
        shortfall = whole[groups : 2 * groups] / time_norm - whole[2 * groups :]
        left = left_of(jnp.where(raised > 0.0, shortfall, 0.0))
        time_grad += add_terms(rows_dot(left, high_ref[here, :], low_ref[here, :]), groups)
    block[:, :day_cols] = time_grad
    block[:, day_cols:] = jnp.broadcast_to(new_sum, (groups, lanes))
    repeat_out(block, out, out_sems)


def fourth_kernel(unit_devices, grads, lam, norms, moved, totals):
    groups, day_cols = lam.shape
    total = tree_sum(grads[pl.ds(u * groups, groups), :] for u in range(unit_devices))
    root = jnp.sqrt(jnp.maximum(norms[:, 2:3], 1.0))
    new = lam[...] * jnp.exp(total[:, :day_cols] * (-step_rate / root))
    moved[...] = new
    lane = lax.broadcasted_iota(jnp.int32, (groups, lanes), 1)
    totals[...] = jnp.where(lane == 0, total[:, day_cols:], jnp.sum(new, axis=1, keepdims=True))


def fifth_kernel(half, *refs):
    totals, refs = refs[:half], refs[half:]
    sent_totals, scaled, sent_scaled, moved, ends, unit_weights, time_weights = refs
    first = lax.axis_index("day") < half
    own = jnp.where(first, totals[0][:, 0:1], sent_totals[:, 0:1])
    unit_weights[...] = jnp.where(first, scaled[...], sent_scaled[...]) / own
    day_total = tree_sum(ref[:, 1:2] for ref in totals)
    time_weights[...] = jnp.where(first, moved[...] / day_total * ends[:, 0:1], 0.0)


def local(outcomes, cohort, pre_end, post_start, unit_logit, time_logit):
    groups = pre_end.shape[0]
    unit_rows, day_cols = outcomes.shape
    day_devices = lax.axis_size("day")
    unit_devices = lax.axis_size("unit")
    half = day_devices // 2
    assert half * 2 == day_devices and half & (half - 1) == 0
    assert unit_devices & (unit_devices - 1) == 0
    chunks = 4
    beside = pl.CostEstimate(flops=10**10, bytes_accessed=0, transcendentals=0)

    def spread(value, day_xor, up):
        pairs = [
            (u * day_devices + d, u * day_devices + (d ^ day_xor) + up) for u in range(unit_devices) for d in range(half)
        ]
        return lax.ppermute(value, ("unit", "day"), pairs)

    def over_days(value):
        return [value] + [spread(value, k, 0) for k in range(1, half)]

    def over_units(value):
        return lax.all_to_all(value, "unit", split_axis=0, concat_axis=0, tiled=True)

    def call(kernel, shapes, name, args, in_specs=None, out_specs=None, **more):
        return pl.pallas_call(
            kernel,
            in_specs=in_specs or [vmem] * len(args),
            out_specs=out_specs or [vmem] * len(shapes),
            out_shape=[
                shape if isinstance(shape, type(in_hbm)) else jax.ShapeDtypeStruct(*shape) for shape in shapes
            ],
            compiler_params=params,
            name=name,
            **more,
        )(*args)

    arguments = (outcomes, cohort[None, :], pre_end[None, :], post_start[None, :], unit_logit, time_logit)
    fixed = [pltpu.with_memory_space_constraint(argument, pltpu.HBM) for argument in arguments]
    held = [pltpu.VMEM(argument.shape, argument.dtype) for argument in arguments]
    small_sems, panel_sems = pltpu.SemaphoreType.DMA((5,)), pltpu.SemaphoreType.DMA((chunks,))
    out_sems = pltpu.SemaphoreType.DMA((unit_devices,))
    width = 2 * day_cols + lanes
    in_hbm = pltpu.HBM((unit_devices * groups, width), f32)
    sums, cross = call(
        functools.partial(first_kernel, day_devices * day_cols, half, chunks),
        [in_hbm, ((groups, unit_rows), f32)],
        "first_product",
        fixed,
        in_specs=[hbm] * 6,
        out_specs=[hbm, vmem],
        scratch_shapes=held
        + [
            pltpu.VMEM((groups, width), f32),
            pltpu.VMEM((4 * groups, unit_rows), bf16),
            small_sems,
            panel_sems,
            out_sems,
        ],
    )
    downward = [
        (u * day_devices + d + half, u * day_devices + d) for u in range(unit_devices) for d in range(half)
    ]
    post = lax.ppermute(cross, ("unit", "day"), downward)
    (token,) = call(token_kernel, [((groups, lanes), f32)], "post_here", (post,), cost_estimate=beside)
    pack, norms, raised_units, raised_days, ends, high, low = call(
        functools.partial(second_kernel, chunks, unit_devices, half),
        [
            ((3 * groups, unit_rows + lanes), f32),
            ((groups, lanes), f32),
            ((groups, unit_rows), f32),
            ((groups, day_cols), f32),
            ((groups, lanes), f32),
            ((unit_rows, day_cols), bf16),
            ((unit_rows, day_cols), bf16),
        ],
        "unit_gradient",
        (*fixed, over_units(sums), post, token),
        in_specs=[hbm] * 6 + [vmem, vmem, any_space],
        scratch_shapes=held + [small_sems, panel_sems],
    )
    width = day_cols + lanes
    scaled, lam, grads = call(
        functools.partial(third_kernel, half, 8),
        [
            ((groups, unit_rows), f32),
            ((groups, day_cols), f32),
            pltpu.HBM((unit_devices * groups, width), f32),
        ],
        "time_gradient",
        (*over_days(pack), high, low, norms, raised_units, raised_days, ends),
        out_specs=[vmem, vmem, hbm],
        scratch_shapes=[pltpu.VMEM((groups, width), f32), out_sems],
    )
    sent_scaled = spread(scaled, 0, half)
    moved, totals = call(
        functools.partial(fourth_kernel, unit_devices),
        [((groups, day_cols), f32), ((groups, lanes), f32)],
        "new_time_weights",
        (over_units(grads), lam, norms),
    )
    sent_totals = spread(totals, 0, half)
    return call(
        functools.partial(fifth_kernel, half),
        [((groups, unit_rows), f32), ((groups, day_cols), f32)],
        "scale_weights",
        (*over_days(totals), sent_totals, scaled, sent_scaled, moved, ends),
    )


def solution(mesh):
    return jax.shard_map(
        local,
        mesh=mesh,
        in_specs=(P("unit", "day"), P("unit"), P(), P(), P(None, "unit"), P(None, "day")),
        out_specs=(P(None, "unit"), P(None, "day")),
        check_vma=False,
    )
```

time: 49 us -> 46.5 us (0.949)
  local copies, waits for them, and re-layouts: 2.92 us -> 0 us
  starting transfers between devices: 20.2 us -> 19 us
  waiting for transfers between devices: 14.9 us -> 15.8 us
  Pallas kernels: 9.78 us -> 10.4 us
    all_to_all x2, waiting for transfers between devices: 6.55 us -> 13 us  [over_units(): lax.all_to_all(value, 'unit', split_axis=0, concat_axis=0, tiled=True)]
    ppermute x1, waiting for transfers between devices: 5.56 us -> 0.01 us  [local(): post = lax.ppermute(cross, ('unit', 'day'), downward)]
    unnamed x4 -> x0, local copies, waits for them, and re-layouts: 2.92 us -> none
    all_to_all x2, starting transfers between devices: 12.5 us -> 10.6 us  [over_units(): lax.all_to_all(value, 'unit', split_axis=0, concat_axis=0, tiled=True)]
    ppermute x4, starting transfers between devices: 6.43 us -> 7.1 us  [spread(): return lax.ppermute(value, ('unit', 'day'), pairs)]
    pallas_call x5 -> x6, Pallas kernels: 9.78 us -> 10.4 us  [call(): pl.pallas_call(kernel, in_specs=in_specs or [vmem] * len(args), out_specs...]
  transfers between devices with their start and end apart: 7 -> 7, of which waited for: 5 -> 4; matrix products, arithmetic and copies ran while one was open for 0% -> 0% of each run, Pallas kernels for 0% -> 0%
where the time goes in v3:
time: 46.5 us; the launch traced here: 45.9 us
  starting transfers between devices  19 us (41%)
  waiting for transfers between devices  15.8 us (34%)
  Pallas kernels  10.4 us (22%)
  between operations  0.73 us (2%)
    all_to_all x2, waiting for transfers between devices, over_units(): lax.all_to_all(value, 'unit', split_axis=0, concat_axis=0, tiled=True)  13 us
    all_to_all x2, starting transfers between devices, over_units(): lax.all_to_all(value, 'unit', split_axis=0, concat_axis=0, tiled=True)  10.6 us
    pallas_call x6, Pallas kernels, call(): pl.pallas_call(kernel, in_specs=in_specs or [vmem] * len(args), out_specs...  10.4 us
    ppermute x4, starting transfers between devices, spread(): return lax.ppermute(value, ('unit', 'day'), pairs)  7.1 us
    ppermute x4, waiting for transfers between devices, spread(): return lax.ppermute(value, ('unit', 'day'), pairs)  2.82 us
    ppermute x1, starting transfers between devices, local(): post = lax.ppermute(cross, ('unit', 'day'), downward)  1.29 us
  transfers between devices with their start and end apart: 7, of which 4 were waited for; matrix products, arithmetic and copies ran while one was open for 0% of the time, Pallas kernels for 0%

profile of v3, /device:TPU:0, one launch (start us, length us, event | category | flops | bytes accessed | tf_op | source)
XLA Modules:
  0.0 45.9 jit_solution(4843041714858131413)
XLA Ops:
  0.6 4.1 %first_product.1 = (f32[64,640]{1,0:T(8,128)}, f32[8,4096]{1,0:T(8,128)S(1)}) custom-call(f32[4096,256]{1,0:T(8,128)} %refs_0_.3, s32[1,4096]{1,0:T(1,128)} %bitcast.11, s32[1,8]{1,0:T(1,128)} %bitcast.13, s32[1,8]{1,0:T(1,128)} %bitcast.15, f32[8,4096]{1,0:T(8,128)} %refs_4_.3, f32[8,256]{1,0:T(8,128)} %refs_5_.3), custom_call_target="tpu_custom_call" | custom-call | tf_op jit(solution)/shard_map/first_product/pallas_call | solution.py:252
  4.7 1.3 %collective-permute-start = (f32[8,4096]{1,0:T(8,128)S(1)}, f32[8,4096]{1,0:T(8,128)S(1)}, u32[]{:S(2)}, u32[]{:S(2)}) collective-permute-start(f32[8,4096]{1,0:T(8,128)S(1)} %get-tuple-element.17), channel_id=1, source_target_pairs={{2,0},{3,1},{6,4},{7,5},{10,8},{11,9},{14,12},{15,13},{18,16},{19,... | collective-permute-start | bytes 393224 | tf_op jit(solution)/shard_map/ppermute | solution.py:290
  6.0 7.3 %all-to-all-start = ((f32[8,8,640]{2,1,0:T(8,128)}), f32[8,8,640]{2,1,0:T(8,128)S(1)}, u32[]{:S(2)}, u32[]{:S(2)}) async-start(f32[8,8,640]{2,1,0:T(8,128)} %bitcast.9), calls=%async_computation | async-start | bytes 327680 | tf_op jit(solution)/shard_map/all_to_all | solution.py:249
  13.3 0.0 collective-permute-done.value.refs_7_
  13.3 7.5 %all-to-all-done = f32[8,8,640]{2,1,0:T(8,128)S(1)} async-done(((f32[8,8,640]{2,1,0:T(8,128)}), f32[8,8,640]{2,1,0:T(8,128)S(1)}, u32[]{:S(2)}, u32[]{:S(2)}) %all-to-all-start) | async-done | bytes 163872 | tf_op jit(solution)/shard_map/all_to_all | solution.py:249
  20.8 3.8 %unit_gradient.1 = (f32[24,4224]{1,0:T(8,128)S(1)}, f32[8,128]{1,0:T(8,128)S(1)}, f32[8,4096]{1,0:T(8,128)S(1)}, f32[8,256]{1,0:T(8,128)S(1)}, f32[8,128]{1,0:T(...) custom-call(f32[4096,256]{1,0:T(8,128)} %refs_0_.3, s32[1,4096]{1,0:T(1,128)} %bitcast.12, ...), custom_call_target="tpu_custom_call" | custom-call | tf_op jit(solution)/shard_map/unit_gradient/pallas_call | solution.py:252
  24.7 1.9 %collective-permute-start.1 = (f32[24,4224]{1,0:T(8,128)S(1)}, f32[24,4224]{1,0:T(8,128)S(1)}, u32[]{:S(2)}, u32[]{:S(2)}) collective-permute-start(f32[24,4224]{1,0:T(8,128)S(1)} %get-tuple-element.18.refs_0_), channel_id=1, source_target_pairs={{0,1},{1,0},{4,5},{5,4},{8,9},{9,8},{12,13},{13,12},{16,17},{17,16... | collective-permute-start | bytes 1216520 | tf_op jit(solution)/shard_map/ppermute | solution.py:243
  26.6 1.7 %collective-permute-done.1.refs_1_ = f32[24,4224]{1,0:T(8,128)S(1)} collective-permute-done((f32[24,4224]{1,0:T(8,128)S(1)}, f32[24,4224]{1,0:T(8,128)S(1)}, u32[]{:S(2)}, u32[]{:S(2)}) %collective-permute-start.1) | collective-permute-done | bytes 405536 | tf_op jit(solution)/shard_map/ppermute | solution.py:243
  28.3 1.6 %time_gradient.1 = (f32[8,4096]{1,0:T(8,128)S(1)}, f32[8,256]{1,0:T(8,128)S(1)}, f32[64,384]{1,0:T(8,128)}) custom-call(f32[24,4224]{1,0:T(8,128)S(1)} %get-tuple-element.18.refs_0_, f32[24,4224]{1,0:T(8,128)S(1)} %collective-permute-done.1.refs_1_, bf16[4096,256]{1,0:T(8,128)(2,1)S(1)} %get-tuple-element.19.refs_2_, ...), custom_call_target="tpu_custom_call" | custom-call | tf_op jit(solution)/shard_map/time_gradient/pallas_call | solution.py:252
  29.9 3.4 %all-to-all-start.1 = ((f32[8,8,384]{2,1,0:T(8,128)}), f32[8,8,384]{2,1,0:T(8,128)S(1)}, u32[]{:S(2)}, u32[]{:S(2)}) async-start(f32[8,8,384]{2,1,0:T(8,128)} %bitcast.10), calls=%async_computation.1 | async-start | bytes 196608 | tf_op jit(solution)/shard_map/all_to_all | solution.py:249
  33.3 1.6 %collective-permute-start.4 = (f32[8,4096]{1,0:T(8,128)S(1)}, f32[8,4096]{1,0:T(8,128)S(1)}, u32[]{:S(2)}, u32[]{:S(2)}) collective-permute-start(f32[8,4096]{1,0:T(8,128)S(1)} %get-tuple-element.28.refs_3_), channel_id=1, source_target_pairs={{0,2},{1,3},{4,6},{5,7},{8,10},{9,11},{12,14},{13,15},{16,18},{17,... | collective-permute-start | bytes 393224 | tf_op jit(solution)/shard_map/ppermute | solution.py:243
  34.9 5.4 %all-to-all-done.1 = f32[8,8,384]{2,1,0:T(8,128)S(1)} async-done(((f32[8,8,384]{2,1,0:T(8,128)}), f32[8,8,384]{2,1,0:T(8,128)S(1)}, u32[]{:S(2)}, u32[]{:S(2)}) %all-to-all-start.1) | async-done | bytes 98336 | tf_op jit(solution)/shard_map/all_to_all | solution.py:249
  40.3 0.2 new_time_weights.1
  40.5 1.6 %collective-permute-start.3 = (f32[8,128]{1,0:T(8,128)S(1)}, f32[8,128]{1,0:T(8,128)S(1)}, u32[]{:S(2)}, u32[]{:S(2)}) collective-permute-start(f32[8,128]{1,0:T(8,128)S(1)} %get-tuple-element.27.refs_0_), channel_id=1, source_target_pairs={{0,2},{1,3},{4,6},{5,7},{8,10},{9,11},{12,14},{13,15},{16,18},{17,... | collective-permute-start | bytes 12296 | tf_op jit(solution)/shard_map/ppermute | solution.py:243
  42.1 1.9 %collective-permute-start.2 = (f32[8,128]{1,0:T(8,128)S(1)}, f32[8,128]{1,0:T(8,128)S(1)}, u32[]{:S(2)}, u32[]{:S(2)}) collective-permute-start(f32[8,128]{1,0:T(8,128)S(1)} %get-tuple-element.27.refs_0_), channel_id=1, source_target_pairs={{0,1},{1,0},{4,5},{5,4},{8,9},{9,8},{12,13},{13,12},{16,17},{17,16... | collective-permute-start | bytes 12296 | tf_op jit(solution)/shard_map/ppermute | solution.py:243
  44.1 0.0 collective-permute-done.4.refs_4_
  44.1 0.0 collective-permute-done.3.refs_2_
  44.1 1.1 %collective-permute-done.2.refs_1_ = f32[8,128]{1,0:T(8,128)S(1)} collective-permute-done((f32[8,128]{1,0:T(8,128)S(1)}, f32[8,128]{1,0:T(8,128)S(1)}, u32[]{:S(2)}, u32[]{:S(2)}) %collective-permute-start.2) | collective-permute-done | bytes 4128 | tf_op jit(solution)/shard_map/ppermute | solution.py:243
  45.2 0.8 %scale_weights.1 = (f32[8,4096]{1,0:T(8,128)}, f32[8,256]{1,0:T(8,128)}) custom-call(f32[8,128]{1,0:T(8,128)S(1)} %get-tuple-element.27.refs_0_, f32[8,128]{1,0:T(8,128)S(1)} %collective-permute-done.2.refs_1_, f32[8,128]{1,0:T(8,128)S(1)} %collective-permute-done.3.refs_2_, f32[8,4096]{1,0:T(8,128)S(1)} %get-tuple-element.28.refs_3_, ...), custom_call_target="tpu_custom_call" | custom-call | tf_op jit(solution)/shard_map/scale_weights/pallas_call | solution.py:252
  (1 shorter events, 0.0 us)
Async XLA Ops:
  4.7 8.6 %collective-permute-start = (f32[8,4096]{1,0:T(8,128)S(1)}, f32[8,4096]{1,0:T(8,128)S(1)}, u32[]{:S(2)}, u32[]{:S(2)}) collective-permute-start(f32[8,4096]{1,0:T(8,128)S(1)} %get-tuple-element.17), channel_id=1, source_target_pairs={{2,0},{3,1},{6,4},{7,5},{10,8},{11,9},{14,12},{15,13},{18,16},{19,... | collective-permute-start | bytes 393224 | tf_op jit(solution)/shard_map/ppermute | solution.py:290
  6.0 14.8 %all-to-all-start = ((f32[8,8,640]{2,1,0:T(8,128)}), f32[8,8,640]{2,1,0:T(8,128)S(1)}, u32[]{:S(2)}, u32[]{:S(2)}) async-start(f32[8,8,640]{2,1,0:T(8,128)} %bitcast.9), calls=%async_computation | async-start | bytes 327680 | tf_op jit(solution)/shard_map/all_to_all | solution.py:249
  24.7 3.6 %collective-permute-start.1 = (f32[24,4224]{1,0:T(8,128)S(1)}, f32[24,4224]{1,0:T(8,128)S(1)}, u32[]{:S(2)}, u32[]{:S(2)}) collective-permute-start(f32[24,4224]{1,0:T(8,128)S(1)} %get-tuple-element.18.refs_0_), channel_id=1, source_target_pairs={{0,1},{1,0},{4,5},{5,4},{8,9},{9,8},{12,13},{13,12},{16,17},{17,16... | collective-permute-start | bytes 1216520 | tf_op jit(solution)/shard_map/ppermute | solution.py:243
  29.9 10.4 %all-to-all-start.1 = ((f32[8,8,384]{2,1,0:T(8,128)}), f32[8,8,384]{2,1,0:T(8,128)S(1)}, u32[]{:S(2)}, u32[]{:S(2)}) async-start(f32[8,8,384]{2,1,0:T(8,128)} %bitcast.10), calls=%async_computation.1 | async-start | bytes 196608 | tf_op jit(solution)/shard_map/all_to_all | solution.py:249
  33.3 10.8 %collective-permute-start.4 = (f32[8,4096]{1,0:T(8,128)S(1)}, f32[8,4096]{1,0:T(8,128)S(1)}, u32[]{:S(2)}, u32[]{:S(2)}) collective-permute-start(f32[8,4096]{1,0:T(8,128)S(1)} %get-tuple-element.28.refs_3_), channel_id=1, source_target_pairs={{0,2},{1,3},{4,6},{5,7},{8,10},{9,11},{12,14},{13,15},{16,18},{17,... | collective-permute-start | bytes 393224 | tf_op jit(solution)/shard_map/ppermute | solution.py:243
  40.5 3.6 %collective-permute-start.3 = (f32[8,128]{1,0:T(8,128)S(1)}, f32[8,128]{1,0:T(8,128)S(1)}, u32[]{:S(2)}, u32[]{:S(2)}) collective-permute-start(f32[8,128]{1,0:T(8,128)S(1)} %get-tuple-element.27.refs_0_), channel_id=1, source_target_pairs={{0,2},{1,3},{4,6},{5,7},{8,10},{9,11},{12,14},{13,15},{16,18},{17,... | collective-permute-start | bytes 12296 | tf_op jit(solution)/shard_map/ppermute | solution.py:243
  42.1 3.1 %collective-permute-start.2 = (f32[8,128]{1,0:T(8,128)S(1)}, f32[8,128]{1,0:T(8,128)S(1)}, u32[]{:S(2)}, u32[]{:S(2)}) collective-permute-start(f32[8,128]{1,0:T(8,128)S(1)} %get-tuple-element.27.refs_0_), channel_id=1, source_target_pairs={{0,1},{1,0},{4,5},{5,4},{8,9},{9,8},{12,13},{13,12},{16,17},{17,16... | collective-permute-start | bytes 12296 | tf_op jit(solution)/shard_map/ppermute | solution.py:243

commit v4 on v3

--- a/solution.py
+++ b/solution.py
@@ -95,7 +95,7 @@
 
 def first_kernel(all_count, half, chunks, *refs):
     arguments, refs = refs[:6], refs[6:]
-    out, cross, *held, block, left_ref, small_sems, panel_sems, out_sems = refs
+    block, cross, *held, left_ref, small_sems, panel_sems = refs
     groups, day_cols = held[5].shape
     unit_rows = held[0].shape[0]
     small = fetch(arguments[1:], held[1:], small_sems)
@@ -125,7 +125,6 @@
             product += rows_dot(left_ref[:, here], *split_panel(panel[here, :]))
         block[:, :day_cols] = add_terms(product, groups)
         block[:, day_cols : 2 * day_cols] = product[3 * groups :]
-        repeat_out(block, out, out_sems)
 
     @pl.when(me >= half)
     def _():
@@ -137,20 +136,30 @@
             cross[:, here] = add_terms(days_dot(left, *split_panel(panel[here, :])), groups)
 
 
-def token_kernel(value, token):
-    token[...] = value[:, : token.shape[1]]
-
-
-def second_kernel(chunks, unit_devices, half, *refs):
+def pair_kernel(gathered, out, block, out_sems):
+    block[...] = gathered[0] + gathered[1]
+    repeat_out(block, out, out_sems)
+
+
+def corner_kernel(half, day_cols, gathered, _, out, carried, block, out_sems):
+    for day in range(half):
+        block[:, day * day_cols : (day + 1) * day_cols] = (
+            gathered[day, :, :day_cols] + gathered[half + day, :, :day_cols]
+        )
+    block[:, half * day_cols :] = gathered[0, :, day_cols:] + gathered[half, :, day_cols:]
+    repeat_out(block, out, out_sems)
+
+
+def second_kernel(chunks, lines, *refs):
     arguments, refs = refs[:6], refs[6:]
-    sums, post, _, pack, norms, raised_units, raised_days, ends, high_ref, low_ref, *refs = refs
+    sums, post, pack, norms, raised_units, ends, high_ref, low_ref, *refs = refs
     held, small_sems, panel_sems = refs[:6], refs[6], refs[7]
-    groups, day_cols = raised_days.shape
-    unit_rows = raised_units.shape[1]
+    groups, unit_rows = raised_units.shape
+    day_cols = held[5].shape[1]
     small = fetch(arguments[1:], held[1:], small_sems)
     parts = fetch_rows(arguments[0], held[0], panel_sems, chunks)
     panel, cohort, pre_row, _, unit_logit, time_logit = held
-    total = tree_sum(sums[pl.ds(u * groups, groups), :] for u in range(unit_devices))
+    total = tree_sum(sums[pl.ds(u * groups, groups), :] for u in range(lines))
     unit_norm = total[:, 2 * day_cols : 2 * day_cols + 1]
     treat_count = jnp.maximum(total[:, 2 * day_cols + 1 : 2 * day_cols + 2], 1.0)
     norms[...] = total[:, 2 * day_cols :]
@@ -161,9 +170,8 @@
     before = days_of(lax.axis_index("day"), (groups, day_cols)) < pre_end
     gap = total[:, :day_cols] / unit_norm - total[:, day_cols : 2 * day_cols] / treat_count
     raised_time = jnp.where(before, jnp.exp(time_logit[...]), 0.0)
-    raised_days[...] = raised_time
-    time_norm = jnp.sum(raised_time, axis=1, keepdims=True)
-    pack[:, unit_rows:] = jnp.broadcast_to(jnp.concatenate([time_norm] * 3, axis=0), (3 * groups, lanes))
+    pack[:groups, unit_rows:] = raised_time
+    pack[groups:, unit_rows:] = jnp.zeros((2 * groups, day_cols), f32)
     left = split_left(jnp.where(before, gap, 0.0)) + split_left(raised_time)
     left = jnp.concatenate(left, axis=0).astype(bf16)
     label = lax.broadcasted_iota(jnp.int32, (groups, unit_rows), 0)
@@ -180,14 +188,20 @@
 
 def third_kernel(half, chunks, *refs):
     parts, refs = refs[:half], refs[half:]
-    high_ref, low_ref, norms, raised_units, raised_days, ends, scaled, lam, out, block, out_sems = refs
+    high_ref, low_ref, norms, raised_units, ends, scaled, lam, block = refs
     groups, unit_rows = raised_units.shape
-    day_cols = raised_days.shape[1]
+    day_cols = high_ref.shape[1]
     rows = unit_rows // chunks
     unit_norm, ctrl_count = norms[:, 0:1], norms[:, 2:3]
     factor = -step_rate / jnp.sqrt(ends[:, 0:1])
-    time_norm = tree_sum(ref[:groups, unit_rows : unit_rows + 1] for ref in parts)
-    lam[...] = raised_days[...] / time_norm
+    raised_days = [ref[:groups, unit_rows:] for ref in parts]
+    time_norm = tree_sum(jnp.sum(value, axis=1, keepdims=True) for value in raised_days)
+    me = lax.rem(lax.axis_index("day"), half)
+    for day in range(half):
+        here = raised_days[0]
+        for k in range(1, half):
+            here = jnp.where(jnp.bitwise_xor(me, k) == day, raised_days[k], here)
+        lam[:, day * day_cols : (day + 1) * day_cols] = here / time_norm
     time_grad = jnp.zeros((groups, day_cols), f32)
     new_sum = jnp.zeros((groups, 1), f32)
     for chunk in range(chunks):
@@ -202,27 +216,27 @@
         time_grad += add_terms(rows_dot(left, high_ref[here, :], low_ref[here, :]), groups)
     block[:, :day_cols] = time_grad
     block[:, day_cols:] = jnp.broadcast_to(new_sum, (groups, lanes))
-    repeat_out(block, out, out_sems)
-
-
-def fourth_kernel(unit_devices, grads, lam, norms, moved, totals):
-    groups, day_cols = lam.shape
-    total = tree_sum(grads[pl.ds(u * groups, groups), :] for u in range(unit_devices))
+
+
+def fourth_kernel(lines, half, grads, lam, norms, ends, own_days, totals):
+    groups, day_cols = own_days.shape
+    total = tree_sum(grads[pl.ds(u * groups, groups), :] for u in range(lines))
     root = jnp.sqrt(jnp.maximum(norms[:, 2:3], 1.0))
-    new = lam[...] * jnp.exp(total[:, :day_cols] * (-step_rate / root))
-    moved[...] = new
-    lane = lax.broadcasted_iota(jnp.int32, (groups, lanes), 1)
-    totals[...] = jnp.where(lane == 0, total[:, day_cols:], jnp.sum(new, axis=1, keepdims=True))
-
-
-def fifth_kernel(half, *refs):
-    totals, refs = refs[:half], refs[half:]
-    sent_totals, scaled, sent_scaled, moved, ends, unit_weights, time_weights = refs
+    moved = lam[...] * jnp.exp(total[:, : half * day_cols] * (-step_rate / root))
+    scale = ends[:, 0:1] / jnp.sum(moved, axis=1, keepdims=True)
+    me = lax.axis_index("day")
+    own = jnp.zeros((groups, day_cols), f32)
+    for day in range(half):
+        own = jnp.where(me == day, moved[:, day * day_cols : (day + 1) * day_cols], own)
+    own_days[...] = jnp.where(me < half, own * scale, 0.0)
+    totals[...] = total[:, half * day_cols :]
+
+
+def fifth_kernel(half, totals, sent_totals, scaled, sent_scaled, own_days, unit_weights, time_weights):
     first = lax.axis_index("day") < half
-    own = jnp.where(first, totals[0][:, 0:1], sent_totals[:, 0:1])
-    unit_weights[...] = jnp.where(first, scaled[...], sent_scaled[...]) / own
-    day_total = tree_sum(ref[:, 1:2] for ref in totals)
-    time_weights[...] = jnp.where(first, moved[...] / day_total * ends[:, 0:1], 0.0)
+    total = jnp.where(first, totals[:, 0:1], sent_totals[:, 0:1])
+    unit_weights[...] = jnp.where(first, scaled[...], sent_scaled[...]) / total
+    time_weights[...] = own_days[...]
 
 
 def local(outcomes, cohort, pre_end, post_start, unit_logit, time_logit):
@@ -233,8 +247,8 @@
     half = day_devices // 2
     assert half * 2 == day_devices and half & (half - 1) == 0
     assert unit_devices & (unit_devices - 1) == 0
-    chunks = 4
-    beside = pl.CostEstimate(flops=10**10, bytes_accessed=0, transcendentals=0)
+    chunks = 8
+    lines = unit_devices // 2
 
     def spread(value, day_xor, up):
         pairs = [
@@ -245,8 +259,9 @@
     def over_days(value):
         return [value] + [spread(value, k, 0) for k in range(1, half)]
 
-    def over_units(value):
-        return lax.all_to_all(value, "unit", split_axis=0, concat_axis=0, tiled=True)
+    def over_lines(value):
+        members = [[2 * line + side for line in range(lines)] for side in range(2)]
+        return lax.all_to_all(value, "unit", split_axis=0, concat_axis=0, axis_index_groups=members, tiled=True)
 
     def call(kernel, shapes, name, args, in_specs=None, out_specs=None, **more):
         return pl.pallas_call(
@@ -265,72 +280,87 @@
     fixed = [pltpu.with_memory_space_constraint(argument, pltpu.HBM) for argument in arguments]
     held = [pltpu.VMEM(argument.shape, argument.dtype) for argument in arguments]
     small_sems, panel_sems = pltpu.SemaphoreType.DMA((5,)), pltpu.SemaphoreType.DMA((chunks,))
-    out_sems = pltpu.SemaphoreType.DMA((unit_devices,))
+    out_sems = pltpu.SemaphoreType.DMA((lines,))
     width = 2 * day_cols + lanes
-    in_hbm = pltpu.HBM((unit_devices * groups, width), f32)
+    in_hbm = pltpu.HBM((lines * groups, width), f32)
     sums, cross = call(
-        functools.partial(first_kernel, day_devices * day_cols, half, chunks),
-        [in_hbm, ((groups, unit_rows), f32)],
+        functools.partial(first_kernel, day_devices * day_cols, half, chunks // 2),
+        [((groups, width), f32), ((groups, unit_rows), f32)],
         "first_product",
         fixed,
         in_specs=[hbm] * 6,
-        out_specs=[hbm, vmem],
         scratch_shapes=held
         + [
-            pltpu.VMEM((groups, width), f32),
             pltpu.VMEM((4 * groups, unit_rows), bf16),
             small_sems,
             panel_sems,
-            out_sems,
         ],
     )
+    pairs = [[2 * line, 2 * line + 1] for line in range(lines)]
     downward = [
         (u * day_devices + d + half, u * day_devices + d) for u in range(unit_devices) for d in range(half)
     ]
     post = lax.ppermute(cross, ("unit", "day"), downward)
-    (token,) = call(token_kernel, [((groups, lanes), f32)], "post_here", (post,), cost_estimate=beside)
-    pack, norms, raised_units, raised_days, ends, high, low = call(
-        functools.partial(second_kernel, chunks, unit_devices, half),
+    (sums,) = call(
+        pair_kernel,
+        [in_hbm],
+        "pair_sums",
+        (lax.all_gather(sums, "unit", axis_index_groups=pairs),),
+        out_specs=[hbm],
+        scratch_shapes=[pltpu.VMEM((groups, width), f32), out_sems],
+    )
+    all_sums = over_lines(sums)
+    pack, norms, raised_units, ends, high, low = call(
+        functools.partial(second_kernel, chunks, lines),
         [
-            ((3 * groups, unit_rows + lanes), f32),
+            ((3 * groups, unit_rows + day_cols), f32),
             ((groups, lanes), f32),
             ((groups, unit_rows), f32),
-            ((groups, day_cols), f32),
             ((groups, lanes), f32),
             ((unit_rows, day_cols), bf16),
             ((unit_rows, day_cols), bf16),
         ],
         "unit_gradient",
-        (*fixed, over_units(sums), post, token),
-        in_specs=[hbm] * 6 + [vmem, vmem, any_space],
+        (*fixed, all_sums, post),
+        in_specs=[hbm] * 6 + [vmem] * 2,
         scratch_shapes=held + [small_sems, panel_sems],
     )
     width = day_cols + lanes
     scaled, lam, grads = call(
         functools.partial(third_kernel, half, 8),
-        [
-            ((groups, unit_rows), f32),
-            ((groups, day_cols), f32),
-            pltpu.HBM((unit_devices * groups, width), f32),
-        ],
+        [((groups, unit_rows), f32), ((groups, half * day_cols), f32), ((groups, width), f32)],
         "time_gradient",
-        (*over_days(pack), high, low, norms, raised_units, raised_days, ends),
-        out_specs=[vmem, vmem, hbm],
+        (*over_days(pack), high, low, norms, raised_units, ends),
+    )
+    corners = [
+        [unit * day_devices + day for unit in pair for day in range(start, start + half)]
+        for pair in pairs
+        for start in (0, half)
+    ]
+    width = half * day_cols + lanes
+    grads, scaled = call(
+        functools.partial(corner_kernel, half, day_cols),
+        [pltpu.HBM((lines * groups, width), f32), ((groups, unit_rows), f32)],
+        "corner_sums",
+        (lax.all_gather(grads, ("unit", "day"), axis_index_groups=corners), scaled),
+        in_specs=[vmem, any_space],
+        out_specs=[hbm, any_space],
+        input_output_aliases={1: 1},
         scratch_shapes=[pltpu.VMEM((groups, width), f32), out_sems],
     )
+    all_grads = over_lines(grads)
     sent_scaled = spread(scaled, 0, half)
-    moved, totals = call(
-        functools.partial(fourth_kernel, unit_devices),
+    own_days, totals = call(
+        functools.partial(fourth_kernel, lines, half),
         [((groups, day_cols), f32), ((groups, lanes), f32)],
         "new_time_weights",
-        (over_units(grads), lam, norms),
-    )
-    sent_totals = spread(totals, 0, half)
+        (all_grads, lam, norms, ends),
+    )
     return call(
         functools.partial(fifth_kernel, half),
         [((groups, unit_rows), f32), ((groups, day_cols), f32)],
         "scale_weights",
-        (*over_days(totals), sent_totals, scaled, sent_scaled, moved, ends),
+        (totals, spread(totals, 0, half), scaled, sent_scaled, own_days),
     )
 
 

time: 46.5 us -> 52.1 us (1.12)
  blocking collectives: 0 us -> 30.9 us
  starting transfers between devices: 19 us -> 6.13 us
  waiting for transfers between devices: 15.8 us -> 3.04 us
  Pallas kernels: 10.4 us -> 11 us
    all_to_all x0 -> x2, blocking collectives: none -> 20.3 us  [over_lines(): lax.all_to_all(value, 'unit', split_axis=0, concat_axis=0, axis_index_gro...]
    all_to_all x2 -> x0, waiting for transfers between devices: 13 us -> none  [over_units(): lax.all_to_all(value, 'unit', split_axis=0, concat_axis=0, tiled=True)]
    all_to_all x2 -> x0, starting transfers between devices: 10.6 us -> none  [over_units(): lax.all_to_all(value, 'unit', split_axis=0, concat_axis=0, tiled=True)]
    all_gather x0 -> x2, blocking collectives: none -> 10.6 us  [the longest x1 5.35 us: local(): lax.all_gather(sums, 'unit', axis_index_groups=pairs)]
    ppermute x4 -> x3, starting transfers between devices: 7.1 us -> 4.84 us  [spread(): return lax.ppermute(value, ('unit', 'day'), pairs)]
    pallas_call x6 -> x7, Pallas kernels: 10.4 us -> 11 us  [call(): pl.pallas_call(kernel, in_specs=in_specs or [vmem] * len(args), out_specs...]
    ppermute x4 -> x3, waiting for transfers between devices: 2.82 us -> 3.04 us  [spread(): return lax.ppermute(value, ('unit', 'day'), pairs)]
  transfers between devices with their start and end apart: 7 -> 4, of which waited for: 4 -> 2; matrix products, arithmetic and copies ran while one was open for 0% -> 0% of each run, Pallas kernels for 0% -> 2%
where the time goes in v4:
time: 52.1 us; the launch traced here: 51.7 us
  blocking collectives  30.9 us (59%)
  Pallas kernels  11 us (21%)
  starting transfers between devices  6.13 us (12%)
  waiting for transfers between devices  3.04 us (6%)
  between operations  0.7 us (1%)
    all_to_all x2, blocking collectives, over_lines(): lax.all_to_all(value, 'unit', split_axis=0, concat_axis=0, axis_index_gro...  20.3 us
    pallas_call x7, Pallas kernels, call(): pl.pallas_call(kernel, in_specs=in_specs or [vmem] * len(args), out_specs...  11 us
    all_gather x1, blocking collectives, local(): lax.all_gather(sums, 'unit', axis_index_groups=pairs)  5.35 us
    all_gather x1, blocking collectives, local(): lax.all_gather(grads, ('unit', 'day'), axis_index_groups=corners)  5.23 us
    ppermute x3, starting transfers between devices, spread(): return lax.ppermute(value, ('unit', 'day'), pairs)  4.84 us
    ppermute x3, waiting for transfers between devices, spread(): return lax.ppermute(value, ('unit', 'day'), pairs)  3.04 us
    ppermute x1, starting transfers between devices, local(): post = lax.ppermute(cross, ('unit', 'day'), downward)  1.29 us
  transfers between devices with their start and end apart: 4, of which 2 were waited for; matrix products, arithmetic and copies ran while one was open for 0% of the time, Pallas kernels for 2%

profile of v4, /device:TPU:0, one launch (start us, length us, event | category | flops | bytes accessed | tf_op | source)
XLA Modules:
  0.0 51.7 jit_solution(8708452299051009686)
XLA Ops:
  0.6 3.4 %first_product.1 = (f32[8,640]{1,0:T(8,128)S(1)}, f32[8,4096]{1,0:T(8,128)S(1)}) custom-call(f32[4096,256]{1,0:T(8,128)} %refs_0_.3, s32[1,4096]{1,0:T(1,128)} %bitcast.15, s32[1,8]{1,0:T(1,128)} %bitcast.17, s32[1,8]{1,0:T(1,128)} %bitcast.19, f32[8,4096]{1,0:T(8,128)} %refs_4_.3, f32[8,256]{1,0:T(8,128)} %refs_5_.3), custom_call_target="tpu_custom_call" | custom-call | tf_op jit(solution)/shard_map/first_product/pallas_call | solution.py:267
  4.0 1.3 %collective-permute-start = (f32[8,4096]{1,0:T(8,128)S(1)}, f32[8,4096]{1,0:T(8,128)S(1)}, u32[]{:S(2)}, u32[]{:S(2)}) collective-permute-start(f32[8,4096]{1,0:T(8,128)S(1)} %get-tuple-element.18), channel_id=1, source_target_pairs={{2,0},{3,1},{6,4},{7,5},{10,8},{11,9},{14,12},{15,13},{18,16},{19,... | collective-permute-start | bytes 393224 | tf_op jit(solution)/shard_map/ppermute | solution.py:303
  5.3 5.3 %all-gather = f32[16,640]{1,0:T(8,128)S(1)} all-gather(f32[8,640]{1,0:T(8,128)S(1)} %get-tuple-element.17), channel_id=2, replica_groups={{0,4},{8,12},{16,20},{24,28},{1,5},{9,13},{17,21},{25,29},{2,6},{10,14}..., dimensions={0}, use_global_device_ids=true | all-gather | bytes 61440 | tf_op jit(solution)/shard_map/all_gather | solution.py:308
  10.6 0.7 %pair_sums.1 = f32[32,640]{1,0:T(8,128)} custom-call(f32[2,8,640]{2,1,0:T(8,128)S(1)} %bitcast.12), custom_call_target="tpu_custom_call" | custom-call | tf_op jit(solution)/shard_map/pair_sums/pallas_call | solution.py:267
  11.3 11.2 %all_to_all.22 = f32[4,8,640]{2,1,0:T(8,128)S(1)} all-to-all(f32[4,8,640]{2,1,0:T(8,128)} %bitcast.13), channel_id=1, replica_groups={{0,8,16,24},{4,12,20,28},{1,9,17,25},{5,13,21,29},{2,10,18,26},{6,14,22..., dimensions={0} | all-to-all | bytes 163840 | tf_op jit(solution)/shard_map/all_to_all | solution.py:264
  22.5 0.0 collective-permute-done.refs_7_
  22.5 4.4 %unit_gradient.1 = (f32[24,4352]{1,0:T(8,128)S(1)}, f32[8,128]{1,0:T(8,128)S(1)}, f32[8,4096]{1,0:T(8,128)S(1)}, f32[8,128]{1,0:T(8,128)S(1)}, bf16[4096,256]{1,...) custom-call(f32[4096,256]{1,0:T(8,128)} %refs_0_.3, s32[1,4096]{1,0:T(1,128)} %bitcast.16, s32[1,8]{1,0:T(1,128)} %bitcast.18, ...), custom_call_target="tpu_custom_call" | custom-call | tf_op jit(solution)/shard_map/unit_gradient/pallas_call | solution.py:267
  26.9 1.9 %collective-permute-start.1 = (f32[24,4352]{1,0:T(8,128)S(1)}, f32[24,4352]{1,0:T(8,128)S(1)}, u32[]{:S(2)}, u32[]{:S(2)}) collective-permute-start(f32[24,4352]{1,0:T(8,128)S(1)} %get-tuple-element.19.refs_0_), channel_id=1, source_target_pairs={{0,1},{1,0},{4,5},{5,4},{8,9},{9,8},{12,13},{13,12},{16,17},{17,16... | collective-permute-start | bytes 1253384 | tf_op jit(solution)/shard_map/ppermute | solution.py:257
  28.8 1.7 %collective-permute-done.1.refs_1_ = f32[24,4352]{1,0:T(8,128)S(1)} collective-permute-done((f32[24,4352]{1,0:T(8,128)S(1)}, f32[24,4352]{1,0:T(8,128)S(1)}, u32[]{:S(2)}, u32[]{:S(2)}) %collective-permute-start.1) | collective-permute-done | bytes 417824 | tf_op jit(solution)/shard_map/ppermute | solution.py:257
  30.6 0.9 %time_gradient.1 = (f32[8,4096]{1,0:T(8,128)S(1)}, f32[8,512]{1,0:T(8,128)S(1)}, f32[8,384]{1,0:T(8,128)S(1)}) custom-call(f32[24,4352]{1,0:T(8,128)S(1)} %get-tuple-element.19.refs_0_, f32[24,4352]{1,0:T(8,128)S(1)} %collective-permute-done.1.refs_1_, bf16[4096,256]{1,0:T(8,128)(2,1)S(1)} %get-tuple-element.20.refs_2_, ...), custom_call_target="tpu_custom_call" | custom-call | tf_op jit(solution)/shard_map/time_gradient/pallas_call | solution.py:267
  31.5 5.2 %all-gather.1 = f32[32,384]{1,0:T(8,128)S(1)} all-gather(f32[8,384]{1,0:T(8,128)S(1)} %get-tuple-element.25), channel_id=3, replica_groups={{0,1,4,5},{2,3,6,7},{8,9,12,13},{10,11,14,15},{16,17,20,21},{18,19,22,2..., dimensions={0}, use_global_device_ids=true | all-gather | bytes 61440 | tf_op jit(solution)/shard_map/all_gather | solution.py:345
  36.7 0.7 %corner_sums.1 = (f32[32,640]{1,0:T(8,128)}, f32[8,4096]{1,0:T(8,128)S(1)}) custom-call(f32[4,8,384]{2,1,0:T(8,128)S(1)} %bitcast.11, f32[8,4096]{1,0:T(8,128)S(1)} %get-tuple-element.26._), custom_call_target="tpu_custom_call", output_to_operand_aliasing={{1}: (1, {})} | custom-call | tf_op jit(solution)/shard_map/corner_sums/pallas_call | solution.py:267
  37.4 1.6 %collective-permute-start.3 = (f32[8,4096]{1,0:T(8,128)S(1)}, f32[8,4096]{1,0:T(8,128)S(1)}, u32[]{:S(2)}, u32[]{:S(2)}) collective-permute-start(f32[8,4096]{1,0:T(8,128)S(1)} %get-tuple-element.30.scaled), channel_id=1, source_target_pairs={{0,2},{1,3},{4,6},{5,7},{8,10},{9,11},{12,14},{13,15},{16,18},{17,... | collective-permute-start | bytes 393224 | tf_op jit(solution)/shard_map/ppermute | solution.py:257
  39.0 9.1 %all_to_all.23 = f32[4,8,640]{2,1,0:T(8,128)S(1)} all-to-all(f32[4,8,640]{2,1,0:T(8,128)} %bitcast.14), channel_id=1, replica_groups={{0,8,16,24},{4,12,20,28},{1,9,17,25},{5,13,21,29},{2,10,18,26},{6,14,22..., dimensions={0} | all-to-all | bytes 163840 | tf_op jit(solution)/shard_map/all_to_all | solution.py:264
  48.1 0.2 new_time_weights.1
  48.3 1.3 %collective-permute-start.2 = (f32[8,128]{1,0:T(8,128)S(1)}, f32[8,128]{1,0:T(8,128)S(1)}, u32[]{:S(2)}, u32[]{:S(2)}) collective-permute-start(f32[8,128]{1,0:T(8,128)S(1)} %get-tuple-element.29.totals), channel_id=1, source_target_pairs={{0,2},{1,3},{4,6},{5,7},{8,10},{9,11},{12,14},{13,15},{16,18},{17,... | collective-permute-start | bytes 12296 | tf_op jit(solution)/shard_map/ppermute | solution.py:257
  49.6 1.3 %collective-permute-done.2.sent_totals = f32[8,128]{1,0:T(8,128)S(1)} collective-permute-done((f32[8,128]{1,0:T(8,128)S(1)}, f32[8,128]{1,0:T(8,128)S(1)}, u32[]{:S(2)}, u32[]{:S(2)}) %collective-permute-start.2) | collective-permute-done | bytes 4128 | tf_op jit(solution)/shard_map/ppermute | solution.py:257
  50.9 0.0 collective-permute-done.3.sent_scaled
  50.9 0.8 %scale_weights.1 = (f32[8,4096]{1,0:T(8,128)}, f32[8,256]{1,0:T(8,128)}) custom-call(f32[8,128]{1,0:T(8,128)S(1)} %get-tuple-element.29.totals, f32[8,128]{1,0:T(8,128)S(1)} %collective-permute-done.2.sent_totals, f32[8,4096]{1,0:T(8,128)S(1)} %get-tuple-element.30.scaled, f32[8,4096]{1,0:T(8,128)S(1)} %collective-permute-done.3.sent_scaled, ...), custom_call_target="tpu_custom_call" | custom-call | tf_op jit(solution)/shard_map/scale_weights/pallas_call | solution.py:267
Async XLA Ops:
  4.0 18.6 %collective-permute-start = (f32[8,4096]{1,0:T(8,128)S(1)}, f32[8,4096]{1,0:T(8,128)S(1)}, u32[]{:S(2)}, u32[]{:S(2)}) collective-permute-start(f32[8,4096]{1,0:T(8,128)S(1)} %get-tuple-element.18), channel_id=1, source_target_pairs={{2,0},{3,1},{6,4},{7,5},{10,8},{11,9},{14,12},{15,13},{18,16},{19,... | collective-permute-start | bytes 393224 | tf_op jit(solution)/shard_map/ppermute | solution.py:303
  26.9 3.7 %collective-permute-start.1 = (f32[24,4352]{1,0:T(8,128)S(1)}, f32[24,4352]{1,0:T(8,128)S(1)}, u32[]{:S(2)}, u32[]{:S(2)}) collective-permute-start(f32[24,4352]{1,0:T(8,128)S(1)} %get-tuple-element.19.refs_0_), channel_id=1, source_target_pairs={{0,1},{1,0},{4,5},{5,4},{8,9},{9,8},{12,13},{13,12},{16,17},{17,16... | collective-permute-start | bytes 1253384 | tf_op jit(solution)/shard_map/ppermute | solution.py:257
  37.4 13.5 %collective-permute-start.3 = (f32[8,4096]{1,0:T(8,128)S(1)}, f32[8,4096]{1,0:T(8,128)S(1)}, u32[]{:S(2)}, u32[]{:S(2)}) collective-permute-start(f32[8,4096]{1,0:T(8,128)S(1)} %get-tuple-element.30.scaled), channel_id=1, source_target_pairs={{0,2},{1,3},{4,6},{5,7},{8,10},{9,11},{12,14},{13,15},{16,18},{17,... | collective-permute-start | bytes 393224 | tf_op jit(solution)/shard_map/ppermute | solution.py:257
  48.3 2.6 %collective-permute-start.2 = (f32[8,128]{1,0:T(8,128)S(1)}, f32[8,128]{1,0:T(8,128)S(1)}, u32[]{:S(2)}, u32[]{:S(2)}) collective-permute-start(f32[8,128]{1,0:T(8,128)S(1)} %get-tuple-element.29.totals), channel_id=1, source_target_pairs={{0,2},{1,3},{4,6},{5,7},{8,10},{9,11},{12,14},{13,15},{16,18},{17,... | collective-permute-start | bytes 12296 | tf_op jit(solution)/shard_map/ppermute | solution.py:257

commit v5 on v3

--- a/solution.py
+++ b/solution.py
@@ -11,10 +11,10 @@
 f32 = jnp.float32
 bf16 = jnp.bfloat16
 lanes = 128
+block_rows = 256
 params = pltpu.CompilerParams(vmem_limit_bytes=24 * 1024 * 1024)
 vmem = pl.BlockSpec(memory_space=pltpu.VMEM)
 hbm = pl.BlockSpec(memory_space=pltpu.HBM)
-any_space = pl.BlockSpec(memory_space=pl.ANY)
 
 
 def split_left(value):
@@ -79,7 +79,8 @@
     rows = source.shape[0] // chunks
     parts = [pl.ds(chunk * rows, rows) for chunk in range(chunks)]
     copies = fetch([source.at[here] for here in parts], [target.at[here] for here in parts], sems)
-    return list(zip(parts, copies))
+    blocks = [[pl.ds(part.start + i, block_rows) for i in range(0, rows, block_rows)] for part in parts]
+    return list(zip(blocks, copies))
 
 
 def wait_all(copies):
@@ -120,9 +121,10 @@
             ),
         )
         product = jnp.zeros((4 * groups, day_cols), f32)
-        for here, copy in parts:
+        for blocks, copy in parts:
             copy.wait()
-            product += rows_dot(left_ref[:, here], *split_panel(panel[here, :]))
+            for here in blocks:
+                product += rows_dot(left_ref[:, here], *split_panel(panel[here, :]))
         block[:, :day_cols] = add_terms(product, groups)
         block[:, day_cols : 2 * day_cols] = product[3 * groups :]
         repeat_out(block, out, out_sems)
@@ -132,18 +134,15 @@
         post_start = column(post_row)
         after = jnp.where(days_of(me, (groups, day_cols)) >= post_start, 1.0, 0.0)
         left = left_of(after / (all_count - post_start).astype(f32))
-        for here, copy in parts:
+        for blocks, copy in parts:
             copy.wait()
-            cross[:, here] = add_terms(days_dot(left, *split_panel(panel[here, :])), groups)
-
-
-def token_kernel(value, token):
-    token[...] = value[:, : token.shape[1]]
+            for here in blocks:
+                cross[:, here] = add_terms(days_dot(left, *split_panel(panel[here, :])), groups)
 
 
 def second_kernel(chunks, unit_devices, half, *refs):
     arguments, refs = refs[:6], refs[6:]
-    sums, post, _, pack, norms, raised_units, raised_days, ends, high_ref, low_ref, *refs = refs
+    sums, post, pack, norms, raised_units, raised_days, ends, high_ref, low_ref, *refs = refs
     held, small_sems, panel_sems = refs[:6], refs[6], refs[7]
     groups, day_cols = raised_days.shape
     unit_rows = raised_units.shape[1]
@@ -168,14 +167,15 @@
     left = jnp.concatenate(left, axis=0).astype(bf16)
     label = lax.broadcasted_iota(jnp.int32, (groups, unit_rows), 0)
     raised_units[...] = jnp.where(cohort[...] > label, jnp.exp(unit_logit[...]), 0.0)
-    for here, copy in parts:
+    for blocks, copy in parts:
         copy.wait()
-        high, low = split_panel(panel[here, :])
-        high_ref[here, :] = high
-        low_ref[here, :] = low
-        product = days_dot(left, high, low)
-        pack[:groups, here] = add_terms(product, groups)
-        pack[groups : 2 * groups, here] = add_terms(product[3 * groups :], groups)
+        for here in blocks:
+            high, low = split_panel(panel[here, :])
+            high_ref[here, :] = high
+            low_ref[here, :] = low
+            product = days_dot(left, high, low)
+            pack[:groups, here] = add_terms(product, groups)
+            pack[groups : 2 * groups, here] = add_terms(product[3 * groups :], groups)
 
 
 def third_kernel(half, chunks, *refs):
@@ -205,23 +205,23 @@
     repeat_out(block, out, out_sems)
 
 
-def fourth_kernel(unit_devices, grads, lam, norms, moved, totals):
+def fourth_kernel(unit_devices, grads, lam, norms, moved, moved_sum, totals):
     groups, day_cols = lam.shape
     total = tree_sum(grads[pl.ds(u * groups, groups), :] for u in range(unit_devices))
     root = jnp.sqrt(jnp.maximum(norms[:, 2:3], 1.0))
     new = lam[...] * jnp.exp(total[:, :day_cols] * (-step_rate / root))
     moved[...] = new
-    lane = lax.broadcasted_iota(jnp.int32, (groups, lanes), 1)
-    totals[...] = jnp.where(lane == 0, total[:, day_cols:], jnp.sum(new, axis=1, keepdims=True))
+    totals[...] = total[:, day_cols:]
+    moved_sum[...] = jnp.broadcast_to(jnp.sum(new, axis=1, keepdims=True), moved_sum.shape)
 
 
 def fifth_kernel(half, *refs):
-    totals, refs = refs[:half], refs[half:]
-    sent_totals, scaled, sent_scaled, moved, ends, unit_weights, time_weights = refs
+    moved_sums, refs = refs[:half], refs[half:]
+    totals, sent_totals, scaled, sent_scaled, moved, ends, unit_weights, time_weights = refs
     first = lax.axis_index("day") < half
-    own = jnp.where(first, totals[0][:, 0:1], sent_totals[:, 0:1])
+    own = jnp.where(first, totals[:, 0:1], sent_totals[:, 0:1])
     unit_weights[...] = jnp.where(first, scaled[...], sent_scaled[...]) / own
-    day_total = tree_sum(ref[:, 1:2] for ref in totals)
+    day_total = tree_sum(ref[:, 0:1] for ref in moved_sums)
     time_weights[...] = jnp.where(first, moved[...] / day_total * ends[:, 0:1], 0.0)
 
 
@@ -234,8 +234,6 @@
     assert half * 2 == day_devices and half & (half - 1) == 0
     assert unit_devices & (unit_devices - 1) == 0
     chunks = 4
-    beside = pl.CostEstimate(flops=10**10, bytes_accessed=0, transcendentals=0)
-
     def spread(value, day_xor, up):
         pairs = [
             (u * day_devices + d, u * day_devices + (d ^ day_xor) + up) for u in range(unit_devices) for d in range(half)
@@ -288,7 +286,6 @@
         (u * day_devices + d + half, u * day_devices + d) for u in range(unit_devices) for d in range(half)
     ]
     post = lax.ppermute(cross, ("unit", "day"), downward)
-    (token,) = call(token_kernel, [((groups, lanes), f32)], "post_here", (post,), cost_estimate=beside)
     pack, norms, raised_units, raised_days, ends, high, low = call(
         functools.partial(second_kernel, chunks, unit_devices, half),
         [
@@ -301,8 +298,8 @@
             ((unit_rows, day_cols), bf16),
         ],
         "unit_gradient",
-        (*fixed, over_units(sums), post, token),
-        in_specs=[hbm] * 6 + [vmem, vmem, any_space],
+        (*fixed, over_units(sums), post),
+        in_specs=[hbm] * 6 + [vmem] * 2,
         scratch_shapes=held + [small_sems, panel_sems],
     )
     width = day_cols + lanes
@@ -319,18 +316,17 @@
         scratch_shapes=[pltpu.VMEM((groups, width), f32), out_sems],
     )
     sent_scaled = spread(scaled, 0, half)
-    moved, totals = call(
+    moved, moved_sum, totals = call(
         functools.partial(fourth_kernel, unit_devices),
-        [((groups, day_cols), f32), ((groups, lanes), f32)],
+        [((groups, day_cols), f32), ((groups, lanes), f32), ((groups, lanes), f32)],
         "new_time_weights",
         (over_units(grads), lam, norms),
     )
-    sent_totals = spread(totals, 0, half)
     return call(
         functools.partial(fifth_kernel, half),
         [((groups, unit_rows), f32), ((groups, day_cols), f32)],
         "scale_weights",
-        (*over_days(totals), sent_totals, scaled, sent_scaled, moved, ends),
+        (*over_days(moved_sum), totals, spread(totals, 0, half), scaled, sent_scaled, moved, ends),
     )
 
 

time: 46.5 us -> 47 us (1.011)
  starting transfers between devices: 19 us -> 20.3 us
  waiting for transfers between devices: 15.8 us -> 15.1 us
    all_to_all x2, waiting for transfers between devices: 13 us -> 6.54 us  [over_units(): lax.all_to_all(value, 'unit', split_axis=0, concat_axis=0, tiled=True)]
    ppermute x1, waiting for transfers between devices: 0.01 us -> 5.56 us  [local(): post = lax.ppermute(cross, ('unit', 'day'), downward)]
    all_to_all x2, starting transfers between devices: 10.6 us -> 12.6 us  [over_units(): lax.all_to_all(value, 'unit', split_axis=0, concat_axis=0, tiled=True)]
    ppermute x4, starting transfers between devices: 7.1 us -> 6.41 us  [spread(): return lax.ppermute(value, ('unit', 'day'), pairs)]
    pallas_call x6 -> x5, Pallas kernels: 10.4 us -> 10.4 us  [call(): pl.pallas_call(kernel, in_specs=in_specs or [vmem] * len(args), out_specs...]
  transfers between devices with their start and end apart: 7 -> 7, of which waited for: 4 -> 5; matrix products, arithmetic and copies ran while one was open for 0% -> 0% of each run, Pallas kernels for 0% -> 0%
where the time goes in v5:
time: 47 us; the launch traced here: 46.5 us
  starting transfers between devices  20.3 us (43%)
  waiting for transfers between devices  15.1 us (32%)
  Pallas kernels  10.4 us (22%)
  between operations  0.71 us (2%)
    all_to_all x2, starting transfers between devices, over_units(): lax.all_to_all(value, 'unit', split_axis=0, concat_axis=0, tiled=True)  12.6 us
    pallas_call x5, Pallas kernels, call(): pl.pallas_call(kernel, in_specs=in_specs or [vmem] * len(args), out_specs...  10.4 us
    all_to_all x2, waiting for transfers between devices, over_units(): lax.all_to_all(value, 'unit', split_axis=0, concat_axis=0, tiled=True)  6.54 us
    ppermute x4, starting transfers between devices, spread(): return lax.ppermute(value, ('unit', 'day'), pairs)  6.41 us
    ppermute x1, waiting for transfers between devices, local(): post = lax.ppermute(cross, ('unit', 'day'), downward)  5.56 us
    ppermute x4, waiting for transfers between devices, spread(): return lax.ppermute(value, ('unit', 'day'), pairs)  3 us
    ppermute x1, starting transfers between devices, local(): post = lax.ppermute(cross, ('unit', 'day'), downward)  1.28 us
  transfers between devices with their start and end apart: 7, of which 5 were waited for; matrix products, arithmetic and copies ran while one was open for 0% of the time, Pallas kernels for 0%

profile of v5, /device:TPU:0, one launch (start us, length us, event | category | flops | bytes accessed | tf_op | source)
XLA Modules:
  0.0 46.5 jit_solution(10099034635613376756)
XLA Ops:
  0.6 4.0 %first_product.1 = (f32[64,640]{1,0:T(8,128)}, f32[8,4096]{1,0:T(8,128)S(1)}) custom-call(f32[4096,256]{1,0:T(8,128)} %refs_0_.3, s32[1,4096]{1,0:T(1,128)} %bitcast.11, s32[1,8]{1,0:T(1,128)} %bitcast.13, s32[1,8]{1,0:T(1,128)} %bitcast.15, f32[8,4096]{1,0:T(8,128)} %refs_4_.3, f32[8,256]{1,0:T(8,128)} %refs_5_.3), custom_call_target="tpu_custom_call" | custom-call | tf_op jit(solution)/shard_map/first_product/pallas_call | solution.py:250
  4.7 7.3 %all-to-all-start = ((f32[8,8,640]{2,1,0:T(8,128)}), f32[8,8,640]{2,1,0:T(8,128)S(1)}, u32[]{:S(2)}, u32[]{:S(2)}) async-start(f32[8,8,640]{2,1,0:T(8,128)} %bitcast.9), calls=%async_computation | async-start | bytes 327680 | tf_op jit(solution)/shard_map/all_to_all | solution.py:247
  11.9 1.3 %collective-permute-start = (f32[8,4096]{1,0:T(8,128)S(1)}, f32[8,4096]{1,0:T(8,128)S(1)}, u32[]{:S(2)}, u32[]{:S(2)}) collective-permute-start(f32[8,4096]{1,0:T(8,128)S(1)} %get-tuple-element.18), channel_id=1, source_target_pairs={{2,0},{3,1},{6,4},{7,5},{10,8},{11,9},{14,12},{15,13},{18,16},{19,... | collective-permute-start | bytes 393224 | tf_op jit(solution)/shard_map/ppermute | solution.py:288
  13.2 5.6 %collective-permute-done.refs_7_ = f32[8,4096]{1,0:T(8,128)S(1)} collective-permute-done((f32[8,4096]{1,0:T(8,128)S(1)}, f32[8,4096]{1,0:T(8,128)S(1)}, u32[]{:S(2)}, u32[]{:S(2)}) %collective-permute-start) | collective-permute-done | bytes 131104 | tf_op jit(solution)/shard_map/ppermute | solution.py:288
  18.8 0.7 %all-to-all-done = f32[8,8,640]{2,1,0:T(8,128)S(1)} async-done(((f32[8,8,640]{2,1,0:T(8,128)}), f32[8,8,640]{2,1,0:T(8,128)S(1)}, u32[]{:S(2)}, u32[]{:S(2)}) %all-to-all-start) | async-done | bytes 163872 | tf_op jit(solution)/shard_map/all_to_all | solution.py:247
  19.5 3.8 %unit_gradient.1 = (f32[24,4224]{1,0:T(8,128)S(1)}, f32[8,128]{1,0:T(8,128)S(1)}, f32[8,4096]{1,0:T(8,128)S(1)}, f32[8,256]{1,0:T(8,128)S(1)}, f32[8,128]{1,0:T(...) custom-call(f32[4096,256]{1,0:T(8,128)} %refs_0_.3, s32[1,4096]{1,0:T(1,128)} %bitcast.12, ...), custom_call_target="tpu_custom_call" | custom-call | tf_op jit(solution)/shard_map/unit_gradient/pallas_call | solution.py:250
  23.4 1.9 %collective-permute-start.1 = (f32[24,4224]{1,0:T(8,128)S(1)}, f32[24,4224]{1,0:T(8,128)S(1)}, u32[]{:S(2)}, u32[]{:S(2)}) collective-permute-start(f32[24,4224]{1,0:T(8,128)S(1)} %get-tuple-element.19.refs_0_), channel_id=1, source_target_pairs={{0,1},{1,0},{4,5},{5,4},{8,9},{9,8},{12,13},{13,12},{16,17},{17,16... | collective-permute-start | bytes 1216520 | tf_op jit(solution)/shard_map/ppermute | solution.py:241
  25.3 1.7 %collective-permute-done.1.refs_1_ = f32[24,4224]{1,0:T(8,128)S(1)} collective-permute-done((f32[24,4224]{1,0:T(8,128)S(1)}, f32[24,4224]{1,0:T(8,128)S(1)}, u32[]{:S(2)}, u32[]{:S(2)}) %collective-permute-start.1) | collective-permute-done | bytes 405536 | tf_op jit(solution)/shard_map/ppermute | solution.py:241
  27.0 1.6 %time_gradient.1 = (f32[8,4096]{1,0:T(8,128)S(1)}, f32[8,256]{1,0:T(8,128)S(1)}, f32[64,384]{1,0:T(8,128)}) custom-call(f32[24,4224]{1,0:T(8,128)S(1)} %get-tuple-element.19.refs_0_, f32[24,4224]{1,0:T(8,128)S(1)} %collective-permute-done.1.refs_1_, bf16[4096,256]{1,0:T(8,128)(2,1)S(1)} %get-tuple-element.20.refs_2_, ...), custom_call_target="tpu_custom_call" | custom-call | tf_op jit(solution)/shard_map/time_gradient/pallas_call | solution.py:250
  28.6 5.3 %all-to-all-start.1 = ((f32[8,8,384]{2,1,0:T(8,128)}), f32[8,8,384]{2,1,0:T(8,128)S(1)}, u32[]{:S(2)}, u32[]{:S(2)}) async-start(f32[8,8,384]{2,1,0:T(8,128)} %bitcast.10), calls=%async_computation.1 | async-start | bytes 196608 | tf_op jit(solution)/shard_map/all_to_all | solution.py:247
  33.9 1.3 %collective-permute-start.4 = (f32[8,4096]{1,0:T(8,128)S(1)}, f32[8,4096]{1,0:T(8,128)S(1)}, u32[]{:S(2)}, u32[]{:S(2)}) collective-permute-start(f32[8,4096]{1,0:T(8,128)S(1)} %get-tuple-element.30.refs_4_), channel_id=1, source_target_pairs={{0,2},{1,3},{4,6},{5,7},{8,10},{9,11},{12,14},{13,15},{16,18},{17,... | collective-permute-start | bytes 393224 | tf_op jit(solution)/shard_map/ppermute | solution.py:241
  35.2 5.8 %all-to-all-done.1 = f32[8,8,384]{2,1,0:T(8,128)S(1)} async-done(((f32[8,8,384]{2,1,0:T(8,128)}), f32[8,8,384]{2,1,0:T(8,128)S(1)}, u32[]{:S(2)}, u32[]{:S(2)}) %all-to-all-start.1) | async-done | bytes 98336 | tf_op jit(solution)/shard_map/all_to_all | solution.py:247
  41.0 0.2 new_time_weights.1
  41.2 1.9 %collective-permute-start.2 = (f32[8,128]{1,0:T(8,128)S(1)}, f32[8,128]{1,0:T(8,128)S(1)}, u32[]{:S(2)}, u32[]{:S(2)}) collective-permute-start(f32[8,128]{1,0:T(8,128)S(1)} %get-tuple-element.28.refs_0_), channel_id=1, source_target_pairs={{0,1},{1,0},{4,5},{5,4},{8,9},{9,8},{12,13},{13,12},{16,17},{17,16... | collective-permute-start | bytes 12296 | tf_op jit(solution)/shard_map/ppermute | solution.py:241
  43.1 1.3 %collective-permute-start.3 = (f32[8,128]{1,0:T(8,128)S(1)}, f32[8,128]{1,0:T(8,128)S(1)}, u32[]{:S(2)}, u32[]{:S(2)}) collective-permute-start(f32[8,128]{1,0:T(8,128)S(1)} %get-tuple-element.29.refs_2_), channel_id=1, source_target_pairs={{0,2},{1,3},{4,6},{5,7},{8,10},{9,11},{12,14},{13,15},{16,18},{17,... | collective-permute-start | bytes 12296 | tf_op jit(solution)/shard_map/ppermute | solution.py:241
  44.4 0.0 collective-permute-done.4.refs_5_
  44.4 0.0 collective-permute-done.2.refs_1_
  44.4 1.3 %collective-permute-done.3.refs_3_ = f32[8,128]{1,0:T(8,128)S(1)} collective-permute-done((f32[8,128]{1,0:T(8,128)S(1)}, f32[8,128]{1,0:T(8,128)S(1)}, u32[]{:S(2)}, u32[]{:S(2)}) %collective-permute-start.3) | collective-permute-done | bytes 4128 | tf_op jit(solution)/shard_map/ppermute | solution.py:241
  45.7 0.8 %scale_weights.1 = (f32[8,4096]{1,0:T(8,128)}, f32[8,256]{1,0:T(8,128)}) custom-call(f32[8,128]{1,0:T(8,128)S(1)} %get-tuple-element.28.refs_0_, f32[8,128]{1,0:T(8,128)S(1)} %collective-permute-done.2.refs_1_, f32[8,128]{1,0:T(8,128)S(1)} %get-tuple-element.29.refs_2_, f32[8,128]{1,0:T(8,128)S(1)} %collective-permute-done.3.refs_3_, ...), custom_call_target="tpu_custom_call" | custom-call | tf_op jit(solution)/shard_map/scale_weights/pallas_call | solution.py:250
Async XLA Ops:
  4.7 14.8 %all-to-all-start = ((f32[8,8,640]{2,1,0:T(8,128)}), f32[8,8,640]{2,1,0:T(8,128)S(1)}, u32[]{:S(2)}, u32[]{:S(2)}) async-start(f32[8,8,640]{2,1,0:T(8,128)} %bitcast.9), calls=%async_computation | async-start | bytes 327680 | tf_op jit(solution)/shard_map/all_to_all | solution.py:247
  11.9 6.8 %collective-permute-start = (f32[8,4096]{1,0:T(8,128)S(1)}, f32[8,4096]{1,0:T(8,128)S(1)}, u32[]{:S(2)}, u32[]{:S(2)}) collective-permute-start(f32[8,4096]{1,0:T(8,128)S(1)} %get-tuple-element.18), channel_id=1, source_target_pairs={{2,0},{3,1},{6,4},{7,5},{10,8},{11,9},{14,12},{15,13},{18,16},{19,... | collective-permute-start | bytes 393224 | tf_op jit(solution)/shard_map/ppermute | solution.py:288
  23.4 3.6 %collective-permute-start.1 = (f32[24,4224]{1,0:T(8,128)S(1)}, f32[24,4224]{1,0:T(8,128)S(1)}, u32[]{:S(2)}, u32[]{:S(2)}) collective-permute-start(f32[24,4224]{1,0:T(8,128)S(1)} %get-tuple-element.19.refs_0_), channel_id=1, source_target_pairs={{0,1},{1,0},{4,5},{5,4},{8,9},{9,8},{12,13},{13,12},{16,17},{17,16... | collective-permute-start | bytes 1216520 | tf_op jit(solution)/shard_map/ppermute | solution.py:241
  28.6 12.4 %all-to-all-start.1 = ((f32[8,8,384]{2,1,0:T(8,128)}), f32[8,8,384]{2,1,0:T(8,128)S(1)}, u32[]{:S(2)}, u32[]{:S(2)}) async-start(f32[8,8,384]{2,1,0:T(8,128)} %bitcast.10), calls=%async_computation.1 | async-start | bytes 196608 | tf_op jit(solution)/shard_map/all_to_all | solution.py:247
  33.9 10.5 %collective-permute-start.4 = (f32[8,4096]{1,0:T(8,128)S(1)}, f32[8,4096]{1,0:T(8,128)S(1)}, u32[]{:S(2)}, u32[]{:S(2)}) collective-permute-start(f32[8,4096]{1,0:T(8,128)S(1)} %get-tuple-element.30.refs_4_), channel_id=1, source_target_pairs={{0,2},{1,3},{4,6},{5,7},{8,10},{9,11},{12,14},{13,15},{16,18},{17,... | collective-permute-start | bytes 393224 | tf_op jit(solution)/shard_map/ppermute | solution.py:241
  41.2 3.2 %collective-permute-start.2 = (f32[8,128]{1,0:T(8,128)S(1)}, f32[8,128]{1,0:T(8,128)S(1)}, u32[]{:S(2)}, u32[]{:S(2)}) collective-permute-start(f32[8,128]{1,0:T(8,128)S(1)} %get-tuple-element.28.refs_0_), channel_id=1, source_target_pairs={{0,1},{1,0},{4,5},{5,4},{8,9},{9,8},{12,13},{13,12},{16,17},{17,16... | collective-permute-start | bytes 12296 | tf_op jit(solution)/shard_map/ppermute | solution.py:241
  43.1 2.6 %collective-permute-start.3 = (f32[8,128]{1,0:T(8,128)S(1)}, f32[8,128]{1,0:T(8,128)S(1)}, u32[]{:S(2)}, u32[]{:S(2)}) collective-permute-start(f32[8,128]{1,0:T(8,128)S(1)} %get-tuple-element.29.refs_2_), channel_id=1, source_target_pairs={{0,2},{1,3},{4,6},{5,7},{8,10},{9,11},{12,14},{13,15},{16,18},{17,... | collective-permute-start | bytes 12296 | tf_op jit(solution)/shard_map/ppermute | solution.py:241

commit v6 on v5

--- a/solution.py
+++ b/solution.py
@@ -75,9 +75,9 @@
     return copies
 
 
-def fetch_rows(source, target, sems, chunks):
-    rows = source.shape[0] // chunks
-    parts = [pl.ds(chunk * rows, rows) for chunk in range(chunks)]
+def fetch_rows(source, target, sems, chunks, first=0):
+    rows = (source.shape[0] - first) // chunks
+    parts = [pl.ds(first + chunk * rows, rows) for chunk in range(chunks)]
     copies = fetch([source.at[here] for here in parts], [target.at[here] for here in parts], sems)
     blocks = [[pl.ds(part.start + i, block_rows) for i in range(0, rows, block_rows)] for part in parts]
     return list(zip(blocks, copies))
@@ -96,7 +96,7 @@
 
 def first_kernel(all_count, half, chunks, *refs):
     arguments, refs = refs[:6], refs[6:]
-    out, cross, *held, block, left_ref, small_sems, panel_sems, out_sems = refs
+    out, cross, high_ref, low_ref, *held, block, left_ref, small_sems, panel_sems, out_sems = refs
     groups, day_cols = held[5].shape
     unit_rows = held[0].shape[0]
     small = fetch(arguments[1:], held[1:], small_sems)
@@ -124,7 +124,11 @@
         for blocks, copy in parts:
             copy.wait()
             for here in blocks:
-                product += rows_dot(left_ref[:, here], *split_panel(panel[here, :]))
+                high, low = split_panel(panel[here, :])
+                if here.start < high_ref.shape[0]:
+                    high_ref[here, :] = high
+                    low_ref[here, :] = low
+                product += rows_dot(left_ref[:, here], high, low)
         block[:, :day_cols] = add_terms(product, groups)
         block[:, day_cols : 2 * day_cols] = product[3 * groups :]
         repeat_out(block, out, out_sems)
@@ -140,58 +144,71 @@
                 cross[:, here] = add_terms(days_dot(left, *split_panel(panel[here, :])), groups)
 
 
-def second_kernel(chunks, unit_devices, half, *refs):
+def second_kernel(chunks, unit_devices, *refs):
     arguments, refs = refs[:6], refs[6:]
-    sums, post, pack, norms, raised_units, raised_days, ends, high_ref, low_ref, *refs = refs
+    sums, high_ref, low_ref, pack, norms, raised_units, ends, more_high, more_low, *refs = refs
     held, small_sems, panel_sems = refs[:6], refs[6], refs[7]
-    groups, day_cols = raised_days.shape
-    unit_rows = raised_units.shape[1]
+    groups, unit_rows = raised_units.shape
+    resident, day_cols = high_ref.shape
+    panel, cohort, pre_row, _, unit_logit, time_logit = held
     small = fetch(arguments[1:], held[1:], small_sems)
-    parts = fetch_rows(arguments[0], held[0], panel_sems, chunks)
-    panel, cohort, pre_row, _, unit_logit, time_logit = held
+    parts = fetch_rows(arguments[0], panel, panel_sems, chunks, resident)
     total = tree_sum(sums[pl.ds(u * groups, groups), :] for u in range(unit_devices))
     unit_norm = total[:, 2 * day_cols : 2 * day_cols + 1]
     treat_count = jnp.maximum(total[:, 2 * day_cols + 1 : 2 * day_cols + 2], 1.0)
     norms[...] = total[:, 2 * day_cols :]
-    pack[2 * groups :, :unit_rows] = post[...]
+    gap = total[:, :day_cols] / unit_norm - total[:, day_cols : 2 * day_cols] / treat_count
     wait_all(small)
     pre_end = column(pre_row)
     ends[...] = jnp.broadcast_to(pre_end.astype(f32), ends.shape)
     before = days_of(lax.axis_index("day"), (groups, day_cols)) < pre_end
-    gap = total[:, :day_cols] / unit_norm - total[:, day_cols : 2 * day_cols] / treat_count
     raised_time = jnp.where(before, jnp.exp(time_logit[...]), 0.0)
-    raised_days[...] = raised_time
-    time_norm = jnp.sum(raised_time, axis=1, keepdims=True)
-    pack[:, unit_rows:] = jnp.broadcast_to(jnp.concatenate([time_norm] * 3, axis=0), (3 * groups, lanes))
+    pack[:groups, unit_rows:] = raised_time
+    pack[groups:, unit_rows:] = jnp.zeros_like(raised_time)
     left = split_left(jnp.where(before, gap, 0.0)) + split_left(raised_time)
     left = jnp.concatenate(left, axis=0).astype(bf16)
     label = lax.broadcasted_iota(jnp.int32, (groups, unit_rows), 0)
     raised_units[...] = jnp.where(cohort[...] > label, jnp.exp(unit_logit[...]), 0.0)
+
+    def multiply(here, high, low):
+        product = days_dot(left, high, low)
+        pack[:groups, here] = add_terms(product, groups)
+        pack[groups:, here] = add_terms(product[3 * groups :], groups)
+
+    for start in range(0, resident, block_rows):
+        here = pl.ds(start, block_rows)
+        multiply(here, high_ref[here, :], low_ref[here, :])
     for blocks, copy in parts:
         copy.wait()
         for here in blocks:
+            there = pl.ds(here.start - resident, block_rows)
             high, low = split_panel(panel[here, :])
-            high_ref[here, :] = high
-            low_ref[here, :] = low
-            product = days_dot(left, high, low)
-            pack[:groups, here] = add_terms(product, groups)
-            pack[groups : 2 * groups, here] = add_terms(product[3 * groups :], groups)
-
-
-def third_kernel(half, chunks, *refs):
+            more_high[there, :] = high
+            more_low[there, :] = low
+            multiply(here, high, low)
+
+
+def join_kernel(pack, post, out):
+    rows, width = pack.shape
+    out[:rows, :] = pack[...]
+    out[rows:, : post.shape[1]] = post[...]
+    out[rows:, post.shape[1] :] = jnp.zeros((post.shape[0], width - post.shape[1]), f32)
+
+
+def third_kernel(half, *refs):
     parts, refs = refs[:half], refs[half:]
-    high_ref, low_ref, norms, raised_units, raised_days, ends, scaled, lam, out, block, out_sems = refs
+    high_ref, low_ref, more_high, more_low, norms, raised_units, ends, scaled, lam, out, block, out_sems = refs
     groups, unit_rows = raised_units.shape
-    day_cols = raised_days.shape[1]
-    rows = unit_rows // chunks
+    resident, day_cols = high_ref.shape
     unit_norm, ctrl_count = norms[:, 0:1], norms[:, 2:3]
     factor = -step_rate / jnp.sqrt(ends[:, 0:1])
-    time_norm = tree_sum(ref[:groups, unit_rows : unit_rows + 1] for ref in parts)
-    lam[...] = raised_days[...] / time_norm
+    raised_days = [ref[:groups, unit_rows:] for ref in parts]
+    time_norm = tree_sum(jnp.sum(value, axis=1, keepdims=True) for value in raised_days)
+    lam[...] = raised_days[0] / time_norm
     time_grad = jnp.zeros((groups, day_cols), f32)
     new_sum = jnp.zeros((groups, 1), f32)
-    for chunk in range(chunks):
-        here = pl.ds(chunk * rows, rows)
+    for start in range(0, unit_rows, 2 * block_rows):
+        here = pl.ds(start, 2 * block_rows)
         whole = tree_sum(ref[:, here] for ref in parts)
         raised = raised_units[:, here]
         new = raised / unit_norm * jnp.exp(whole[:groups] * factor)
@@ -199,7 +216,12 @@
         scaled[:, here] = new * ctrl_count
         shortfall = whole[groups : 2 * groups] / time_norm - whole[2 * groups :]
         left = left_of(jnp.where(raised > 0.0, shortfall, 0.0))
-        time_grad += add_terms(rows_dot(left, high_ref[here, :], low_ref[here, :]), groups)
+        if start < resident:
+            high, low = high_ref[here, :], low_ref[here, :]
+        else:
+            there = pl.ds(start - resident, 2 * block_rows)
+            high, low = more_high[there, :], more_low[there, :]
+        time_grad += add_terms(rows_dot(left, high, low), groups)
     block[:, :day_cols] = time_grad
     block[:, day_cols:] = jnp.broadcast_to(new_sum, (groups, lanes))
     repeat_out(block, out, out_sems)
@@ -217,12 +239,18 @@
 
 def fifth_kernel(half, *refs):
     moved_sums, refs = refs[:half], refs[half:]
-    totals, sent_totals, scaled, sent_scaled, moved, ends, unit_weights, time_weights = refs
+    totals, scaled, moved, ends, unit_weights, time_weights = refs
     first = lax.axis_index("day") < half
-    own = jnp.where(first, totals[:, 0:1], sent_totals[:, 0:1])
-    unit_weights[...] = jnp.where(first, scaled[...], sent_scaled[...]) / own
+    unit_weights[...] = scaled[...] / totals[:, 0:1]
     day_total = tree_sum(ref[:, 0:1] for ref in moved_sums)
     time_weights[...] = jnp.where(first, moved[...] / day_total * ends[:, 0:1], 0.0)
+
+
+def sixth_kernel(half, sent_totals, sent_scaled, _, unit_weights, block, out_sem):
+    @pl.when(lax.axis_index("day") >= half)
+    def _():
+        block[...] = sent_scaled[...] / sent_totals[:, 0:1]
+        wait_all(fetch([block], [unit_weights], out_sem))
 
 
 def local(outcomes, cohort, pre_end, post_start, unit_logit, time_logit):
@@ -234,6 +262,7 @@
     assert half * 2 == day_devices and half & (half - 1) == 0
     assert unit_devices & (unit_devices - 1) == 0
     chunks = 4
+    resident = unit_rows * 5 // 8 // (2 * block_rows) * (2 * block_rows)
     def spread(value, day_xor, up):
         pairs = [
             (u * day_devices + d, u * day_devices + (d ^ day_xor) + up) for u in range(unit_devices) for d in range(half)
@@ -263,16 +292,18 @@
     fixed = [pltpu.with_memory_space_constraint(argument, pltpu.HBM) for argument in arguments]
     held = [pltpu.VMEM(argument.shape, argument.dtype) for argument in arguments]
     small_sems, panel_sems = pltpu.SemaphoreType.DMA((5,)), pltpu.SemaphoreType.DMA((chunks,))
+    panel_terms = [((resident, day_cols), bf16)] * 2
+    other_terms = [((unit_rows - resident, day_cols), bf16)] * 2
     out_sems = pltpu.SemaphoreType.DMA((unit_devices,))
     width = 2 * day_cols + lanes
     in_hbm = pltpu.HBM((unit_devices * groups, width), f32)
-    sums, cross = call(
+    sums, cross, high, low = call(
         functools.partial(first_kernel, day_devices * day_cols, half, chunks),
-        [in_hbm, ((groups, unit_rows), f32)],
+        [in_hbm, ((groups, unit_rows), f32), *panel_terms],
         "first_product",
         fixed,
         in_specs=[hbm] * 6,
-        out_specs=[hbm, vmem],
+        out_specs=[hbm, vmem, vmem, vmem],
         scratch_shapes=held
         + [
             pltpu.VMEM((groups, width), f32),
@@ -286,32 +317,33 @@
         (u * day_devices + d + half, u * day_devices + d) for u in range(unit_devices) for d in range(half)
     ]
     post = lax.ppermute(cross, ("unit", "day"), downward)
-    pack, norms, raised_units, raised_days, ends, high, low = call(
-        functools.partial(second_kernel, chunks, unit_devices, half),
+    pack, norms, raised_units, ends, more_high, more_low = call(
+        functools.partial(second_kernel, 3, unit_devices),
         [
-            ((3 * groups, unit_rows + lanes), f32),
+            ((2 * groups, unit_rows + day_cols), f32),
             ((groups, lanes), f32),
             ((groups, unit_rows), f32),
-            ((groups, day_cols), f32),
             ((groups, lanes), f32),
-            ((unit_rows, day_cols), bf16),
-            ((unit_rows, day_cols), bf16),
+            *other_terms,
         ],
         "unit_gradient",
-        (*fixed, over_units(sums), post),
-        in_specs=[hbm] * 6 + [vmem] * 2,
+        (*fixed, over_units(sums), high, low),
+        in_specs=[hbm] * 6 + [vmem] * 3,
         scratch_shapes=held + [small_sems, panel_sems],
+    )
+    (pack,) = call(
+        join_kernel, [((3 * groups, unit_rows + day_cols), f32)], "join_post", (pack, post)
     )
     width = day_cols + lanes
     scaled, lam, grads = call(
-        functools.partial(third_kernel, half, 8),
+        functools.partial(third_kernel, half),
         [
             ((groups, unit_rows), f32),
             ((groups, day_cols), f32),
             pltpu.HBM((unit_devices * groups, width), f32),
         ],
         "time_gradient",
-        (*over_days(pack), high, low, norms, raised_units, raised_days, ends),
+        (*over_days(pack), high, low, more_high, more_low, norms, raised_units, ends),
         out_specs=[vmem, vmem, hbm],
         scratch_shapes=[pltpu.VMEM((groups, width), f32), out_sems],
     )
@@ -322,12 +354,23 @@
         "new_time_weights",
         (over_units(grads), lam, norms),
     )
-    return call(
+    unit_weights, time_weights = call(
         functools.partial(fifth_kernel, half),
         [((groups, unit_rows), f32), ((groups, day_cols), f32)],
         "scale_weights",
-        (*over_days(moved_sum), totals, spread(totals, 0, half), scaled, sent_scaled, moved, ends),
-    )
+        (*over_days(moved_sum), totals, scaled, moved, ends),
+    )
+    (unit_weights,) = call(
+        functools.partial(sixth_kernel, half),
+        [((groups, unit_rows), f32)],
+        "other_half",
+        (spread(totals, 0, half), sent_scaled, unit_weights),
+        in_specs=[vmem, vmem, hbm],
+        out_specs=[hbm],
+        input_output_aliases={2: 0},
+        scratch_shapes=[pltpu.VMEM((groups, unit_rows), f32), pltpu.SemaphoreType.DMA((1,))],
+    )
+    return unit_weights, time_weights
 
 
 def solution(mesh):

time: 47 us -> 43.6 us (0.928)
  starting transfers between devices: 20.3 us -> 18.3 us
  Pallas kernels: 10.4 us -> 9.6 us
  waiting for transfers between devices: 15.1 us -> 14.3 us
    ppermute x1, waiting for transfers between devices: 5.56 us -> 0.01 us  [local(): post = lax.ppermute(cross, ('unit', 'day'), downward)]
    all_to_all x2, waiting for transfers between devices: 6.54 us -> 12 us  [over_units(): lax.all_to_all(value, 'unit', split_axis=0, concat_axis=0, tiled=True)]
    all_to_all x2, starting transfers between devices: 12.6 us -> 10.6 us  [over_units(): lax.all_to_all(value, 'unit', split_axis=0, concat_axis=0, tiled=True)]
    pallas_call x5 -> x7, Pallas kernels: 10.4 us -> 9.6 us  [call(): pl.pallas_call(kernel, in_specs=in_specs or [vmem] * len(args), out_specs...]
    ppermute x4, waiting for transfers between devices: 3 us -> 2.28 us  [spread(): return lax.ppermute(value, ('unit', 'day'), pairs)]
  transfers between devices with their start and end apart: 7 -> 7, of which waited for: 5 -> 4; matrix products, arithmetic and copies ran while one was open for 0% -> 0% of each run, Pallas kernels for 0% -> 9%
where the time goes in v6:
time: 43.6 us; the launch traced here: 43 us
  starting transfers between devices  18.3 us (42%)
  waiting for transfers between devices  14.3 us (33%)
  Pallas kernels  9.6 us (22%)
  between operations  0.73 us (2%)
    all_to_all x2, waiting for transfers between devices, over_units(): lax.all_to_all(value, 'unit', split_axis=0, concat_axis=0, tiled=True)  12 us
    all_to_all x2, starting transfers between devices, over_units(): lax.all_to_all(value, 'unit', split_axis=0, concat_axis=0, tiled=True)  10.6 us
    pallas_call x7, Pallas kernels, call(): pl.pallas_call(kernel, in_specs=in_specs or [vmem] * len(args), out_specs...  9.6 us
    ppermute x4, starting transfers between devices, spread(): return lax.ppermute(value, ('unit', 'day'), pairs)  6.43 us
    ppermute x4, waiting for transfers between devices, spread(): return lax.ppermute(value, ('unit', 'day'), pairs)  2.28 us
    ppermute x1, starting transfers between devices, local(): post = lax.ppermute(cross, ('unit', 'day'), downward)  1.28 us
  transfers between devices with their start and end apart: 7, of which 4 were waited for; matrix products, arithmetic and copies ran while one was open for 0% of the time, Pallas kernels for 9%

profile of v6, /device:TPU:0, one launch (start us, length us, event | category | flops | bytes accessed | tf_op | source)
XLA Modules:
  0.0 43.0 jit_solution(4154089407996940952)
XLA Ops:
  0.6 4.1 %first_product.1 = (f32[64,640]{1,0:T(8,128)}, f32[8,4096]{1,0:T(8,128)S(1)}, bf16[2560,256]{1,0:T(8,128)(2,1)S(1)}, bf16[2560,256]{1,0:T(8,128)(2,1)S(1)}) custom-call(f32[4096,256]{1,0:T(8,128)} %refs_0_.3, s32[1,4096]{1,0:T(1,128)} %bitcast.11, s32[1,8]{1,0:T(1,128)} %bitcast.13, s32[1,8]{1,0:T(1,128)} %bitcast.15, f32[8,4096]{1,0:T(8,128)} %refs_4_.3, ...), custom_call_target="tpu_custom_call" | custom-call | tf_op jit(solution)/shard_map/first_product/pallas_call | solution.py:279
  4.7 7.3 %all-to-all-start = ((f32[8,8,640]{2,1,0:T(8,128)}), f32[8,8,640]{2,1,0:T(8,128)S(1)}, u32[]{:S(2)}, u32[]{:S(2)}) async-start(f32[8,8,640]{2,1,0:T(8,128)} %bitcast.9), calls=%async_computation | async-start | bytes 327680 | tf_op jit(solution)/shard_map/all_to_all | solution.py:276
  12.0 1.3 %collective-permute-start = (f32[8,4096]{1,0:T(8,128)S(1)}, f32[8,4096]{1,0:T(8,128)S(1)}, u32[]{:S(2)}, u32[]{:S(2)}) collective-permute-start(f32[8,4096]{1,0:T(8,128)S(1)} %get-tuple-element.24), channel_id=1, source_target_pairs={{2,0},{3,1},{6,4},{7,5},{10,8},{11,9},{14,12},{15,13},{18,16},{19,... | collective-permute-start | bytes 393224 | tf_op jit(solution)/shard_map/ppermute | solution.py:319
  13.3 6.3 %all-to-all-done = f32[8,8,640]{2,1,0:T(8,128)S(1)} async-done(((f32[8,8,640]{2,1,0:T(8,128)}), f32[8,8,640]{2,1,0:T(8,128)S(1)}, u32[]{:S(2)}, u32[]{:S(2)}) %all-to-all-start) | async-done | bytes 163872 | tf_op jit(solution)/shard_map/all_to_all | solution.py:276
  19.5 2.9 %unit_gradient.1 = (f32[16,4352]{1,0:T(8,128)S(1)}, f32[8,128]{1,0:T(8,128)S(1)}, f32[8,4096]{1,0:T(8,128)S(1)}, f32[8,128]{1,0:T(8,128)S(1)}, bf16[1536,256]{1,...) custom-call(f32[4096,256]{1,0:T(8,128)} %refs_0_.3, s32[1,4096]{1,0:T(1,128)} %bitcast.12, s32[1,8]{1,0:T(1,128)} %bitcast.14, ...), custom_call_target="tpu_custom_call" | custom-call | tf_op jit(solution)/shard_map/unit_gradient/pallas_call | solution.py:279
  22.5 0.0 collective-permute-done.post
  22.5 1.9 %collective-permute-start.1 = (f32[24,4352]{1,0:T(8,128)S(1)}, f32[24,4352]{1,0:T(8,128)S(1)}, u32[]{:S(2)}, u32[]{:S(2)}) collective-permute-start(f32[24,4352]{1,0:T(8,128)S(1)} %join_post.1.refs_0_), channel_id=1, source_target_pairs={{0,1},{1,0},{4,5},{5,4},{8,9},{9,8},{12,13},{13,12},{16,17},{17,16... | collective-permute-start | bytes 1253384 | tf_op jit(solution)/shard_map/ppermute | solution.py:270
  24.5 1.7 %collective-permute-done.1.refs_1_ = f32[24,4352]{1,0:T(8,128)S(1)} collective-permute-done((f32[24,4352]{1,0:T(8,128)S(1)}, f32[24,4352]{1,0:T(8,128)S(1)}, u32[]{:S(2)}, u32[]{:S(2)}) %collective-permute-start.1) | collective-permute-done | bytes 417824 | tf_op jit(solution)/shard_map/ppermute | solution.py:270
  26.2 1.6 %time_gradient.1 = (f32[8,4096]{1,0:T(8,128)S(1)}, f32[8,256]{1,0:T(8,128)S(1)}, f32[64,384]{1,0:T(8,128)}) custom-call(f32[24,4352]{1,0:T(8,128)S(1)} %join_post.1.refs_0_, f32[24,4352]{1,0:T(8,128)S(1)} %collective-permute-done.1.refs_1_, bf16[2560,256]{1,0:T(8,128)(2,1)S(1)} %get-tuple-element.21.refs_7_.refs_2_, ...), custom_call_target="tpu_custom_call" | custom-call | tf_op jit(solution)/shard_map/time_gradient/pallas_call | solution.py:279
  27.8 3.4 %all-to-all-start.1 = ((f32[8,8,384]{2,1,0:T(8,128)}), f32[8,8,384]{2,1,0:T(8,128)S(1)}, u32[]{:S(2)}, u32[]{:S(2)}) async-start(f32[8,8,384]{2,1,0:T(8,128)} %bitcast.10), calls=%async_computation.1 | async-start | bytes 196608 | tf_op jit(solution)/shard_map/all_to_all | solution.py:276
  31.2 1.3 %collective-permute-start.3 = (f32[8,4096]{1,0:T(8,128)S(1)}, f32[8,4096]{1,0:T(8,128)S(1)}, u32[]{:S(2)}, u32[]{:S(2)}) collective-permute-start(f32[8,4096]{1,0:T(8,128)S(1)} %get-tuple-element.33.refs_3_), channel_id=1, source_target_pairs={{0,2},{1,3},{4,6},{5,7},{8,10},{9,11},{12,14},{13,15},{16,18},{17,... | collective-permute-start | bytes 393224 | tf_op jit(solution)/shard_map/ppermute | solution.py:270
  32.5 5.8 %all-to-all-done.1 = f32[8,8,384]{2,1,0:T(8,128)S(1)} async-done(((f32[8,8,384]{2,1,0:T(8,128)}), f32[8,8,384]{2,1,0:T(8,128)S(1)}, u32[]{:S(2)}, u32[]{:S(2)}) %all-to-all-start.1) | async-done | bytes 98336 | tf_op jit(solution)/shard_map/all_to_all | solution.py:276
  38.3 0.2 new_time_weights.1
  38.4 1.9 %collective-permute-start.4 = (f32[8,128]{1,0:T(8,128)S(1)}, f32[8,128]{1,0:T(8,128)S(1)}, u32[]{:S(2)}, u32[]{:S(2)}) collective-permute-start(f32[8,128]{1,0:T(8,128)S(1)} %get-tuple-element.34.refs_0_), channel_id=1, source_target_pairs={{0,1},{1,0},{4,5},{5,4},{8,9},{9,8},{12,13},{13,12},{16,17},{17,16... | collective-permute-start | bytes 12296 | tf_op jit(solution)/shard_map/ppermute | solution.py:270
  40.4 1.3 %collective-permute-start.2 = (f32[8,128]{1,0:T(8,128)S(1)}, f32[8,128]{1,0:T(8,128)S(1)}, u32[]{:S(2)}, u32[]{:S(2)}) collective-permute-start(f32[8,128]{1,0:T(8,128)S(1)} %get-tuple-element.32.refs_2_), channel_id=1, source_target_pairs={{0,2},{1,3},{4,6},{5,7},{8,10},{9,11},{12,14},{13,15},{16,18},{17,... | collective-permute-start | bytes 12296 | tf_op jit(solution)/shard_map/ppermute | solution.py:270
  41.7 0.0 collective-permute-done.4.refs_1_
  41.7 0.7 %scale_weights.1 = (f32[8,4096]{1,0:T(8,128)}, f32[8,256]{1,0:T(8,128)}) custom-call(f32[8,128]{1,0:T(8,128)S(1)} %get-tuple-element.34.refs_0_, f32[8,128]{1,0:T(8,128)S(1)} %collective-permute-done.4.refs_1_, f32[8,128]{1,0:T(8,128)S(1)} %get-tuple-element.32.refs_2_, f32[8,4096]{1,0:T(8,128)S(1)} %get-tuple-element.33.refs_3_, ...), custom_call_target="tpu_custom_call" | custom-call | tf_op jit(solution)/shard_map/scale_weights/pallas_call | solution.py:279
  42.4 0.0 collective-permute-done.3.sent_scaled
  42.4 0.6 %collective-permute-done.2.sent_totals = f32[8,128]{1,0:T(8,128)S(1)} collective-permute-done((f32[8,128]{1,0:T(8,128)S(1)}, f32[8,128]{1,0:T(8,128)S(1)}, u32[]{:S(2)}, u32[]{:S(2)}) %collective-permute-start.2) | collective-permute-done | bytes 4128 | tf_op jit(solution)/shard_map/ppermute | solution.py:270
  (2 shorter events, 0.0 us)
Async XLA Ops:
  4.7 14.8 %all-to-all-start = ((f32[8,8,640]{2,1,0:T(8,128)}), f32[8,8,640]{2,1,0:T(8,128)S(1)}, u32[]{:S(2)}, u32[]{:S(2)}) async-start(f32[8,8,640]{2,1,0:T(8,128)} %bitcast.9), calls=%async_computation | async-start | bytes 327680 | tf_op jit(solution)/shard_map/all_to_all | solution.py:276
  12.0 10.5 %collective-permute-start = (f32[8,4096]{1,0:T(8,128)S(1)}, f32[8,4096]{1,0:T(8,128)S(1)}, u32[]{:S(2)}, u32[]{:S(2)}) collective-permute-start(f32[8,4096]{1,0:T(8,128)S(1)} %get-tuple-element.24), channel_id=1, source_target_pairs={{2,0},{3,1},{6,4},{7,5},{10,8},{11,9},{14,12},{15,13},{18,16},{19,... | collective-permute-start | bytes 393224 | tf_op jit(solution)/shard_map/ppermute | solution.py:319
  22.5 3.7 %collective-permute-start.1 = (f32[24,4352]{1,0:T(8,128)S(1)}, f32[24,4352]{1,0:T(8,128)S(1)}, u32[]{:S(2)}, u32[]{:S(2)}) collective-permute-start(f32[24,4352]{1,0:T(8,128)S(1)} %join_post.1.refs_0_), channel_id=1, source_target_pairs={{0,1},{1,0},{4,5},{5,4},{8,9},{9,8},{12,13},{13,12},{16,17},{17,16... | collective-permute-start | bytes 1253384 | tf_op jit(solution)/shard_map/ppermute | solution.py:270
  27.8 10.4 %all-to-all-start.1 = ((f32[8,8,384]{2,1,0:T(8,128)}), f32[8,8,384]{2,1,0:T(8,128)S(1)}, u32[]{:S(2)}, u32[]{:S(2)}) async-start(f32[8,8,384]{2,1,0:T(8,128)} %bitcast.10), calls=%async_computation.1 | async-start | bytes 196608 | tf_op jit(solution)/shard_map/all_to_all | solution.py:276
  31.2 11.2 %collective-permute-start.3 = (f32[8,4096]{1,0:T(8,128)S(1)}, f32[8,4096]{1,0:T(8,128)S(1)}, u32[]{:S(2)}, u32[]{:S(2)}) collective-permute-start(f32[8,4096]{1,0:T(8,128)S(1)} %get-tuple-element.33.refs_3_), channel_id=1, source_target_pairs={{0,2},{1,3},{4,6},{5,7},{8,10},{9,11},{12,14},{13,15},{16,18},{17,... | collective-permute-start | bytes 393224 | tf_op jit(solution)/shard_map/ppermute | solution.py:270
  38.4 3.2 %collective-permute-start.4 = (f32[8,128]{1,0:T(8,128)S(1)}, f32[8,128]{1,0:T(8,128)S(1)}, u32[]{:S(2)}, u32[]{:S(2)}) collective-permute-start(f32[8,128]{1,0:T(8,128)S(1)} %get-tuple-element.34.refs_0_), channel_id=1, source_target_pairs={{0,1},{1,0},{4,5},{5,4},{8,9},{9,8},{12,13},{13,12},{16,17},{17,16... | collective-permute-start | bytes 12296 | tf_op jit(solution)/shard_map/ppermute | solution.py:270
  40.4 2.6 %collective-permute-start.2 = (f32[8,128]{1,0:T(8,128)S(1)}, f32[8,128]{1,0:T(8,128)S(1)}, u32[]{:S(2)}, u32[]{:S(2)}) collective-permute-start(f32[8,128]{1,0:T(8,128)S(1)} %get-tuple-element.32.refs_2_), channel_id=1, source_target_pairs={{0,2},{1,3},{4,6},{5,7},{8,10},{9,11},{12,14},{13,15},{16,18},{17,... | collective-permute-start | bytes 12296 | tf_op jit(solution)/shard_map/ppermute | solution.py:270

commit v7 on v6

--- a/solution.py
+++ b/solution.py
@@ -96,12 +96,12 @@
 
 def first_kernel(all_count, half, chunks, *refs):
     arguments, refs = refs[:6], refs[6:]
-    out, cross, high_ref, low_ref, *held, block, left_ref, small_sems, panel_sems, out_sems = refs
+    out, cross, raised_units, raised_days, ends, high_ref, low_ref, *held, block, left_ref, small_sems, panel_sems, out_sems = refs
     groups, day_cols = held[5].shape
     unit_rows = held[0].shape[0]
     small = fetch(arguments[1:], held[1:], small_sems)
     parts = fetch_rows(arguments[0], held[0], panel_sems, chunks)
-    panel, cohort, _, post_row, unit_logit, _ = held
+    panel, cohort, pre_row, post_row, unit_logit, time_logit = held
     wait_all(small)
     me = lax.axis_index("day")
 
@@ -111,7 +111,12 @@
         treated = jnp.where(cohort[...] == label, 1.0, 0.0)
         control = jnp.where(cohort[...] > label, 1.0, 0.0)
         raised = jnp.exp(unit_logit[...]) * control
+        raised_units[...] = raised
         left_ref[...] = left_of(raised, treated)
+        pre_end = column(pre_row)
+        ends[...] = jnp.broadcast_to(pre_end.astype(f32), ends.shape)
+        before = days_of(me, (groups, day_cols)) < pre_end
+        raised_days[...] = jnp.where(before, jnp.exp(time_logit[...]), 0.0)
         lane = lax.broadcasted_iota(jnp.int32, (groups, lanes), 1)
         block[:, 2 * day_cols :] = jnp.where(
             lane == 0,
@@ -144,31 +149,22 @@
                 cross[:, here] = add_terms(days_dot(left, *split_panel(panel[here, :])), groups)
 
 
-def second_kernel(chunks, unit_devices, *refs):
-    arguments, refs = refs[:6], refs[6:]
-    sums, high_ref, low_ref, pack, norms, raised_units, ends, more_high, more_low, *refs = refs
-    held, small_sems, panel_sems = refs[:6], refs[6], refs[7]
-    groups, unit_rows = raised_units.shape
-    resident, day_cols = high_ref.shape
-    panel, cohort, pre_row, _, unit_logit, time_logit = held
-    small = fetch(arguments[1:], held[1:], small_sems)
-    parts = fetch_rows(arguments[0], panel, panel_sems, chunks, resident)
+def second_kernel(chunks, unit_devices, panel, sums, raised_days, ends, high_ref, low_ref, *refs):
+    pack, norms, more_high, more_low, held, panel_sems = refs
+    groups, day_cols = raised_days.shape
+    unit_rows, resident = panel.shape[0], high_ref.shape[0]
+    parts = fetch_rows(panel, held, panel_sems, chunks, resident)
     total = tree_sum(sums[pl.ds(u * groups, groups), :] for u in range(unit_devices))
     unit_norm = total[:, 2 * day_cols : 2 * day_cols + 1]
     treat_count = jnp.maximum(total[:, 2 * day_cols + 1 : 2 * day_cols + 2], 1.0)
     norms[...] = total[:, 2 * day_cols :]
     gap = total[:, :day_cols] / unit_norm - total[:, day_cols : 2 * day_cols] / treat_count
-    wait_all(small)
-    pre_end = column(pre_row)
-    ends[...] = jnp.broadcast_to(pre_end.astype(f32), ends.shape)
-    before = days_of(lax.axis_index("day"), (groups, day_cols)) < pre_end
-    raised_time = jnp.where(before, jnp.exp(time_logit[...]), 0.0)
+    before = days_of(lax.axis_index("day"), (groups, day_cols)).astype(f32) < ends[:, 0:1]
+    raised_time = raised_days[...]
     pack[:groups, unit_rows:] = raised_time
     pack[groups:, unit_rows:] = jnp.zeros_like(raised_time)
     left = split_left(jnp.where(before, gap, 0.0)) + split_left(raised_time)
     left = jnp.concatenate(left, axis=0).astype(bf16)
-    label = lax.broadcasted_iota(jnp.int32, (groups, unit_rows), 0)
-    raised_units[...] = jnp.where(cohort[...] > label, jnp.exp(unit_logit[...]), 0.0)
 
     def multiply(here, high, low):
         product = days_dot(left, high, low)
@@ -182,7 +178,7 @@
         copy.wait()
         for here in blocks:
             there = pl.ds(here.start - resident, block_rows)
-            high, low = split_panel(panel[here, :])
+            high, low = split_panel(held[here, :])
             more_high[there, :] = high
             more_low[there, :] = low
             multiply(here, high, low)
@@ -273,7 +269,8 @@
         return [value] + [spread(value, k, 0) for k in range(1, half)]
 
     def over_units(value):
-        return lax.all_to_all(value, "unit", split_axis=0, concat_axis=0, tiled=True)
+        members = list(reversed(range(unit_devices)))
+        return lax.all_to_all(value, "unit", split_axis=0, concat_axis=0, axis_index_groups=[members], tiled=True)
 
     def call(kernel, shapes, name, args, in_specs=None, out_specs=None, **more):
         return pl.pallas_call(
@@ -297,13 +294,20 @@
     out_sems = pltpu.SemaphoreType.DMA((unit_devices,))
     width = 2 * day_cols + lanes
     in_hbm = pltpu.HBM((unit_devices * groups, width), f32)
-    sums, cross, high, low = call(
+    sums, cross, raised_units, raised_days, ends, high, low = call(
         functools.partial(first_kernel, day_devices * day_cols, half, chunks),
-        [in_hbm, ((groups, unit_rows), f32), *panel_terms],
+        [
+            in_hbm,
+            ((groups, unit_rows), f32),
+            ((groups, unit_rows), f32),
+            ((groups, day_cols), f32),
+            ((groups, lanes), f32),
+            *panel_terms,
+        ],
         "first_product",
         fixed,
         in_specs=[hbm] * 6,
-        out_specs=[hbm, vmem, vmem, vmem],
+        out_specs=[hbm] + [vmem] * 6,
         scratch_shapes=held
         + [
             pltpu.VMEM((groups, width), f32),
@@ -317,19 +321,17 @@
         (u * day_devices + d + half, u * day_devices + d) for u in range(unit_devices) for d in range(half)
     ]
     post = lax.ppermute(cross, ("unit", "day"), downward)
-    pack, norms, raised_units, ends, more_high, more_low = call(
+    pack, norms, more_high, more_low = call(
         functools.partial(second_kernel, 3, unit_devices),
         [
             ((2 * groups, unit_rows + day_cols), f32),
             ((groups, lanes), f32),
-            ((groups, unit_rows), f32),
-            ((groups, lanes), f32),
             *other_terms,
         ],
         "unit_gradient",
-        (*fixed, over_units(sums), high, low),
-        in_specs=[hbm] * 6 + [vmem] * 3,
-        scratch_shapes=held + [small_sems, panel_sems],
+        (fixed[0], over_units(sums), raised_days, ends, high, low),
+        in_specs=[hbm] + [vmem] * 5,
+        scratch_shapes=[held[0], panel_sems],
     )
     (pack,) = call(
         join_kernel, [((3 * groups, unit_rows + day_cols), f32)], "join_post", (pack, post)

time: 43.6 us -> 41.8 us (0.959)
  waiting for transfers between devices: 14.3 us -> 7.88 us
  starting transfers between devices: 18.3 us -> 23.4 us
    all_to_all x2, waiting for transfers between devices: 12 us -> 5.6 us  [over_units(): lax.all_to_all(value, 'unit', split_axis=0, concat_axis=0, axis_index_gro...]
    all_to_all x2, starting transfers between devices: 10.6 us -> 15.7 us  [over_units(): lax.all_to_all(value, 'unit', split_axis=0, concat_axis=0, axis_index_gro...]
where the time goes in v7:
time: 41.8 us; the launch traced here: 41.4 us
  starting transfers between devices  23.4 us (56%)
  Pallas kernels  9.32 us (22%)
  waiting for transfers between devices  7.88 us (19%)
  between operations  0.72 us (2%)
    all_to_all x2, starting transfers between devices, over_units(): lax.all_to_all(value, 'unit', split_axis=0, concat_axis=0, axis_index_gro...  15.7 us
    pallas_call x7, Pallas kernels, call(): pl.pallas_call(kernel, in_specs=in_specs or [vmem] * len(args), out_specs...  9.32 us
    ppermute x4, starting transfers between devices, spread(): return lax.ppermute(value, ('unit', 'day'), pairs)  6.41 us
    all_to_all x2, waiting for transfers between devices, over_units(): lax.all_to_all(value, 'unit', split_axis=0, concat_axis=0, axis_index_gro...  5.6 us
    ppermute x4, waiting for transfers between devices, spread(): return lax.ppermute(value, ('unit', 'day'), pairs)  2.28 us
    ppermute x1, starting transfers between devices, local(): post = lax.ppermute(cross, ('unit', 'day'), downward)  1.28 us
  transfers between devices with their start and end apart: 7, of which 4 were waited for; matrix products, arithmetic and copies ran while one was open for 0% of the time, Pallas kernels for 9%

profile of v7, /device:TPU:0, one launch (start us, length us, event | category | flops | bytes accessed | tf_op | source)
XLA Modules:
  0.0 41.4 jit_solution(7789843463255792783)
XLA Ops:
  0.6 4.1 %first_product.1 = (f32[64,640]{1,0:T(8,128)}, f32[8,4096]{1,0:T(8,128)S(1)}, f32[8,4096]{1,0:T(8,128)S(1)}, f32[8,256]{1,0:T(8,128)S(1)}, f32[8,128]{1,0:T(8,12...) custom-call(f32[4096,256]{1,0:T(8,128)} %panel.1, s32[1,4096]{1,0:T(1,128)} %bitcast.11, ...), custom_call_target="tpu_custom_call" | custom-call | tf_op jit(solution)/shard_map/first_product/pallas_call | solution.py:276
  4.7 9.3 %all-to-all-start = ((f32[8,8,640]{2,1,0:T(8,128)}), f32[8,8,640]{2,1,0:T(8,128)S(1)}, u32[]{:S(2)}, u32[]{:S(2)}) async-start(f32[8,8,640]{2,1,0:T(8,128)} %bitcast.9), calls=%async_computation | async-start | bytes 327680 | tf_op jit(solution)/shard_map/all_to_all | solution.py:273
  14.0 1.3 %collective-permute-start = (f32[8,4096]{1,0:T(8,128)S(1)}, f32[8,4096]{1,0:T(8,128)S(1)}, u32[]{:S(2)}, u32[]{:S(2)}) collective-permute-start(f32[8,4096]{1,0:T(8,128)S(1)} %get-tuple-element.27), channel_id=1, source_target_pairs={{2,0},{3,1},{6,4},{7,5},{10,8},{11,9},{14,12},{15,13},{18,16},{19,... | collective-permute-start | bytes 393224 | tf_op jit(solution)/shard_map/ppermute | solution.py:323
  15.3 3.4 %all-to-all-done = f32[8,8,640]{2,1,0:T(8,128)S(1)} async-done(((f32[8,8,640]{2,1,0:T(8,128)}), f32[8,8,640]{2,1,0:T(8,128)S(1)}, u32[]{:S(2)}, u32[]{:S(2)}) %all-to-all-start) | async-done | bytes 163872 | tf_op jit(solution)/shard_map/all_to_all | solution.py:273
  18.7 2.7 %unit_gradient.1 = (f32[16,4352]{1,0:T(8,128)S(1)}, f32[8,128]{1,0:T(8,128)S(1)}, bf16[1536,256]{1,0:T(8,128)(2,1)S(1)}, bf16[1536,256]{1,0:T(8,128)(2,1)S(1)}) custom-call(f32[4096,256]{1,0:T(8,128)} %panel.1, f32[64,640]{1,0:T(8,128)S(1)} %bitcast.7, f32[8,256]{1,0:T(8,128)S(1)} %get-tuple-element.22.raised_days, ...), custom_call_target="tpu_custom_call" | custom-call | tf_op jit(solution)/shard_map/unit_gradient/pallas_call | solution.py:276
  21.3 0.0 collective-permute-done.post
  21.4 1.9 %collective-permute-start.1 = (f32[24,4352]{1,0:T(8,128)S(1)}, f32[24,4352]{1,0:T(8,128)S(1)}, u32[]{:S(2)}, u32[]{:S(2)}) collective-permute-start(f32[24,4352]{1,0:T(8,128)S(1)} %join_post.1.refs_0_), channel_id=1, source_target_pairs={{0,1},{1,0},{4,5},{5,4},{8,9},{9,8},{12,13},{13,12},{16,17},{17,16... | collective-permute-start | bytes 1253384 | tf_op jit(solution)/shard_map/ppermute | solution.py:266
  23.3 1.7 %collective-permute-done.1.refs_1_ = f32[24,4352]{1,0:T(8,128)S(1)} collective-permute-done((f32[24,4352]{1,0:T(8,128)S(1)}, f32[24,4352]{1,0:T(8,128)S(1)}, u32[]{:S(2)}, u32[]{:S(2)}) %collective-permute-start.1) | collective-permute-done | bytes 417824 | tf_op jit(solution)/shard_map/ppermute | solution.py:266
  25.0 1.6 %time_gradient.1 = (f32[8,4096]{1,0:T(8,128)S(1)}, f32[8,256]{1,0:T(8,128)S(1)}, f32[64,384]{1,0:T(8,128)}) custom-call(f32[24,4352]{1,0:T(8,128)S(1)} %join_post.1.refs_0_, f32[24,4352]{1,0:T(8,128)S(1)} %collective-permute-done.1.refs_1_, bf16[2560,256]{1,0:T(8,128)(2,1)S(1)} %get-tuple-element.24.high_ref.refs_2_, ...), custom_call_target="tpu_custom_call" | custom-call | tf_op jit(solution)/shard_map/time_gradient/pallas_call | solution.py:276
  26.7 6.4 %all-to-all-start.1 = ((f32[8,8,384]{2,1,0:T(8,128)}), f32[8,8,384]{2,1,0:T(8,128)S(1)}, u32[]{:S(2)}, u32[]{:S(2)}) async-start(f32[8,8,384]{2,1,0:T(8,128)} %bitcast.10), calls=%async_computation.1 | async-start | bytes 196608 | tf_op jit(solution)/shard_map/all_to_all | solution.py:273
  33.1 1.3 %collective-permute-start.3 = (f32[8,4096]{1,0:T(8,128)S(1)}, f32[8,4096]{1,0:T(8,128)S(1)}, u32[]{:S(2)}, u32[]{:S(2)}) collective-permute-start(f32[8,4096]{1,0:T(8,128)S(1)} %get-tuple-element.35.refs_3_), channel_id=1, source_target_pairs={{0,2},{1,3},{4,6},{5,7},{8,10},{9,11},{12,14},{13,15},{16,18},{17,... | collective-permute-start | bytes 393224 | tf_op jit(solution)/shard_map/ppermute | solution.py:266
  34.4 2.2 %all-to-all-done.1 = f32[8,8,384]{2,1,0:T(8,128)S(1)} async-done(((f32[8,8,384]{2,1,0:T(8,128)}), f32[8,8,384]{2,1,0:T(8,128)S(1)}, u32[]{:S(2)}, u32[]{:S(2)}) %all-to-all-start.1) | async-done | bytes 98336 | tf_op jit(solution)/shard_map/all_to_all | solution.py:273
  36.7 0.2 new_time_weights.1
  36.8 1.9 %collective-permute-start.4 = (f32[8,128]{1,0:T(8,128)S(1)}, f32[8,128]{1,0:T(8,128)S(1)}, u32[]{:S(2)}, u32[]{:S(2)}) collective-permute-start(f32[8,128]{1,0:T(8,128)S(1)} %get-tuple-element.36.refs_0_), channel_id=1, source_target_pairs={{0,1},{1,0},{4,5},{5,4},{8,9},{9,8},{12,13},{13,12},{16,17},{17,16... | collective-permute-start | bytes 12296 | tf_op jit(solution)/shard_map/ppermute | solution.py:266
  38.7 1.3 %collective-permute-start.2 = (f32[8,128]{1,0:T(8,128)S(1)}, f32[8,128]{1,0:T(8,128)S(1)}, u32[]{:S(2)}, u32[]{:S(2)}) collective-permute-start(f32[8,128]{1,0:T(8,128)S(1)} %get-tuple-element.34.refs_2_), channel_id=1, source_target_pairs={{0,2},{1,3},{4,6},{5,7},{8,10},{9,11},{12,14},{13,15},{16,18},{17,... | collective-permute-start | bytes 12296 | tf_op jit(solution)/shard_map/ppermute | solution.py:266
  40.0 0.0 collective-permute-done.4.refs_1_
  40.0 0.7 %scale_weights.1 = (f32[8,4096]{1,0:T(8,128)}, f32[8,256]{1,0:T(8,128)}) custom-call(f32[8,128]{1,0:T(8,128)S(1)} %get-tuple-element.36.refs_0_, f32[8,128]{1,0:T(8,128)S(1)} %collective-permute-done.4.refs_1_, f32[8,128]{1,0:T(8,128)S(1)} %get-tuple-element.34.refs_2_, f32[8,4096]{1,0:T(8,128)S(1)} %get-tuple-element.35.refs_3_, ...), custom_call_target="tpu_custom_call" | custom-call | tf_op jit(solution)/shard_map/scale_weights/pallas_call | solution.py:276
  40.8 0.0 collective-permute-done.3.sent_scaled
  40.8 0.6 %collective-permute-done.2.sent_totals = f32[8,128]{1,0:T(8,128)S(1)} collective-permute-done((f32[8,128]{1,0:T(8,128)S(1)}, f32[8,128]{1,0:T(8,128)S(1)}, u32[]{:S(2)}, u32[]{:S(2)}) %collective-permute-start.2) | collective-permute-done | bytes 4128 | tf_op jit(solution)/shard_map/ppermute | solution.py:266
  (2 shorter events, 0.0 us)
Async XLA Ops:
  4.7 14.0 %all-to-all-start = ((f32[8,8,640]{2,1,0:T(8,128)}), f32[8,8,640]{2,1,0:T(8,128)S(1)}, u32[]{:S(2)}, u32[]{:S(2)}) async-start(f32[8,8,640]{2,1,0:T(8,128)} %bitcast.9), calls=%async_computation | async-start | bytes 327680 | tf_op jit(solution)/shard_map/all_to_all | solution.py:273
  14.0 7.3 %collective-permute-start = (f32[8,4096]{1,0:T(8,128)S(1)}, f32[8,4096]{1,0:T(8,128)S(1)}, u32[]{:S(2)}, u32[]{:S(2)}) collective-permute-start(f32[8,4096]{1,0:T(8,128)S(1)} %get-tuple-element.27), channel_id=1, source_target_pairs={{2,0},{3,1},{6,4},{7,5},{10,8},{11,9},{14,12},{15,13},{18,16},{19,... | collective-permute-start | bytes 393224 | tf_op jit(solution)/shard_map/ppermute | solution.py:323
  21.4 3.7 %collective-permute-start.1 = (f32[24,4352]{1,0:T(8,128)S(1)}, f32[24,4352]{1,0:T(8,128)S(1)}, u32[]{:S(2)}, u32[]{:S(2)}) collective-permute-start(f32[24,4352]{1,0:T(8,128)S(1)} %join_post.1.refs_0_), channel_id=1, source_target_pairs={{0,1},{1,0},{4,5},{5,4},{8,9},{9,8},{12,13},{13,12},{16,17},{17,16... | collective-permute-start | bytes 1253384 | tf_op jit(solution)/shard_map/ppermute | solution.py:266
  26.7 10.0 %all-to-all-start.1 = ((f32[8,8,384]{2,1,0:T(8,128)}), f32[8,8,384]{2,1,0:T(8,128)S(1)}, u32[]{:S(2)}, u32[]{:S(2)}) async-start(f32[8,8,384]{2,1,0:T(8,128)} %bitcast.10), calls=%async_computation.1 | async-start | bytes 196608 | tf_op jit(solution)/shard_map/all_to_all | solution.py:273
  33.1 7.7 %collective-permute-start.3 = (f32[8,4096]{1,0:T(8,128)S(1)}, f32[8,4096]{1,0:T(8,128)S(1)}, u32[]{:S(2)}, u32[]{:S(2)}) collective-permute-start(f32[8,4096]{1,0:T(8,128)S(1)} %get-tuple-element.35.refs_3_), channel_id=1, source_target_pairs={{0,2},{1,3},{4,6},{5,7},{8,10},{9,11},{12,14},{13,15},{16,18},{17,... | collective-permute-start | bytes 393224 | tf_op jit(solution)/shard_map/ppermute | solution.py:266
  36.8 3.2 %collective-permute-start.4 = (f32[8,128]{1,0:T(8,128)S(1)}, f32[8,128]{1,0:T(8,128)S(1)}, u32[]{:S(2)}, u32[]{:S(2)}) collective-permute-start(f32[8,128]{1,0:T(8,128)S(1)} %get-tuple-element.36.refs_0_), channel_id=1, source_target_pairs={{0,1},{1,0},{4,5},{5,4},{8,9},{9,8},{12,13},{13,12},{16,17},{17,16... | collective-permute-start | bytes 12296 | tf_op jit(solution)/shard_map/ppermute | solution.py:266
  38.7 2.6 %collective-permute-start.2 = (f32[8,128]{1,0:T(8,128)S(1)}, f32[8,128]{1,0:T(8,128)S(1)}, u32[]{:S(2)}, u32[]{:S(2)}) collective-permute-start(f32[8,128]{1,0:T(8,128)S(1)} %get-tuple-element.34.refs_2_), channel_id=1, source_target_pairs={{0,2},{1,3},{4,6},{5,7},{8,10},{9,11},{12,14},{13,15},{16,18},{17,... | collective-permute-start | bytes 12296 | tf_op jit(solution)/shard_map/ppermute | solution.py:266

commit v8 on v7

--- a/solution.py
+++ b/solution.py
@@ -19,14 +19,11 @@
 
 def split_left(value):
     first = value.astype(bf16).astype(f32)
-    rest = value - first
-    second = rest.astype(bf16).astype(f32)
-    return [first, second, rest - second]
-
-
-def left_of(value, other=None):
-    other = jnp.zeros_like(value) if other is None else other
-    return jnp.concatenate(split_left(value) + [other], axis=0).astype(bf16)
+    return [first, value - first]
+
+
+def left_of(*values):
+    return jnp.concatenate([term for value in values for term in split_left(value)], axis=0).astype(bf16)
 
 
 def split_panel(value):
@@ -45,8 +42,8 @@
     )
 
 
-def add_terms(stack, groups):
-    return stack[:groups] + stack[groups : 2 * groups] + stack[2 * groups : 3 * groups]
+def add_terms(stack, groups, place=0):
+    return stack[2 * place * groups :][:groups] + stack[(2 * place + 1) * groups :][:groups]
 
 
 def tree_sum(values):
@@ -77,10 +74,20 @@
 
 def fetch_rows(source, target, sems, chunks, first=0):
     rows = (source.shape[0] - first) // chunks
-    parts = [pl.ds(first + chunk * rows, rows) for chunk in range(chunks)]
+    starts = [first + chunk * rows for chunk in range(chunks)]
+    parts = [pl.ds(start, rows) for start in starts]
     copies = fetch([source.at[here] for here in parts], [target.at[here] for here in parts], sems)
-    blocks = [[pl.ds(part.start + i, block_rows) for i in range(0, rows, block_rows)] for part in parts]
-    return list(zip(blocks, copies))
+    return [(start, rows, copy) for start, copy in zip(starts, copies)]
+
+
+def blocks_of(start, rows):
+    return [pl.ds(here, block_rows) for here in range(start, start + rows, block_rows)]
+
+
+def split_chunk(panel, start, rows, high_ref, low_ref, offset):
+    for here in blocks_of(start, rows):
+        there = pl.ds(here.start - offset, block_rows)
+        high_ref[there, :], low_ref[there, :] = split_panel(panel[here, :])
 
 
 def wait_all(copies):
@@ -96,9 +103,9 @@
 
 def first_kernel(all_count, half, chunks, *refs):
     arguments, refs = refs[:6], refs[6:]
-    out, cross, raised_units, raised_days, ends, high_ref, low_ref, *held, block, left_ref, small_sems, panel_sems, out_sems = refs
+    out, cross, raised_units, raised_days, ends, high_ref, low_ref, *held, block, left_ref, more_high, more_low, small_sems, panel_sems, out_sems = refs
     groups, day_cols = held[5].shape
-    unit_rows = held[0].shape[0]
+    unit_rows, resident = held[0].shape[0], high_ref.shape[0]
     small = fetch(arguments[1:], held[1:], small_sems)
     parts = fetch_rows(arguments[0], held[0], panel_sems, chunks)
     panel, cohort, pre_row, post_row, unit_logit, time_logit = held
@@ -126,16 +133,27 @@
             ),
         )
         product = jnp.zeros((4 * groups, day_cols), f32)
-        for blocks, copy in parts:
+
+        def terms_of(start):
+            if start < resident:
+                return high_ref, low_ref, 0
+            return more_high, more_low, resident
+
+        def multiply(start, rows):
+            high, low, offset = terms_of(start)
+            there = pl.ds(start - offset, rows)
+            return rows_dot(left_ref[:, start : start + rows], high[there, :], low[there, :])
+
+        before_it = None
+        for start, rows, copy in parts:
             copy.wait()
-            for here in blocks:
-                high, low = split_panel(panel[here, :])
-                if here.start < high_ref.shape[0]:
-                    high_ref[here, :] = high
-                    low_ref[here, :] = low
-                product += rows_dot(left_ref[:, here], high, low)
+            if before_it:
+                product += multiply(*before_it)
+            split_chunk(panel, start, rows, *terms_of(start))
+            before_it = start, rows
+        product += multiply(*before_it)
         block[:, :day_cols] = add_terms(product, groups)
-        block[:, day_cols : 2 * day_cols] = product[3 * groups :]
+        block[:, day_cols : 2 * day_cols] = product[2 * groups :][:groups]
         repeat_out(block, out, out_sems)
 
     @pl.when(me >= half)
@@ -143,9 +161,9 @@
         post_start = column(post_row)
         after = jnp.where(days_of(me, (groups, day_cols)) >= post_start, 1.0, 0.0)
         left = left_of(after / (all_count - post_start).astype(f32))
-        for blocks, copy in parts:
+        for start, rows, copy in parts:
             copy.wait()
-            for here in blocks:
+            for here in blocks_of(start, rows):
                 cross[:, here] = add_terms(days_dot(left, *split_panel(panel[here, :])), groups)
 
 
@@ -163,25 +181,24 @@
     raised_time = raised_days[...]
     pack[:groups, unit_rows:] = raised_time
     pack[groups:, unit_rows:] = jnp.zeros_like(raised_time)
-    left = split_left(jnp.where(before, gap, 0.0)) + split_left(raised_time)
-    left = jnp.concatenate(left, axis=0).astype(bf16)
-
-    def multiply(here, high, low):
-        product = days_dot(left, high, low)
-        pack[:groups, here] = add_terms(product, groups)
-        pack[groups:, here] = add_terms(product[3 * groups :], groups)
-
-    for start in range(0, resident, block_rows):
-        here = pl.ds(start, block_rows)
-        multiply(here, high_ref[here, :], low_ref[here, :])
-    for blocks, copy in parts:
+    left = left_of(jnp.where(before, gap, 0.0), raised_time)
+
+    def multiply(start, rows, high, low, offset):
+        for here in blocks_of(start, rows):
+            there = pl.ds(here.start - offset, block_rows)
+            product = days_dot(left, high[there, :], low[there, :])
+            pack[:groups, here] = add_terms(product, groups)
+            pack[groups:, here] = add_terms(product, groups, 1)
+
+    early = resident // block_rows // 2 * block_rows
+    multiply(0, early, high_ref, low_ref, 0)
+    before_it = early, resident - early, high_ref, low_ref, 0
+    for start, rows, copy in parts:
         copy.wait()
-        for here in blocks:
-            there = pl.ds(here.start - resident, block_rows)
-            high, low = split_panel(held[here, :])
-            more_high[there, :] = high
-            more_low[there, :] = low
-            multiply(here, high, low)
+        multiply(*before_it)
+        split_chunk(held, start, rows, more_high, more_low, resident)
+        before_it = start, rows, more_high, more_low, resident
+    multiply(*before_it)
 
 
 def join_kernel(pack, post, out):
@@ -199,18 +216,19 @@
     unit_norm, ctrl_count = norms[:, 0:1], norms[:, 2:3]
     factor = -step_rate / jnp.sqrt(ends[:, 0:1])
     raised_days = [ref[:groups, unit_rows:] for ref in parts]
-    time_norm = tree_sum(jnp.sum(value, axis=1, keepdims=True) for value in raised_days)
-    lam[...] = raised_days[0] / time_norm
+    over_time = 1.0 / tree_sum(jnp.sum(value, axis=1, keepdims=True) for value in raised_days)
+    over_unit = 1.0 / unit_norm
+    lam[...] = raised_days[0] * over_time
     time_grad = jnp.zeros((groups, day_cols), f32)
     new_sum = jnp.zeros((groups, 1), f32)
     for start in range(0, unit_rows, 2 * block_rows):
         here = pl.ds(start, 2 * block_rows)
         whole = tree_sum(ref[:, here] for ref in parts)
         raised = raised_units[:, here]
-        new = raised / unit_norm * jnp.exp(whole[:groups] * factor)
+        new = raised * over_unit * jnp.exp(whole[:groups] * factor)
         new_sum += jnp.sum(new, axis=1, keepdims=True)
         scaled[:, here] = new * ctrl_count
-        shortfall = whole[groups : 2 * groups] / time_norm - whole[2 * groups :]
+        shortfall = whole[groups : 2 * groups] * over_time - whole[2 * groups :]
         left = left_of(jnp.where(raised > 0.0, shortfall, 0.0))
         if start < resident:
             high, low = high_ref[here, :], low_ref[here, :]
@@ -257,7 +275,7 @@
     half = day_devices // 2
     assert half * 2 == day_devices and half & (half - 1) == 0
     assert unit_devices & (unit_devices - 1) == 0
-    chunks = 4
+    chunks = 8
     resident = unit_rows * 5 // 8 // (2 * block_rows) * (2 * block_rows)
     def spread(value, day_xor, up):
         pairs = [
@@ -312,6 +330,7 @@
         + [
             pltpu.VMEM((groups, width), f32),
             pltpu.VMEM((4 * groups, unit_rows), bf16),
+            *[pltpu.VMEM(*shape) for shape in other_terms],
             small_sems,
             panel_sems,
             out_sems,

time: 41.8 us -> 42.2 us (level)
  transfers between devices with their start and end apart: 7 -> 7, of which waited for: 4 -> 4; matrix products, arithmetic and copies ran while one was open for 0% -> 0% of each run, Pallas kernels for 9% -> 8%
where the time goes in v8:
time: 42.2 us; the launch traced here: 41.7 us
  starting transfers between devices  23.4 us (55%)
  Pallas kernels  9.68 us (23%)
  waiting for transfers between devices  7.88 us (19%)
  between operations  0.72 us (2%)
    all_to_all x2, starting transfers between devices, over_units(): lax.all_to_all(value, 'unit', split_axis=0, concat_axis=0, axis_index_gro...  15.7 us
    pallas_call x7, Pallas kernels, call(): pl.pallas_call(kernel, in_specs=in_specs or [vmem] * len(args), out_specs...  9.68 us
    ppermute x4, starting transfers between devices, spread(): return lax.ppermute(value, ('unit', 'day'), pairs)  6.41 us
    all_to_all x2, waiting for transfers between devices, over_units(): lax.all_to_all(value, 'unit', split_axis=0, concat_axis=0, axis_index_gro...  5.6 us
    ppermute x4, waiting for transfers between devices, spread(): return lax.ppermute(value, ('unit', 'day'), pairs)  2.28 us
    ppermute x1, starting transfers between devices, local(): post = lax.ppermute(cross, ('unit', 'day'), downward)  1.28 us
  transfers between devices with their start and end apart: 7, of which 4 were waited for; matrix products, arithmetic and copies ran while one was open for 0% of the time, Pallas kernels for 8%

profile of v8, /device:TPU:0, one launch (start us, length us, event | category | flops | bytes accessed | tf_op | source)
XLA Modules:
  0.0 41.7 jit_solution(2349577988706669216)
XLA Ops:
  0.6 4.8 %first_product.1 = (f32[64,640]{1,0:T(8,128)}, f32[8,4096]{1,0:T(8,128)S(1)}, f32[8,4096]{1,0:T(8,128)S(1)}, f32[8,256]{1,0:T(8,128)S(1)}, f32[8,128]{1,0:T(8,12...) custom-call(f32[4096,256]{1,0:T(8,128)} %panel.1, s32[1,4096]{1,0:T(1,128)} %bitcast.11, ...), custom_call_target="tpu_custom_call" | custom-call | tf_op jit(solution)/shard_map/first_product/pallas_call | solution.py:294
  5.4 9.3 %all-to-all-start = ((f32[8,8,640]{2,1,0:T(8,128)}), f32[8,8,640]{2,1,0:T(8,128)S(1)}, u32[]{:S(2)}, u32[]{:S(2)}) async-start(f32[8,8,640]{2,1,0:T(8,128)} %bitcast.9), calls=%async_computation | async-start | bytes 327680 | tf_op jit(solution)/shard_map/all_to_all | solution.py:291
  14.7 1.3 %collective-permute-start = (f32[8,4096]{1,0:T(8,128)S(1)}, f32[8,4096]{1,0:T(8,128)S(1)}, u32[]{:S(2)}, u32[]{:S(2)}) collective-permute-start(f32[8,4096]{1,0:T(8,128)S(1)} %get-tuple-element.27), channel_id=1, source_target_pairs={{2,0},{3,1},{6,4},{7,5},{10,8},{11,9},{14,12},{15,13},{18,16},{19,... | collective-permute-start | bytes 393224 | tf_op jit(solution)/shard_map/ppermute | solution.py:342
  16.0 3.4 %all-to-all-done = f32[8,8,640]{2,1,0:T(8,128)S(1)} async-done(((f32[8,8,640]{2,1,0:T(8,128)}), f32[8,8,640]{2,1,0:T(8,128)S(1)}, u32[]{:S(2)}, u32[]{:S(2)}) %all-to-all-start) | async-done | bytes 163872 | tf_op jit(solution)/shard_map/all_to_all | solution.py:291
  19.3 2.5 %unit_gradient.1 = (f32[16,4352]{1,0:T(8,128)S(1)}, f32[8,128]{1,0:T(8,128)S(1)}, bf16[1536,256]{1,0:T(8,128)(2,1)S(1)}, bf16[1536,256]{1,0:T(8,128)(2,1)S(1)}) custom-call(f32[4096,256]{1,0:T(8,128)} %panel.1, f32[64,640]{1,0:T(8,128)S(1)} %bitcast.7, f32[8,256]{1,0:T(8,128)S(1)} %get-tuple-element.22.raised_days, ...), custom_call_target="tpu_custom_call" | custom-call | tf_op jit(solution)/shard_map/unit_gradient/pallas_call | solution.py:294
  21.9 0.0 collective-permute-done.post
  21.9 1.9 %collective-permute-start.1 = (f32[24,4352]{1,0:T(8,128)S(1)}, f32[24,4352]{1,0:T(8,128)S(1)}, u32[]{:S(2)}, u32[]{:S(2)}) collective-permute-start(f32[24,4352]{1,0:T(8,128)S(1)} %join_post.1.refs_0_), channel_id=1, source_target_pairs={{0,1},{1,0},{4,5},{5,4},{8,9},{9,8},{12,13},{13,12},{16,17},{17,16... | collective-permute-start | bytes 1253384 | tf_op jit(solution)/shard_map/ppermute | solution.py:284
  23.9 1.7 %collective-permute-done.1.refs_1_ = f32[24,4352]{1,0:T(8,128)S(1)} collective-permute-done((f32[24,4352]{1,0:T(8,128)S(1)}, f32[24,4352]{1,0:T(8,128)S(1)}, u32[]{:S(2)}, u32[]{:S(2)}) %collective-permute-start.1) | collective-permute-done | bytes 417824 | tf_op jit(solution)/shard_map/ppermute | solution.py:284
  25.6 1.5 %time_gradient.1 = (f32[8,4096]{1,0:T(8,128)S(1)}, f32[8,256]{1,0:T(8,128)S(1)}, f32[64,384]{1,0:T(8,128)}) custom-call(f32[24,4352]{1,0:T(8,128)S(1)} %join_post.1.refs_0_, f32[24,4352]{1,0:T(8,128)S(1)} %collective-permute-done.1.refs_1_, bf16[2560,256]{1,0:T(8,128)(2,1)S(1)} %get-tuple-element.24.high_ref.refs_2_, ...), custom_call_target="tpu_custom_call" | custom-call | tf_op jit(solution)/shard_map/time_gradient/pallas_call | solution.py:294
  27.0 6.4 %all-to-all-start.1 = ((f32[8,8,384]{2,1,0:T(8,128)}), f32[8,8,384]{2,1,0:T(8,128)S(1)}, u32[]{:S(2)}, u32[]{:S(2)}) async-start(f32[8,8,384]{2,1,0:T(8,128)} %bitcast.10), calls=%async_computation.1 | async-start | bytes 196608 | tf_op jit(solution)/shard_map/all_to_all | solution.py:291
  33.5 1.3 %collective-permute-start.3 = (f32[8,4096]{1,0:T(8,128)S(1)}, f32[8,4096]{1,0:T(8,128)S(1)}, u32[]{:S(2)}, u32[]{:S(2)}) collective-permute-start(f32[8,4096]{1,0:T(8,128)S(1)} %get-tuple-element.35.refs_3_), channel_id=1, source_target_pairs={{0,2},{1,3},{4,6},{5,7},{8,10},{9,11},{12,14},{13,15},{16,18},{17,... | collective-permute-start | bytes 393224 | tf_op jit(solution)/shard_map/ppermute | solution.py:284
  34.8 2.2 %all-to-all-done.1 = f32[8,8,384]{2,1,0:T(8,128)S(1)} async-done(((f32[8,8,384]{2,1,0:T(8,128)}), f32[8,8,384]{2,1,0:T(8,128)S(1)}, u32[]{:S(2)}, u32[]{:S(2)}) %all-to-all-start.1) | async-done | bytes 98336 | tf_op jit(solution)/shard_map/all_to_all | solution.py:291
  37.0 0.2 new_time_weights.1
  37.2 1.9 %collective-permute-start.4 = (f32[8,128]{1,0:T(8,128)S(1)}, f32[8,128]{1,0:T(8,128)S(1)}, u32[]{:S(2)}, u32[]{:S(2)}) collective-permute-start(f32[8,128]{1,0:T(8,128)S(1)} %get-tuple-element.36.refs_0_), channel_id=1, source_target_pairs={{0,1},{1,0},{4,5},{5,4},{8,9},{9,8},{12,13},{13,12},{16,17},{17,16... | collective-permute-start | bytes 12296 | tf_op jit(solution)/shard_map/ppermute | solution.py:284
  39.1 1.3 %collective-permute-start.2 = (f32[8,128]{1,0:T(8,128)S(1)}, f32[8,128]{1,0:T(8,128)S(1)}, u32[]{:S(2)}, u32[]{:S(2)}) collective-permute-start(f32[8,128]{1,0:T(8,128)S(1)} %get-tuple-element.34.refs_2_), channel_id=1, source_target_pairs={{0,2},{1,3},{4,6},{5,7},{8,10},{9,11},{12,14},{13,15},{16,18},{17,... | collective-permute-start | bytes 12296 | tf_op jit(solution)/shard_map/ppermute | solution.py:284
  40.4 0.0 collective-permute-done.4.refs_1_
  40.4 0.7 %scale_weights.1 = (f32[8,4096]{1,0:T(8,128)}, f32[8,256]{1,0:T(8,128)}) custom-call(f32[8,128]{1,0:T(8,128)S(1)} %get-tuple-element.36.refs_0_, f32[8,128]{1,0:T(8,128)S(1)} %collective-permute-done.4.refs_1_, f32[8,128]{1,0:T(8,128)S(1)} %get-tuple-element.34.refs_2_, f32[8,4096]{1,0:T(8,128)S(1)} %get-tuple-element.35.refs_3_, ...), custom_call_target="tpu_custom_call" | custom-call | tf_op jit(solution)/shard_map/scale_weights/pallas_call | solution.py:294
  41.2 0.0 collective-permute-done.3.sent_scaled
  41.2 0.6 %collective-permute-done.2.sent_totals = f32[8,128]{1,0:T(8,128)S(1)} collective-permute-done((f32[8,128]{1,0:T(8,128)S(1)}, f32[8,128]{1,0:T(8,128)S(1)}, u32[]{:S(2)}, u32[]{:S(2)}) %collective-permute-start.2) | collective-permute-done | bytes 4128 | tf_op jit(solution)/shard_map/ppermute | solution.py:284
  (2 shorter events, 0.0 us)
Async XLA Ops:
  5.4 14.0 %all-to-all-start = ((f32[8,8,640]{2,1,0:T(8,128)}), f32[8,8,640]{2,1,0:T(8,128)S(1)}, u32[]{:S(2)}, u32[]{:S(2)}) async-start(f32[8,8,640]{2,1,0:T(8,128)} %bitcast.9), calls=%async_computation | async-start | bytes 327680 | tf_op jit(solution)/shard_map/all_to_all | solution.py:291
  14.7 7.2 %collective-permute-start = (f32[8,4096]{1,0:T(8,128)S(1)}, f32[8,4096]{1,0:T(8,128)S(1)}, u32[]{:S(2)}, u32[]{:S(2)}) collective-permute-start(f32[8,4096]{1,0:T(8,128)S(1)} %get-tuple-element.27), channel_id=1, source_target_pairs={{2,0},{3,1},{6,4},{7,5},{10,8},{11,9},{14,12},{15,13},{18,16},{19,... | collective-permute-start | bytes 393224 | tf_op jit(solution)/shard_map/ppermute | solution.py:342
  21.9 3.7 %collective-permute-start.1 = (f32[24,4352]{1,0:T(8,128)S(1)}, f32[24,4352]{1,0:T(8,128)S(1)}, u32[]{:S(2)}, u32[]{:S(2)}) collective-permute-start(f32[24,4352]{1,0:T(8,128)S(1)} %join_post.1.refs_0_), channel_id=1, source_target_pairs={{0,1},{1,0},{4,5},{5,4},{8,9},{9,8},{12,13},{13,12},{16,17},{17,16... | collective-permute-start | bytes 1253384 | tf_op jit(solution)/shard_map/ppermute | solution.py:284
  27.0 10.0 %all-to-all-start.1 = ((f32[8,8,384]{2,1,0:T(8,128)}), f32[8,8,384]{2,1,0:T(8,128)S(1)}, u32[]{:S(2)}, u32[]{:S(2)}) async-start(f32[8,8,384]{2,1,0:T(8,128)} %bitcast.10), calls=%async_computation.1 | async-start | bytes 196608 | tf_op jit(solution)/shard_map/all_to_all | solution.py:291
  33.5 7.7 %collective-permute-start.3 = (f32[8,4096]{1,0:T(8,128)S(1)}, f32[8,4096]{1,0:T(8,128)S(1)}, u32[]{:S(2)}, u32[]{:S(2)}) collective-permute-start(f32[8,4096]{1,0:T(8,128)S(1)} %get-tuple-element.35.refs_3_), channel_id=1, source_target_pairs={{0,2},{1,3},{4,6},{5,7},{8,10},{9,11},{12,14},{13,15},{16,18},{17,... | collective-permute-start | bytes 393224 | tf_op jit(solution)/shard_map/ppermute | solution.py:284
  37.2 3.2 %collective-permute-start.4 = (f32[8,128]{1,0:T(8,128)S(1)}, f32[8,128]{1,0:T(8,128)S(1)}, u32[]{:S(2)}, u32[]{:S(2)}) collective-permute-start(f32[8,128]{1,0:T(8,128)S(1)} %get-tuple-element.36.refs_0_), channel_id=1, source_target_pairs={{0,1},{1,0},{4,5},{5,4},{8,9},{9,8},{12,13},{13,12},{16,17},{17,16... | collective-permute-start | bytes 12296 | tf_op jit(solution)/shard_map/ppermute | solution.py:284
  39.1 2.6 %collective-permute-start.2 = (f32[8,128]{1,0:T(8,128)S(1)}, f32[8,128]{1,0:T(8,128)S(1)}, u32[]{:S(2)}, u32[]{:S(2)}) collective-permute-start(f32[8,128]{1,0:T(8,128)S(1)} %get-tuple-element.34.refs_2_), channel_id=1, source_target_pairs={{0,2},{1,3},{4,6},{5,7},{8,10},{9,11},{12,14},{13,15},{16,18},{17,... | collective-permute-start | bytes 12296 | tf_op jit(solution)/shard_map/ppermute | solution.py:284

commit v9 on v8

--- a/solution.py
+++ b/solution.py
@@ -72,22 +72,15 @@
     return copies
 
 
-def fetch_rows(source, target, sems, chunks, first=0):
-    rows = (source.shape[0] - first) // chunks
-    starts = [first + chunk * rows for chunk in range(chunks)]
-    parts = [pl.ds(start, rows) for start in starts]
+def fetch_rows(source, target, sems, starts):
+    spans = [(start, stop - start) for start, stop in zip(starts, starts[1:])]
+    parts = [pl.ds(*span) for span in spans]
     copies = fetch([source.at[here] for here in parts], [target.at[here] for here in parts], sems)
-    return [(start, rows, copy) for start, copy in zip(starts, copies)]
+    return [(*span, copy) for span, copy in zip(spans, copies)]
 
 
 def blocks_of(start, rows):
     return [pl.ds(here, block_rows) for here in range(start, start + rows, block_rows)]
-
-
-def split_chunk(panel, start, rows, high_ref, low_ref, offset):
-    for here in blocks_of(start, rows):
-        there = pl.ds(here.start - offset, block_rows)
-        high_ref[there, :], low_ref[there, :] = split_panel(panel[here, :])
 
 
 def wait_all(copies):
@@ -101,13 +94,13 @@
     wait_all(fetch([block] * len(places), places, sems))
 
 
-def first_kernel(all_count, half, chunks, *refs):
+def first_kernel(all_count, half, starts, *refs):
     arguments, refs = refs[:6], refs[6:]
-    out, cross, raised_units, raised_days, ends, high_ref, low_ref, *held, block, left_ref, more_high, more_low, small_sems, panel_sems, out_sems = refs
+    out, cross, raised_units, raised_days, ends, high_ref, low_ref, *held, block, left_ref, small_sems, panel_sems, out_sems = refs
     groups, day_cols = held[5].shape
     unit_rows, resident = held[0].shape[0], high_ref.shape[0]
     small = fetch(arguments[1:], held[1:], small_sems)
-    parts = fetch_rows(arguments[0], held[0], panel_sems, chunks)
+    parts = fetch_rows(arguments[0], held[0], panel_sems, starts)
     panel, cohort, pre_row, post_row, unit_logit, time_logit = held
     wait_all(small)
     me = lax.axis_index("day")
@@ -132,26 +125,17 @@
                 lane == 1, jnp.sum(treated, axis=1, keepdims=True), jnp.sum(control, axis=1, keepdims=True)
             ),
         )
-        product = jnp.zeros((4 * groups, day_cols), f32)
-
-        def terms_of(start):
-            if start < resident:
-                return high_ref, low_ref, 0
-            return more_high, more_low, resident
-
-        def multiply(start, rows):
-            high, low, offset = terms_of(start)
-            there = pl.ds(start - offset, rows)
-            return rows_dot(left_ref[:, start : start + rows], high[there, :], low[there, :])
-
-        before_it = None
+        product = jnp.zeros((4 * groups, 2 * day_cols), f32)
         for start, rows, copy in parts:
             copy.wait()
-            if before_it:
-                product += multiply(*before_it)
-            split_chunk(panel, start, rows, *terms_of(start))
-            before_it = start, rows
-        product += multiply(*before_it)
+            for here in blocks_of(start, rows):
+                high, low = split_panel(panel[here, :])
+                if here.start < resident:
+                    high_ref[here, :] = high
+                    low_ref[here, :] = low
+                both = jnp.concatenate([high, low], axis=1)
+                product += jnp.dot(left_ref[:, here], both, preferred_element_type=f32)
+        product = product[:, :day_cols] + product[:, day_cols:]
         block[:, :day_cols] = add_terms(product, groups)
         block[:, day_cols : 2 * day_cols] = product[2 * groups :][:groups]
         repeat_out(block, out, out_sems)
@@ -167,11 +151,12 @@
                 cross[:, here] = add_terms(days_dot(left, *split_panel(panel[here, :])), groups)
 
 
-def second_kernel(chunks, unit_devices, panel, sums, raised_days, ends, high_ref, low_ref, *refs):
+def second_kernel(unit_devices, panel, sums, raised_days, ends, high_ref, low_ref, *refs):
     pack, norms, more_high, more_low, held, panel_sems = refs
     groups, day_cols = raised_days.shape
     unit_rows, resident = panel.shape[0], high_ref.shape[0]
-    parts = fetch_rows(panel, held, panel_sems, chunks, resident)
+    rest = pl.ds(resident, unit_rows - resident)
+    (copy,) = fetch([panel.at[rest]], [held.at[rest]], panel_sems)
     total = tree_sum(sums[pl.ds(u * groups, groups), :] for u in range(unit_devices))
     unit_norm = total[:, 2 * day_cols : 2 * day_cols + 1]
     treat_count = jnp.maximum(total[:, 2 * day_cols + 1 : 2 * day_cols + 2], 1.0)
@@ -183,22 +168,20 @@
     pack[groups:, unit_rows:] = jnp.zeros_like(raised_time)
     left = left_of(jnp.where(before, gap, 0.0), raised_time)
 
-    def multiply(start, rows, high, low, offset):
-        for here in blocks_of(start, rows):
-            there = pl.ds(here.start - offset, block_rows)
-            product = days_dot(left, high[there, :], low[there, :])
-            pack[:groups, here] = add_terms(product, groups)
-            pack[groups:, here] = add_terms(product, groups, 1)
-
-    early = resident // block_rows // 2 * block_rows
-    multiply(0, early, high_ref, low_ref, 0)
-    before_it = early, resident - early, high_ref, low_ref, 0
-    for start, rows, copy in parts:
-        copy.wait()
-        multiply(*before_it)
-        split_chunk(held, start, rows, more_high, more_low, resident)
-        before_it = start, rows, more_high, more_low, resident
-    multiply(*before_it)
+    def multiply(here, high, low):
+        product = days_dot(left, high, low)
+        pack[:groups, here] = add_terms(product, groups)
+        pack[groups:, here] = add_terms(product, groups, 1)
+
+    for here in blocks_of(0, resident):
+        multiply(here, high_ref[here, :], low_ref[here, :])
+    copy.wait()
+    for here in blocks_of(resident, unit_rows - resident):
+        there = pl.ds(here.start - resident, block_rows)
+        high, low = split_panel(held[here, :])
+        more_high[there, :] = high
+        more_low[there, :] = low
+        multiply(here, high, low)
 
 
 def join_kernel(pack, post, out):
@@ -218,7 +201,12 @@
     raised_days = [ref[:groups, unit_rows:] for ref in parts]
     over_time = 1.0 / tree_sum(jnp.sum(value, axis=1, keepdims=True) for value in raised_days)
     over_unit = 1.0 / unit_norm
-    lam[...] = raised_days[0] * over_time
+    me = lax.rem(lax.axis_index("day"), half)
+    for day in range(half):
+        here = raised_days[0]
+        for k in range(1, half):
+            here = jnp.where(jnp.bitwise_xor(me, k) == day, raised_days[k], here)
+        lam[:, day * day_cols : (day + 1) * day_cols] = here * over_time
     time_grad = jnp.zeros((groups, day_cols), f32)
     new_sum = jnp.zeros((groups, 1), f32)
     for start in range(0, unit_rows, 2 * block_rows):
@@ -236,28 +224,31 @@
             there = pl.ds(start - resident, 2 * block_rows)
             high, low = more_high[there, :], more_low[there, :]
         time_grad += add_terms(rows_dot(left, high, low), groups)
-    block[:, :day_cols] = time_grad
-    block[:, day_cols:] = jnp.broadcast_to(new_sum, (groups, lanes))
+    lane = lax.broadcasted_iota(jnp.int32, (groups, day_cols), 1)
+    spare = (lane == day_cols - 1) & (me == half - 1)
+    block[...] = jnp.where(spare, new_sum, time_grad)
     repeat_out(block, out, out_sems)
 
 
-def fourth_kernel(unit_devices, grads, lam, norms, moved, moved_sum, totals):
-    groups, day_cols = lam.shape
-    total = tree_sum(grads[pl.ds(u * groups, groups), :] for u in range(unit_devices))
+def fourth_kernel(unit_devices, half, grads, lam, norms, ends, own_days, totals):
+    groups, day_cols = own_days.shape
     root = jnp.sqrt(jnp.maximum(norms[:, 2:3], 1.0))
-    new = lam[...] * jnp.exp(total[:, :day_cols] * (-step_rate / root))
-    moved[...] = new
-    totals[...] = total[:, day_cols:]
-    moved_sum[...] = jnp.broadcast_to(jnp.sum(new, axis=1, keepdims=True), moved_sum.shape)
-
-
-def fifth_kernel(half, *refs):
-    moved_sums, refs = refs[:half], refs[half:]
-    totals, scaled, moved, ends, unit_weights, time_weights = refs
-    first = lax.axis_index("day") < half
+    me = lax.axis_index("day")
+    moved_total = jnp.zeros((groups, 1), f32)
+    own = jnp.zeros((groups, day_cols), f32)
+    for day in range(half):
+        places = [(unit * half + half - 1 - day) * groups for unit in range(unit_devices)]
+        total = tree_sum(grads[pl.ds(place, groups), :] for place in places)
+        moved = lam[:, day * day_cols : (day + 1) * day_cols] * jnp.exp(total * (-step_rate / root))
+        moved_total += jnp.sum(moved, axis=1, keepdims=True)
+        own = jnp.where(me == day, moved, own)
+    totals[...] = jnp.broadcast_to(total[:, day_cols - 1 :], totals.shape)
+    own_days[...] = own * (ends[:, 0:1] / moved_total)
+
+
+def fifth_kernel(half, totals, scaled, own_days, unit_weights, time_weights):
     unit_weights[...] = scaled[...] / totals[:, 0:1]
-    day_total = tree_sum(ref[:, 0:1] for ref in moved_sums)
-    time_weights[...] = jnp.where(first, moved[...] / day_total * ends[:, 0:1], 0.0)
+    time_weights[...] = jnp.where(lax.axis_index("day") < half, own_days[...], 0.0)
 
 
 def sixth_kernel(half, sent_totals, sent_scaled, _, unit_weights, block, out_sem):
@@ -275,7 +266,7 @@
     half = day_devices // 2
     assert half * 2 == day_devices and half & (half - 1) == 0
     assert unit_devices & (unit_devices - 1) == 0
-    chunks = 8
+    panel_starts = [0, unit_rows // 4, unit_rows // 8 * 5, unit_rows]
     resident = unit_rows * 5 // 8 // (2 * block_rows) * (2 * block_rows)
     def spread(value, day_xor, up):
         pairs = [
@@ -285,6 +276,15 @@
 
     def over_days(value):
         return [value] + [spread(value, k, 0) for k in range(1, half)]
+
+    def over_first_half(value):
+        members = [
+            [unit * day_devices + day for unit in reversed(range(unit_devices)) for day in reversed(days)]
+            for days in (range(half), range(half, day_devices))
+        ]
+        return lax.all_to_all(
+            value, ("unit", "day"), split_axis=0, concat_axis=0, axis_index_groups=members, tiled=True
+        )
 
     def over_units(value):
         members = list(reversed(range(unit_devices)))
@@ -306,14 +306,14 @@
     arguments = (outcomes, cohort[None, :], pre_end[None, :], post_start[None, :], unit_logit, time_logit)
     fixed = [pltpu.with_memory_space_constraint(argument, pltpu.HBM) for argument in arguments]
     held = [pltpu.VMEM(argument.shape, argument.dtype) for argument in arguments]
-    small_sems, panel_sems = pltpu.SemaphoreType.DMA((5,)), pltpu.SemaphoreType.DMA((chunks,))
+    small_sems, panel_sems = pltpu.SemaphoreType.DMA((5,)), pltpu.SemaphoreType.DMA((3,))
     panel_terms = [((resident, day_cols), bf16)] * 2
     other_terms = [((unit_rows - resident, day_cols), bf16)] * 2
     out_sems = pltpu.SemaphoreType.DMA((unit_devices,))
     width = 2 * day_cols + lanes
     in_hbm = pltpu.HBM((unit_devices * groups, width), f32)
     sums, cross, raised_units, raised_days, ends, high, low = call(
-        functools.partial(first_kernel, day_devices * day_cols, half, chunks),
+        functools.partial(first_kernel, day_devices * day_cols, half, panel_starts),
         [
             in_hbm,
             ((groups, unit_rows), f32),
@@ -330,7 +330,6 @@
         + [
             pltpu.VMEM((groups, width), f32),
             pltpu.VMEM((4 * groups, unit_rows), bf16),
-            *[pltpu.VMEM(*shape) for shape in other_terms],
             small_sems,
             panel_sems,
             out_sems,
@@ -341,7 +340,7 @@
     ]
     post = lax.ppermute(cross, ("unit", "day"), downward)
     pack, norms, more_high, more_low = call(
-        functools.partial(second_kernel, 3, unit_devices),
+        functools.partial(second_kernel, unit_devices),
         [
             ((2 * groups, unit_rows + day_cols), f32),
             ((groups, lanes), f32),
@@ -355,31 +354,31 @@
     (pack,) = call(
         join_kernel, [((3 * groups, unit_rows + day_cols), f32)], "join_post", (pack, post)
     )
-    width = day_cols + lanes
+    members = unit_devices * half
     scaled, lam, grads = call(
         functools.partial(third_kernel, half),
         [
             ((groups, unit_rows), f32),
-            ((groups, day_cols), f32),
-            pltpu.HBM((unit_devices * groups, width), f32),
+            ((groups, half * day_cols), f32),
+            pltpu.HBM((members * groups, day_cols), f32),
         ],
         "time_gradient",
         (*over_days(pack), high, low, more_high, more_low, norms, raised_units, ends),
         out_specs=[vmem, vmem, hbm],
-        scratch_shapes=[pltpu.VMEM((groups, width), f32), out_sems],
+        scratch_shapes=[pltpu.VMEM((groups, day_cols), f32), pltpu.SemaphoreType.DMA((members,))],
     )
     sent_scaled = spread(scaled, 0, half)
-    moved, moved_sum, totals = call(
-        functools.partial(fourth_kernel, unit_devices),
-        [((groups, day_cols), f32), ((groups, lanes), f32), ((groups, lanes), f32)],
+    own_days, totals = call(
+        functools.partial(fourth_kernel, unit_devices, half),
+        [((groups, day_cols), f32), ((groups, lanes), f32)],
         "new_time_weights",
-        (over_units(grads), lam, norms),
+        (over_first_half(grads), lam, norms, ends),
     )
     unit_weights, time_weights = call(
         functools.partial(fifth_kernel, half),
         [((groups, unit_rows), f32), ((groups, day_cols), f32)],
         "scale_weights",
-        (*over_days(moved_sum), totals, scaled, moved, ends),
+        (totals, scaled, own_days),
     )
     (unit_weights,) = call(
         functools.partial(sixth_kernel, half),

time: 42.2 us -> 40.2 us (0.953)
  starting transfers between devices: 23.4 us -> 21.4 us
  waiting for transfers between devices: 7.88 us -> 8.49 us
  Pallas kernels: 9.68 us -> 9.15 us
    all_to_all x2 -> x1, starting transfers between devices: 15.7 us -> 9.31 us  [over_units(): lax.all_to_all(value, 'unit', split_axis=0, concat_axis=0, axis_index_gro...]
    all_to_all x0 -> x1, starting transfers between devices: none -> 6.28 us  [over_first_half(): lax.all_to_all(value, ('unit', 'day'), split_axis=0, concat_axis=0, axis_...]
    all_to_all x0 -> x1, waiting for transfers between devices: none -> 2.84 us  [over_first_half(): lax.all_to_all(value, ('unit', 'day'), split_axis=0, concat_axis=0, axis_...]
    all_to_all x2 -> x1, waiting for transfers between devices: 5.6 us -> 3.36 us  [over_units(): lax.all_to_all(value, 'unit', split_axis=0, concat_axis=0, axis_index_gro...]
    ppermute x4 -> x3, starting transfers between devices: 6.41 us -> 4.5 us  [spread(): return lax.ppermute(value, ('unit', 'day'), pairs)]
    pallas_call x7, Pallas kernels: 9.68 us -> 9.15 us  [call(): pl.pallas_call(kernel, in_specs=in_specs or [vmem] * len(args), out_specs...]
    ppermute x4 -> x3, waiting for transfers between devices: 2.28 us -> 2.29 us  [spread(): return lax.ppermute(value, ('unit', 'day'), pairs)]
  transfers between devices with their start and end apart: 7 -> 6, of which waited for: 4 -> 4; matrix products, arithmetic and copies ran while one was open for 0% -> 0% of each run, Pallas kernels for 8% -> 9%
where the time goes in v9:
time: 40.2 us; the launch traced here: 39.7 us
  starting transfers between devices  21.4 us (53%)
  Pallas kernels  9.15 us (23%)
  waiting for transfers between devices  8.49 us (21%)
  between operations  0.71 us (2%)
    all_to_all x1, starting transfers between devices, over_units(): lax.all_to_all(value, 'unit', split_axis=0, concat_axis=0, axis_index_gro...  9.31 us
    pallas_call x7, Pallas kernels, call(): pl.pallas_call(kernel, in_specs=in_specs or [vmem] * len(args), out_specs...  9.15 us
    all_to_all x1, starting transfers between devices, over_first_half(): lax.all_to_all(value, ('unit', 'day'), split_axis=0, concat_axis=0, axis_...  6.28 us
    ppermute x3, starting transfers between devices, spread(): return lax.ppermute(value, ('unit', 'day'), pairs)  4.5 us
    all_to_all x1, waiting for transfers between devices, over_units(): lax.all_to_all(value, 'unit', split_axis=0, concat_axis=0, axis_index_gro...  3.36 us
    all_to_all x1, waiting for transfers between devices, over_first_half(): lax.all_to_all(value, ('unit', 'day'), split_axis=0, concat_axis=0, axis_...  2.84 us
    ppermute x3, waiting for transfers between devices, spread(): return lax.ppermute(value, ('unit', 'day'), pairs)  2.29 us
    ppermute x1, starting transfers between devices, local(): post = lax.ppermute(cross, ('unit', 'day'), downward)  1.28 us
  transfers between devices with their start and end apart: 6, of which 4 were waited for; matrix products, arithmetic and copies ran while one was open for 0% of the time, Pallas kernels for 9%

profile of v9, /device:TPU:0, one launch (start us, length us, event | category | flops | bytes accessed | tf_op | source)
XLA Modules:
  0.0 39.7 jit_solution(15490741159382277529)
XLA Ops:
  0.6 3.8 %first_product.1 = (f32[64,640]{1,0:T(8,128)}, f32[8,4096]{1,0:T(8,128)S(1)}, f32[8,4096]{1,0:T(8,128)S(1)}, f32[8,256]{1,0:T(8,128)S(1)}, f32[8,128]{1,0:T(8,12...) custom-call(f32[4096,256]{1,0:T(8,128)} %panel.1, s32[1,4096]{1,0:T(1,128)} %bitcast.11, ...), custom_call_target="tpu_custom_call" | custom-call | tf_op jit(solution)/shard_map/first_product/pallas_call | solution.py:294
  4.4 9.3 %all-to-all-start = ((f32[8,8,640]{2,1,0:T(8,128)}), f32[8,8,640]{2,1,0:T(8,128)S(1)}, u32[]{:S(2)}, u32[]{:S(2)}) async-start(f32[8,8,640]{2,1,0:T(8,128)} %bitcast.9), calls=%async_computation | async-start | bytes 327680 | tf_op jit(solution)/shard_map/all_to_all | solution.py:291
  13.8 1.3 %collective-permute-start = (f32[8,4096]{1,0:T(8,128)S(1)}, f32[8,4096]{1,0:T(8,128)S(1)}, u32[]{:S(2)}, u32[]{:S(2)}) collective-permute-start(f32[8,4096]{1,0:T(8,128)S(1)} %get-tuple-element.26), channel_id=1, source_target_pairs={{2,0},{3,1},{6,4},{7,5},{10,8},{11,9},{14,12},{15,13},{18,16},{19,... | collective-permute-start | bytes 393224 | tf_op jit(solution)/shard_map/ppermute | solution.py:341
  15.0 3.4 %all-to-all-done = f32[8,8,640]{2,1,0:T(8,128)S(1)} async-done(((f32[8,8,640]{2,1,0:T(8,128)}), f32[8,8,640]{2,1,0:T(8,128)S(1)}, u32[]{:S(2)}, u32[]{:S(2)}) %all-to-all-start) | async-done | bytes 163872 | tf_op jit(solution)/shard_map/all_to_all | solution.py:291
  18.4 2.8 %unit_gradient.1 = (f32[16,4352]{1,0:T(8,128)S(1)}, f32[8,128]{1,0:T(8,128)S(1)}, bf16[1536,256]{1,0:T(8,128)(2,1)S(1)}, bf16[1536,256]{1,0:T(8,128)(2,1)S(1)}) custom-call(f32[4096,256]{1,0:T(8,128)} %panel.1, f32[64,640]{1,0:T(8,128)S(1)} %bitcast.7, f32[8,256]{1,0:T(8,128)S(1)} %get-tuple-element.21.raised_days, ...), custom_call_target="tpu_custom_call" | custom-call | tf_op jit(solution)/shard_map/unit_gradient/pallas_call | solution.py:294
  21.2 0.0 collective-permute-done.post
  21.2 1.9 %collective-permute-start.1 = (f32[24,4352]{1,0:T(8,128)S(1)}, f32[24,4352]{1,0:T(8,128)S(1)}, u32[]{:S(2)}, u32[]{:S(2)}) collective-permute-start(f32[24,4352]{1,0:T(8,128)S(1)} %join_post.1.refs_0_), channel_id=1, source_target_pairs={{0,1},{1,0},{4,5},{5,4},{8,9},{9,8},{12,13},{13,12},{16,17},{17,16... | collective-permute-start | bytes 1253384 | tf_op jit(solution)/shard_map/ppermute | solution.py:275
  23.2 1.7 %collective-permute-done.1.refs_1_ = f32[24,4352]{1,0:T(8,128)S(1)} collective-permute-done((f32[24,4352]{1,0:T(8,128)S(1)}, f32[24,4352]{1,0:T(8,128)S(1)}, u32[]{:S(2)}, u32[]{:S(2)}) %collective-permute-start.1) | collective-permute-done | bytes 417824 | tf_op jit(solution)/shard_map/ppermute | solution.py:275
  24.9 1.6 %time_gradient.1 = (f32[8,4096]{1,0:T(8,128)S(1)}, f32[8,512]{1,0:T(8,128)S(1)}, f32[128,256]{1,0:T(8,128)}) custom-call(f32[24,4352]{1,0:T(8,128)S(1)} %join_post.1.refs_0_, f32[24,4352]{1,0:T(8,128)S(1)} %collective-permute-done.1.refs_1_, bf16[2560,256]{1,0:T(8,128)(2,1)S(1)} %get-tuple-element.23.high_ref.refs_2_, ...), custom_call_target="tpu_custom_call" | custom-call | tf_op jit(solution)/shard_map/time_gradient/pallas_call | solution.py:294
  26.4 6.3 %all-to-all-start.1 = ((f32[16,8,256]{2,1,0:T(8,128)}), f32[16,8,256]{2,1,0:T(8,128)S(1)}, u32[]{:S(2)}, u32[]{:S(2)}) async-start(f32[16,8,256]{2,1,0:T(8,128)} %bitcast.10), calls=%async_computation.1 | async-start | bytes 262144 | tf_op jit(solution)/shard_map/all_to_all | solution.py:285
  32.7 1.3 %collective-permute-start.3 = (f32[8,4096]{1,0:T(8,128)S(1)}, f32[8,4096]{1,0:T(8,128)S(1)}, u32[]{:S(2)}, u32[]{:S(2)}) collective-permute-start(f32[8,4096]{1,0:T(8,128)S(1)} %get-tuple-element.34.scaled), channel_id=1, source_target_pairs={{0,2},{1,3},{4,6},{5,7},{8,10},{9,11},{12,14},{13,15},{16,18},{17,... | collective-permute-start | bytes 393224 | tf_op jit(solution)/shard_map/ppermute | solution.py:275
  34.0 2.8 %all-to-all-done.1 = f32[16,8,256]{2,1,0:T(8,128)S(1)} async-done(((f32[16,8,256]{2,1,0:T(8,128)}), f32[16,8,256]{2,1,0:T(8,128)S(1)}, u32[]{:S(2)}, u32[]{:S(2)}) %all-to-all-start.1) | async-done | bytes 131104 | tf_op jit(solution)/shard_map/all_to_all | solution.py:285
  36.9 0.2 new_time_weights.1
  37.1 1.3 %collective-permute-start.2 = (f32[8,128]{1,0:T(8,128)S(1)}, f32[8,128]{1,0:T(8,128)S(1)}, u32[]{:S(2)}, u32[]{:S(2)}) collective-permute-start(f32[8,128]{1,0:T(8,128)S(1)} %get-tuple-element.33.totals), channel_id=1, source_target_pairs={{0,2},{1,3},{4,6},{5,7},{8,10},{9,11},{12,14},{13,15},{16,18},{17,... | collective-permute-start | bytes 12296 | tf_op jit(solution)/shard_map/ppermute | solution.py:275
  38.4 0.7 %scale_weights.1 = (f32[8,4096]{1,0:T(8,128)}, f32[8,256]{1,0:T(8,128)}) custom-call(f32[8,128]{1,0:T(8,128)S(1)} %get-tuple-element.33.totals, f32[8,4096]{1,0:T(8,128)S(1)} %get-tuple-element.34.scaled, f32[8,256]{1,0:T(8,128)S(1)} %get-tuple-element.35.own_days), custom_call_target="tpu_custom_call" | custom-call | tf_op jit(solution)/shard_map/scale_weights/pallas_call | solution.py:294
  39.1 0.0 collective-permute-done.3.sent_scaled
  39.1 0.6 %collective-permute-done.2.sent_totals = f32[8,128]{1,0:T(8,128)S(1)} collective-permute-done((f32[8,128]{1,0:T(8,128)S(1)}, f32[8,128]{1,0:T(8,128)S(1)}, u32[]{:S(2)}, u32[]{:S(2)}) %collective-permute-start.2) | collective-permute-done | bytes 4128 | tf_op jit(solution)/shard_map/ppermute | solution.py:275
  (2 shorter events, 0.0 us)
Async XLA Ops:
  4.4 14.0 %all-to-all-start = ((f32[8,8,640]{2,1,0:T(8,128)}), f32[8,8,640]{2,1,0:T(8,128)S(1)}, u32[]{:S(2)}, u32[]{:S(2)}) async-start(f32[8,8,640]{2,1,0:T(8,128)} %bitcast.9), calls=%async_computation | async-start | bytes 327680 | tf_op jit(solution)/shard_map/all_to_all | solution.py:291
  13.8 7.4 %collective-permute-start = (f32[8,4096]{1,0:T(8,128)S(1)}, f32[8,4096]{1,0:T(8,128)S(1)}, u32[]{:S(2)}, u32[]{:S(2)}) collective-permute-start(f32[8,4096]{1,0:T(8,128)S(1)} %get-tuple-element.26), channel_id=1, source_target_pairs={{2,0},{3,1},{6,4},{7,5},{10,8},{11,9},{14,12},{15,13},{18,16},{19,... | collective-permute-start | bytes 393224 | tf_op jit(solution)/shard_map/ppermute | solution.py:341
  21.2 3.7 %collective-permute-start.1 = (f32[24,4352]{1,0:T(8,128)S(1)}, f32[24,4352]{1,0:T(8,128)S(1)}, u32[]{:S(2)}, u32[]{:S(2)}) collective-permute-start(f32[24,4352]{1,0:T(8,128)S(1)} %join_post.1.refs_0_), channel_id=1, source_target_pairs={{0,1},{1,0},{4,5},{5,4},{8,9},{9,8},{12,13},{13,12},{16,17},{17,16... | collective-permute-start | bytes 1253384 | tf_op jit(solution)/shard_map/ppermute | solution.py:275
  26.4 10.4 %all-to-all-start.1 = ((f32[16,8,256]{2,1,0:T(8,128)}), f32[16,8,256]{2,1,0:T(8,128)S(1)}, u32[]{:S(2)}, u32[]{:S(2)}) async-start(f32[16,8,256]{2,1,0:T(8,128)} %bitcast.10), calls=%async_computation.1 | async-start | bytes 262144 | tf_op jit(solution)/shard_map/all_to_all | solution.py:285
  32.7 6.4 %collective-permute-start.3 = (f32[8,4096]{1,0:T(8,128)S(1)}, f32[8,4096]{1,0:T(8,128)S(1)}, u32[]{:S(2)}, u32[]{:S(2)}) collective-permute-start(f32[8,4096]{1,0:T(8,128)S(1)} %get-tuple-element.34.scaled), channel_id=1, source_target_pairs={{0,2},{1,3},{4,6},{5,7},{8,10},{9,11},{12,14},{13,15},{16,18},{17,... | collective-permute-start | bytes 393224 | tf_op jit(solution)/shard_map/ppermute | solution.py:275
  37.1 2.6 %collective-permute-start.2 = (f32[8,128]{1,0:T(8,128)S(1)}, f32[8,128]{1,0:T(8,128)S(1)}, u32[]{:S(2)}, u32[]{:S(2)}) collective-permute-start(f32[8,128]{1,0:T(8,128)S(1)} %get-tuple-element.33.totals), channel_id=1, source_target_pairs={{0,2},{1,3},{4,6},{5,7},{8,10},{9,11},{12,14},{13,15},{16,18},{17,... | collective-permute-start | bytes 12296 | tf_op jit(solution)/shard_map/ppermute | solution.py:275

commit v10 on v9

--- a/solution.py
+++ b/solution.py
@@ -96,7 +96,7 @@
 
 def first_kernel(all_count, half, starts, *refs):
     arguments, refs = refs[:6], refs[6:]
-    out, cross, raised_units, raised_days, ends, high_ref, low_ref, *held, block, left_ref, small_sems, panel_sems, out_sems = refs
+    out, cross, raised_days, ends, high_ref, low_ref, *held, block, left_ref, cross_block, small_sems, panel_sems, out_sems = refs
     groups, day_cols = held[5].shape
     unit_rows, resident = held[0].shape[0], high_ref.shape[0]
     small = fetch(arguments[1:], held[1:], small_sems)
@@ -111,7 +111,6 @@
         treated = jnp.where(cohort[...] == label, 1.0, 0.0)
         control = jnp.where(cohort[...] > label, 1.0, 0.0)
         raised = jnp.exp(unit_logit[...]) * control
-        raised_units[...] = raised
         left_ref[...] = left_of(raised, treated)
         pre_end = column(pre_row)
         ends[...] = jnp.broadcast_to(pre_end.astype(f32), ends.shape)
@@ -148,15 +147,16 @@
         for start, rows, copy in parts:
             copy.wait()
             for here in blocks_of(start, rows):
-                cross[:, here] = add_terms(days_dot(left, *split_panel(panel[here, :])), groups)
-
-
-def second_kernel(unit_devices, panel, sums, raised_days, ends, high_ref, low_ref, *refs):
-    pack, norms, more_high, more_low, held, panel_sems = refs
+                cross_block[:, here] = add_terms(days_dot(left, *split_panel(panel[here, :])), groups)
+        wait_all(fetch([cross_block], [cross], out_sems))
+
+
+def second_kernel(unit_devices, panel, cohort, unit_logit, sums, raised_days, ends, high_ref, low_ref, *refs):
+    pack, norms, raised_units, more_high, more_low, held, held_cohort, held_logit, sems = refs
     groups, day_cols = raised_days.shape
     unit_rows, resident = panel.shape[0], high_ref.shape[0]
     rest = pl.ds(resident, unit_rows - resident)
-    (copy,) = fetch([panel.at[rest]], [held.at[rest]], panel_sems)
+    copies = fetch([panel.at[rest], cohort, unit_logit], [held, held_cohort, held_logit], sems)
     total = tree_sum(sums[pl.ds(u * groups, groups), :] for u in range(unit_devices))
     unit_norm = total[:, 2 * day_cols : 2 * day_cols + 1]
     treat_count = jnp.maximum(total[:, 2 * day_cols + 1 : 2 * day_cols + 2], 1.0)
@@ -175,10 +175,12 @@
 
     for here in blocks_of(0, resident):
         multiply(here, high_ref[here, :], low_ref[here, :])
-    copy.wait()
+    wait_all(copies)
+    label = lax.broadcasted_iota(jnp.int32, raised_units.shape, 0)
+    raised_units[...] = jnp.where(held_cohort[...] > label, jnp.exp(held_logit[...]), 0.0)
     for here in blocks_of(resident, unit_rows - resident):
         there = pl.ds(here.start - resident, block_rows)
-        high, low = split_panel(held[here, :])
+        high, low = split_panel(held[there, :])
         more_high[there, :] = high
         more_low[there, :] = low
         multiply(here, high, low)
@@ -192,7 +194,7 @@
 
 
 def third_kernel(half, *refs):
-    parts, refs = refs[:half], refs[half:]
+    parts, refs = [refs[0].at[day] for day in range(half)], refs[1:]
     high_ref, low_ref, more_high, more_low, norms, raised_units, ends, scaled, lam, out, block, out_sems = refs
     groups, unit_rows = raised_units.shape
     resident, day_cols = high_ref.shape
@@ -203,10 +205,7 @@
     over_unit = 1.0 / unit_norm
     me = lax.rem(lax.axis_index("day"), half)
     for day in range(half):
-        here = raised_days[0]
-        for k in range(1, half):
-            here = jnp.where(jnp.bitwise_xor(me, k) == day, raised_days[k], here)
-        lam[:, day * day_cols : (day + 1) * day_cols] = here * over_time
+        lam[:, day * day_cols : (day + 1) * day_cols] = raised_days[day] * over_time
     time_grad = jnp.zeros((groups, day_cols), f32)
     new_sum = jnp.zeros((groups, 1), f32)
     for start in range(0, unit_rows, 2 * block_rows):
@@ -267,15 +266,14 @@
     assert half * 2 == day_devices and half & (half - 1) == 0
     assert unit_devices & (unit_devices - 1) == 0
     panel_starts = [0, unit_rows // 4, unit_rows // 8 * 5, unit_rows]
-    resident = unit_rows * 5 // 8 // (2 * block_rows) * (2 * block_rows)
-    def spread(value, day_xor, up):
-        pairs = [
-            (u * day_devices + d, u * day_devices + (d ^ day_xor) + up) for u in range(unit_devices) for d in range(half)
-        ]
+    resident = unit_rows * 3 // 4 // (2 * block_rows) * (2 * block_rows)
+    def to_other_half(value):
+        pairs = [(u * day_devices + d, u * day_devices + d + half) for u in range(unit_devices) for d in range(half)]
         return lax.ppermute(value, ("unit", "day"), pairs)
 
     def over_days(value):
-        return [value] + [spread(value, k, 0) for k in range(1, half)]
+        halves = [list(range(half)), list(range(half, day_devices))]
+        return lax.all_gather(value, "day", axis_index_groups=halves)
 
     def over_first_half(value):
         members = [
@@ -312,12 +310,11 @@
     out_sems = pltpu.SemaphoreType.DMA((unit_devices,))
     width = 2 * day_cols + lanes
     in_hbm = pltpu.HBM((unit_devices * groups, width), f32)
-    sums, cross, raised_units, raised_days, ends, high, low = call(
+    sums, cross, raised_days, ends, high, low = call(
         functools.partial(first_kernel, day_devices * day_cols, half, panel_starts),
         [
             in_hbm,
-            ((groups, unit_rows), f32),
-            ((groups, unit_rows), f32),
+            pltpu.HBM((groups, unit_rows), f32),
             ((groups, day_cols), f32),
             ((groups, lanes), f32),
             *panel_terms,
@@ -325,11 +322,12 @@
         "first_product",
         fixed,
         in_specs=[hbm] * 6,
-        out_specs=[hbm] + [vmem] * 6,
+        out_specs=[hbm, hbm] + [vmem] * 4,
         scratch_shapes=held
         + [
             pltpu.VMEM((groups, width), f32),
             pltpu.VMEM((4 * groups, unit_rows), bf16),
+            pltpu.VMEM((groups, unit_rows), f32),
             small_sems,
             panel_sems,
             out_sems,
@@ -339,17 +337,18 @@
         (u * day_devices + d + half, u * day_devices + d) for u in range(unit_devices) for d in range(half)
     ]
     post = lax.ppermute(cross, ("unit", "day"), downward)
-    pack, norms, more_high, more_low = call(
+    pack, norms, raised_units, more_high, more_low = call(
         functools.partial(second_kernel, unit_devices),
         [
             ((2 * groups, unit_rows + day_cols), f32),
             ((groups, lanes), f32),
+            ((groups, unit_rows), f32),
             *other_terms,
         ],
         "unit_gradient",
-        (fixed[0], over_units(sums), raised_days, ends, high, low),
-        in_specs=[hbm] + [vmem] * 5,
-        scratch_shapes=[held[0], panel_sems],
+        (fixed[0], fixed[1], fixed[4], over_units(sums), raised_days, ends, high, low),
+        in_specs=[hbm] * 3 + [vmem] * 5,
+        scratch_shapes=[pltpu.VMEM((unit_rows - resident, day_cols), f32), held[1], held[4], panel_sems],
     )
     (pack,) = call(
         join_kernel, [((3 * groups, unit_rows + day_cols), f32)], "join_post", (pack, post)
@@ -363,11 +362,11 @@
             pltpu.HBM((members * groups, day_cols), f32),
         ],
         "time_gradient",
-        (*over_days(pack), high, low, more_high, more_low, norms, raised_units, ends),
+        (over_days(pack), high, low, more_high, more_low, norms, raised_units, ends),
         out_specs=[vmem, vmem, hbm],
         scratch_shapes=[pltpu.VMEM((groups, day_cols), f32), pltpu.SemaphoreType.DMA((members,))],
     )
-    sent_scaled = spread(scaled, 0, half)
+    sent_scaled = to_other_half(scaled)
     own_days, totals = call(
         functools.partial(fourth_kernel, unit_devices, half),
         [((groups, day_cols), f32), ((groups, lanes), f32)],
@@ -384,7 +383,7 @@
         functools.partial(sixth_kernel, half),
         [((groups, unit_rows), f32)],
         "other_half",
-        (spread(totals, 0, half), sent_scaled, unit_weights),
+        (to_other_half(totals), sent_scaled, unit_weights),
         in_specs=[vmem, vmem, hbm],
         out_specs=[hbm],
         input_output_aliases={2: 0},

time: 40.2 us -> 41 us (1.020)
  waiting for transfers between devices: 8.49 us -> 4.53 us
  starting transfers between devices: 21.4 us -> 23.9 us
  blocking collectives: 0 us -> 2.4 us
    ppermute x3 -> x2, starting transfers between devices: 4.5 us -> 7.06 us  [to_other_half(): return lax.ppermute(value, ('unit', 'day'), pairs)]
    all_gather x0 -> x1, blocking collectives: none -> 2.4 us  [over_days(): return lax.all_gather(value, 'day', axis_index_groups=halves)]
    all_to_all x1, waiting for transfers between devices: 2.84 us -> 0.6 us  [over_first_half(): lax.all_to_all(value, ('unit', 'day'), split_axis=0, concat_axis=0, axis_...]
    ppermute x3 -> x2, waiting for transfers between devices: 2.29 us -> 0.57 us  [to_other_half(): return lax.ppermute(value, ('unit', 'day'), pairs)]
  transfers between devices with their start and end apart: 6 -> 5, of which waited for: 4 -> 3; matrix products, arithmetic and copies ran while one was open for 0% -> 0% of each run, Pallas kernels for 9% -> 9%
where the time goes in v10:
time: 41 us; the launch traced here: 40.5 us
  starting transfers between devices  23.9 us (58%)
  Pallas kernels  8.98 us (22%)
  waiting for transfers between devices  4.53 us (11%)
  blocking collectives  2.4 us (6%)
  between operations  0.7 us (2%)
    all_to_all x1, starting transfers between devices, over_units(): lax.all_to_all(value, 'unit', split_axis=0, concat_axis=0, axis_index_gro...  9.31 us
    pallas_call x7, Pallas kernels, call(): pl.pallas_call(kernel, in_specs=in_specs or [vmem] * len(args), out_specs...  8.98 us
    ppermute x2, starting transfers between devices, to_other_half(): return lax.ppermute(value, ('unit', 'day'), pairs)  7.06 us
    all_to_all x1, starting transfers between devices, over_first_half(): lax.all_to_all(value, ('unit', 'day'), split_axis=0, concat_axis=0, axis_...  6.28 us
    all_to_all x1, waiting for transfers between devices, over_units(): lax.all_to_all(value, 'unit', split_axis=0, concat_axis=0, axis_index_gro...  3.36 us
    all_gather x1, blocking collectives, over_days(): return lax.all_gather(value, 'day', axis_index_groups=halves)  2.4 us
    ppermute x1, starting transfers between devices, local(): post = lax.ppermute(cross, ('unit', 'day'), downward)  1.28 us
  transfers between devices with their start and end apart: 5, of which 3 were waited for; matrix products, arithmetic and copies ran while one was open for 0% of the time, Pallas kernels for 9%

profile of v10, /device:TPU:0, one launch (start us, length us, event | category | flops | bytes accessed | tf_op | source)
XLA Modules:
  0.0 40.5 jit_solution(1780553781642002849)
XLA Ops:
  0.6 3.8 %first_product.1 = (f32[64,640]{1,0:T(8,128)}, f32[8,4096]{1,0:T(8,128)}, f32[8,256]{1,0:T(8,128)S(1)}, f32[8,128]{1,0:T(8,128)S(1)}, bf16[3072,256]{1,0:T(8,128)(2,1)S(1)}, /*index=5*/bf16[3072,256]{1,0:T(8,128)(2,1)S(1)}) custom-call(f32[4096,256]{1,0:T(8,128)} %panel.1, s32[1,4096]{1,0:T(1,128)} %bitcast.13, s32[1,8]{1,0:T(1,128)} %bitcast.15, ...), custom_call_target="tpu_custom_call" | custom-call | tf_op jit(solution)/shard_map/first_product/pallas_call | solution.py:292
  4.5 9.3 %all-to-all-start = ((f32[8,8,640]{2,1,0:T(8,128)}), f32[8,8,640]{2,1,0:T(8,128)S(1)}, u32[]{:S(2)}, u32[]{:S(2)}) async-start(f32[8,8,640]{2,1,0:T(8,128)} %bitcast.11), calls=%async_computation | async-start | bytes 327680 | tf_op jit(solution)/shard_map/all_to_all | solution.py:289
  13.8 1.3 %collective-permute-start = (f32[8,4096]{1,0:T(8,128)}, f32[8,4096]{1,0:T(8,128)S(1)}, u32[]{:S(2)}, u32[]{:S(2)}) collective-permute-start(f32[8,4096]{1,0:T(8,128)} %get-tuple-element.26), channel_id=1, source_target_pairs={{2,0},{3,1},{6,4},{7,5},{10,8},{11,9},{14,12},{15,13},{18,16},{19,... | collective-permute-start | bytes 393224 | tf_op jit(solution)/shard_map/ppermute | solution.py:339
  15.1 3.4 %all-to-all-done = f32[8,8,640]{2,1,0:T(8,128)S(1)} async-done(((f32[8,8,640]{2,1,0:T(8,128)}), f32[8,8,640]{2,1,0:T(8,128)S(1)}, u32[]{:S(2)}, u32[]{:S(2)}) %all-to-all-start) | async-done | bytes 163872 | tf_op jit(solution)/shard_map/all_to_all | solution.py:289
  18.4 2.6 %unit_gradient.1 = (f32[16,4352]{1,0:T(8,128)S(1)}, f32[8,128]{1,0:T(8,128)S(1)}, f32[8,4096]{1,0:T(8,128)S(1)}, bf16[1024,256]{1,0:T(8,128)(2,1)S(1)}, bf16[1024,256]{1,0:T(8,128)(2,1)S(1)}) custom-call(f32[4096,256]{1,0:T(8,128)} %panel.1, s32[1,4096]{1,0:T(1,128)} %bitcast.14, f32[8,4096]{1,0:T(8,128)} %unit_logit.1, f32[64,640]{1,0:T(8,128)S(1)} %bitcast.9, ...), custom_call_target="tpu_custom_call" | custom-call | tf_op jit(solution)/shard_map/unit_gradient/pallas_call | solution.py:292
  21.0 0.0 collective-permute-done.post
  21.1 2.4 %all-gather = f32[48,4352]{1,0:T(8,128)S(1)} all-gather(f32[24,4352]{1,0:T(8,128)S(1)} %join_post.1), channel_id=2, replica_groups={{0,1},{2,3},{4,5},{6,7},{8,9},{10,11},{12,13},{14,15},{16,17},{18,19},{..., dimensions={0}, use_global_device_ids=true | all-gather | bytes 1253376 | tf_op jit(solution)/shard_map/all_gather | solution.py:276
  23.5 1.5 %time_gradient.1 = (f32[8,4096]{1,0:T(8,128)S(1)}, f32[8,512]{1,0:T(8,128)S(1)}, f32[128,256]{1,0:T(8,128)}) custom-call(f32[2,24,4352]{2,1,0:T(8,128)S(1)} %bitcast.8, bf16[3072,256]{1,0:T(8,128)(2,1)S(1)} %get-tuple-element.23.high_ref.refs_1_, bf16[3072,256]{1,0:T(8,128)(2,1)S(1)} %get-tuple-element.24.low_ref.refs_2_, ...), custom_call_target="tpu_custom_call" | custom-call | tf_op jit(solution)/shard_map/time_gradient/pallas_call | solution.py:292
  25.0 6.3 %all-to-all-start.1 = ((f32[16,8,256]{2,1,0:T(8,128)}), f32[16,8,256]{2,1,0:T(8,128)S(1)}, u32[]{:S(2)}, u32[]{:S(2)}) async-start(f32[16,8,256]{2,1,0:T(8,128)} %bitcast.12), calls=%async_computation.1 | async-start | bytes 262144 | tf_op jit(solution)/shard_map/all_to_all | solution.py:283
  31.3 3.5 %collective-permute-start.2 = (f32[8,4096]{1,0:T(8,128)S(1)}, f32[8,4096]{1,0:T(8,128)S(1)}, u32[]{:S(2)}, u32[]{:S(2)}) collective-permute-start(f32[8,4096]{1,0:T(8,128)S(1)} %get-tuple-element.34.scaled), channel_id=1, source_target_pairs={{0,2},{1,3},{4,6},{5,7},{8,10},{9,11},{12,14},{13,15},{16,18},{17,... | collective-permute-start | bytes 393224 | tf_op jit(solution)/shard_map/ppermute | solution.py:272
  34.8 0.6 %all-to-all-done.1 = f32[16,8,256]{2,1,0:T(8,128)S(1)} async-done(((f32[16,8,256]{2,1,0:T(8,128)}), f32[16,8,256]{2,1,0:T(8,128)S(1)}, u32[]{:S(2)}, u32[]{:S(2)}) %all-to-all-start.1) | async-done | bytes 131104 | tf_op jit(solution)/shard_map/all_to_all | solution.py:283
  35.4 0.2 new_time_weights.1
  35.7 3.5 %collective-permute-start.1 = (f32[8,128]{1,0:T(8,128)S(1)}, f32[8,128]{1,0:T(8,128)S(1)}, u32[]{:S(2)}, u32[]{:S(2)}) collective-permute-start(f32[8,128]{1,0:T(8,128)S(1)} %get-tuple-element.33.totals), channel_id=1, source_target_pairs={{0,2},{1,3},{4,6},{5,7},{8,10},{9,11},{12,14},{13,15},{16,18},{17,... | collective-permute-start | bytes 12296 | tf_op jit(solution)/shard_map/ppermute | solution.py:272
  39.2 0.7 %scale_weights.1 = (f32[8,4096]{1,0:T(8,128)}, f32[8,256]{1,0:T(8,128)}) custom-call(f32[8,128]{1,0:T(8,128)S(1)} %get-tuple-element.33.totals, f32[8,4096]{1,0:T(8,128)S(1)} %get-tuple-element.34.scaled, f32[8,256]{1,0:T(8,128)S(1)} %get-tuple-element.35.own_days), custom_call_target="tpu_custom_call" | custom-call | tf_op jit(solution)/shard_map/scale_weights/pallas_call | solution.py:292
  40.0 0.0 collective-permute-done.2.sent_scaled
  40.0 0.6 %collective-permute-done.1.sent_totals = f32[8,128]{1,0:T(8,128)S(1)} collective-permute-done((f32[8,128]{1,0:T(8,128)S(1)}, f32[8,128]{1,0:T(8,128)S(1)}, u32[]{:S(2)}, u32[]{:S(2)}) %collective-permute-start.1) | collective-permute-done | bytes 4128 | tf_op jit(solution)/shard_map/ppermute | solution.py:272
  (2 shorter events, 0.0 us)
Async XLA Ops:
  4.5 14.0 %all-to-all-start = ((f32[8,8,640]{2,1,0:T(8,128)}), f32[8,8,640]{2,1,0:T(8,128)S(1)}, u32[]{:S(2)}, u32[]{:S(2)}) async-start(f32[8,8,640]{2,1,0:T(8,128)} %bitcast.11), calls=%async_computation | async-start | bytes 327680 | tf_op jit(solution)/shard_map/all_to_all | solution.py:289
  13.8 7.3 %collective-permute-start = (f32[8,4096]{1,0:T(8,128)}, f32[8,4096]{1,0:T(8,128)S(1)}, u32[]{:S(2)}, u32[]{:S(2)}) collective-permute-start(f32[8,4096]{1,0:T(8,128)} %get-tuple-element.26), channel_id=1, source_target_pairs={{2,0},{3,1},{6,4},{7,5},{10,8},{11,9},{14,12},{15,13},{18,16},{19,... | collective-permute-start | bytes 393224 | tf_op jit(solution)/shard_map/ppermute | solution.py:339
  25.0 10.4 %all-to-all-start.1 = ((f32[16,8,256]{2,1,0:T(8,128)}), f32[16,8,256]{2,1,0:T(8,128)S(1)}, u32[]{:S(2)}, u32[]{:S(2)}) async-start(f32[16,8,256]{2,1,0:T(8,128)} %bitcast.12), calls=%async_computation.1 | async-start | bytes 262144 | tf_op jit(solution)/shard_map/all_to_all | solution.py:283
  31.3 8.7 %collective-permute-start.2 = (f32[8,4096]{1,0:T(8,128)S(1)}, f32[8,4096]{1,0:T(8,128)S(1)}, u32[]{:S(2)}, u32[]{:S(2)}) collective-permute-start(f32[8,4096]{1,0:T(8,128)S(1)} %get-tuple-element.34.scaled), channel_id=1, source_target_pairs={{0,2},{1,3},{4,6},{5,7},{8,10},{9,11},{12,14},{13,15},{16,18},{17,... | collective-permute-start | bytes 393224 | tf_op jit(solution)/shard_map/ppermute | solution.py:272
  35.7 4.9 %collective-permute-start.1 = (f32[8,128]{1,0:T(8,128)S(1)}, f32[8,128]{1,0:T(8,128)S(1)}, u32[]{:S(2)}, u32[]{:S(2)}) collective-permute-start(f32[8,128]{1,0:T(8,128)S(1)} %get-tuple-element.33.totals), channel_id=1, source_target_pairs={{0,2},{1,3},{4,6},{5,7},{8,10},{9,11},{12,14},{13,15},{16,18},{17,... | collective-permute-start | bytes 12296 | tf_op jit(solution)/shard_map/ppermute | solution.py:272

commit v11 on v10

--- a/solution.py
+++ b/solution.py
@@ -11,7 +11,7 @@
 f32 = jnp.float32
 bf16 = jnp.bfloat16
 lanes = 128
-block_rows = 256
+block_rows = 512
 params = pltpu.CompilerParams(vmem_limit_bytes=24 * 1024 * 1024)
 vmem = pl.BlockSpec(memory_space=pltpu.VMEM)
 hbm = pl.BlockSpec(memory_space=pltpu.HBM)
@@ -63,6 +63,16 @@
 
 def days_of(device, shape):
     return device * shape[1] + lax.broadcasted_iota(jnp.int32, shape, 1)
+
+
+def first_half_only(kernel):
+    @functools.wraps(kernel)
+    def guarded(half, *refs):
+        @pl.when(lax.axis_index("day") < half)
+        def _():
+            kernel(half, *refs)
+
+    return guarded
 
 
 def fetch(sources, targets, sems):
@@ -151,7 +161,8 @@
         wait_all(fetch([cross_block], [cross], out_sems))
 
 
-def second_kernel(unit_devices, panel, cohort, unit_logit, sums, raised_days, ends, high_ref, low_ref, *refs):
+@first_half_only
+def second_kernel(half, unit_devices, panel, cohort, unit_logit, sums, raised_days, ends, high_ref, low_ref, *refs):
     pack, norms, raised_units, more_high, more_low, held, held_cohort, held_logit, sems = refs
     groups, day_cols = raised_days.shape
     unit_rows, resident = panel.shape[0], high_ref.shape[0]
@@ -186,13 +197,15 @@
         multiply(here, high, low)
 
 
-def join_kernel(pack, post, out):
+@first_half_only
+def join_kernel(half, pack, post, out):
     rows, width = pack.shape
     out[:rows, :] = pack[...]
     out[rows:, : post.shape[1]] = post[...]
     out[rows:, post.shape[1] :] = jnp.zeros((post.shape[0], width - post.shape[1]), f32)
 
 
+@first_half_only
 def third_kernel(half, *refs):
     parts, refs = [refs[0].at[day] for day in range(half)], refs[1:]
     high_ref, low_ref, more_high, more_low, norms, raised_units, ends, scaled, lam, out, block, out_sems = refs
@@ -208,8 +221,8 @@
         lam[:, day * day_cols : (day + 1) * day_cols] = raised_days[day] * over_time
     time_grad = jnp.zeros((groups, day_cols), f32)
     new_sum = jnp.zeros((groups, 1), f32)
-    for start in range(0, unit_rows, 2 * block_rows):
-        here = pl.ds(start, 2 * block_rows)
+    for start in range(0, unit_rows, block_rows):
+        here = pl.ds(start, block_rows)
         whole = tree_sum(ref[:, here] for ref in parts)
         raised = raised_units[:, here]
         new = raised * over_unit * jnp.exp(whole[:groups] * factor)
@@ -220,7 +233,7 @@
         if start < resident:
             high, low = high_ref[here, :], low_ref[here, :]
         else:
-            there = pl.ds(start - resident, 2 * block_rows)
+            there = pl.ds(start - resident, block_rows)
             high, low = more_high[there, :], more_low[there, :]
         time_grad += add_terms(rows_dot(left, high, low), groups)
     lane = lax.broadcasted_iota(jnp.int32, (groups, day_cols), 1)
@@ -229,7 +242,8 @@
     repeat_out(block, out, out_sems)
 
 
-def fourth_kernel(unit_devices, half, grads, lam, norms, ends, own_days, totals):
+@first_half_only
+def fourth_kernel(half, unit_devices, grads, lam, norms, ends, own_days, totals):
     groups, day_cols = own_days.shape
     root = jnp.sqrt(jnp.maximum(norms[:, 2:3], 1.0))
     me = lax.axis_index("day")
@@ -266,7 +280,7 @@
     assert half * 2 == day_devices and half & (half - 1) == 0
     assert unit_devices & (unit_devices - 1) == 0
     panel_starts = [0, unit_rows // 4, unit_rows // 8 * 5, unit_rows]
-    resident = unit_rows * 3 // 4 // (2 * block_rows) * (2 * block_rows)
+    resident = unit_rows * 3 // 4 // block_rows * block_rows
     def to_other_half(value):
         pairs = [(u * day_devices + d, u * day_devices + d + half) for u in range(unit_devices) for d in range(half)]
         return lax.ppermute(value, ("unit", "day"), pairs)
@@ -338,7 +352,7 @@
     ]
     post = lax.ppermute(cross, ("unit", "day"), downward)
     pack, norms, raised_units, more_high, more_low = call(
-        functools.partial(second_kernel, unit_devices),
+        functools.partial(second_kernel, half, unit_devices),
         [
             ((2 * groups, unit_rows + day_cols), f32),
             ((groups, lanes), f32),
@@ -351,7 +365,7 @@
         scratch_shapes=[pltpu.VMEM((unit_rows - resident, day_cols), f32), held[1], held[4], panel_sems],
     )
     (pack,) = call(
-        join_kernel, [((3 * groups, unit_rows + day_cols), f32)], "join_post", (pack, post)
+        functools.partial(join_kernel, half), [((3 * groups, unit_rows + day_cols), f32)], "join_post", (pack, post)
     )
     members = unit_devices * half
     scaled, lam, grads = call(
@@ -368,7 +382,7 @@
     )
     sent_scaled = to_other_half(scaled)
     own_days, totals = call(
-        functools.partial(fourth_kernel, unit_devices, half),
+        functools.partial(fourth_kernel, half, unit_devices),
         [((groups, day_cols), f32), ((groups, lanes), f32)],
         "new_time_weights",
         (over_first_half(grads), lam, norms, ends),

time: 41 us -> 38.8 us (0.946)
  starting transfers between devices: 23.9 us -> 19.5 us
  waiting for transfers between devices: 4.53 us -> 6.77 us
    ppermute x2, starting transfers between devices: 7.06 us -> 2.58 us  [to_other_half(): return lax.ppermute(value, ('unit', 'day'), pairs)]
    all_to_all x1, waiting for transfers between devices: 0.6 us -> 2.84 us  [over_first_half(): lax.all_to_all(value, ('unit', 'day'), split_axis=0, concat_axis=0, axis_...]
where the time goes in v11:
time: 38.8 us; the launch traced here: 38.3 us
  starting transfers between devices  19.5 us (50%)
  Pallas kernels  9 us (23%)
  waiting for transfers between devices  6.77 us (17%)
  blocking collectives  2.4 us (6%)
  between operations  0.7 us (2%)
    all_to_all x1, starting transfers between devices, over_units(): lax.all_to_all(value, 'unit', split_axis=0, concat_axis=0, axis_index_gro...  9.31 us
    pallas_call x7, Pallas kernels, call(): pl.pallas_call(kernel, in_specs=in_specs or [vmem] * len(args), out_specs...  9 us
    all_to_all x1, starting transfers between devices, over_first_half(): lax.all_to_all(value, ('unit', 'day'), split_axis=0, concat_axis=0, axis_...  6.28 us
    all_to_all x1, waiting for transfers between devices, over_units(): lax.all_to_all(value, 'unit', split_axis=0, concat_axis=0, axis_index_gro...  3.36 us
    all_to_all x1, waiting for transfers between devices, over_first_half(): lax.all_to_all(value, ('unit', 'day'), split_axis=0, concat_axis=0, axis_...  2.84 us
    ppermute x2, starting transfers between devices, to_other_half(): return lax.ppermute(value, ('unit', 'day'), pairs)  2.58 us
    all_gather x1, blocking collectives, over_days(): return lax.all_gather(value, 'day', axis_index_groups=halves)  2.4 us
    ppermute x1, starting transfers between devices, local(): post = lax.ppermute(cross, ('unit', 'day'), downward)  1.28 us
  transfers between devices with their start and end apart: 5, of which 3 were waited for; matrix products, arithmetic and copies ran while one was open for 0% of the time, Pallas kernels for 9%

profile of v11, /device:TPU:0, one launch (start us, length us, event | category | flops | bytes accessed | tf_op | source)
XLA Modules:
  0.0 38.3 jit_solution(12992095214633342848)
XLA Ops:
  0.6 3.8 %first_product.1 = (f32[64,640]{1,0:T(8,128)}, f32[8,4096]{1,0:T(8,128)}, f32[8,256]{1,0:T(8,128)S(1)}, f32[8,128]{1,0:T(8,128)S(1)}, bf16[3072,256]{1,0:T(8,128)(2,1)S(1)}, /*index=5*/bf16[3072,256]{1,0:T(8,128)(2,1)S(1)}) custom-call(f32[4096,256]{1,0:T(8,128)} %panel.1, s32[1,4096]{1,0:T(1,128)} %bitcast.13, s32[1,8]{1,0:T(1,128)} %bitcast.15, ...), custom_call_target="tpu_custom_call" | custom-call | tf_op jit(solution)/shard_map/first_product/pallas_call | solution.py:306
  4.5 9.3 %all-to-all-start = ((f32[8,8,640]{2,1,0:T(8,128)}), f32[8,8,640]{2,1,0:T(8,128)S(1)}, u32[]{:S(2)}, u32[]{:S(2)}) async-start(f32[8,8,640]{2,1,0:T(8,128)} %bitcast.11), calls=%async_computation | async-start | bytes 327680 | tf_op jit(solution)/shard_map/all_to_all | solution.py:303
  13.8 1.3 %collective-permute-start = (f32[8,4096]{1,0:T(8,128)}, f32[8,4096]{1,0:T(8,128)S(1)}, u32[]{:S(2)}, u32[]{:S(2)}) collective-permute-start(f32[8,4096]{1,0:T(8,128)} %get-tuple-element.26), channel_id=1, source_target_pairs={{2,0},{3,1},{6,4},{7,5},{10,8},{11,9},{14,12},{15,13},{18,16},{19,... | collective-permute-start | bytes 393224 | tf_op jit(solution)/shard_map/ppermute | solution.py:353
  15.1 3.4 %all-to-all-done = f32[8,8,640]{2,1,0:T(8,128)S(1)} async-done(((f32[8,8,640]{2,1,0:T(8,128)}), f32[8,8,640]{2,1,0:T(8,128)S(1)}, u32[]{:S(2)}, u32[]{:S(2)}) %all-to-all-start) | async-done | bytes 163872 | tf_op jit(solution)/shard_map/all_to_all | solution.py:303
  18.4 2.6 %unit_gradient.1 = (f32[16,4352]{1,0:T(8,128)S(1)}, f32[8,128]{1,0:T(8,128)S(1)}, f32[8,4096]{1,0:T(8,128)S(1)}, bf16[1024,256]{1,0:T(8,128)(2,1)S(1)}, bf16[1024,256]{1,0:T(8,128)(2,1)S(1)}) custom-call(f32[4096,256]{1,0:T(8,128)} %panel.1, s32[1,4096]{1,0:T(1,128)} %bitcast.14, f32[8,4096]{1,0:T(8,128)} %unit_logit.1, f32[64,640]{1,0:T(8,128)S(1)} %bitcast.9, ...), custom_call_target="tpu_custom_call" | custom-call | tf_op jit(solution)/shard_map/unit_gradient/pallas_call | solution.py:306
  21.0 0.0 collective-permute-done.post
  21.1 2.4 %all-gather = f32[48,4352]{1,0:T(8,128)S(1)} all-gather(f32[24,4352]{1,0:T(8,128)S(1)} %join_post.1), channel_id=2, replica_groups={{0,1},{2,3},{4,5},{6,7},{8,9},{10,11},{12,13},{14,15},{16,17},{18,19},{..., dimensions={0}, use_global_device_ids=true | all-gather | bytes 1253376 | tf_op jit(solution)/shard_map/all_gather | solution.py:290
  23.5 1.5 %time_gradient.1 = (f32[8,4096]{1,0:T(8,128)S(1)}, f32[8,512]{1,0:T(8,128)S(1)}, f32[128,256]{1,0:T(8,128)}) custom-call(f32[2,24,4352]{2,1,0:T(8,128)S(1)} %bitcast.8, bf16[3072,256]{1,0:T(8,128)(2,1)S(1)} %get-tuple-element.23.high_ref.refs_1_, bf16[3072,256]{1,0:T(8,128)(2,1)S(1)} %get-tuple-element.24.low_ref.refs_2_, ...), custom_call_target="tpu_custom_call" | custom-call | tf_op jit(solution)/shard_map/time_gradient/pallas_call | solution.py:306
  25.1 6.3 %all-to-all-start.1 = ((f32[16,8,256]{2,1,0:T(8,128)}), f32[16,8,256]{2,1,0:T(8,128)S(1)}, u32[]{:S(2)}, u32[]{:S(2)}) async-start(f32[16,8,256]{2,1,0:T(8,128)} %bitcast.12), calls=%async_computation.1 | async-start | bytes 262144 | tf_op jit(solution)/shard_map/all_to_all | solution.py:297
  31.3 1.3 %collective-permute-start.2 = (f32[8,4096]{1,0:T(8,128)S(1)}, f32[8,4096]{1,0:T(8,128)S(1)}, u32[]{:S(2)}, u32[]{:S(2)}) collective-permute-start(f32[8,4096]{1,0:T(8,128)S(1)} %get-tuple-element.34.scaled), channel_id=1, source_target_pairs={{0,2},{1,3},{4,6},{5,7},{8,10},{9,11},{12,14},{13,15},{16,18},{17,... | collective-permute-start | bytes 393224 | tf_op jit(solution)/shard_map/ppermute | solution.py:286
  32.6 2.8 %all-to-all-done.1 = f32[16,8,256]{2,1,0:T(8,128)S(1)} async-done(((f32[16,8,256]{2,1,0:T(8,128)}), f32[16,8,256]{2,1,0:T(8,128)S(1)}, u32[]{:S(2)}, u32[]{:S(2)}) %all-to-all-start.1) | async-done | bytes 131104 | tf_op jit(solution)/shard_map/all_to_all | solution.py:297
  35.5 0.2 new_time_weights.1
  35.7 1.3 %collective-permute-start.1 = (f32[8,128]{1,0:T(8,128)S(1)}, f32[8,128]{1,0:T(8,128)S(1)}, u32[]{:S(2)}, u32[]{:S(2)}) collective-permute-start(f32[8,128]{1,0:T(8,128)S(1)} %get-tuple-element.33.totals), channel_id=1, source_target_pairs={{0,2},{1,3},{4,6},{5,7},{8,10},{9,11},{12,14},{13,15},{16,18},{17,... | collective-permute-start | bytes 12296 | tf_op jit(solution)/shard_map/ppermute | solution.py:286
  37.0 0.7 %scale_weights.1 = (f32[8,4096]{1,0:T(8,128)}, f32[8,256]{1,0:T(8,128)}) custom-call(f32[8,128]{1,0:T(8,128)S(1)} %get-tuple-element.33.totals, f32[8,4096]{1,0:T(8,128)S(1)} %get-tuple-element.34.scaled, f32[8,256]{1,0:T(8,128)S(1)} %get-tuple-element.35.own_days), custom_call_target="tpu_custom_call" | custom-call | tf_op jit(solution)/shard_map/scale_weights/pallas_call | solution.py:306
  37.8 0.0 collective-permute-done.2.sent_scaled
  37.8 0.6 %collective-permute-done.1.sent_totals = f32[8,128]{1,0:T(8,128)S(1)} collective-permute-done((f32[8,128]{1,0:T(8,128)S(1)}, f32[8,128]{1,0:T(8,128)S(1)}, u32[]{:S(2)}, u32[]{:S(2)}) %collective-permute-start.1) | collective-permute-done | bytes 4128 | tf_op jit(solution)/shard_map/ppermute | solution.py:286
  (2 shorter events, 0.0 us)
Async XLA Ops:
  4.5 14.0 %all-to-all-start = ((f32[8,8,640]{2,1,0:T(8,128)}), f32[8,8,640]{2,1,0:T(8,128)S(1)}, u32[]{:S(2)}, u32[]{:S(2)}) async-start(f32[8,8,640]{2,1,0:T(8,128)} %bitcast.11), calls=%async_computation | async-start | bytes 327680 | tf_op jit(solution)/shard_map/all_to_all | solution.py:303
  13.8 7.3 %collective-permute-start = (f32[8,4096]{1,0:T(8,128)}, f32[8,4096]{1,0:T(8,128)S(1)}, u32[]{:S(2)}, u32[]{:S(2)}) collective-permute-start(f32[8,4096]{1,0:T(8,128)} %get-tuple-element.26), channel_id=1, source_target_pairs={{2,0},{3,1},{6,4},{7,5},{10,8},{11,9},{14,12},{15,13},{18,16},{19,... | collective-permute-start | bytes 393224 | tf_op jit(solution)/shard_map/ppermute | solution.py:353
  25.1 10.4 %all-to-all-start.1 = ((f32[16,8,256]{2,1,0:T(8,128)}), f32[16,8,256]{2,1,0:T(8,128)S(1)}, u32[]{:S(2)}, u32[]{:S(2)}) async-start(f32[16,8,256]{2,1,0:T(8,128)} %bitcast.12), calls=%async_computation.1 | async-start | bytes 262144 | tf_op jit(solution)/shard_map/all_to_all | solution.py:297
  31.3 6.4 %collective-permute-start.2 = (f32[8,4096]{1,0:T(8,128)S(1)}, f32[8,4096]{1,0:T(8,128)S(1)}, u32[]{:S(2)}, u32[]{:S(2)}) collective-permute-start(f32[8,4096]{1,0:T(8,128)S(1)} %get-tuple-element.34.scaled), channel_id=1, source_target_pairs={{0,2},{1,3},{4,6},{5,7},{8,10},{9,11},{12,14},{13,15},{16,18},{17,... | collective-permute-start | bytes 393224 | tf_op jit(solution)/shard_map/ppermute | solution.py:286
  35.7 2.6 %collective-permute-start.1 = (f32[8,128]{1,0:T(8,128)S(1)}, f32[8,128]{1,0:T(8,128)S(1)}, u32[]{:S(2)}, u32[]{:S(2)}) collective-permute-start(f32[8,128]{1,0:T(8,128)S(1)} %get-tuple-element.33.totals), channel_id=1, source_target_pairs={{0,2},{1,3},{4,6},{5,7},{8,10},{9,11},{12,14},{13,15},{16,18},{17,... | collective-permute-start | bytes 12296 | tf_op jit(solution)/shard_map/ppermute | solution.py:286

commit v12 on v11

--- a/solution.py
+++ b/solution.py
@@ -281,6 +281,9 @@
     assert unit_devices & (unit_devices - 1) == 0
     panel_starts = [0, unit_rows // 4, unit_rows // 8 * 5, unit_rows]
     resident = unit_rows * 3 // 4 // block_rows * block_rows
+    middle = unit_devices // 2 - 1
+    unit_order = [middle] + [unit for unit in reversed(range(unit_devices)) if unit != middle]
+
     def to_other_half(value):
         pairs = [(u * day_devices + d, u * day_devices + d + half) for u in range(unit_devices) for d in range(half)]
         return lax.ppermute(value, ("unit", "day"), pairs)
@@ -291,7 +294,7 @@
 
     def over_first_half(value):
         members = [
-            [unit * day_devices + day for unit in reversed(range(unit_devices)) for day in reversed(days)]
+            [unit * day_devices + day for unit in unit_order for day in reversed(days)]
             for days in (range(half), range(half, day_devices))
         ]
         return lax.all_to_all(
@@ -299,8 +302,7 @@
         )
 
     def over_units(value):
-        members = list(reversed(range(unit_devices)))
-        return lax.all_to_all(value, "unit", split_axis=0, concat_axis=0, axis_index_groups=[members], tiled=True)
+        return lax.all_to_all(value, "unit", split_axis=0, concat_axis=0, axis_index_groups=[unit_order], tiled=True)
 
     def call(kernel, shapes, name, args, in_specs=None, out_specs=None, **more):
         return pl.pallas_call(

time: 38.8 us -> 36.9 us (0.951)
  starting transfers between devices: 19.5 us -> 16 us
  waiting for transfers between devices: 6.77 us -> 8.37 us
    all_to_all x1, starting transfers between devices: 6.28 us -> 4.27 us  [over_first_half(): lax.all_to_all(value, ('unit', 'day'), split_axis=0, concat_axis=0, axis_...]
    all_to_all x1, starting transfers between devices: 9.31 us -> 7.83 us  [over_units(): lax.all_to_all(value, 'unit', split_axis=0, concat_axis=0, axis_index_gro...]
    all_to_all x1, waiting for transfers between devices: 3.36 us -> 4.25 us  [over_units(): lax.all_to_all(value, 'unit', split_axis=0, concat_axis=0, axis_index_gro...]
    all_to_all x1, waiting for transfers between devices: 2.84 us -> 3.55 us  [over_first_half(): lax.all_to_all(value, ('unit', 'day'), split_axis=0, concat_axis=0, axis_...]
  transfers between devices with their start and end apart: 5 -> 5, of which waited for: 3 -> 3; matrix products, arithmetic and copies ran while one was open for 0% -> 0% of each run, Pallas kernels for 9% -> 10%
where the time goes in v12:
time: 36.9 us; the launch traced here: 36.4 us
  starting transfers between devices  16 us (43%)
  Pallas kernels  9.01 us (24%)
  waiting for transfers between devices  8.37 us (23%)
  blocking collectives  2.4 us (7%)
  between operations  0.7 us (2%)
    pallas_call x7, Pallas kernels, call(): pl.pallas_call(kernel, in_specs=in_specs or [vmem] * len(args), out_specs...  9.01 us
    all_to_all x1, starting transfers between devices, over_units(): lax.all_to_all(value, 'unit', split_axis=0, concat_axis=0, axis_index_gro...  7.83 us
    all_to_all x1, starting transfers between devices, over_first_half(): lax.all_to_all(value, ('unit', 'day'), split_axis=0, concat_axis=0, axis_...  4.27 us
    all_to_all x1, waiting for transfers between devices, over_units(): lax.all_to_all(value, 'unit', split_axis=0, concat_axis=0, axis_index_gro...  4.25 us
    all_to_all x1, waiting for transfers between devices, over_first_half(): lax.all_to_all(value, ('unit', 'day'), split_axis=0, concat_axis=0, axis_...  3.55 us
    ppermute x2, starting transfers between devices, to_other_half(): return lax.ppermute(value, ('unit', 'day'), pairs)  2.58 us
    all_gather x1, blocking collectives, over_days(): return lax.all_gather(value, 'day', axis_index_groups=halves)  2.4 us
    ppermute x1, starting transfers between devices, local(): post = lax.ppermute(cross, ('unit', 'day'), downward)  1.28 us
  transfers between devices with their start and end apart: 5, of which 3 were waited for; matrix products, arithmetic and copies ran while one was open for 0% of the time, Pallas kernels for 10%

profile of v12, /device:TPU:0, one launch (start us, length us, event | category | flops | bytes accessed | tf_op | source)
XLA Modules:
  0.0 36.4 jit_solution(1834628646767905693)
XLA Ops:
  0.6 3.8 %first_product.1 = (f32[64,640]{1,0:T(8,128)}, f32[8,4096]{1,0:T(8,128)}, f32[8,256]{1,0:T(8,128)S(1)}, f32[8,128]{1,0:T(8,128)S(1)}, bf16[3072,256]{1,0:T(8,128)(2,1)S(1)}, /*index=5*/bf16[3072,256]{1,0:T(8,128)(2,1)S(1)}) custom-call(f32[4096,256]{1,0:T(8,128)} %panel.1, s32[1,4096]{1,0:T(1,128)} %bitcast.13, s32[1,8]{1,0:T(1,128)} %bitcast.15, ...), custom_call_target="tpu_custom_call" | custom-call | tf_op jit(solution)/shard_map/first_product/pallas_call | solution.py:308
  4.5 7.8 %all-to-all-start = ((f32[8,8,640]{2,1,0:T(8,128)}), f32[8,8,640]{2,1,0:T(8,128)S(1)}, u32[]{:S(2)}, u32[]{:S(2)}) async-start(f32[8,8,640]{2,1,0:T(8,128)} %bitcast.11), calls=%async_computation | async-start | bytes 327680 | tf_op jit(solution)/shard_map/all_to_all | solution.py:305
  12.3 1.3 %collective-permute-start = (f32[8,4096]{1,0:T(8,128)}, f32[8,4096]{1,0:T(8,128)S(1)}, u32[]{:S(2)}, u32[]{:S(2)}) collective-permute-start(f32[8,4096]{1,0:T(8,128)} %get-tuple-element.26), channel_id=1, source_target_pairs={{2,0},{3,1},{6,4},{7,5},{10,8},{11,9},{14,12},{15,13},{18,16},{19,... | collective-permute-start | bytes 393224 | tf_op jit(solution)/shard_map/ppermute | solution.py:355
  13.6 4.3 %all-to-all-done = f32[8,8,640]{2,1,0:T(8,128)S(1)} async-done(((f32[8,8,640]{2,1,0:T(8,128)}), f32[8,8,640]{2,1,0:T(8,128)S(1)}, u32[]{:S(2)}, u32[]{:S(2)}) %all-to-all-start) | async-done | bytes 163872 | tf_op jit(solution)/shard_map/all_to_all | solution.py:305
  17.8 2.6 %unit_gradient.1 = (f32[16,4352]{1,0:T(8,128)S(1)}, f32[8,128]{1,0:T(8,128)S(1)}, f32[8,4096]{1,0:T(8,128)S(1)}, bf16[1024,256]{1,0:T(8,128)(2,1)S(1)}, bf16[1024,256]{1,0:T(8,128)(2,1)S(1)}) custom-call(f32[4096,256]{1,0:T(8,128)} %panel.1, s32[1,4096]{1,0:T(1,128)} %bitcast.14, f32[8,4096]{1,0:T(8,128)} %unit_logit.1, f32[64,640]{1,0:T(8,128)S(1)} %bitcast.9, ...), custom_call_target="tpu_custom_call" | custom-call | tf_op jit(solution)/shard_map/unit_gradient/pallas_call | solution.py:308
  20.5 0.0 collective-permute-done.post
  20.5 2.4 %all-gather = f32[48,4352]{1,0:T(8,128)S(1)} all-gather(f32[24,4352]{1,0:T(8,128)S(1)} %join_post.1), channel_id=2, replica_groups={{0,1},{2,3},{4,5},{6,7},{8,9},{10,11},{12,13},{14,15},{16,17},{18,19},{..., dimensions={0}, use_global_device_ids=true | all-gather | bytes 1253376 | tf_op jit(solution)/shard_map/all_gather | solution.py:293
  22.9 1.5 %time_gradient.1 = (f32[8,4096]{1,0:T(8,128)S(1)}, f32[8,512]{1,0:T(8,128)S(1)}, f32[128,256]{1,0:T(8,128)}) custom-call(f32[2,24,4352]{2,1,0:T(8,128)S(1)} %bitcast.8, bf16[3072,256]{1,0:T(8,128)(2,1)S(1)} %get-tuple-element.23.high_ref.refs_1_, bf16[3072,256]{1,0:T(8,128)(2,1)S(1)} %get-tuple-element.24.low_ref.refs_2_, ...), custom_call_target="tpu_custom_call" | custom-call | tf_op jit(solution)/shard_map/time_gradient/pallas_call | solution.py:308
  24.5 4.3 %all-to-all-start.1 = ((f32[16,8,256]{2,1,0:T(8,128)}), f32[16,8,256]{2,1,0:T(8,128)S(1)}, u32[]{:S(2)}, u32[]{:S(2)}) async-start(f32[16,8,256]{2,1,0:T(8,128)} %bitcast.12), calls=%async_computation.1 | async-start | bytes 262144 | tf_op jit(solution)/shard_map/all_to_all | solution.py:300
  28.7 1.3 %collective-permute-start.2 = (f32[8,4096]{1,0:T(8,128)S(1)}, f32[8,4096]{1,0:T(8,128)S(1)}, u32[]{:S(2)}, u32[]{:S(2)}) collective-permute-start(f32[8,4096]{1,0:T(8,128)S(1)} %get-tuple-element.34.scaled), channel_id=1, source_target_pairs={{0,2},{1,3},{4,6},{5,7},{8,10},{9,11},{12,14},{13,15},{16,18},{17,... | collective-permute-start | bytes 393224 | tf_op jit(solution)/shard_map/ppermute | solution.py:289
  30.0 3.5 %all-to-all-done.1 = f32[16,8,256]{2,1,0:T(8,128)S(1)} async-done(((f32[16,8,256]{2,1,0:T(8,128)}), f32[16,8,256]{2,1,0:T(8,128)S(1)}, u32[]{:S(2)}, u32[]{:S(2)}) %all-to-all-start.1) | async-done | bytes 131104 | tf_op jit(solution)/shard_map/all_to_all | solution.py:300
  33.6 0.2 new_time_weights.1
  33.8 1.3 %collective-permute-start.1 = (f32[8,128]{1,0:T(8,128)S(1)}, f32[8,128]{1,0:T(8,128)S(1)}, u32[]{:S(2)}, u32[]{:S(2)}) collective-permute-start(f32[8,128]{1,0:T(8,128)S(1)} %get-tuple-element.33.totals), channel_id=1, source_target_pairs={{0,2},{1,3},{4,6},{5,7},{8,10},{9,11},{12,14},{13,15},{16,18},{17,... | collective-permute-start | bytes 12296 | tf_op jit(solution)/shard_map/ppermute | solution.py:289
  35.1 0.7 %scale_weights.1 = (f32[8,4096]{1,0:T(8,128)}, f32[8,256]{1,0:T(8,128)}) custom-call(f32[8,128]{1,0:T(8,128)S(1)} %get-tuple-element.33.totals, f32[8,4096]{1,0:T(8,128)S(1)} %get-tuple-element.34.scaled, f32[8,256]{1,0:T(8,128)S(1)} %get-tuple-element.35.own_days), custom_call_target="tpu_custom_call" | custom-call | tf_op jit(solution)/shard_map/scale_weights/pallas_call | solution.py:308
  35.9 0.0 collective-permute-done.2.sent_scaled
  35.9 0.6 %collective-permute-done.1.sent_totals = f32[8,128]{1,0:T(8,128)S(1)} collective-permute-done((f32[8,128]{1,0:T(8,128)S(1)}, f32[8,128]{1,0:T(8,128)S(1)}, u32[]{:S(2)}, u32[]{:S(2)}) %collective-permute-start.1) | collective-permute-done | bytes 4128 | tf_op jit(solution)/shard_map/ppermute | solution.py:289
  (2 shorter events, 0.0 us)
Async XLA Ops:
  4.5 13.4 %all-to-all-start = ((f32[8,8,640]{2,1,0:T(8,128)}), f32[8,8,640]{2,1,0:T(8,128)S(1)}, u32[]{:S(2)}, u32[]{:S(2)}) async-start(f32[8,8,640]{2,1,0:T(8,128)} %bitcast.11), calls=%async_computation | async-start | bytes 327680 | tf_op jit(solution)/shard_map/all_to_all | solution.py:305
  12.3 8.2 %collective-permute-start = (f32[8,4096]{1,0:T(8,128)}, f32[8,4096]{1,0:T(8,128)S(1)}, u32[]{:S(2)}, u32[]{:S(2)}) collective-permute-start(f32[8,4096]{1,0:T(8,128)} %get-tuple-element.26), channel_id=1, source_target_pairs={{2,0},{3,1},{6,4},{7,5},{10,8},{11,9},{14,12},{15,13},{18,16},{19,... | collective-permute-start | bytes 393224 | tf_op jit(solution)/shard_map/ppermute | solution.py:355
  24.5 9.1 %all-to-all-start.1 = ((f32[16,8,256]{2,1,0:T(8,128)}), f32[16,8,256]{2,1,0:T(8,128)S(1)}, u32[]{:S(2)}, u32[]{:S(2)}) async-start(f32[16,8,256]{2,1,0:T(8,128)} %bitcast.12), calls=%async_computation.1 | async-start | bytes 262144 | tf_op jit(solution)/shard_map/all_to_all | solution.py:300
  28.7 7.1 %collective-permute-start.2 = (f32[8,4096]{1,0:T(8,128)S(1)}, f32[8,4096]{1,0:T(8,128)S(1)}, u32[]{:S(2)}, u32[]{:S(2)}) collective-permute-start(f32[8,4096]{1,0:T(8,128)S(1)} %get-tuple-element.34.scaled), channel_id=1, source_target_pairs={{0,2},{1,3},{4,6},{5,7},{8,10},{9,11},{12,14},{13,15},{16,18},{17,... | collective-permute-start | bytes 393224 | tf_op jit(solution)/shard_map/ppermute | solution.py:289
  33.8 2.6 %collective-permute-start.1 = (f32[8,128]{1,0:T(8,128)S(1)}, f32[8,128]{1,0:T(8,128)S(1)}, u32[]{:S(2)}, u32[]{:S(2)}) collective-permute-start(f32[8,128]{1,0:T(8,128)S(1)} %get-tuple-element.33.totals), channel_id=1, source_target_pairs={{0,2},{1,3},{4,6},{5,7},{8,10},{9,11},{12,14},{13,15},{16,18},{17,... | collective-permute-start | bytes 12296 | tf_op jit(solution)/shard_map/ppermute | solution.py:289

commit v13 on v12

--- a/solution.py
+++ b/solution.py
@@ -98,10 +98,10 @@
         copy.wait()
 
 
-def repeat_out(block, out, sems):
+def repeat_start(block, out, sems):
     rows = block.shape[0]
     places = [out.at[pl.ds(i * rows, rows)] for i in range(out.shape[0] // rows)]
-    wait_all(fetch([block] * len(places), places, sems))
+    return fetch([block] * len(places), places, sems)
 
 
 def first_kernel(all_count, half, starts, *refs):
@@ -109,10 +109,13 @@
     out, cross, raised_days, ends, high_ref, low_ref, *held, block, left_ref, cross_block, small_sems, panel_sems, out_sems = refs
     groups, day_cols = held[5].shape
     unit_rows, resident = held[0].shape[0], high_ref.shape[0]
-    small = fetch(arguments[1:], held[1:], small_sems)
+    units = (1, 4)
+    days = (2, 3, 5)
+    unit_copies = fetch([arguments[i] for i in units], [held[i] for i in units], small_sems)
     parts = fetch_rows(arguments[0], held[0], panel_sems, starts)
+    day_copies = fetch([arguments[i] for i in days], [held[i] for i in days], small_sems.at[pl.ds(2, 3)])
     panel, cohort, pre_row, post_row, unit_logit, time_logit = held
-    wait_all(small)
+    wait_all(unit_copies)
     me = lax.axis_index("day")
 
     @pl.when(me < half)
@@ -122,10 +125,6 @@
         control = jnp.where(cohort[...] > label, 1.0, 0.0)
         raised = jnp.exp(unit_logit[...]) * control
         left_ref[...] = left_of(raised, treated)
-        pre_end = column(pre_row)
-        ends[...] = jnp.broadcast_to(pre_end.astype(f32), ends.shape)
-        before = days_of(me, (groups, day_cols)) < pre_end
-        raised_days[...] = jnp.where(before, jnp.exp(time_logit[...]), 0.0)
         lane = lax.broadcasted_iota(jnp.int32, (groups, lanes), 1)
         block[:, 2 * day_cols :] = jnp.where(
             lane == 0,
@@ -147,10 +146,17 @@
         product = product[:, :day_cols] + product[:, day_cols:]
         block[:, :day_cols] = add_terms(product, groups)
         block[:, day_cols : 2 * day_cols] = product[2 * groups :][:groups]
-        repeat_out(block, out, out_sems)
+        sends = repeat_start(block, out, out_sems)
+        wait_all(day_copies)
+        pre_end = column(pre_row)
+        ends[...] = jnp.broadcast_to(pre_end.astype(f32), ends.shape)
+        before = days_of(me, (groups, day_cols)) < pre_end
+        raised_days[...] = jnp.where(before, jnp.exp(time_logit[...]), 0.0)
+        wait_all(sends)
 
     @pl.when(me >= half)
     def _():
+        wait_all(day_copies)
         post_start = column(post_row)
         after = jnp.where(days_of(me, (groups, day_cols)) >= post_start, 1.0, 0.0)
         left = left_of(after / (all_count - post_start).astype(f32))
@@ -239,35 +245,47 @@
     lane = lax.broadcasted_iota(jnp.int32, (groups, day_cols), 1)
     spare = (lane == day_cols - 1) & (me == half - 1)
     block[...] = jnp.where(spare, new_sum, time_grad)
-    repeat_out(block, out, out_sems)
+    wait_all(repeat_start(block, out, out_sems))
+
+
+def time_grad_of(grads, unit_devices, half, day, groups):
+    places = [(unit * half + half - 1 - day) * groups for unit in range(unit_devices)]
+    return tree_sum(grads[pl.ds(place, groups), :] for place in places)
 
 
 @first_half_only
-def fourth_kernel(half, unit_devices, grads, lam, norms, ends, own_days, totals):
-    groups, day_cols = own_days.shape
-    root = jnp.sqrt(jnp.maximum(norms[:, 2:3], 1.0))
+def fourth_kernel(half, unit_devices, grads, totals):
+    groups, day_cols = totals.shape[0], grads.shape[1]
+    last = time_grad_of(grads, unit_devices, half, half - 1, groups)
+    totals[...] = jnp.broadcast_to(last[:, day_cols - 1 :], totals.shape)
+
+
+def fifth_kernel(half, unit_devices, totals, scaled, grads, lam, norms, ends, unit_weights, time_weights):
+    groups, day_cols = time_weights.shape
     me = lax.axis_index("day")
-    moved_total = jnp.zeros((groups, 1), f32)
-    own = jnp.zeros((groups, day_cols), f32)
-    for day in range(half):
-        places = [(unit * half + half - 1 - day) * groups for unit in range(unit_devices)]
-        total = tree_sum(grads[pl.ds(place, groups), :] for place in places)
-        moved = lam[:, day * day_cols : (day + 1) * day_cols] * jnp.exp(total * (-step_rate / root))
-        moved_total += jnp.sum(moved, axis=1, keepdims=True)
-        own = jnp.where(me == day, moved, own)
-    totals[...] = jnp.broadcast_to(total[:, day_cols - 1 :], totals.shape)
-    own_days[...] = own * (ends[:, 0:1] / moved_total)
-
-
-def fifth_kernel(half, totals, scaled, own_days, unit_weights, time_weights):
-    unit_weights[...] = scaled[...] / totals[:, 0:1]
-    time_weights[...] = jnp.where(lax.axis_index("day") < half, own_days[...], 0.0)
+
+    @pl.when(me < half)
+    def _():
+        unit_weights[...] = scaled[...] * (1.0 / totals[:, 0:1])
+        root = jnp.sqrt(jnp.maximum(norms[:, 2:3], 1.0))
+        moved_total = jnp.zeros((groups, 1), f32)
+        own = jnp.zeros((groups, day_cols), f32)
+        for day in range(half):
+            total = time_grad_of(grads, unit_devices, half, day, groups)
+            moved = lam[:, day * day_cols : (day + 1) * day_cols] * jnp.exp(total * (-step_rate / root))
+            moved_total += jnp.sum(moved, axis=1, keepdims=True)
+            own = jnp.where(me == day, moved, own)
+        time_weights[...] = own * (ends[:, 0:1] / moved_total)
+
+    @pl.when(me >= half)
+    def _():
+        time_weights[...] = jnp.zeros_like(time_weights)
 
 
 def sixth_kernel(half, sent_totals, sent_scaled, _, unit_weights, block, out_sem):
     @pl.when(lax.axis_index("day") >= half)
     def _():
-        block[...] = sent_scaled[...] / sent_totals[:, 0:1]
+        block[...] = sent_scaled[...] * (1.0 / sent_totals[:, 0:1])
         wait_all(fetch([block], [unit_weights], out_sem))
 
 
@@ -279,7 +297,7 @@
     half = day_devices // 2
     assert half * 2 == day_devices and half & (half - 1) == 0
     assert unit_devices & (unit_devices - 1) == 0
-    panel_starts = [0, unit_rows // 4, unit_rows // 8 * 5, unit_rows]
+    panel_starts = [0, unit_rows // 2, unit_rows]
     resident = unit_rows * 3 // 4 // block_rows * block_rows
     middle = unit_devices // 2 - 1
     unit_order = [middle] + [unit for unit in reversed(range(unit_devices)) if unit != middle]
@@ -383,17 +401,15 @@
         scratch_shapes=[pltpu.VMEM((groups, day_cols), f32), pltpu.SemaphoreType.DMA((members,))],
     )
     sent_scaled = to_other_half(scaled)
-    own_days, totals = call(
-        functools.partial(fourth_kernel, half, unit_devices),
-        [((groups, day_cols), f32), ((groups, lanes), f32)],
-        "new_time_weights",
-        (over_first_half(grads), lam, norms, ends),
+    all_grads = over_first_half(grads)
+    (totals,) = call(
+        functools.partial(fourth_kernel, half, unit_devices), [((groups, lanes), f32)], "unit_totals", (all_grads,)
     )
     unit_weights, time_weights = call(
-        functools.partial(fifth_kernel, half),
+        functools.partial(fifth_kernel, half, unit_devices),
         [((groups, unit_rows), f32), ((groups, day_cols), f32)],
         "scale_weights",
-        (totals, scaled, own_days),
+        (totals, scaled, all_grads, lam, norms, ends),
     )
     (unit_weights,) = call(
         functools.partial(sixth_kernel, half),

time: 36.9 us -> 36.8 us (level)
  no operation moved by 1% of the time
where the time goes in v13:
time: 36.8 us; the launch traced here: 36.3 us
  starting transfers between devices  15.9 us (43%)
  Pallas kernels  9.07 us (25%)
  waiting for transfers between devices  8.2 us (22%)
  blocking collectives  2.4 us (7%)
  between operations  0.7 us (2%)
    pallas_call x7, Pallas kernels, call(): pl.pallas_call(kernel, in_specs=in_specs or [vmem] * len(args), out_specs...  9.07 us
    all_to_all x1, starting transfers between devices, over_units(): lax.all_to_all(value, 'unit', split_axis=0, concat_axis=0, axis_index_gro...  7.83 us
    all_to_all x1, starting transfers between devices, over_first_half(): lax.all_to_all(value, ('unit', 'day'), split_axis=0, concat_axis=0, axis_...  4.28 us
    all_to_all x1, waiting for transfers between devices, over_units(): lax.all_to_all(value, 'unit', split_axis=0, concat_axis=0, axis_index_gro...  4.25 us
    all_to_all x1, waiting for transfers between devices, over_first_half(): lax.all_to_all(value, ('unit', 'day'), split_axis=0, concat_axis=0, axis_...  3.55 us
    ppermute x2, starting transfers between devices, to_other_half(): return lax.ppermute(value, ('unit', 'day'), pairs)  2.56 us
    all_gather x1, blocking collectives, over_days(): return lax.all_gather(value, 'day', axis_index_groups=halves)  2.4 us
    ppermute x1, starting transfers between devices, local(): post = lax.ppermute(cross, ('unit', 'day'), downward)  1.28 us
  transfers between devices with their start and end apart: 5, of which 3 were waited for; matrix products, arithmetic and copies ran while one was open for 0% of the time, Pallas kernels for 10%

profile of v13, /device:TPU:0, one launch (start us, length us, event | category | flops | bytes accessed | tf_op | source)
XLA Modules:
  0.0 36.3 jit_solution(14567249490274644168)
XLA Ops:
  0.6 3.9 %first_product.1 = (f32[64,640]{1,0:T(8,128)}, f32[8,4096]{1,0:T(8,128)}, f32[8,256]{1,0:T(8,128)S(1)}, f32[8,128]{1,0:T(8,128)S(1)}, bf16[3072,256]{1,0:T(8,128)(2,1)S(1)}, /*index=5*/bf16[3072,256]{1,0:T(8,128)(2,1)S(1)}) custom-call(f32[4096,256]{1,0:T(8,128)} %panel.1, s32[1,4096]{1,0:T(1,128)} %bitcast.14, s32[1,8]{1,0:T(1,128)} %bitcast.16, ...), custom_call_target="tpu_custom_call" | custom-call | tf_op jit(solution)/shard_map/first_product/pallas_call | solution.py:326
  4.5 7.8 %all-to-all-start = ((f32[8,8,640]{2,1,0:T(8,128)}), f32[8,8,640]{2,1,0:T(8,128)S(1)}, u32[]{:S(2)}, u32[]{:S(2)}) async-start(f32[8,8,640]{2,1,0:T(8,128)} %bitcast.12), calls=%async_computation | async-start | bytes 327680 | tf_op jit(solution)/shard_map/all_to_all | solution.py:323
  12.4 1.3 %collective-permute-start = (f32[8,4096]{1,0:T(8,128)}, f32[8,4096]{1,0:T(8,128)S(1)}, u32[]{:S(2)}, u32[]{:S(2)}) collective-permute-start(f32[8,4096]{1,0:T(8,128)} %get-tuple-element.24), channel_id=1, source_target_pairs={{2,0},{3,1},{6,4},{7,5},{10,8},{11,9},{14,12},{15,13},{18,16},{19,... | collective-permute-start | bytes 393224 | tf_op jit(solution)/shard_map/ppermute | solution.py:373
  13.6 4.3 %all-to-all-done = f32[8,8,640]{2,1,0:T(8,128)S(1)} async-done(((f32[8,8,640]{2,1,0:T(8,128)}), f32[8,8,640]{2,1,0:T(8,128)S(1)}, u32[]{:S(2)}, u32[]{:S(2)}) %all-to-all-start) | async-done | bytes 163872 | tf_op jit(solution)/shard_map/all_to_all | solution.py:323
  17.9 2.6 %unit_gradient.1 = (f32[16,4352]{1,0:T(8,128)S(1)}, f32[8,128]{1,0:T(8,128)S(1)}, f32[8,4096]{1,0:T(8,128)S(1)}, bf16[1024,256]{1,0:T(8,128)(2,1)S(1)}, bf16[1024,256]{1,0:T(8,128)(2,1)S(1)}) custom-call(f32[4096,256]{1,0:T(8,128)} %panel.1, s32[1,4096]{1,0:T(1,128)} %bitcast.15, f32[8,4096]{1,0:T(8,128)} %unit_logit.1, f32[64,640]{1,0:T(8,128)S(1)} %bitcast.11, ...), custom_call_target="tpu_custom_call" | custom-call | tf_op jit(solution)/shard_map/unit_gradient/pallas_call | solution.py:326
  20.5 0.0 collective-permute-done.post
  20.6 2.4 %all-gather = f32[48,4352]{1,0:T(8,128)S(1)} all-gather(f32[24,4352]{1,0:T(8,128)S(1)} %join_post.1), channel_id=2, replica_groups={{0,1},{2,3},{4,5},{6,7},{8,9},{10,11},{12,13},{14,15},{16,17},{18,19},{..., dimensions={0}, use_global_device_ids=true | all-gather | bytes 1253376 | tf_op jit(solution)/shard_map/all_gather | solution.py:311
  23.0 1.5 %time_gradient.1 = (f32[8,4096]{1,0:T(8,128)S(1)}, f32[8,512]{1,0:T(8,128)S(1)}, f32[128,256]{1,0:T(8,128)}) custom-call(f32[2,24,4352]{2,1,0:T(8,128)S(1)} %bitcast.8, bf16[3072,256]{1,0:T(8,128)(2,1)S(1)} %get-tuple-element.21.high_ref.refs_1_, bf16[3072,256]{1,0:T(8,128)(2,1)S(1)} %get-tuple-element.22.low_ref.refs_2_, ...), custom_call_target="tpu_custom_call" | custom-call | tf_op jit(solution)/shard_map/time_gradient/pallas_call | solution.py:326
  24.5 4.3 %all-to-all-start.1 = ((f32[16,8,256]{2,1,0:T(8,128)}), f32[16,8,256]{2,1,0:T(8,128)S(1)}, u32[]{:S(2)}, u32[]{:S(2)}) async-start(f32[16,8,256]{2,1,0:T(8,128)} %bitcast.13), calls=%async_computation.1 | async-start | bytes 262144 | tf_op jit(solution)/shard_map/all_to_all | solution.py:318
  28.8 1.3 %collective-permute-start.2 = (f32[8,4096]{1,0:T(8,128)S(1)}, f32[8,4096]{1,0:T(8,128)S(1)}, u32[]{:S(2)}, u32[]{:S(2)}) collective-permute-start(f32[8,4096]{1,0:T(8,128)S(1)} %get-tuple-element.30.scaled), channel_id=1, source_target_pairs={{0,2},{1,3},{4,6},{5,7},{8,10},{9,11},{12,14},{13,15},{16,18},{17,... | collective-permute-start | bytes 393224 | tf_op jit(solution)/shard_map/ppermute | solution.py:307
  30.1 3.5 %all-to-all-done.1 = f32[16,8,256]{2,1,0:T(8,128)S(1)} async-done(((f32[16,8,256]{2,1,0:T(8,128)}), f32[16,8,256]{2,1,0:T(8,128)S(1)}, u32[]{:S(2)}, u32[]{:S(2)}) %all-to-all-start.1) | async-done | bytes 131104 | tf_op jit(solution)/shard_map/all_to_all | solution.py:318
  33.6 0.1 unit_totals.1.totals
  33.7 1.3 %collective-permute-start.1 = (f32[8,128]{1,0:T(8,128)S(1)}, f32[8,128]{1,0:T(8,128)S(1)}, u32[]{:S(2)}, u32[]{:S(2)}) collective-permute-start(f32[8,128]{1,0:T(8,128)S(1)} %unit_totals.1.totals), channel_id=1, source_target_pairs={{0,2},{1,3},{4,6},{5,7},{8,10},{9,11},{12,14},{13,15},{16,18},{17,... | collective-permute-start | bytes 12296 | tf_op jit(solution)/shard_map/ppermute | solution.py:307
  35.0 0.9 %scale_weights.1 = (f32[8,4096]{1,0:T(8,128)}, f32[8,256]{1,0:T(8,128)}) custom-call(f32[8,128]{1,0:T(8,128)S(1)} %unit_totals.1.totals, f32[8,4096]{1,0:T(8,128)S(1)} %get-tuple-element.30.scaled, f32[128,256]{1,0:T(8,128)S(1)} %bitcast.10, f32[8,512]{1,0:T(8,128)S(1)} %get-tuple-element.31.lam, f32[8,128]{1,0:T(8,128)S(1)} %get-tuple-element.27.refs_5_.norms, ...), custom_call_target="tpu_custom_call" | custom-call | tf_op jit(solution)/shard_map/scale_weights/pallas_call | solution.py:326
  35.9 0.0 collective-permute-done.2.sent_scaled
  35.9 0.4 %collective-permute-done.1.sent_totals = f32[8,128]{1,0:T(8,128)S(1)} collective-permute-done((f32[8,128]{1,0:T(8,128)S(1)}, f32[8,128]{1,0:T(8,128)S(1)}, u32[]{:S(2)}, u32[]{:S(2)}) %collective-permute-start.1) | collective-permute-done | bytes 4128 | tf_op jit(solution)/shard_map/ppermute | solution.py:307
  (2 shorter events, 0.0 us)
Async XLA Ops:
  4.5 13.4 %all-to-all-start = ((f32[8,8,640]{2,1,0:T(8,128)}), f32[8,8,640]{2,1,0:T(8,128)S(1)}, u32[]{:S(2)}, u32[]{:S(2)}) async-start(f32[8,8,640]{2,1,0:T(8,128)} %bitcast.12), calls=%async_computation | async-start | bytes 327680 | tf_op jit(solution)/shard_map/all_to_all | solution.py:323
  12.4 8.2 %collective-permute-start = (f32[8,4096]{1,0:T(8,128)}, f32[8,4096]{1,0:T(8,128)S(1)}, u32[]{:S(2)}, u32[]{:S(2)}) collective-permute-start(f32[8,4096]{1,0:T(8,128)} %get-tuple-element.24), channel_id=1, source_target_pairs={{2,0},{3,1},{6,4},{7,5},{10,8},{11,9},{14,12},{15,13},{18,16},{19,... | collective-permute-start | bytes 393224 | tf_op jit(solution)/shard_map/ppermute | solution.py:373
  24.5 9.1 %all-to-all-start.1 = ((f32[16,8,256]{2,1,0:T(8,128)}), f32[16,8,256]{2,1,0:T(8,128)S(1)}, u32[]{:S(2)}, u32[]{:S(2)}) async-start(f32[16,8,256]{2,1,0:T(8,128)} %bitcast.13), calls=%async_computation.1 | async-start | bytes 262144 | tf_op jit(solution)/shard_map/all_to_all | solution.py:318
  28.8 7.1 %collective-permute-start.2 = (f32[8,4096]{1,0:T(8,128)S(1)}, f32[8,4096]{1,0:T(8,128)S(1)}, u32[]{:S(2)}, u32[]{:S(2)}) collective-permute-start(f32[8,4096]{1,0:T(8,128)S(1)} %get-tuple-element.30.scaled), channel_id=1, source_target_pairs={{0,2},{1,3},{4,6},{5,7},{8,10},{9,11},{12,14},{13,15},{16,18},{17,... | collective-permute-start | bytes 393224 | tf_op jit(solution)/shard_map/ppermute | solution.py:307
  33.7 2.6 %collective-permute-start.1 = (f32[8,128]{1,0:T(8,128)S(1)}, f32[8,128]{1,0:T(8,128)S(1)}, u32[]{:S(2)}, u32[]{:S(2)}) collective-permute-start(f32[8,128]{1,0:T(8,128)S(1)} %unit_totals.1.totals), channel_id=1, source_target_pairs={{0,2},{1,3},{4,6},{5,7},{8,10},{9,11},{12,14},{13,15},{16,18},{17,... | collective-permute-start | bytes 12296 | tf_op jit(solution)/shard_map/ppermute | solution.py:307

commit v14 on v13

--- a/solution.py
+++ b/solution.py
@@ -99,8 +99,7 @@
 
 
 def repeat_start(block, out, sems):
-    rows = block.shape[0]
-    places = [out.at[pl.ds(i * rows, rows)] for i in range(out.shape[0] // rows)]
+    places = [out.at[i] for i in range(out.shape[0])]
     return fetch([block] * len(places), places, sems)
 
 
@@ -126,13 +125,12 @@
         raised = jnp.exp(unit_logit[...]) * control
         left_ref[...] = left_of(raised, treated)
         lane = lax.broadcasted_iota(jnp.int32, (groups, lanes), 1)
-        block[:, 2 * day_cols :] = jnp.where(
-            lane == 0,
-            jnp.sum(raised, axis=1, keepdims=True),
-            jnp.where(
-                lane == 1, jnp.sum(treated, axis=1, keepdims=True), jnp.sum(control, axis=1, keepdims=True)
-            ),
-        )
+        counts = [jnp.sum(value, axis=1, keepdims=True) for value in (raised, treated, control)]
+        slot = lax.broadcasted_iota(jnp.int32, (groups, lanes), 0)
+        norms = jnp.zeros((groups, lanes), f32)
+        for i, count in enumerate(counts):
+            norms += jnp.where(lane == i * groups + slot, count, 0.0)
+        block[:, 2 * groups * day_cols :] = jnp.sum(norms, axis=0, keepdims=True)
         product = jnp.zeros((4 * groups, 2 * day_cols), f32)
         for start, rows, copy in parts:
             copy.wait()
@@ -144,8 +142,9 @@
                 both = jnp.concatenate([high, low], axis=1)
                 product += jnp.dot(left_ref[:, here], both, preferred_element_type=f32)
         product = product[:, :day_cols] + product[:, day_cols:]
-        block[:, :day_cols] = add_terms(product, groups)
-        block[:, day_cols : 2 * day_cols] = product[2 * groups :][:groups]
+        both_sums = jnp.concatenate([add_terms(product, groups), product[2 * groups :][:groups]], axis=0)
+        for row in range(2 * groups):
+            block[:, row * day_cols : (row + 1) * day_cols] = both_sums[row : row + 1, :]
         sends = repeat_start(block, out, out_sems)
         wait_all(day_copies)
         pre_end = column(pre_row)
@@ -173,12 +172,24 @@
     groups, day_cols = raised_days.shape
     unit_rows, resident = panel.shape[0], high_ref.shape[0]
     rest = pl.ds(resident, unit_rows - resident)
-    copies = fetch([panel.at[rest], cohort, unit_logit], [held, held_cohort, held_logit], sems)
-    total = tree_sum(sums[pl.ds(u * groups, groups), :] for u in range(unit_devices))
-    unit_norm = total[:, 2 * day_cols : 2 * day_cols + 1]
-    treat_count = jnp.maximum(total[:, 2 * day_cols + 1 : 2 * day_cols + 2], 1.0)
-    norms[...] = total[:, 2 * day_cols :]
-    gap = total[:, :day_cols] / unit_norm - total[:, day_cols : 2 * day_cols] / treat_count
+    rows = (unit_rows - resident) // 4
+    quarters = [pl.ds(i * rows, rows) for i in range(4)]
+    copies = fetch([panel.at[rest].at[here] for here in quarters], [held.at[here] for here in quarters], sems)
+    copies += fetch([cohort, unit_logit], [held_cohort, held_logit], sems.at[pl.ds(4, 2)])
+    total = tree_sum(sums[u] for u in range(unit_devices))
+
+    def group_rows(first):
+        starts = [(first + row) * day_cols for row in range(groups)]
+        return jnp.concatenate([total[:, start : start + day_cols] for start in starts], axis=0)
+
+    counts = jnp.broadcast_to(total[:, 2 * groups * day_cols :], (groups, lanes))
+    slot = lax.broadcasted_iota(jnp.int32, (groups, lanes), 0)
+    lane = lax.broadcasted_iota(jnp.int32, (groups, lanes), 1)
+    unit_norm, treat_count, ctrl_count = [
+        jnp.sum(jnp.where(lane == i * groups + slot, counts, 0.0), axis=1, keepdims=True) for i in range(3)
+    ]
+    norms[...] = jnp.where(lane == 0, unit_norm, ctrl_count)
+    gap = group_rows(0) / unit_norm - group_rows(groups) / jnp.maximum(treat_count, 1.0)
     before = days_of(lax.axis_index("day"), (groups, day_cols)).astype(f32) < ends[:, 0:1]
     raised_time = raised_days[...]
     pack[:groups, unit_rows:] = raised_time
@@ -217,7 +228,7 @@
     high_ref, low_ref, more_high, more_low, norms, raised_units, ends, scaled, lam, out, block, out_sems = refs
     groups, unit_rows = raised_units.shape
     resident, day_cols = high_ref.shape
-    unit_norm, ctrl_count = norms[:, 0:1], norms[:, 2:3]
+    unit_norm, ctrl_count = norms[:, 0:1], norms[:, 1:2]
     factor = -step_rate / jnp.sqrt(ends[:, 0:1])
     raised_days = [ref[:groups, unit_rows:] for ref in parts]
     over_time = 1.0 / tree_sum(jnp.sum(value, axis=1, keepdims=True) for value in raised_days)
@@ -248,15 +259,14 @@
     wait_all(repeat_start(block, out, out_sems))
 
 
-def time_grad_of(grads, unit_devices, half, day, groups):
-    places = [(unit * half + half - 1 - day) * groups for unit in range(unit_devices)]
-    return tree_sum(grads[pl.ds(place, groups), :] for place in places)
+def time_grad_of(grads, unit_devices, half, day):
+    return tree_sum(grads[unit * half + half - 1 - day] for unit in range(unit_devices))
 
 
 @first_half_only
 def fourth_kernel(half, unit_devices, grads, totals):
-    groups, day_cols = totals.shape[0], grads.shape[1]
-    last = time_grad_of(grads, unit_devices, half, half - 1, groups)
+    day_cols = grads.shape[2]
+    last = time_grad_of(grads, unit_devices, half, half - 1)
     totals[...] = jnp.broadcast_to(last[:, day_cols - 1 :], totals.shape)
 
 
@@ -267,11 +277,11 @@
     @pl.when(me < half)
     def _():
         unit_weights[...] = scaled[...] * (1.0 / totals[:, 0:1])
-        root = jnp.sqrt(jnp.maximum(norms[:, 2:3], 1.0))
+        root = jnp.sqrt(jnp.maximum(norms[:, 1:2], 1.0))
         moved_total = jnp.zeros((groups, 1), f32)
         own = jnp.zeros((groups, day_cols), f32)
         for day in range(half):
-            total = time_grad_of(grads, unit_devices, half, day, groups)
+            total = time_grad_of(grads, unit_devices, half, day)
             moved = lam[:, day * day_cols : (day + 1) * day_cols] * jnp.exp(total * (-step_rate / root))
             moved_total += jnp.sum(moved, axis=1, keepdims=True)
             own = jnp.where(me == day, moved, own)
@@ -297,7 +307,7 @@
     half = day_devices // 2
     assert half * 2 == day_devices and half & (half - 1) == 0
     assert unit_devices & (unit_devices - 1) == 0
-    panel_starts = [0, unit_rows // 2, unit_rows]
+    panel_starts = [0, unit_rows // 4, unit_rows // 8 * 5, unit_rows]
     resident = unit_rows * 3 // 4 // block_rows * block_rows
     middle = unit_devices // 2 - 1
     unit_order = [middle] + [unit for unit in reversed(range(unit_devices)) if unit != middle]
@@ -342,8 +352,8 @@
     panel_terms = [((resident, day_cols), bf16)] * 2
     other_terms = [((unit_rows - resident, day_cols), bf16)] * 2
     out_sems = pltpu.SemaphoreType.DMA((unit_devices,))
-    width = 2 * day_cols + lanes
-    in_hbm = pltpu.HBM((unit_devices * groups, width), f32)
+    width = 2 * groups * day_cols + lanes
+    in_hbm = pltpu.HBM((unit_devices, 1, width), f32)
     sums, cross, raised_days, ends, high, low = call(
         functools.partial(first_kernel, day_devices * day_cols, half, panel_starts),
         [
@@ -359,7 +369,7 @@
         out_specs=[hbm, hbm] + [vmem] * 4,
         scratch_shapes=held
         + [
-            pltpu.VMEM((groups, width), f32),
+            pltpu.VMEM((1, width), f32),
             pltpu.VMEM((4 * groups, unit_rows), bf16),
             pltpu.VMEM((groups, unit_rows), f32),
             small_sems,
@@ -382,7 +392,12 @@
         "unit_gradient",
         (fixed[0], fixed[1], fixed[4], over_units(sums), raised_days, ends, high, low),
         in_specs=[hbm] * 3 + [vmem] * 5,
-        scratch_shapes=[pltpu.VMEM((unit_rows - resident, day_cols), f32), held[1], held[4], panel_sems],
+        scratch_shapes=[
+            pltpu.VMEM((unit_rows - resident, day_cols), f32),
+            held[1],
+            held[4],
+            pltpu.SemaphoreType.DMA((6,)),
+        ],
     )
     (pack,) = call(
         functools.partial(join_kernel, half), [((3 * groups, unit_rows + day_cols), f32)], "join_post", (pack, post)
@@ -393,7 +408,7 @@
         [
             ((groups, unit_rows), f32),
             ((groups, half * day_cols), f32),
-            pltpu.HBM((members * groups, day_cols), f32),
+            pltpu.HBM((members, groups, day_cols), f32),
         ],
         "time_gradient",
         (over_days(pack), high, low, more_high, more_low, norms, raised_units, ends),

time: 36.8 us -> 36.3 us (0.986)
  waiting for transfers between devices: 8.2 us -> 7.49 us
  starting transfers between devices: 15.9 us -> 16.3 us
    all_to_all x1, waiting for transfers between devices: 4.25 us -> 3.54 us  [over_units(): lax.all_to_all(value, 'unit', split_axis=0, concat_axis=0, axis_index_gro...]
where the time goes in v14:
time: 36.3 us; the launch traced here: 35.8 us
  starting transfers between devices  16.3 us (45%)
  Pallas kernels  8.9 us (25%)
  waiting for transfers between devices  7.49 us (21%)
  blocking collectives  2.4 us (7%)
  between operations  0.7 us (2%)
    pallas_call x7, Pallas kernels, call(): pl.pallas_call(kernel, in_specs=in_specs or [vmem] * len(args), out_specs...  8.9 us
    all_to_all x1, starting transfers between devices, over_units(): lax.all_to_all(value, 'unit', split_axis=0, concat_axis=0, axis_index_gro...  7.83 us
    all_to_all x1, starting transfers between devices, over_first_half(): lax.all_to_all(value, ('unit', 'day'), split_axis=0, concat_axis=0, axis_...  4.64 us
    all_to_all x1, waiting for transfers between devices, over_first_half(): lax.all_to_all(value, ('unit', 'day'), split_axis=0, concat_axis=0, axis_...  3.55 us
    all_to_all x1, waiting for transfers between devices, over_units(): lax.all_to_all(value, 'unit', split_axis=0, concat_axis=0, axis_index_gro...  3.54 us
    ppermute x2, starting transfers between devices, to_other_half(): return lax.ppermute(value, ('unit', 'day'), pairs)  2.56 us
    all_gather x1, blocking collectives, over_days(): return lax.all_gather(value, 'day', axis_index_groups=halves)  2.4 us
    ppermute x1, starting transfers between devices, local(): post = lax.ppermute(cross, ('unit', 'day'), downward)  1.28 us
  transfers between devices with their start and end apart: 5, of which 3 were waited for; matrix products, arithmetic and copies ran while one was open for 0% of the time, Pallas kernels for 10%

profile of v14, /device:TPU:0, one launch (start us, length us, event | category | flops | bytes accessed | tf_op | source)
XLA Modules:
  0.0 35.8 jit_solution(7101990299610503005)
XLA Ops:
  0.6 3.7 %first_product.1 = (f32[8,1,4224]{2,1,0:T(1,128)}, f32[8,4096]{1,0:T(8,128)}, f32[8,256]{1,0:T(8,128)S(1)}, f32[8,128]{1,0:T(8,128)S(1)}, bf16[3072,256]{1,0:T(8,128)(2,1)S(1)}, /*index=5*/bf16[3072,256]{1,0:T(8,128)(2,1)S(1)}) custom-call(f32[4096,256]{1,0:T(8,128)} %panel.1, s32[1,4096]{1,0:T(1,128)} %bitcast.5, s32[1,8]{1,0:T(1,128)} %bitcast.7, ...), custom_call_target="tpu_custom_call" | custom-call | tf_op jit(solution)/shard_map/first_product/pallas_call | solution.py:336
  4.3 7.8 %all-to-all-start = ((f32[8,1,4224]{2,1,0:T(1,128)}), f32[8,1,4224]{2,1,0:T(1,128)S(1)}, u32[]{:S(2)}, u32[]{:S(2)}) async-start(f32[8,1,4224]{2,1,0:T(1,128)} %get-tuple-element.18), calls=%async_computation | async-start | bytes 270336 | tf_op jit(solution)/shard_map/all_to_all | solution.py:333
  12.1 1.3 %collective-permute-start = (f32[8,4096]{1,0:T(8,128)}, f32[8,4096]{1,0:T(8,128)S(1)}, u32[]{:S(2)}, u32[]{:S(2)}) collective-permute-start(f32[8,4096]{1,0:T(8,128)} %get-tuple-element.24), channel_id=1, source_target_pairs={{2,0},{3,1},{6,4},{7,5},{10,8},{11,9},{14,12},{15,13},{18,16},{19,... | collective-permute-start | bytes 393224 | tf_op jit(solution)/shard_map/ppermute | solution.py:383
  13.4 3.5 %all-to-all-done.sums = f32[8,1,4224]{2,1,0:T(1,128)S(1)} async-done(((f32[8,1,4224]{2,1,0:T(1,128)}), f32[8,1,4224]{2,1,0:T(1,128)S(1)}, u32[]{:S(2)}, u32[]{:S(2)}) %all-to-all-start) | async-done | bytes 135200 | tf_op jit(solution)/shard_map/all_to_all | solution.py:333
  17.0 2.6 %unit_gradient.1 = (f32[16,4352]{1,0:T(8,128)S(1)}, f32[8,128]{1,0:T(8,128)S(1)}, f32[8,4096]{1,0:T(8,128)S(1)}, bf16[1024,256]{1,0:T(8,128)(2,1)S(1)}, bf16[1024,256]{1,0:T(8,128)(2,1)S(1)}) custom-call(f32[4096,256]{1,0:T(8,128)} %panel.1, s32[1,4096]{1,0:T(1,128)} %bitcast.6, f32[8,4096]{1,0:T(8,128)} %unit_logit.1, f32[8,1,4224]{2,1,0:T(1,128)S(1)} %all-to-all-done.sums, ...), custom_call_target="tpu_custom_call" | custom-call | tf_op jit(solution)/shard_map/unit_gradient/pallas_call | solution.py:336
  19.6 0.0 collective-permute-done.post
  19.7 2.4 %all-gather = f32[48,4352]{1,0:T(8,128)S(1)} all-gather(f32[24,4352]{1,0:T(8,128)S(1)} %join_post.1), channel_id=2, replica_groups={{0,1},{2,3},{4,5},{6,7},{8,9},{10,11},{12,13},{14,15},{16,17},{18,19},{..., dimensions={0}, use_global_device_ids=true | all-gather | bytes 1253376 | tf_op jit(solution)/shard_map/all_gather | solution.py:321
  22.1 1.5 %time_gradient.1 = (f32[8,4096]{1,0:T(8,128)S(1)}, f32[8,512]{1,0:T(8,128)S(1)}, f32[16,8,256]{2,1,0:T(8,128)}) custom-call(f32[2,24,4352]{2,1,0:T(8,128)S(1)} %bitcast.4, bf16[3072,256]{1,0:T(8,128)(2,1)S(1)} %get-tuple-element.21.high_ref.refs_1_, bf16[3072,256]{1,0:T(8,128)(2,1)S(1)} %get-tuple-element.22.low_ref.refs_2_, ...), custom_call_target="tpu_custom_call" | custom-call | tf_op jit(solution)/shard_map/time_gradient/pallas_call | solution.py:336
  23.6 4.6 %all-to-all-start.1 = ((f32[16,8,256]{2,1,0:T(8,128)}), f32[16,8,256]{2,1,0:T(8,128)S(1)}, u32[]{:S(2)}, u32[]{:S(2)}) async-start(f32[16,8,256]{2,1,0:T(8,128)} %get-tuple-element.29), calls=%async_computation.1 | async-start | bytes 262144 | tf_op jit(solution)/shard_map/all_to_all | solution.py:328
  28.3 1.3 %collective-permute-start.2 = (f32[8,4096]{1,0:T(8,128)S(1)}, f32[8,4096]{1,0:T(8,128)S(1)}, u32[]{:S(2)}, u32[]{:S(2)}) collective-permute-start(f32[8,4096]{1,0:T(8,128)S(1)} %get-tuple-element.30.scaled), channel_id=1, source_target_pairs={{0,2},{1,3},{4,6},{5,7},{8,10},{9,11},{12,14},{13,15},{16,18},{17,... | collective-permute-start | bytes 393224 | tf_op jit(solution)/shard_map/ppermute | solution.py:317
  29.6 3.5 %all-to-all-done.1.grads = f32[16,8,256]{2,1,0:T(8,128)S(1)} async-done(((f32[16,8,256]{2,1,0:T(8,128)}), f32[16,8,256]{2,1,0:T(8,128)S(1)}, u32[]{:S(2)}, u32[]{:S(2)}) %all-to-all-start.1) | async-done | bytes 131104 | tf_op jit(solution)/shard_map/all_to_all | solution.py:328
  33.1 0.1 unit_totals.1.totals
  33.2 1.3 %collective-permute-start.1 = (f32[8,128]{1,0:T(8,128)S(1)}, f32[8,128]{1,0:T(8,128)S(1)}, u32[]{:S(2)}, u32[]{:S(2)}) collective-permute-start(f32[8,128]{1,0:T(8,128)S(1)} %unit_totals.1.totals), channel_id=1, source_target_pairs={{0,2},{1,3},{4,6},{5,7},{8,10},{9,11},{12,14},{13,15},{16,18},{17,... | collective-permute-start | bytes 12296 | tf_op jit(solution)/shard_map/ppermute | solution.py:317
  34.5 0.9 %scale_weights.1 = (f32[8,4096]{1,0:T(8,128)}, f32[8,256]{1,0:T(8,128)}) custom-call(f32[8,128]{1,0:T(8,128)S(1)} %unit_totals.1.totals, f32[8,4096]{1,0:T(8,128)S(1)} %get-tuple-element.30.scaled, f32[16,8,256]{2,1,0:T(8,128)S(1)} %all-to-all-done.1.grads, f32[8,512]{1,0:T(8,128)S(1)} %get-tuple-element.31.lam, ...), custom_call_target="tpu_custom_call" | custom-call | tf_op jit(solution)/shard_map/scale_weights/pallas_call | solution.py:336
  35.4 0.0 collective-permute-done.2.sent_scaled
  35.4 0.4 %collective-permute-done.1.sent_totals = f32[8,128]{1,0:T(8,128)S(1)} collective-permute-done((f32[8,128]{1,0:T(8,128)S(1)}, f32[8,128]{1,0:T(8,128)S(1)}, u32[]{:S(2)}, u32[]{:S(2)}) %collective-permute-start.1) | collective-permute-done | bytes 4128 | tf_op jit(solution)/shard_map/ppermute | solution.py:317
  (2 shorter events, 0.0 us)
Async XLA Ops:
  4.3 12.7 %all-to-all-start = ((f32[8,1,4224]{2,1,0:T(1,128)}), f32[8,1,4224]{2,1,0:T(1,128)S(1)}, u32[]{:S(2)}, u32[]{:S(2)}) async-start(f32[8,1,4224]{2,1,0:T(1,128)} %get-tuple-element.18), calls=%async_computation | async-start | bytes 270336 | tf_op jit(solution)/shard_map/all_to_all | solution.py:333
  12.1 7.5 %collective-permute-start = (f32[8,4096]{1,0:T(8,128)}, f32[8,4096]{1,0:T(8,128)S(1)}, u32[]{:S(2)}, u32[]{:S(2)}) collective-permute-start(f32[8,4096]{1,0:T(8,128)} %get-tuple-element.24), channel_id=1, source_target_pairs={{2,0},{3,1},{6,4},{7,5},{10,8},{11,9},{14,12},{15,13},{18,16},{19,... | collective-permute-start | bytes 393224 | tf_op jit(solution)/shard_map/ppermute | solution.py:383
  23.6 9.5 %all-to-all-start.1 = ((f32[16,8,256]{2,1,0:T(8,128)}), f32[16,8,256]{2,1,0:T(8,128)S(1)}, u32[]{:S(2)}, u32[]{:S(2)}) async-start(f32[16,8,256]{2,1,0:T(8,128)} %get-tuple-element.29), calls=%async_computation.1 | async-start | bytes 262144 | tf_op jit(solution)/shard_map/all_to_all | solution.py:328
  28.3 7.1 %collective-permute-start.2 = (f32[8,4096]{1,0:T(8,128)S(1)}, f32[8,4096]{1,0:T(8,128)S(1)}, u32[]{:S(2)}, u32[]{:S(2)}) collective-permute-start(f32[8,4096]{1,0:T(8,128)S(1)} %get-tuple-element.30.scaled), channel_id=1, source_target_pairs={{0,2},{1,3},{4,6},{5,7},{8,10},{9,11},{12,14},{13,15},{16,18},{17,... | collective-permute-start | bytes 393224 | tf_op jit(solution)/shard_map/ppermute | solution.py:317
  33.2 2.6 %collective-permute-start.1 = (f32[8,128]{1,0:T(8,128)S(1)}, f32[8,128]{1,0:T(8,128)S(1)}, u32[]{:S(2)}, u32[]{:S(2)}) collective-permute-start(f32[8,128]{1,0:T(8,128)S(1)} %unit_totals.1.totals), channel_id=1, source_target_pairs={{0,2},{1,3},{4,6},{5,7},{8,10},{9,11},{12,14},{13,15},{16,18},{17,... | collective-permute-start | bytes 12296 | tf_op jit(solution)/shard_map/ppermute | solution.py:317

commit v15 on v14

--- a/solution.py
+++ b/solution.py
@@ -105,15 +105,15 @@
 
 def first_kernel(all_count, half, starts, *refs):
     arguments, refs = refs[:6], refs[6:]
-    out, cross, raised_days, ends, high_ref, low_ref, *held, block, left_ref, cross_block, small_sems, panel_sems, out_sems = refs
+    out, cross, raised_units, raised_days, time_norm, ends, high_ref, low_ref, *held, block, left_ref, cross_block, small_sems, panel_sems, out_sems = refs
     groups, day_cols = held[5].shape
     unit_rows, resident = held[0].shape[0], high_ref.shape[0]
-    units = (1, 4)
-    days = (2, 3, 5)
-    unit_copies = fetch([arguments[i] for i in units], [held[i] for i in units], small_sems)
+    (post_copy,) = fetch(arguments[3:4], held[3:4], small_sems)
+    unit_copies = fetch(arguments[1:5:3], held[1:5:3], small_sems.at[pl.ds(1, 2)])
     parts = fetch_rows(arguments[0], held[0], panel_sems, starts)
-    day_copies = fetch([arguments[i] for i in days], [held[i] for i in days], small_sems.at[pl.ds(2, 3)])
+    day_copies = fetch(arguments[2:6:3], held[2:6:3], small_sems.at[pl.ds(3, 2)])
     panel, cohort, pre_row, post_row, unit_logit, time_logit = held
+    post_copy.wait()
     wait_all(unit_copies)
     me = lax.axis_index("day")
 
@@ -123,6 +123,7 @@
         treated = jnp.where(cohort[...] == label, 1.0, 0.0)
         control = jnp.where(cohort[...] > label, 1.0, 0.0)
         raised = jnp.exp(unit_logit[...]) * control
+        raised_units[...] = raised
         left_ref[...] = left_of(raised, treated)
         lane = lax.broadcasted_iota(jnp.int32, (groups, lanes), 1)
         counts = [jnp.sum(value, axis=1, keepdims=True) for value in (raised, treated, control)]
@@ -150,12 +151,13 @@
         pre_end = column(pre_row)
         ends[...] = jnp.broadcast_to(pre_end.astype(f32), ends.shape)
         before = days_of(me, (groups, day_cols)) < pre_end
-        raised_days[...] = jnp.where(before, jnp.exp(time_logit[...]), 0.0)
+        raised_time = jnp.where(before, jnp.exp(time_logit[...]), 0.0)
+        raised_days[...] = raised_time
+        time_norm[...] = jnp.broadcast_to(jnp.sum(raised_time, axis=1, keepdims=True), time_norm.shape)
         wait_all(sends)
 
     @pl.when(me >= half)
     def _():
-        wait_all(day_copies)
         post_start = column(post_row)
         after = jnp.where(days_of(me, (groups, day_cols)) >= post_start, 1.0, 0.0)
         left = left_of(after / (all_count - post_start).astype(f32))
@@ -163,19 +165,18 @@
             copy.wait()
             for here in blocks_of(start, rows):
                 cross_block[:, here] = add_terms(days_dot(left, *split_panel(panel[here, :])), groups)
-        wait_all(fetch([cross_block], [cross], out_sems))
+        sends = fetch([cross_block], [cross], out_sems)
+        wait_all(day_copies)
+        wait_all(sends)
 
 
 @first_half_only
-def second_kernel(half, unit_devices, panel, cohort, unit_logit, sums, raised_days, ends, high_ref, low_ref, *refs):
-    pack, norms, raised_units, more_high, more_low, held, held_cohort, held_logit, sems = refs
+def second_kernel(half, unit_devices, panel, sums, raised_days, ends, high_ref, low_ref, *refs):
+    pack, norms, more_high, more_low, held, sems = refs
     groups, day_cols = raised_days.shape
     unit_rows, resident = panel.shape[0], high_ref.shape[0]
     rest = pl.ds(resident, unit_rows - resident)
-    rows = (unit_rows - resident) // 4
-    quarters = [pl.ds(i * rows, rows) for i in range(4)]
-    copies = fetch([panel.at[rest].at[here] for here in quarters], [held.at[here] for here in quarters], sems)
-    copies += fetch([cohort, unit_logit], [held_cohort, held_logit], sems.at[pl.ds(4, 2)])
+    (copy,) = fetch([panel.at[rest]], [held], sems)
     total = tree_sum(sums[u] for u in range(unit_devices))
 
     def group_rows(first):
@@ -203,9 +204,7 @@
 
     for here in blocks_of(0, resident):
         multiply(here, high_ref[here, :], low_ref[here, :])
-    wait_all(copies)
-    label = lax.broadcasted_iota(jnp.int32, raised_units.shape, 0)
-    raised_units[...] = jnp.where(held_cohort[...] > label, jnp.exp(held_logit[...]), 0.0)
+    copy.wait()
     for here in blocks_of(resident, unit_rows - resident):
         there = pl.ds(here.start - resident, block_rows)
         high, low = split_panel(held[there, :])
@@ -215,11 +214,14 @@
 
 
 @first_half_only
-def join_kernel(half, pack, post, out):
-    rows, width = pack.shape
-    out[:rows, :] = pack[...]
-    out[rows:, : post.shape[1]] = post[...]
-    out[rows:, post.shape[1] :] = jnp.zeros((post.shape[0], width - post.shape[1]), f32)
+def join_kernel(half, pack, post, *refs):
+    norms, out = refs[:half], refs[half]
+    groups, unit_rows = post.shape
+    over_time = 1.0 / tree_sum(ref[:, 0:1] for ref in norms)
+    out[:groups, :unit_rows] = pack[:groups, :unit_rows]
+    out[:groups, unit_rows:] = pack[:groups, unit_rows:] * over_time
+    out[groups:, :unit_rows] = pack[groups:, :unit_rows] * over_time - post[...]
+    out[groups:, unit_rows:] = pack[groups:, unit_rows:]
 
 
 @first_half_only
@@ -230,12 +232,10 @@
     resident, day_cols = high_ref.shape
     unit_norm, ctrl_count = norms[:, 0:1], norms[:, 1:2]
     factor = -step_rate / jnp.sqrt(ends[:, 0:1])
-    raised_days = [ref[:groups, unit_rows:] for ref in parts]
-    over_time = 1.0 / tree_sum(jnp.sum(value, axis=1, keepdims=True) for value in raised_days)
     over_unit = 1.0 / unit_norm
     me = lax.rem(lax.axis_index("day"), half)
     for day in range(half):
-        lam[:, day * day_cols : (day + 1) * day_cols] = raised_days[day] * over_time
+        lam[:, day * day_cols : (day + 1) * day_cols] = parts[day][:groups, unit_rows:]
     time_grad = jnp.zeros((groups, day_cols), f32)
     new_sum = jnp.zeros((groups, 1), f32)
     for start in range(0, unit_rows, block_rows):
@@ -245,8 +245,7 @@
         new = raised * over_unit * jnp.exp(whole[:groups] * factor)
         new_sum += jnp.sum(new, axis=1, keepdims=True)
         scaled[:, here] = new * ctrl_count
-        shortfall = whole[groups : 2 * groups] * over_time - whole[2 * groups :]
-        left = left_of(jnp.where(raised > 0.0, shortfall, 0.0))
+        left = left_of(jnp.where(raised > 0.0, whole[groups:], 0.0))
         if start < resident:
             high, low = high_ref[here, :], low_ref[here, :]
         else:
@@ -354,19 +353,21 @@
     out_sems = pltpu.SemaphoreType.DMA((unit_devices,))
     width = 2 * groups * day_cols + lanes
     in_hbm = pltpu.HBM((unit_devices, 1, width), f32)
-    sums, cross, raised_days, ends, high, low = call(
+    sums, cross, raised_units, raised_days, time_norm, ends, high, low = call(
         functools.partial(first_kernel, day_devices * day_cols, half, panel_starts),
         [
             in_hbm,
             pltpu.HBM((groups, unit_rows), f32),
+            ((groups, unit_rows), f32),
             ((groups, day_cols), f32),
+            ((groups, lanes), f32),
             ((groups, lanes), f32),
             *panel_terms,
         ],
         "first_product",
         fixed,
         in_specs=[hbm] * 6,
-        out_specs=[hbm, hbm] + [vmem] * 4,
+        out_specs=[hbm, hbm] + [vmem] * 6,
         scratch_shapes=held
         + [
             pltpu.VMEM((1, width), f32),
@@ -381,26 +382,30 @@
         (u * day_devices + d + half, u * day_devices + d) for u in range(unit_devices) for d in range(half)
     ]
     post = lax.ppermute(cross, ("unit", "day"), downward)
-    pack, norms, raised_units, more_high, more_low = call(
+    pack, norms, more_high, more_low = call(
         functools.partial(second_kernel, half, unit_devices),
         [
             ((2 * groups, unit_rows + day_cols), f32),
             ((groups, lanes), f32),
-            ((groups, unit_rows), f32),
             *other_terms,
         ],
         "unit_gradient",
-        (fixed[0], fixed[1], fixed[4], over_units(sums), raised_days, ends, high, low),
-        in_specs=[hbm] * 3 + [vmem] * 5,
+        (fixed[0], over_units(sums), raised_days, ends, high, low),
+        in_specs=[hbm] + [vmem] * 5,
         scratch_shapes=[
             pltpu.VMEM((unit_rows - resident, day_cols), f32),
-            held[1],
-            held[4],
-            pltpu.SemaphoreType.DMA((6,)),
+            pltpu.SemaphoreType.DMA((1,)),
         ],
     )
+    time_norms = [time_norm]
+    for k in range(1, half):
+        pairs = [(u * day_devices + d, u * day_devices + (d ^ k)) for u in range(unit_devices) for d in range(half)]
+        time_norms.append(lax.ppermute(time_norm, ("unit", "day"), pairs))
     (pack,) = call(
-        functools.partial(join_kernel, half), [((3 * groups, unit_rows + day_cols), f32)], "join_post", (pack, post)
+        functools.partial(join_kernel, half),
+        [((2 * groups, unit_rows + day_cols), f32)],
+        "join_post",
+        (pack, post, *time_norms),
     )
     members = unit_devices * half
     scaled, lam, grads = call(

time: 36.3 us -> 37.5 us (1.033)
  waiting for transfers between devices: 7.49 us -> 5.56 us
  starting transfers between devices: 16.3 us -> 18.2 us
  local copies, waits for them, and re-layouts: 0 us -> 0.7 us
  Pallas kernels: 8.9 us -> 9.52 us
    all_to_all x1, waiting for transfers between devices: 3.54 us -> 1.61 us  [over_units(): lax.all_to_all(value, 'unit', split_axis=0, concat_axis=0, axis_index_gro...]
    ppermute x0 -> x1, starting transfers between devices: none -> 1.92 us  [local(): time_norms.append(lax.ppermute(time_norm, ('unit', 'day'), pairs))]
    unnamed x0 -> x4, local copies, waits for them, and re-layouts: none -> 0.7 us
    pallas_call x7, Pallas kernels: 8.9 us -> 9.52 us  [call(): pl.pallas_call(kernel, in_specs=in_specs or [vmem] * len(args), out_specs...]
  transfers between devices with their start and end apart: 5 -> 6, of which waited for: 3 -> 3; matrix products, arithmetic and copies ran while one was open for 0% -> 0% of each run, Pallas kernels for 10% -> 10%
where the time goes in v15:
time: 37.5 us; the launch traced here: 36.9 us
  starting transfers between devices  18.2 us (49%)
  Pallas kernels  9.52 us (25%)
  waiting for transfers between devices  5.56 us (15%)
  blocking collectives  2.2 us (6%)
  between operations  0.72 us (2%)
  local copies, waits for them, and re-layouts  0.7 us (2%)
    pallas_call x7, Pallas kernels, call(): pl.pallas_call(kernel, in_specs=in_specs or [vmem] * len(args), out_specs...  9.52 us
    all_to_all x1, starting transfers between devices, over_units(): lax.all_to_all(value, 'unit', split_axis=0, concat_axis=0, axis_index_gro...  7.83 us
    all_to_all x1, starting transfers between devices, over_first_half(): lax.all_to_all(value, ('unit', 'day'), split_axis=0, concat_axis=0, axis_...  4.64 us
    all_to_all x1, waiting for transfers between devices, over_first_half(): lax.all_to_all(value, ('unit', 'day'), split_axis=0, concat_axis=0, axis_...  3.55 us
    ppermute x2, starting transfers between devices, to_other_half(): return lax.ppermute(value, ('unit', 'day'), pairs)  2.56 us
    all_gather x1, blocking collectives, over_days(): return lax.all_gather(value, 'day', axis_index_groups=halves)  2.2 us
    ppermute x1, starting transfers between devices, local(): time_norms.append(lax.ppermute(time_norm, ('unit', 'day'), pairs))  1.92 us
    all_to_all x1, waiting for transfers between devices, over_units(): lax.all_to_all(value, 'unit', split_axis=0, concat_axis=0, axis_index_gro...  1.61 us
  transfers between devices with their start and end apart: 6, of which 3 were waited for; matrix products, arithmetic and copies ran while one was open for 0% of the time, Pallas kernels for 10%

profile of v15, /device:TPU:0, one launch (start us, length us, event | category | flops | bytes accessed | tf_op | source)
XLA Modules:
  0.0 36.9 jit_solution(14053230330347305929)
XLA Ops:
  0.6 3.7 %first_product.1 = (f32[8,1,4224]{2,1,0:T(1,128)}, f32[8,4096]{1,0:T(8,128)}, f32[8,4096]{1,0:T(8,128)S(1)}, f32[8,256]{1,0:T(8,128)S(1)}, f32[8,128]{1,0:T(8,12...) custom-call(f32[4096,256]{1,0:T(8,128)} %panel.1, s32[1,4096]{1,0:T(1,128)} %bitcast.5, ...), custom_call_target="tpu_custom_call" | custom-call | tf_op jit(solution)/shard_map/first_product/pallas_call | solution.py:335
  4.3 0.0 copy-start
  4.3 7.8 %all-to-all-start = ((f32[8,1,4224]{2,1,0:T(1,128)}), f32[8,1,4224]{2,1,0:T(1,128)S(1)}, u32[]{:S(2)}, u32[]{:S(2)}) async-start(f32[8,1,4224]{2,1,0:T(1,128)} %get-tuple-element.19), calls=%async_computation | async-start | bytes 270336 | tf_op jit(solution)/shard_map/all_to_all | solution.py:332
  12.2 0.0 copy-done
  12.2 1.3 %collective-permute-start = (f32[8,4096]{1,0:T(8,128)}, f32[8,4096]{1,0:T(8,128)S(1)}, u32[]{:S(2)}, u32[]{:S(2)}) collective-permute-start(f32[8,4096]{1,0:T(8,128)} %get-tuple-element.25), channel_id=1, source_target_pairs={{2,0},{3,1},{6,4},{7,5},{10,8},{11,9},{14,12},{15,13},{18,16},{19,... | collective-permute-start | bytes 393224 | tf_op jit(solution)/shard_map/ppermute | solution.py:384
  13.4 1.9 %collective-permute-start.1 = (f32[8,128]{1,0:T(8,128)S(1)}, f32[8,128]{1,0:T(8,128)}, u32[]{:S(2)}, u32[]{:S(2)}) collective-permute-start(f32[8,128]{1,0:T(8,128)S(1)} %get-tuple-element.26.refs_0_), channel_id=1, source_target_pairs={{0,1},{1,0},{4,5},{5,4},{8,9},{9,8},{12,13},{13,12},{16,17},{17,16... | collective-permute-start | bytes 12296 | tf_op jit(solution)/shard_map/ppermute | solution.py:403
  15.4 1.6 %all-to-all-done.sums = f32[8,1,4224]{2,1,0:T(1,128)S(1)} async-done(((f32[8,1,4224]{2,1,0:T(1,128)}), f32[8,1,4224]{2,1,0:T(1,128)S(1)}, u32[]{:S(2)}, u32[]{:S(2)}) %all-to-all-start) | async-done | bytes 135200 | tf_op jit(solution)/shard_map/all_to_all | solution.py:332
  17.0 0.0 copy-start.1
  17.0 0.7 %copy-done.1 = f32[8,256]{1,0:T(8,128)S(1)} copy-done((f32[8,256]{1,0:T(8,128)S(1)}, f32[8,256]{1,0:T(8,128)}, u32[]{:S(2)}) %copy-start.1) | copy-done | bytes 8216
  17.7 2.6 %unit_gradient.1 = (f32[16,4352]{1,0:T(8,128)S(1)}, f32[8,128]{1,0:T(8,128)S(1)}, bf16[1024,256]{1,0:T(8,128)(2,1)S(1)}, bf16[1024,256]{1,0:T(8,128)(2,1)S(1)}) custom-call(f32[4096,256]{1,0:T(8,128)} %panel.1, f32[8,1,4224]{2,1,0:T(1,128)S(1)} %all-to-all-done.sums, f32[8,256]{1,0:T(8,128)S(1)} %copy-done.1, f32[8,128]{1,0:T(8,128)S(1)} %get-tuple-element.21.ends.refs_7_, ...), custom_call_target="tpu_custom_call" | custom-call | tf_op jit(solution)/shard_map/unit_gradient/pallas_call | solution.py:335
  20.3 0.0 collective-permute-done.1.refs_1_
  20.3 0.0 collective-permute-done.post
  20.3 0.8 %join_post.1 = f32[16,4352]{1,0:T(8,128)S(1)} custom-call(f32[16,4352]{1,0:T(8,128)S(1)} %get-tuple-element.24.pack, f32[8,4096]{1,0:T(8,128)S(1)} %collective-permute-done.post, f32[8,128]{1,0:T(8,128)S(1)} %get-tuple-element.26.refs_0_, f32[8,128]{1,0:T(8,128)} %collective-permute-done.1.refs_1_), custom_call_target="tpu_custom_call" | custom-call | tf_op jit(solution)/shard_map/join_post/pallas_call | solution.py:335
  21.1 2.2 %all-gather = f32[32,4352]{1,0:T(8,128)S(1)} all-gather(f32[16,4352]{1,0:T(8,128)S(1)} %join_post.1), channel_id=2, replica_groups={{0,1},{2,3},{4,5},{6,7},{8,9},{10,11},{12,13},{14,15},{16,17},{18,19},{..., dimensions={0}, use_global_device_ids=true | all-gather | bytes 835584 | tf_op jit(solution)/shard_map/all_gather | solution.py:320
  23.3 1.5 %time_gradient.1 = (f32[8,4096]{1,0:T(8,128)S(1)}, f32[8,512]{1,0:T(8,128)S(1)}, f32[16,8,256]{2,1,0:T(8,128)}) custom-call(f32[2,16,4352]{2,1,0:T(8,128)S(1)} %bitcast.4, bf16[3072,256]{1,0:T(8,128)(2,1)S(1)} %get-tuple-element.22.high_ref.refs_1_, bf16[3072,256]{1,0:T(8,128)(2,1)S(1)} %get-tuple-element.23.low_ref.refs_2_, ...), custom_call_target="tpu_custom_call" | custom-call | tf_op jit(solution)/shard_map/time_gradient/pallas_call | solution.py:335
  24.8 4.6 %all-to-all-start.1 = ((f32[16,8,256]{2,1,0:T(8,128)}), f32[16,8,256]{2,1,0:T(8,128)S(1)}, u32[]{:S(2)}, u32[]{:S(2)}) async-start(f32[16,8,256]{2,1,0:T(8,128)} %get-tuple-element.31), calls=%async_computation.1 | async-start | bytes 262144 | tf_op jit(solution)/shard_map/all_to_all | solution.py:327
  29.4 1.3 %collective-permute-start.3 = (f32[8,4096]{1,0:T(8,128)S(1)}, f32[8,4096]{1,0:T(8,128)S(1)}, u32[]{:S(2)}, u32[]{:S(2)}) collective-permute-start(f32[8,4096]{1,0:T(8,128)S(1)} %get-tuple-element.32.scaled), channel_id=1, source_target_pairs={{0,2},{1,3},{4,6},{5,7},{8,10},{9,11},{12,14},{13,15},{16,18},{17,... | collective-permute-start | bytes 393224 | tf_op jit(solution)/shard_map/ppermute | solution.py:316
  30.7 3.5 %all-to-all-done.1.grads = f32[16,8,256]{2,1,0:T(8,128)S(1)} async-done(((f32[16,8,256]{2,1,0:T(8,128)}), f32[16,8,256]{2,1,0:T(8,128)S(1)}, u32[]{:S(2)}, u32[]{:S(2)}) %all-to-all-start.1) | async-done | bytes 131104 | tf_op jit(solution)/shard_map/all_to_all | solution.py:327
  34.3 0.1 unit_totals.1.totals
  34.3 1.3 %collective-permute-start.2 = (f32[8,128]{1,0:T(8,128)S(1)}, f32[8,128]{1,0:T(8,128)S(1)}, u32[]{:S(2)}, u32[]{:S(2)}) collective-permute-start(f32[8,128]{1,0:T(8,128)S(1)} %unit_totals.1.totals), channel_id=1, source_target_pairs={{0,2},{1,3},{4,6},{5,7},{8,10},{9,11},{12,14},{13,15},{16,18},{17,... | collective-permute-start | bytes 12296 | tf_op jit(solution)/shard_map/ppermute | solution.py:316
  35.6 0.9 %scale_weights.1 = (f32[8,4096]{1,0:T(8,128)}, f32[8,256]{1,0:T(8,128)}) custom-call(f32[8,128]{1,0:T(8,128)S(1)} %unit_totals.1.totals, f32[8,4096]{1,0:T(8,128)S(1)} %get-tuple-element.32.scaled, f32[16,8,256]{2,1,0:T(8,128)S(1)} %all-to-all-done.1.grads, f32[8,512]{1,0:T(8,128)S(1)} %get-tuple-element.33.lam, ...), custom_call_target="tpu_custom_call" | custom-call | tf_op jit(solution)/shard_map/scale_weights/pallas_call | solution.py:335
  36.5 0.0 collective-permute-done.3.sent_scaled
  36.5 0.4 %collective-permute-done.2.sent_totals = f32[8,128]{1,0:T(8,128)S(1)} collective-permute-done((f32[8,128]{1,0:T(8,128)S(1)}, f32[8,128]{1,0:T(8,128)S(1)}, u32[]{:S(2)}, u32[]{:S(2)}) %collective-permute-start.2) | collective-permute-done | bytes 4128 | tf_op jit(solution)/shard_map/ppermute | solution.py:316
  (1 shorter events, 0.0 us)
Async XLA Ops:
  4.3 7.8 %copy-start = (f32[8,256]{1,0:T(8,128)}, f32[8,256]{1,0:T(8,128)S(1)}, u32[]{:S(2)}) copy-start(f32[8,256]{1,0:T(8,128)S(1)} %get-tuple-element.20.raised_days) | copy-start | bytes 24580
  4.3 12.7 %all-to-all-start = ((f32[8,1,4224]{2,1,0:T(1,128)}), f32[8,1,4224]{2,1,0:T(1,128)S(1)}, u32[]{:S(2)}, u32[]{:S(2)}) async-start(f32[8,1,4224]{2,1,0:T(1,128)} %get-tuple-element.19), calls=%async_computation | async-start | bytes 270336 | tf_op jit(solution)/shard_map/all_to_all | solution.py:332
  12.2 8.1 %collective-permute-start = (f32[8,4096]{1,0:T(8,128)}, f32[8,4096]{1,0:T(8,128)S(1)}, u32[]{:S(2)}, u32[]{:S(2)}) collective-permute-start(f32[8,4096]{1,0:T(8,128)} %get-tuple-element.25), channel_id=1, source_target_pairs={{2,0},{3,1},{6,4},{7,5},{10,8},{11,9},{14,12},{15,13},{18,16},{19,... | collective-permute-start | bytes 393224 | tf_op jit(solution)/shard_map/ppermute | solution.py:384
  13.4 6.8 %collective-permute-start.1 = (f32[8,128]{1,0:T(8,128)S(1)}, f32[8,128]{1,0:T(8,128)}, u32[]{:S(2)}, u32[]{:S(2)}) collective-permute-start(f32[8,128]{1,0:T(8,128)S(1)} %get-tuple-element.26.refs_0_), channel_id=1, source_target_pairs={{0,1},{1,0},{4,5},{5,4},{8,9},{9,8},{12,13},{13,12},{16,17},{17,16... | collective-permute-start | bytes 12296 | tf_op jit(solution)/shard_map/ppermute | solution.py:403
  17.0 0.7 %copy-start.1 = (f32[8,256]{1,0:T(8,128)S(1)}, f32[8,256]{1,0:T(8,128)}, u32[]{:S(2)}) copy-start(f32[8,256]{1,0:T(8,128)} %copy-done) | copy-start | bytes 24580
  24.8 9.5 %all-to-all-start.1 = ((f32[16,8,256]{2,1,0:T(8,128)}), f32[16,8,256]{2,1,0:T(8,128)S(1)}, u32[]{:S(2)}, u32[]{:S(2)}) async-start(f32[16,8,256]{2,1,0:T(8,128)} %get-tuple-element.31), calls=%async_computation.1 | async-start | bytes 262144 | tf_op jit(solution)/shard_map/all_to_all | solution.py:327
  29.4 7.1 %collective-permute-start.3 = (f32[8,4096]{1,0:T(8,128)S(1)}, f32[8,4096]{1,0:T(8,128)S(1)}, u32[]{:S(2)}, u32[]{:S(2)}) collective-permute-start(f32[8,4096]{1,0:T(8,128)S(1)} %get-tuple-element.32.scaled), channel_id=1, source_target_pairs={{0,2},{1,3},{4,6},{5,7},{8,10},{9,11},{12,14},{13,15},{16,18},{17,... | collective-permute-start | bytes 393224 | tf_op jit(solution)/shard_map/ppermute | solution.py:316
  34.3 2.6 %collective-permute-start.2 = (f32[8,128]{1,0:T(8,128)S(1)}, f32[8,128]{1,0:T(8,128)S(1)}, u32[]{:S(2)}, u32[]{:S(2)}) collective-permute-start(f32[8,128]{1,0:T(8,128)S(1)} %unit_totals.1.totals), channel_id=1, source_target_pairs={{0,2},{1,3},{4,6},{5,7},{8,10},{9,11},{12,14},{13,15},{16,18},{17,... | collective-permute-start | bytes 12296 | tf_op jit(solution)/shard_map/ppermute | solution.py:316

commit v16 on v15

--- a/solution.py
+++ b/solution.py
@@ -105,7 +105,7 @@
 
 def first_kernel(all_count, half, starts, *refs):
     arguments, refs = refs[:6], refs[6:]
-    out, cross, raised_units, raised_days, time_norm, ends, high_ref, low_ref, *held, block, left_ref, cross_block, small_sems, panel_sems, out_sems = refs
+    out, cross, raised_days, time_norm, ends, high_ref, low_ref, *held, block, left_ref, cross_block, small_sems, panel_sems, out_sems = refs
     groups, day_cols = held[5].shape
     unit_rows, resident = held[0].shape[0], high_ref.shape[0]
     (post_copy,) = fetch(arguments[3:4], held[3:4], small_sems)
@@ -123,7 +123,6 @@
         treated = jnp.where(cohort[...] == label, 1.0, 0.0)
         control = jnp.where(cohort[...] > label, 1.0, 0.0)
         raised = jnp.exp(unit_logit[...]) * control
-        raised_units[...] = raised
         left_ref[...] = left_of(raised, treated)
         lane = lax.broadcasted_iota(jnp.int32, (groups, lanes), 1)
         counts = [jnp.sum(value, axis=1, keepdims=True) for value in (raised, treated, control)]
@@ -171,13 +170,14 @@
 
 
 @first_half_only
-def second_kernel(half, unit_devices, panel, sums, raised_days, ends, high_ref, low_ref, *refs):
-    pack, norms, more_high, more_low, held, sems = refs
+def second_kernel(half, unit_order, panel, cohort, unit_logit, sums, raised_days, ends, high_ref, low_ref, *refs):
+    pack, norms, raised_units, more_high, more_low, held, held_cohort, held_logit, sems = refs
     groups, day_cols = raised_days.shape
     unit_rows, resident = panel.shape[0], high_ref.shape[0]
     rest = pl.ds(resident, unit_rows - resident)
-    (copy,) = fetch([panel.at[rest]], [held], sems)
-    total = tree_sum(sums[u] for u in range(unit_devices))
+    copies = fetch([panel.at[rest], cohort, unit_logit], [held, held_cohort, held_logit], sems)
+    odd = lax.rem(lax.axis_index("day"), 2) == 1
+    total = tree_sum(sums[jnp.where(odd, unit, unit_order.index(unit))] for unit in range(len(unit_order)))
 
     def group_rows(first):
         starts = [(first + row) * day_cols for row in range(groups)]
@@ -204,7 +204,9 @@
 
     for here in blocks_of(0, resident):
         multiply(here, high_ref[here, :], low_ref[here, :])
-    copy.wait()
+    wait_all(copies)
+    label = lax.broadcasted_iota(jnp.int32, raised_units.shape, 0)
+    raised_units[...] = jnp.where(held_cohort[...] > label, jnp.exp(held_logit[...]), 0.0)
     for here in blocks_of(resident, unit_rows - resident):
         there = pl.ds(here.start - resident, block_rows)
         high, low = split_panel(held[there, :])
@@ -329,7 +331,13 @@
         )
 
     def over_units(value):
-        return lax.all_to_all(value, "unit", split_axis=0, concat_axis=0, axis_index_groups=[unit_order], tiled=True)
+        members = [
+            [unit * day_devices + day for unit in (range(unit_devices) if day % 2 else unit_order)]
+            for day in range(day_devices)
+        ]
+        return lax.all_to_all(
+            value, ("unit", "day"), split_axis=0, concat_axis=0, axis_index_groups=members, tiled=True
+        )
 
     def call(kernel, shapes, name, args, in_specs=None, out_specs=None, **more):
         return pl.pallas_call(
@@ -353,12 +361,11 @@
     out_sems = pltpu.SemaphoreType.DMA((unit_devices,))
     width = 2 * groups * day_cols + lanes
     in_hbm = pltpu.HBM((unit_devices, 1, width), f32)
-    sums, cross, raised_units, raised_days, time_norm, ends, high, low = call(
+    sums, cross, raised_days, time_norm, ends, high, low = call(
         functools.partial(first_kernel, day_devices * day_cols, half, panel_starts),
         [
             in_hbm,
             pltpu.HBM((groups, unit_rows), f32),
-            ((groups, unit_rows), f32),
             ((groups, day_cols), f32),
             ((groups, lanes), f32),
             ((groups, lanes), f32),
@@ -367,7 +374,7 @@
         "first_product",
         fixed,
         in_specs=[hbm] * 6,
-        out_specs=[hbm, hbm] + [vmem] * 6,
+        out_specs=[hbm, hbm] + [vmem] * 5,
         scratch_shapes=held
         + [
             pltpu.VMEM((1, width), f32),
@@ -382,19 +389,22 @@
         (u * day_devices + d + half, u * day_devices + d) for u in range(unit_devices) for d in range(half)
     ]
     post = lax.ppermute(cross, ("unit", "day"), downward)
-    pack, norms, more_high, more_low = call(
-        functools.partial(second_kernel, half, unit_devices),
+    pack, norms, raised_units, more_high, more_low = call(
+        functools.partial(second_kernel, half, unit_order),
         [
             ((2 * groups, unit_rows + day_cols), f32),
             ((groups, lanes), f32),
+            ((groups, unit_rows), f32),
             *other_terms,
         ],
         "unit_gradient",
-        (fixed[0], over_units(sums), raised_days, ends, high, low),
-        in_specs=[hbm] + [vmem] * 5,
+        (fixed[0], fixed[1], fixed[4], over_units(sums), raised_days, ends, high, low),
+        in_specs=[hbm] * 3 + [vmem] * 5,
         scratch_shapes=[
             pltpu.VMEM((unit_rows - resident, day_cols), f32),
-            pltpu.SemaphoreType.DMA((1,)),
+            held[1],
+            held[4],
+            pltpu.SemaphoreType.DMA((3,)),
         ],
     )
     time_norms = [time_norm]

time: 37.5 us -> 36.5 us (0.973)
  local copies, waits for them, and re-layouts: 0.7 us -> 0 us
  waiting for transfers between devices: 5.56 us -> 6.21 us
  Pallas kernels: 9.52 us -> 8.89 us
    unnamed x4 -> x0, local copies, waits for them, and re-layouts: 0.7 us -> none
    pallas_call x7, Pallas kernels: 9.52 us -> 8.89 us  [call(): pl.pallas_call(kernel, in_specs=in_specs or [vmem] * len(args), out_specs...]
    all_to_all x1, waiting for transfers between devices: 1.61 us -> 2.19 us  [over_units(): lax.all_to_all(value, ('unit', 'day'), split_axis=0, concat_axis=0, axis_...]
where the time goes in v16:
time: 36.5 us; the launch traced here: 36.1 us
  starting transfers between devices  17.9 us (49%)
  Pallas kernels  8.89 us (24%)
  waiting for transfers between devices  6.21 us (17%)
  blocking collectives  2.35 us (6%)
  between operations  0.71 us (2%)
    pallas_call x7, Pallas kernels, call(): pl.pallas_call(kernel, in_specs=in_specs or [vmem] * len(args), out_specs...  8.89 us
    all_to_all x1, starting transfers between devices, over_units(): lax.all_to_all(value, ('unit', 'day'), split_axis=0, concat_axis=0, axis_...  7.83 us
    all_to_all x1, starting transfers between devices, over_first_half(): lax.all_to_all(value, ('unit', 'day'), split_axis=0, concat_axis=0, axis_...  4.34 us
    all_to_all x1, waiting for transfers between devices, over_first_half(): lax.all_to_all(value, ('unit', 'day'), split_axis=0, concat_axis=0, axis_...  3.62 us
    ppermute x2, starting transfers between devices, to_other_half(): return lax.ppermute(value, ('unit', 'day'), pairs)  2.56 us
    all_gather x1, blocking collectives, over_days(): return lax.all_gather(value, 'day', axis_index_groups=halves)  2.35 us
    all_to_all x1, waiting for transfers between devices, over_units(): lax.all_to_all(value, ('unit', 'day'), split_axis=0, concat_axis=0, axis_...  2.19 us
    ppermute x1, starting transfers between devices, local(): time_norms.append(lax.ppermute(time_norm, ('unit', 'day'), pairs))  1.92 us
  transfers between devices with their start and end apart: 6, of which 3 were waited for; matrix products, arithmetic and copies ran while one was open for 0% of the time, Pallas kernels for 10%

profile of v16, /device:TPU:0, one launch (start us, length us, event | category | flops | bytes accessed | tf_op | source)
XLA Modules:
  0.0 36.1 jit_solution(17866459118841879847)
XLA Ops:
  0.6 3.7 %first_product.1 = (f32[8,1,4224]{2,1,0:T(1,128)}, f32[8,4096]{1,0:T(8,128)}, f32[8,256]{1,0:T(8,128)S(1)}, f32[8,128]{1,0:T(8,128)S(1)}, f32[8,128]{1,0:T(8,128...) custom-call(f32[4096,256]{1,0:T(8,128)} %panel.1, s32[1,4096]{1,0:T(1,128)} %bitcast.5, ...), custom_call_target="tpu_custom_call" | custom-call | tf_op jit(solution)/shard_map/first_product/pallas_call | solution.py:343
  4.3 7.8 %all-to-all-start = ((f32[8,1,4224]{2,1,0:T(1,128)}), f32[8,1,4224]{2,1,0:T(1,128)S(1)}, u32[]{:S(2)}, u32[]{:S(2)}) async-start(f32[8,1,4224]{2,1,0:T(1,128)} %get-tuple-element.19), calls=%async_computation | async-start | bytes 270336 | tf_op jit(solution)/shard_map/all_to_all | solution.py:338
  12.1 1.3 %collective-permute-start = (f32[8,4096]{1,0:T(8,128)}, f32[8,4096]{1,0:T(8,128)S(1)}, u32[]{:S(2)}, u32[]{:S(2)}) collective-permute-start(f32[8,4096]{1,0:T(8,128)} %get-tuple-element.25), channel_id=1, source_target_pairs={{2,0},{3,1},{6,4},{7,5},{10,8},{11,9},{14,12},{15,13},{18,16},{19,... | collective-permute-start | bytes 393224 | tf_op jit(solution)/shard_map/ppermute | solution.py:391
  13.4 1.9 %collective-permute-start.1 = (f32[8,128]{1,0:T(8,128)S(1)}, f32[8,128]{1,0:T(8,128)S(1)}, u32[]{:S(2)}, u32[]{:S(2)}) collective-permute-start(f32[8,128]{1,0:T(8,128)S(1)} %get-tuple-element.26.refs_0_), channel_id=1, source_target_pairs={{0,1},{1,0},{4,5},{5,4},{8,9},{9,8},{12,13},{13,12},{16,17},{17,16... | collective-permute-start | bytes 12296 | tf_op jit(solution)/shard_map/ppermute | solution.py:413
  15.4 2.2 %all-to-all-done.sums = f32[8,1,4224]{2,1,0:T(1,128)S(1)} async-done(((f32[8,1,4224]{2,1,0:T(1,128)}), f32[8,1,4224]{2,1,0:T(1,128)S(1)}, u32[]{:S(2)}, u32[]{:S(2)}) %all-to-all-start) | async-done | bytes 135200 | tf_op jit(solution)/shard_map/all_to_all | solution.py:338
  17.5 2.6 %unit_gradient.1 = (f32[16,4352]{1,0:T(8,128)S(1)}, f32[8,128]{1,0:T(8,128)S(1)}, f32[8,4096]{1,0:T(8,128)S(1)}, bf16[1024,256]{1,0:T(8,128)(2,1)S(1)}, bf16[1024,256]{1,0:T(8,128)(2,1)S(1)}) custom-call(f32[4096,256]{1,0:T(8,128)} %panel.1, s32[1,4096]{1,0:T(1,128)} %bitcast.6, f32[8,4096]{1,0:T(8,128)} %unit_logit.1, f32[8,1,4224]{2,1,0:T(1,128)S(1)} %all-to-all-done.sums, ...), custom_call_target="tpu_custom_call" | custom-call | tf_op jit(solution)/shard_map/unit_gradient/pallas_call | solution.py:343
  20.2 0.0 collective-permute-done.1.refs_1_
  20.2 0.0 collective-permute-done.post
  20.2 0.1 join_post.1
  20.3 2.3 %all-gather = f32[32,4352]{1,0:T(8,128)S(1)} all-gather(f32[16,4352]{1,0:T(8,128)S(1)} %join_post.1), channel_id=2, replica_groups={{0,1},{2,3},{4,5},{6,7},{8,9},{10,11},{12,13},{14,15},{16,17},{18,19},{..., dimensions={0}, use_global_device_ids=true | all-gather | bytes 835584 | tf_op jit(solution)/shard_map/all_gather | solution.py:322
  22.6 1.5 %time_gradient.1 = (f32[8,4096]{1,0:T(8,128)S(1)}, f32[8,512]{1,0:T(8,128)S(1)}, f32[16,8,256]{2,1,0:T(8,128)}) custom-call(f32[2,16,4352]{2,1,0:T(8,128)S(1)} %bitcast.4, bf16[3072,256]{1,0:T(8,128)(2,1)S(1)} %get-tuple-element.22.high_ref.refs_1_, bf16[3072,256]{1,0:T(8,128)(2,1)S(1)} %get-tuple-element.23.low_ref.refs_2_, ...), custom_call_target="tpu_custom_call" | custom-call | tf_op jit(solution)/shard_map/time_gradient/pallas_call | solution.py:343
  24.1 4.3 %all-to-all-start.1 = ((f32[16,8,256]{2,1,0:T(8,128)}), f32[16,8,256]{2,1,0:T(8,128)S(1)}, u32[]{:S(2)}, u32[]{:S(2)}) async-start(f32[16,8,256]{2,1,0:T(8,128)} %get-tuple-element.31), calls=%async_computation.1 | async-start | bytes 262144 | tf_op jit(solution)/shard_map/all_to_all | solution.py:329
  28.5 1.3 %collective-permute-start.3 = (f32[8,4096]{1,0:T(8,128)S(1)}, f32[8,4096]{1,0:T(8,128)S(1)}, u32[]{:S(2)}, u32[]{:S(2)}) collective-permute-start(f32[8,4096]{1,0:T(8,128)S(1)} %get-tuple-element.32.scaled), channel_id=1, source_target_pairs={{0,2},{1,3},{4,6},{5,7},{8,10},{9,11},{12,14},{13,15},{16,18},{17,... | collective-permute-start | bytes 393224 | tf_op jit(solution)/shard_map/ppermute | solution.py:318
  29.8 3.6 %all-to-all-done.1.grads = f32[16,8,256]{2,1,0:T(8,128)S(1)} async-done(((f32[16,8,256]{2,1,0:T(8,128)}), f32[16,8,256]{2,1,0:T(8,128)S(1)}, u32[]{:S(2)}, u32[]{:S(2)}) %all-to-all-start.1) | async-done | bytes 131104 | tf_op jit(solution)/shard_map/all_to_all | solution.py:329
  33.4 0.1 unit_totals.1.totals
  33.5 1.3 %collective-permute-start.2 = (f32[8,128]{1,0:T(8,128)S(1)}, f32[8,128]{1,0:T(8,128)S(1)}, u32[]{:S(2)}, u32[]{:S(2)}) collective-permute-start(f32[8,128]{1,0:T(8,128)S(1)} %unit_totals.1.totals), channel_id=1, source_target_pairs={{0,2},{1,3},{4,6},{5,7},{8,10},{9,11},{12,14},{13,15},{16,18},{17,... | collective-permute-start | bytes 12296 | tf_op jit(solution)/shard_map/ppermute | solution.py:318
  34.8 0.9 %scale_weights.1 = (f32[8,4096]{1,0:T(8,128)}, f32[8,256]{1,0:T(8,128)}) custom-call(f32[8,128]{1,0:T(8,128)S(1)} %unit_totals.1.totals, f32[8,4096]{1,0:T(8,128)S(1)} %get-tuple-element.32.scaled, f32[16,8,256]{2,1,0:T(8,128)S(1)} %all-to-all-done.1.grads, f32[8,512]{1,0:T(8,128)S(1)} %get-tuple-element.33.lam, ...), custom_call_target="tpu_custom_call" | custom-call | tf_op jit(solution)/shard_map/scale_weights/pallas_call | solution.py:343
  35.7 0.0 collective-permute-done.3.sent_scaled
  35.7 0.4 %collective-permute-done.2.sent_totals = f32[8,128]{1,0:T(8,128)S(1)} collective-permute-done((f32[8,128]{1,0:T(8,128)S(1)}, f32[8,128]{1,0:T(8,128)S(1)}, u32[]{:S(2)}, u32[]{:S(2)}) %collective-permute-start.2) | collective-permute-done | bytes 4128 | tf_op jit(solution)/shard_map/ppermute | solution.py:318
  (1 shorter events, 0.0 us)
Async XLA Ops:
  4.3 13.2 %all-to-all-start = ((f32[8,1,4224]{2,1,0:T(1,128)}), f32[8,1,4224]{2,1,0:T(1,128)S(1)}, u32[]{:S(2)}, u32[]{:S(2)}) async-start(f32[8,1,4224]{2,1,0:T(1,128)} %get-tuple-element.19), calls=%async_computation | async-start | bytes 270336 | tf_op jit(solution)/shard_map/all_to_all | solution.py:338
  12.1 8.0 %collective-permute-start = (f32[8,4096]{1,0:T(8,128)}, f32[8,4096]{1,0:T(8,128)S(1)}, u32[]{:S(2)}, u32[]{:S(2)}) collective-permute-start(f32[8,4096]{1,0:T(8,128)} %get-tuple-element.25), channel_id=1, source_target_pairs={{2,0},{3,1},{6,4},{7,5},{10,8},{11,9},{14,12},{15,13},{18,16},{19,... | collective-permute-start | bytes 393224 | tf_op jit(solution)/shard_map/ppermute | solution.py:391
  13.4 6.7 %collective-permute-start.1 = (f32[8,128]{1,0:T(8,128)S(1)}, f32[8,128]{1,0:T(8,128)S(1)}, u32[]{:S(2)}, u32[]{:S(2)}) collective-permute-start(f32[8,128]{1,0:T(8,128)S(1)} %get-tuple-element.26.refs_0_), channel_id=1, source_target_pairs={{0,1},{1,0},{4,5},{5,4},{8,9},{9,8},{12,13},{13,12},{16,17},{17,16... | collective-permute-start | bytes 12296 | tf_op jit(solution)/shard_map/ppermute | solution.py:413
  24.1 9.3 %all-to-all-start.1 = ((f32[16,8,256]{2,1,0:T(8,128)}), f32[16,8,256]{2,1,0:T(8,128)S(1)}, u32[]{:S(2)}, u32[]{:S(2)}) async-start(f32[16,8,256]{2,1,0:T(8,128)} %get-tuple-element.31), calls=%async_computation.1 | async-start | bytes 262144 | tf_op jit(solution)/shard_map/all_to_all | solution.py:329
  28.5 7.2 %collective-permute-start.3 = (f32[8,4096]{1,0:T(8,128)S(1)}, f32[8,4096]{1,0:T(8,128)S(1)}, u32[]{:S(2)}, u32[]{:S(2)}) collective-permute-start(f32[8,4096]{1,0:T(8,128)S(1)} %get-tuple-element.32.scaled), channel_id=1, source_target_pairs={{0,2},{1,3},{4,6},{5,7},{8,10},{9,11},{12,14},{13,15},{16,18},{17,... | collective-permute-start | bytes 393224 | tf_op jit(solution)/shard_map/ppermute | solution.py:318
  33.5 2.6 %collective-permute-start.2 = (f32[8,128]{1,0:T(8,128)S(1)}, f32[8,128]{1,0:T(8,128)S(1)}, u32[]{:S(2)}, u32[]{:S(2)}) collective-permute-start(f32[8,128]{1,0:T(8,128)S(1)} %unit_totals.1.totals), channel_id=1, source_target_pairs={{0,2},{1,3},{4,6},{5,7},{8,10},{9,11},{12,14},{13,15},{16,18},{17,... | collective-permute-start | bytes 12296 | tf_op jit(solution)/shard_map/ppermute | solution.py:318

commit v17 on v16

--- a/solution.py
+++ b/solution.py
@@ -162,22 +162,25 @@
         left = left_of(after / (all_count - post_start).astype(f32))
         for start, rows, copy in parts:
             copy.wait()
-            for here in blocks_of(start, rows):
+
+            @pl.loop(start // block_rows, (start + rows) // block_rows)
+            def _(block):
+                here = pl.ds(pl.multiple_of(block * block_rows, block_rows), block_rows)
                 cross_block[:, here] = add_terms(days_dot(left, *split_panel(panel[here, :])), groups)
+
         sends = fetch([cross_block], [cross], out_sems)
         wait_all(day_copies)
         wait_all(sends)
 
 
 @first_half_only
-def second_kernel(half, unit_order, panel, cohort, unit_logit, sums, raised_days, ends, high_ref, low_ref, *refs):
+def second_kernel(half, unit_devices, panel, cohort, unit_logit, sums, raised_days, ends, high_ref, low_ref, *refs):
     pack, norms, raised_units, more_high, more_low, held, held_cohort, held_logit, sems = refs
     groups, day_cols = raised_days.shape
     unit_rows, resident = panel.shape[0], high_ref.shape[0]
     rest = pl.ds(resident, unit_rows - resident)
     copies = fetch([panel.at[rest], cohort, unit_logit], [held, held_cohort, held_logit], sems)
-    odd = lax.rem(lax.axis_index("day"), 2) == 1
-    total = tree_sum(sums[jnp.where(odd, unit, unit_order.index(unit))] for unit in range(len(unit_order)))
+    total = tree_sum(sums[u] for u in range(unit_devices))
 
     def group_rows(first):
         starts = [(first + row) * day_cols for row in range(groups)]
@@ -202,8 +205,11 @@
         pack[:groups, here] = add_terms(product, groups)
         pack[groups:, here] = add_terms(product, groups, 1)
 
-    for here in blocks_of(0, resident):
+    @pl.loop(0, resident // block_rows)
+    def _(block):
+        here = pl.ds(pl.multiple_of(block * block_rows, block_rows), block_rows)
         multiply(here, high_ref[here, :], low_ref[here, :])
+
     wait_all(copies)
     label = lax.broadcasted_iota(jnp.int32, raised_units.shape, 0)
     raised_units[...] = jnp.where(held_cohort[...] > label, jnp.exp(held_logit[...]), 0.0)
@@ -331,13 +337,7 @@
         )
 
     def over_units(value):
-        members = [
-            [unit * day_devices + day for unit in (range(unit_devices) if day % 2 else unit_order)]
-            for day in range(day_devices)
-        ]
-        return lax.all_to_all(
-            value, ("unit", "day"), split_axis=0, concat_axis=0, axis_index_groups=members, tiled=True
-        )
+        return lax.all_to_all(value, "unit", split_axis=0, concat_axis=0, axis_index_groups=[unit_order], tiled=True)
 
     def call(kernel, shapes, name, args, in_specs=None, out_specs=None, **more):
         return pl.pallas_call(
@@ -390,7 +390,7 @@
     ]
     post = lax.ppermute(cross, ("unit", "day"), downward)
     pack, norms, raised_units, more_high, more_low = call(
-        functools.partial(second_kernel, half, unit_order),
+        functools.partial(second_kernel, half, unit_devices),
         [
             ((2 * groups, unit_rows + day_cols), f32),
             ((groups, lanes), f32),

time: 36.5 us -> 35.9 us (0.984)
  starting transfers between devices: 17.9 us -> 18.5 us
  waiting for transfers between devices: 6.21 us -> 5.64 us
  Pallas kernels: 8.89 us -> 8.46 us
    all_to_all x1, waiting for transfers between devices: 2.19 us -> 1.61 us  [over_units(): lax.all_to_all(value, 'unit', split_axis=0, concat_axis=0, axis_index_gro...]
    all_to_all x1, starting transfers between devices: 4.34 us -> 4.87 us  [over_first_half(): lax.all_to_all(value, ('unit', 'day'), split_axis=0, concat_axis=0, axis_...]
    pallas_call x7, Pallas kernels: 8.89 us -> 8.46 us  [call(): pl.pallas_call(kernel, in_specs=in_specs or [vmem] * len(args), out_specs...]
  transfers between devices with their start and end apart: 6 -> 6, of which waited for: 3 -> 3; matrix products, arithmetic and copies ran while one was open for 0% -> 0% of each run, Pallas kernels for 10% -> 9%
where the time goes in v17:
time: 35.9 us; the launch traced here: 35.5 us
  starting transfers between devices  18.5 us (52%)
  Pallas kernels  8.46 us (24%)
  waiting for transfers between devices  5.64 us (16%)
  blocking collectives  2.2 us (6%)
  between operations  0.7 us (2%)
    pallas_call x7, Pallas kernels, call(): pl.pallas_call(kernel, in_specs=in_specs or [vmem] * len(args), out_specs...  8.46 us
    all_to_all x1, starting transfers between devices, over_units(): lax.all_to_all(value, 'unit', split_axis=0, concat_axis=0, axis_index_gro...  7.83 us
    all_to_all x1, starting transfers between devices, over_first_half(): lax.all_to_all(value, ('unit', 'day'), split_axis=0, concat_axis=0, axis_...  4.87 us
    all_to_all x1, waiting for transfers between devices, over_first_half(): lax.all_to_all(value, ('unit', 'day'), split_axis=0, concat_axis=0, axis_...  3.62 us
    ppermute x2, starting transfers between devices, to_other_half(): return lax.ppermute(value, ('unit', 'day'), pairs)  2.56 us
    all_gather x1, blocking collectives, over_days(): return lax.all_gather(value, 'day', axis_index_groups=halves)  2.2 us
    ppermute x1, starting transfers between devices, local(): time_norms.append(lax.ppermute(time_norm, ('unit', 'day'), pairs))  1.92 us
    all_to_all x1, waiting for transfers between devices, over_units(): lax.all_to_all(value, 'unit', split_axis=0, concat_axis=0, axis_index_gro...  1.61 us
  transfers between devices with their start and end apart: 6, of which 3 were waited for; matrix products, arithmetic and copies ran while one was open for 0% of the time, Pallas kernels for 9%

profile of v17, /device:TPU:0, one launch (start us, length us, event | category | flops | bytes accessed | tf_op | source)
XLA Modules:
  0.0 35.5 jit_solution(6954722733360315939)
XLA Ops:
  0.6 3.7 %first_product.1 = (f32[8,1,4224]{2,1,0:T(1,128)}, f32[8,4096]{1,0:T(8,128)}, f32[8,256]{1,0:T(8,128)S(1)}, f32[8,128]{1,0:T(8,128)S(1)}, f32[8,128]{1,0:T(8,128...) custom-call(f32[4096,256]{1,0:T(8,128)} %panel.1, s32[1,4096]{1,0:T(1,128)} %bitcast.5, ...), custom_call_target="tpu_custom_call" | custom-call | tf_op jit(solution)/shard_map/first_product/pallas_call | solution.py:343
  4.3 7.8 %all-to-all-start = ((f32[8,1,4224]{2,1,0:T(1,128)}), f32[8,1,4224]{2,1,0:T(1,128)S(1)}, u32[]{:S(2)}, u32[]{:S(2)}) async-start(f32[8,1,4224]{2,1,0:T(1,128)} %get-tuple-element.19), calls=%async_computation | async-start | bytes 270336 | tf_op jit(solution)/shard_map/all_to_all | solution.py:340
  12.1 1.3 %collective-permute-start = (f32[8,4096]{1,0:T(8,128)}, f32[8,4096]{1,0:T(8,128)S(1)}, u32[]{:S(2)}, u32[]{:S(2)}) collective-permute-start(f32[8,4096]{1,0:T(8,128)} %get-tuple-element.25), channel_id=1, source_target_pairs={{2,0},{3,1},{6,4},{7,5},{10,8},{11,9},{14,12},{15,13},{18,16},{19,... | collective-permute-start | bytes 393224 | tf_op jit(solution)/shard_map/ppermute | solution.py:391
  13.4 1.9 %collective-permute-start.1 = (f32[8,128]{1,0:T(8,128)S(1)}, f32[8,128]{1,0:T(8,128)S(1)}, u32[]{:S(2)}, u32[]{:S(2)}) collective-permute-start(f32[8,128]{1,0:T(8,128)S(1)} %get-tuple-element.26.refs_0_), channel_id=1, source_target_pairs={{0,1},{1,0},{4,5},{5,4},{8,9},{9,8},{12,13},{13,12},{16,17},{17,16... | collective-permute-start | bytes 12296 | tf_op jit(solution)/shard_map/ppermute | solution.py:413
  15.4 1.6 %all-to-all-done.sums = f32[8,1,4224]{2,1,0:T(1,128)S(1)} async-done(((f32[8,1,4224]{2,1,0:T(1,128)}), f32[8,1,4224]{2,1,0:T(1,128)S(1)}, u32[]{:S(2)}, u32[]{:S(2)}) %all-to-all-start) | async-done | bytes 135200 | tf_op jit(solution)/shard_map/all_to_all | solution.py:340
  17.0 2.2 %unit_gradient.1 = (f32[16,4352]{1,0:T(8,128)S(1)}, f32[8,128]{1,0:T(8,128)S(1)}, f32[8,4096]{1,0:T(8,128)S(1)}, bf16[1024,256]{1,0:T(8,128)(2,1)S(1)}, bf16[1024,256]{1,0:T(8,128)(2,1)S(1)}) custom-call(f32[4096,256]{1,0:T(8,128)} %panel.1, s32[1,4096]{1,0:T(1,128)} %bitcast.6, f32[8,4096]{1,0:T(8,128)} %unit_logit.1, f32[8,1,4224]{2,1,0:T(1,128)S(1)} %all-to-all-done.sums, ...), custom_call_target="tpu_custom_call" | custom-call | tf_op jit(solution)/shard_map/unit_gradient/pallas_call | solution.py:343
  19.2 0.0 collective-permute-done.1.refs_1_
  19.2 0.0 collective-permute-done.post
  19.2 0.1 join_post.1
  19.3 2.2 %all-gather = f32[32,4352]{1,0:T(8,128)S(1)} all-gather(f32[16,4352]{1,0:T(8,128)S(1)} %join_post.1), channel_id=2, replica_groups={{0,1},{2,3},{4,5},{6,7},{8,9},{10,11},{12,13},{14,15},{16,17},{18,19},{..., dimensions={0}, use_global_device_ids=true | all-gather | bytes 835584 | tf_op jit(solution)/shard_map/all_gather | solution.py:328
  21.5 1.5 %time_gradient.1 = (f32[8,4096]{1,0:T(8,128)S(1)}, f32[8,512]{1,0:T(8,128)S(1)}, f32[16,8,256]{2,1,0:T(8,128)}) custom-call(f32[2,16,4352]{2,1,0:T(8,128)S(1)} %bitcast.4, bf16[3072,256]{1,0:T(8,128)(2,1)S(1)} %get-tuple-element.22.high_ref.refs_1_, bf16[3072,256]{1,0:T(8,128)(2,1)S(1)} %get-tuple-element.23.low_ref.refs_2_, ...), custom_call_target="tpu_custom_call" | custom-call | tf_op jit(solution)/shard_map/time_gradient/pallas_call | solution.py:343
  23.0 4.9 %all-to-all-start.1 = ((f32[16,8,256]{2,1,0:T(8,128)}), f32[16,8,256]{2,1,0:T(8,128)S(1)}, u32[]{:S(2)}, u32[]{:S(2)}) async-start(f32[16,8,256]{2,1,0:T(8,128)} %get-tuple-element.31), calls=%async_computation.1 | async-start | bytes 262144 | tf_op jit(solution)/shard_map/all_to_all | solution.py:335
  27.9 1.3 %collective-permute-start.3 = (f32[8,4096]{1,0:T(8,128)S(1)}, f32[8,4096]{1,0:T(8,128)S(1)}, u32[]{:S(2)}, u32[]{:S(2)}) collective-permute-start(f32[8,4096]{1,0:T(8,128)S(1)} %get-tuple-element.32.scaled), channel_id=1, source_target_pairs={{0,2},{1,3},{4,6},{5,7},{8,10},{9,11},{12,14},{13,15},{16,18},{17,... | collective-permute-start | bytes 393224 | tf_op jit(solution)/shard_map/ppermute | solution.py:324
  29.2 3.6 %all-to-all-done.1.grads = f32[16,8,256]{2,1,0:T(8,128)S(1)} async-done(((f32[16,8,256]{2,1,0:T(8,128)}), f32[16,8,256]{2,1,0:T(8,128)S(1)}, u32[]{:S(2)}, u32[]{:S(2)}) %all-to-all-start.1) | async-done | bytes 131104 | tf_op jit(solution)/shard_map/all_to_all | solution.py:335
  32.8 0.1 unit_totals.1.totals
  32.9 1.3 %collective-permute-start.2 = (f32[8,128]{1,0:T(8,128)S(1)}, f32[8,128]{1,0:T(8,128)S(1)}, u32[]{:S(2)}, u32[]{:S(2)}) collective-permute-start(f32[8,128]{1,0:T(8,128)S(1)} %unit_totals.1.totals), channel_id=1, source_target_pairs={{0,2},{1,3},{4,6},{5,7},{8,10},{9,11},{12,14},{13,15},{16,18},{17,... | collective-permute-start | bytes 12296 | tf_op jit(solution)/shard_map/ppermute | solution.py:324
  34.2 0.9 %scale_weights.1 = (f32[8,4096]{1,0:T(8,128)}, f32[8,256]{1,0:T(8,128)}) custom-call(f32[8,128]{1,0:T(8,128)S(1)} %unit_totals.1.totals, f32[8,4096]{1,0:T(8,128)S(1)} %get-tuple-element.32.scaled, f32[16,8,256]{2,1,0:T(8,128)S(1)} %all-to-all-done.1.grads, f32[8,512]{1,0:T(8,128)S(1)} %get-tuple-element.33.lam, ...), custom_call_target="tpu_custom_call" | custom-call | tf_op jit(solution)/shard_map/scale_weights/pallas_call | solution.py:343
  35.1 0.0 collective-permute-done.3.sent_scaled
  35.1 0.4 %collective-permute-done.2.sent_totals = f32[8,128]{1,0:T(8,128)S(1)} collective-permute-done((f32[8,128]{1,0:T(8,128)S(1)}, f32[8,128]{1,0:T(8,128)S(1)}, u32[]{:S(2)}, u32[]{:S(2)}) %collective-permute-start.2) | collective-permute-done | bytes 4128 | tf_op jit(solution)/shard_map/ppermute | solution.py:324
  (1 shorter events, 0.0 us)
Async XLA Ops:
  4.3 12.7 %all-to-all-start = ((f32[8,1,4224]{2,1,0:T(1,128)}), f32[8,1,4224]{2,1,0:T(1,128)S(1)}, u32[]{:S(2)}, u32[]{:S(2)}) async-start(f32[8,1,4224]{2,1,0:T(1,128)} %get-tuple-element.19), calls=%async_computation | async-start | bytes 270336 | tf_op jit(solution)/shard_map/all_to_all | solution.py:340
  12.1 7.1 %collective-permute-start = (f32[8,4096]{1,0:T(8,128)}, f32[8,4096]{1,0:T(8,128)S(1)}, u32[]{:S(2)}, u32[]{:S(2)}) collective-permute-start(f32[8,4096]{1,0:T(8,128)} %get-tuple-element.25), channel_id=1, source_target_pairs={{2,0},{3,1},{6,4},{7,5},{10,8},{11,9},{14,12},{15,13},{18,16},{19,... | collective-permute-start | bytes 393224 | tf_op jit(solution)/shard_map/ppermute | solution.py:391
  13.4 5.8 %collective-permute-start.1 = (f32[8,128]{1,0:T(8,128)S(1)}, f32[8,128]{1,0:T(8,128)S(1)}, u32[]{:S(2)}, u32[]{:S(2)}) collective-permute-start(f32[8,128]{1,0:T(8,128)S(1)} %get-tuple-element.26.refs_0_), channel_id=1, source_target_pairs={{0,1},{1,0},{4,5},{5,4},{8,9},{9,8},{12,13},{13,12},{16,17},{17,16... | collective-permute-start | bytes 12296 | tf_op jit(solution)/shard_map/ppermute | solution.py:413
  23.0 9.8 %all-to-all-start.1 = ((f32[16,8,256]{2,1,0:T(8,128)}), f32[16,8,256]{2,1,0:T(8,128)S(1)}, u32[]{:S(2)}, u32[]{:S(2)}) async-start(f32[16,8,256]{2,1,0:T(8,128)} %get-tuple-element.31), calls=%async_computation.1 | async-start | bytes 262144 | tf_op jit(solution)/shard_map/all_to_all | solution.py:335
  27.9 7.2 %collective-permute-start.3 = (f32[8,4096]{1,0:T(8,128)S(1)}, f32[8,4096]{1,0:T(8,128)S(1)}, u32[]{:S(2)}, u32[]{:S(2)}) collective-permute-start(f32[8,4096]{1,0:T(8,128)S(1)} %get-tuple-element.32.scaled), channel_id=1, source_target_pairs={{0,2},{1,3},{4,6},{5,7},{8,10},{9,11},{12,14},{13,15},{16,18},{17,... | collective-permute-start | bytes 393224 | tf_op jit(solution)/shard_map/ppermute | solution.py:324
  32.9 2.6 %collective-permute-start.2 = (f32[8,128]{1,0:T(8,128)S(1)}, f32[8,128]{1,0:T(8,128)S(1)}, u32[]{:S(2)}, u32[]{:S(2)}) collective-permute-start(f32[8,128]{1,0:T(8,128)S(1)} %unit_totals.1.totals), channel_id=1, source_target_pairs={{0,2},{1,3},{4,6},{5,7},{8,10},{9,11},{12,14},{13,15},{16,18},{17,... | collective-permute-start | bytes 12296 | tf_op jit(solution)/shard_map/ppermute | solution.py:324

commit v18 on v17

--- a/solution.py
+++ b/solution.py
@@ -87,6 +87,10 @@
     parts = [pl.ds(*span) for span in spans]
     copies = fetch([source.at[here] for here in parts], [target.at[here] for here in parts], sems)
     return [(*span, copy) for span, copy in zip(spans, copies)]
+
+
+def block_at(index):
+    return pl.ds(pl.multiple_of(index * block_rows, block_rows), block_rows)
 
 
 def blocks_of(start, rows):
@@ -162,12 +166,8 @@
         left = left_of(after / (all_count - post_start).astype(f32))
         for start, rows, copy in parts:
             copy.wait()
-
-            @pl.loop(start // block_rows, (start + rows) // block_rows)
-            def _(block):
-                here = pl.ds(pl.multiple_of(block * block_rows, block_rows), block_rows)
+            for here in blocks_of(start, rows):
                 cross_block[:, here] = add_terms(days_dot(left, *split_panel(panel[here, :])), groups)
-
         sends = fetch([cross_block], [cross], out_sems)
         wait_all(day_copies)
         wait_all(sends)
@@ -207,18 +207,20 @@
 
     @pl.loop(0, resident // block_rows)
     def _(block):
-        here = pl.ds(pl.multiple_of(block * block_rows, block_rows), block_rows)
+        here = block_at(block)
         multiply(here, high_ref[here, :], low_ref[here, :])
 
     wait_all(copies)
     label = lax.broadcasted_iota(jnp.int32, raised_units.shape, 0)
     raised_units[...] = jnp.where(held_cohort[...] > label, jnp.exp(held_logit[...]), 0.0)
-    for here in blocks_of(resident, unit_rows - resident):
-        there = pl.ds(here.start - resident, block_rows)
+
+    @pl.loop(0, (unit_rows - resident) // block_rows)
+    def _(block):
+        there = block_at(block)
         high, low = split_panel(held[there, :])
         more_high[there, :] = high
         more_low[there, :] = low
-        multiply(here, high, low)
+        multiply(block_at(block + resident // block_rows), high, low)
 
 
 @first_half_only
@@ -244,22 +246,28 @@
     me = lax.rem(lax.axis_index("day"), half)
     for day in range(half):
         lam[:, day * day_cols : (day + 1) * day_cols] = parts[day][:groups, unit_rows:]
-    time_grad = jnp.zeros((groups, day_cols), f32)
-    new_sum = jnp.zeros((groups, 1), f32)
-    for start in range(0, unit_rows, block_rows):
-        here = pl.ds(start, block_rows)
+
+    def add_block(here, high, low, sums):
+        time_grad, new_sum = sums
         whole = tree_sum(ref[:, here] for ref in parts)
         raised = raised_units[:, here]
         new = raised * over_unit * jnp.exp(whole[:groups] * factor)
-        new_sum += jnp.sum(new, axis=1, keepdims=True)
         scaled[:, here] = new * ctrl_count
         left = left_of(jnp.where(raised > 0.0, whole[groups:], 0.0))
-        if start < resident:
-            high, low = high_ref[here, :], low_ref[here, :]
-        else:
-            there = pl.ds(start - resident, block_rows)
-            high, low = more_high[there, :], more_low[there, :]
-        time_grad += add_terms(rows_dot(left, high, low), groups)
+        return time_grad + add_terms(rows_dot(left, high, low), groups), new_sum + new
+
+    def add_resident(block, sums):
+        here = block_at(block)
+        return add_block(here, high_ref[here, :], low_ref[here, :], sums)
+
+    def add_other(block, sums):
+        there = block_at(block)
+        return add_block(block_at(block + resident // block_rows), more_high[there, :], more_low[there, :], sums)
+
+    sums = jnp.zeros((groups, day_cols), f32), jnp.zeros((groups, block_rows), f32)
+    sums = lax.fori_loop(0, resident // block_rows, add_resident, sums)
+    time_grad, new_sum = lax.fori_loop(0, (unit_rows - resident) // block_rows, add_other, sums)
+    new_sum = jnp.sum(new_sum, axis=1, keepdims=True)
     lane = lax.broadcasted_iota(jnp.int32, (groups, day_cols), 1)
     spare = (lane == day_cols - 1) & (me == half - 1)
     block[...] = jnp.where(spare, new_sum, time_grad)

time: 35.9 us -> 36.8 us (1.025)
  Pallas kernels: 8.46 us -> 9.5 us
    pallas_call x7, Pallas kernels: 8.46 us -> 9.5 us  [call(): pl.pallas_call(kernel, in_specs=in_specs or [vmem] * len(args), out_specs...]
where the time goes in v18:
time: 36.8 us; the launch traced here: 36.4 us
  starting transfers between devices  18.3 us (50%)
  Pallas kernels  9.5 us (26%)
  waiting for transfers between devices  5.63 us (15%)
  blocking collectives  2.2 us (6%)
  between operations  0.71 us (2%)
    pallas_call x7, Pallas kernels, call(): pl.pallas_call(kernel, in_specs=in_specs or [vmem] * len(args), out_specs...  9.5 us
    all_to_all x1, starting transfers between devices, over_units(): lax.all_to_all(value, 'unit', split_axis=0, concat_axis=0, axis_index_gro...  7.83 us
    all_to_all x1, starting transfers between devices, over_first_half(): lax.all_to_all(value, ('unit', 'day'), split_axis=0, concat_axis=0, axis_...  4.75 us
    all_to_all x1, waiting for transfers between devices, over_first_half(): lax.all_to_all(value, ('unit', 'day'), split_axis=0, concat_axis=0, axis_...  3.62 us
    ppermute x2, starting transfers between devices, to_other_half(): return lax.ppermute(value, ('unit', 'day'), pairs)  2.56 us
    all_gather x1, blocking collectives, over_days(): return lax.all_gather(value, 'day', axis_index_groups=halves)  2.2 us
    ppermute x1, starting transfers between devices, local(): time_norms.append(lax.ppermute(time_norm, ('unit', 'day'), pairs))  1.92 us
    all_to_all x1, waiting for transfers between devices, over_units(): lax.all_to_all(value, 'unit', split_axis=0, concat_axis=0, axis_index_gro...  1.61 us
  transfers between devices with their start and end apart: 6, of which 3 were waited for; matrix products, arithmetic and copies ran while one was open for 0% of the time, Pallas kernels for 9%

profile of v18, /device:TPU:0, one launch (start us, length us, event | category | flops | bytes accessed | tf_op | source)
XLA Modules:
  0.0 36.4 jit_solution(1084425780778008983)
XLA Ops:
  0.6 3.7 %first_product.1 = (f32[8,1,4224]{2,1,0:T(1,128)}, f32[8,4096]{1,0:T(8,128)}, f32[8,256]{1,0:T(8,128)S(1)}, f32[8,128]{1,0:T(8,128)S(1)}, f32[8,128]{1,0:T(8,128...) custom-call(f32[4096,256]{1,0:T(8,128)} %panel.1, s32[1,4096]{1,0:T(1,128)} %bitcast.5, ...), custom_call_target="tpu_custom_call" | custom-call | tf_op jit(solution)/shard_map/first_product/pallas_call | solution.py:351
  4.3 7.8 %all-to-all-start = ((f32[8,1,4224]{2,1,0:T(1,128)}), f32[8,1,4224]{2,1,0:T(1,128)S(1)}, u32[]{:S(2)}, u32[]{:S(2)}) async-start(f32[8,1,4224]{2,1,0:T(1,128)} %get-tuple-element.19), calls=%async_computation | async-start | bytes 270336 | tf_op jit(solution)/shard_map/all_to_all | solution.py:348
  12.1 1.3 %collective-permute-start = (f32[8,4096]{1,0:T(8,128)}, f32[8,4096]{1,0:T(8,128)S(1)}, u32[]{:S(2)}, u32[]{:S(2)}) collective-permute-start(f32[8,4096]{1,0:T(8,128)} %get-tuple-element.25), channel_id=1, source_target_pairs={{2,0},{3,1},{6,4},{7,5},{10,8},{11,9},{14,12},{15,13},{18,16},{19,... | collective-permute-start | bytes 393224 | tf_op jit(solution)/shard_map/ppermute | solution.py:399
  13.4 1.9 %collective-permute-start.1 = (f32[8,128]{1,0:T(8,128)S(1)}, f32[8,128]{1,0:T(8,128)S(1)}, u32[]{:S(2)}, u32[]{:S(2)}) collective-permute-start(f32[8,128]{1,0:T(8,128)S(1)} %get-tuple-element.26.refs_0_), channel_id=1, source_target_pairs={{0,1},{1,0},{4,5},{5,4},{8,9},{9,8},{12,13},{13,12},{16,17},{17,16... | collective-permute-start | bytes 12296 | tf_op jit(solution)/shard_map/ppermute | solution.py:421
  15.4 1.6 %all-to-all-done.sums = f32[8,1,4224]{2,1,0:T(1,128)S(1)} async-done(((f32[8,1,4224]{2,1,0:T(1,128)}), f32[8,1,4224]{2,1,0:T(1,128)S(1)}, u32[]{:S(2)}, u32[]{:S(2)}) %all-to-all-start) | async-done | bytes 135200 | tf_op jit(solution)/shard_map/all_to_all | solution.py:348
  17.0 2.3 %unit_gradient.1 = (f32[16,4352]{1,0:T(8,128)S(1)}, f32[8,128]{1,0:T(8,128)S(1)}, f32[8,4096]{1,0:T(8,128)S(1)}, bf16[1024,256]{1,0:T(8,128)(2,1)S(1)}, bf16[1024,256]{1,0:T(8,128)(2,1)S(1)}) custom-call(f32[4096,256]{1,0:T(8,128)} %panel.1, s32[1,4096]{1,0:T(1,128)} %bitcast.6, f32[8,4096]{1,0:T(8,128)} %unit_logit.1, f32[8,1,4224]{2,1,0:T(1,128)S(1)} %all-to-all-done.sums, ...), custom_call_target="tpu_custom_call" | custom-call | tf_op jit(solution)/shard_map/unit_gradient/pallas_call | solution.py:351
  19.3 0.0 collective-permute-done.1.refs_1_
  19.3 0.0 collective-permute-done.post
  19.3 0.1 join_post.1
  19.4 2.2 %all-gather = f32[32,4352]{1,0:T(8,128)S(1)} all-gather(f32[16,4352]{1,0:T(8,128)S(1)} %join_post.1), channel_id=2, replica_groups={{0,1},{2,3},{4,5},{6,7},{8,9},{10,11},{12,13},{14,15},{16,17},{18,19},{..., dimensions={0}, use_global_device_ids=true | all-gather | bytes 835584 | tf_op jit(solution)/shard_map/all_gather | solution.py:336
  21.6 2.4 %time_gradient.1 = (f32[8,4096]{1,0:T(8,128)S(1)}, f32[8,512]{1,0:T(8,128)S(1)}, f32[16,8,256]{2,1,0:T(8,128)}) custom-call(f32[2,16,4352]{2,1,0:T(8,128)S(1)} %bitcast.4, bf16[3072,256]{1,0:T(8,128)(2,1)S(1)} %get-tuple-element.22.high_ref.refs_1_, bf16[3072,256]{1,0:T(8,128)(2,1)S(1)} %get-tuple-element.23.low_ref.refs_2_, ...), custom_call_target="tpu_custom_call" | custom-call | tf_op jit(solution)/shard_map/time_gradient/pallas_call | solution.py:351
  24.0 4.8 %all-to-all-start.1 = ((f32[16,8,256]{2,1,0:T(8,128)}), f32[16,8,256]{2,1,0:T(8,128)S(1)}, u32[]{:S(2)}, u32[]{:S(2)}) async-start(f32[16,8,256]{2,1,0:T(8,128)} %get-tuple-element.31), calls=%async_computation.1 | async-start | bytes 262144 | tf_op jit(solution)/shard_map/all_to_all | solution.py:343
  28.8 1.3 %collective-permute-start.3 = (f32[8,4096]{1,0:T(8,128)S(1)}, f32[8,4096]{1,0:T(8,128)S(1)}, u32[]{:S(2)}, u32[]{:S(2)}) collective-permute-start(f32[8,4096]{1,0:T(8,128)S(1)} %get-tuple-element.32.scaled), channel_id=1, source_target_pairs={{0,2},{1,3},{4,6},{5,7},{8,10},{9,11},{12,14},{13,15},{16,18},{17,... | collective-permute-start | bytes 393224 | tf_op jit(solution)/shard_map/ppermute | solution.py:332
  30.1 3.6 %all-to-all-done.1.grads = f32[16,8,256]{2,1,0:T(8,128)S(1)} async-done(((f32[16,8,256]{2,1,0:T(8,128)}), f32[16,8,256]{2,1,0:T(8,128)S(1)}, u32[]{:S(2)}, u32[]{:S(2)}) %all-to-all-start.1) | async-done | bytes 131104 | tf_op jit(solution)/shard_map/all_to_all | solution.py:343
  33.7 0.1 unit_totals.1.totals
  33.8 1.3 %collective-permute-start.2 = (f32[8,128]{1,0:T(8,128)S(1)}, f32[8,128]{1,0:T(8,128)S(1)}, u32[]{:S(2)}, u32[]{:S(2)}) collective-permute-start(f32[8,128]{1,0:T(8,128)S(1)} %unit_totals.1.totals), channel_id=1, source_target_pairs={{0,2},{1,3},{4,6},{5,7},{8,10},{9,11},{12,14},{13,15},{16,18},{17,... | collective-permute-start | bytes 12296 | tf_op jit(solution)/shard_map/ppermute | solution.py:332
  35.1 0.9 %scale_weights.1 = (f32[8,4096]{1,0:T(8,128)}, f32[8,256]{1,0:T(8,128)}) custom-call(f32[8,128]{1,0:T(8,128)S(1)} %unit_totals.1.totals, f32[8,4096]{1,0:T(8,128)S(1)} %get-tuple-element.32.scaled, f32[16,8,256]{2,1,0:T(8,128)S(1)} %all-to-all-done.1.grads, f32[8,512]{1,0:T(8,128)S(1)} %get-tuple-element.33.lam, ...), custom_call_target="tpu_custom_call" | custom-call | tf_op jit(solution)/shard_map/scale_weights/pallas_call | solution.py:351
  36.0 0.0 collective-permute-done.3.sent_scaled
  36.0 0.4 %collective-permute-done.2.sent_totals = f32[8,128]{1,0:T(8,128)S(1)} collective-permute-done((f32[8,128]{1,0:T(8,128)S(1)}, f32[8,128]{1,0:T(8,128)S(1)}, u32[]{:S(2)}, u32[]{:S(2)}) %collective-permute-start.2) | collective-permute-done | bytes 4128 | tf_op jit(solution)/shard_map/ppermute | solution.py:332
  (1 shorter events, 0.0 us)
Async XLA Ops:
  4.3 12.7 %all-to-all-start = ((f32[8,1,4224]{2,1,0:T(1,128)}), f32[8,1,4224]{2,1,0:T(1,128)S(1)}, u32[]{:S(2)}, u32[]{:S(2)}) async-start(f32[8,1,4224]{2,1,0:T(1,128)} %get-tuple-element.19), calls=%async_computation | async-start | bytes 270336 | tf_op jit(solution)/shard_map/all_to_all | solution.py:348
  12.1 7.2 %collective-permute-start = (f32[8,4096]{1,0:T(8,128)}, f32[8,4096]{1,0:T(8,128)S(1)}, u32[]{:S(2)}, u32[]{:S(2)}) collective-permute-start(f32[8,4096]{1,0:T(8,128)} %get-tuple-element.25), channel_id=1, source_target_pairs={{2,0},{3,1},{6,4},{7,5},{10,8},{11,9},{14,12},{15,13},{18,16},{19,... | collective-permute-start | bytes 393224 | tf_op jit(solution)/shard_map/ppermute | solution.py:399
  13.4 5.9 %collective-permute-start.1 = (f32[8,128]{1,0:T(8,128)S(1)}, f32[8,128]{1,0:T(8,128)S(1)}, u32[]{:S(2)}, u32[]{:S(2)}) collective-permute-start(f32[8,128]{1,0:T(8,128)S(1)} %get-tuple-element.26.refs_0_), channel_id=1, source_target_pairs={{0,1},{1,0},{4,5},{5,4},{8,9},{9,8},{12,13},{13,12},{16,17},{17,16... | collective-permute-start | bytes 12296 | tf_op jit(solution)/shard_map/ppermute | solution.py:421
  24.0 9.7 %all-to-all-start.1 = ((f32[16,8,256]{2,1,0:T(8,128)}), f32[16,8,256]{2,1,0:T(8,128)S(1)}, u32[]{:S(2)}, u32[]{:S(2)}) async-start(f32[16,8,256]{2,1,0:T(8,128)} %get-tuple-element.31), calls=%async_computation.1 | async-start | bytes 262144 | tf_op jit(solution)/shard_map/all_to_all | solution.py:343
  28.8 7.2 %collective-permute-start.3 = (f32[8,4096]{1,0:T(8,128)S(1)}, f32[8,4096]{1,0:T(8,128)S(1)}, u32[]{:S(2)}, u32[]{:S(2)}) collective-permute-start(f32[8,4096]{1,0:T(8,128)S(1)} %get-tuple-element.32.scaled), channel_id=1, source_target_pairs={{0,2},{1,3},{4,6},{5,7},{8,10},{9,11},{12,14},{13,15},{16,18},{17,... | collective-permute-start | bytes 393224 | tf_op jit(solution)/shard_map/ppermute | solution.py:332
  33.8 2.6 %collective-permute-start.2 = (f32[8,128]{1,0:T(8,128)S(1)}, f32[8,128]{1,0:T(8,128)S(1)}, u32[]{:S(2)}, u32[]{:S(2)}) collective-permute-start(f32[8,128]{1,0:T(8,128)S(1)} %unit_totals.1.totals), channel_id=1, source_target_pairs={{0,2},{1,3},{4,6},{5,7},{8,10},{9,11},{12,14},{13,15},{16,18},{17,... | collective-permute-start | bytes 12296 | tf_op jit(solution)/shard_map/ppermute | solution.py:332

commit v19 on v17

--- a/solution.py
+++ b/solution.py
@@ -162,12 +162,8 @@
         left = left_of(after / (all_count - post_start).astype(f32))
         for start, rows, copy in parts:
             copy.wait()
-
-            @pl.loop(start // block_rows, (start + rows) // block_rows)
-            def _(block):
-                here = pl.ds(pl.multiple_of(block * block_rows, block_rows), block_rows)
+            for here in blocks_of(start, rows):
                 cross_block[:, here] = add_terms(days_dot(left, *split_panel(panel[here, :])), groups)
-
         sends = fetch([cross_block], [cross], out_sems)
         wait_all(day_copies)
         wait_all(sends)
@@ -180,45 +176,45 @@
     unit_rows, resident = panel.shape[0], high_ref.shape[0]
     rest = pl.ds(resident, unit_rows - resident)
     copies = fetch([panel.at[rest], cohort, unit_logit], [held, held_cohort, held_logit], sems)
-    total = tree_sum(sums[u] for u in range(unit_devices))
-
-    def group_rows(first):
-        starts = [(first + row) * day_cols for row in range(groups)]
-        return jnp.concatenate([total[:, start : start + day_cols] for start in starts], axis=0)
-
-    counts = jnp.broadcast_to(total[:, 2 * groups * day_cols :], (groups, lanes))
-    slot = lax.broadcasted_iota(jnp.int32, (groups, lanes), 0)
-    lane = lax.broadcasted_iota(jnp.int32, (groups, lanes), 1)
-    unit_norm, treat_count, ctrl_count = [
-        jnp.sum(jnp.where(lane == i * groups + slot, counts, 0.0), axis=1, keepdims=True) for i in range(3)
-    ]
-    norms[...] = jnp.where(lane == 0, unit_norm, ctrl_count)
-    gap = group_rows(0) / unit_norm - group_rows(groups) / jnp.maximum(treat_count, 1.0)
-    before = days_of(lax.axis_index("day"), (groups, day_cols)).astype(f32) < ends[:, 0:1]
-    raised_time = raised_days[...]
-    pack[:groups, unit_rows:] = raised_time
-    pack[groups:, unit_rows:] = jnp.zeros_like(raised_time)
-    left = left_of(jnp.where(before, gap, 0.0), raised_time)
-
-    def multiply(here, high, low):
-        product = days_dot(left, high, low)
-        pack[:groups, here] = add_terms(product, groups)
-        pack[groups:, here] = add_terms(product, groups, 1)
-
-    @pl.loop(0, resident // block_rows)
-    def _(block):
-        here = pl.ds(pl.multiple_of(block * block_rows, block_rows), block_rows)
-        multiply(here, high_ref[here, :], low_ref[here, :])
-
-    wait_all(copies)
-    label = lax.broadcasted_iota(jnp.int32, raised_units.shape, 0)
-    raised_units[...] = jnp.where(held_cohort[...] > label, jnp.exp(held_logit[...]), 0.0)
-    for here in blocks_of(resident, unit_rows - resident):
-        there = pl.ds(here.start - resident, block_rows)
-        high, low = split_panel(held[there, :])
-        more_high[there, :] = high
-        more_low[there, :] = low
-        multiply(here, high, low)
+
+    @pl.when(lax.axis_index("day") < half)
+    def _():
+        total = tree_sum(sums[u] for u in range(unit_devices))
+
+        def group_rows(first):
+            starts = [(first + row) * day_cols for row in range(groups)]
+            return jnp.concatenate([total[:, start : start + day_cols] for start in starts], axis=0)
+
+        counts = jnp.broadcast_to(total[:, 2 * groups * day_cols :], (groups, lanes))
+        slot = lax.broadcasted_iota(jnp.int32, (groups, lanes), 0)
+        lane = lax.broadcasted_iota(jnp.int32, (groups, lanes), 1)
+        unit_norm, treat_count, ctrl_count = [
+            jnp.sum(jnp.where(lane == i * groups + slot, counts, 0.0), axis=1, keepdims=True) for i in range(3)
+        ]
+        norms[...] = jnp.where(lane == 0, unit_norm, ctrl_count)
+        gap = group_rows(0) / unit_norm - group_rows(groups) / jnp.maximum(treat_count, 1.0)
+        before = days_of(lax.axis_index("day"), (groups, day_cols)).astype(f32) < ends[:, 0:1]
+        raised_time = raised_days[...]
+        pack[:groups, unit_rows:] = raised_time
+        pack[groups:, unit_rows:] = jnp.zeros_like(raised_time)
+        left = left_of(jnp.where(before, gap, 0.0), raised_time)
+
+        def multiply(here, high, low):
+            product = days_dot(left, high, low)
+            pack[:groups, here] = add_terms(product, groups)
+            pack[groups:, here] = add_terms(product, groups, 1)
+
+        for here in blocks_of(0, resident):
+            multiply(here, high_ref[here, :], low_ref[here, :])
+        wait_all(copies)
+        label = lax.broadcasted_iota(jnp.int32, raised_units.shape, 0)
+        raised_units[...] = jnp.where(held_cohort[...] > label, jnp.exp(held_logit[...]), 0.0)
+        for here in blocks_of(resident, unit_rows - resident):
+            there = pl.ds(here.start - resident, block_rows)
+            high, low = split_panel(held[there, :])
+            more_high[there, :] = high
+            more_low[there, :] = low
+            multiply(here, high, low)
 
 
 @first_half_only

time: 35.9 us -> 36.1 us (level)
  Pallas kernels: 8.46 us -> 8.89 us
    pallas_call x7, Pallas kernels: 8.46 us -> 8.89 us  [call(): pl.pallas_call(kernel, in_specs=in_specs or [vmem] * len(args), out_specs...]
  transfers between devices with their start and end apart: 6 -> 6, of which waited for: 3 -> 3; matrix products, arithmetic and copies ran while one was open for 0% -> 0% of each run, Pallas kernels for 9% -> 10%
where the time goes in v19:
time: 36.1 us; the launch traced here: 35.6 us
  starting transfers between devices  18.2 us (50%)
  Pallas kernels  8.89 us (25%)
  waiting for transfers between devices  5.56 us (15%)
  blocking collectives  2.2 us (6%)
  between operations  0.71 us (2%)
    pallas_call x7, Pallas kernels, call(): pl.pallas_call(kernel, in_specs=in_specs or [vmem] * len(args), out_specs...  8.89 us
    all_to_all x1, starting transfers between devices, over_units(): lax.all_to_all(value, 'unit', split_axis=0, concat_axis=0, axis_index_gro...  7.83 us
    all_to_all x1, starting transfers between devices, over_first_half(): lax.all_to_all(value, ('unit', 'day'), split_axis=0, concat_axis=0, axis_...  4.64 us
    all_to_all x1, waiting for transfers between devices, over_first_half(): lax.all_to_all(value, ('unit', 'day'), split_axis=0, concat_axis=0, axis_...  3.55 us
    ppermute x2, starting transfers between devices, to_other_half(): return lax.ppermute(value, ('unit', 'day'), pairs)  2.56 us
    all_gather x1, blocking collectives, over_days(): return lax.all_gather(value, 'day', axis_index_groups=halves)  2.2 us
    ppermute x1, starting transfers between devices, local(): time_norms.append(lax.ppermute(time_norm, ('unit', 'day'), pairs))  1.92 us
    all_to_all x1, waiting for transfers between devices, over_units(): lax.all_to_all(value, 'unit', split_axis=0, concat_axis=0, axis_index_gro...  1.61 us
  transfers between devices with their start and end apart: 6, of which 3 were waited for; matrix products, arithmetic and copies ran while one was open for 0% of the time, Pallas kernels for 10%

profile of v19, /device:TPU:0, one launch (start us, length us, event | category | flops | bytes accessed | tf_op | source)
XLA Modules:
  0.0 35.6 jit_solution(6304920016945150076)
XLA Ops:
  0.6 3.7 %first_product.1 = (f32[8,1,4224]{2,1,0:T(1,128)}, f32[8,4096]{1,0:T(8,128)}, f32[8,256]{1,0:T(8,128)S(1)}, f32[8,128]{1,0:T(8,128)S(1)}, f32[8,128]{1,0:T(8,128...) custom-call(f32[4096,256]{1,0:T(8,128)} %panel.1, s32[1,4096]{1,0:T(1,128)} %bitcast.5, ...), custom_call_target="tpu_custom_call" | custom-call | tf_op jit(solution)/shard_map/first_product/pallas_call | solution.py:339
  4.3 7.8 %all-to-all-start = ((f32[8,1,4224]{2,1,0:T(1,128)}), f32[8,1,4224]{2,1,0:T(1,128)S(1)}, u32[]{:S(2)}, u32[]{:S(2)}) async-start(f32[8,1,4224]{2,1,0:T(1,128)} %get-tuple-element.19), calls=%async_computation | async-start | bytes 270336 | tf_op jit(solution)/shard_map/all_to_all | solution.py:336
  12.1 1.3 %collective-permute-start = (f32[8,4096]{1,0:T(8,128)}, f32[8,4096]{1,0:T(8,128)S(1)}, u32[]{:S(2)}, u32[]{:S(2)}) collective-permute-start(f32[8,4096]{1,0:T(8,128)} %get-tuple-element.25), channel_id=1, source_target_pairs={{2,0},{3,1},{6,4},{7,5},{10,8},{11,9},{14,12},{15,13},{18,16},{19,... | collective-permute-start | bytes 393224 | tf_op jit(solution)/shard_map/ppermute | solution.py:387
  13.4 1.9 %collective-permute-start.1 = (f32[8,128]{1,0:T(8,128)S(1)}, f32[8,128]{1,0:T(8,128)S(1)}, u32[]{:S(2)}, u32[]{:S(2)}) collective-permute-start(f32[8,128]{1,0:T(8,128)S(1)} %get-tuple-element.26.refs_0_), channel_id=1, source_target_pairs={{0,1},{1,0},{4,5},{5,4},{8,9},{9,8},{12,13},{13,12},{16,17},{17,16... | collective-permute-start | bytes 12296 | tf_op jit(solution)/shard_map/ppermute | solution.py:409
  15.4 1.6 %all-to-all-done.sums = f32[8,1,4224]{2,1,0:T(1,128)S(1)} async-done(((f32[8,1,4224]{2,1,0:T(1,128)}), f32[8,1,4224]{2,1,0:T(1,128)S(1)}, u32[]{:S(2)}, u32[]{:S(2)}) %all-to-all-start) | async-done | bytes 135200 | tf_op jit(solution)/shard_map/all_to_all | solution.py:336
  17.0 2.6 %unit_gradient.1 = (f32[16,4352]{1,0:T(8,128)S(1)}, f32[8,128]{1,0:T(8,128)S(1)}, f32[8,4096]{1,0:T(8,128)S(1)}, bf16[1024,256]{1,0:T(8,128)(2,1)S(1)}, bf16[1024,256]{1,0:T(8,128)(2,1)S(1)}) custom-call(f32[4096,256]{1,0:T(8,128)} %panel.1, s32[1,4096]{1,0:T(1,128)} %bitcast.6, f32[8,4096]{1,0:T(8,128)} %unit_logit.1, f32[8,1,4224]{2,1,0:T(1,128)S(1)} %all-to-all-done.sums, ...), custom_call_target="tpu_custom_call" | custom-call | tf_op jit(solution)/shard_map/unit_gradient/pallas_call | solution.py:339
  19.6 0.0 collective-permute-done.1.refs_1_
  19.6 0.0 collective-permute-done.post
  19.6 0.1 join_post.1
  19.7 2.2 %all-gather = f32[32,4352]{1,0:T(8,128)S(1)} all-gather(f32[16,4352]{1,0:T(8,128)S(1)} %join_post.1), channel_id=2, replica_groups={{0,1},{2,3},{4,5},{6,7},{8,9},{10,11},{12,13},{14,15},{16,17},{18,19},{..., dimensions={0}, use_global_device_ids=true | all-gather | bytes 835584 | tf_op jit(solution)/shard_map/all_gather | solution.py:324
  21.9 1.5 %time_gradient.1 = (f32[8,4096]{1,0:T(8,128)S(1)}, f32[8,512]{1,0:T(8,128)S(1)}, f32[16,8,256]{2,1,0:T(8,128)}) custom-call(f32[2,16,4352]{2,1,0:T(8,128)S(1)} %bitcast.4, bf16[3072,256]{1,0:T(8,128)(2,1)S(1)} %get-tuple-element.22.high_ref.refs_1_, bf16[3072,256]{1,0:T(8,128)(2,1)S(1)} %get-tuple-element.23.low_ref.refs_2_, ...), custom_call_target="tpu_custom_call" | custom-call | tf_op jit(solution)/shard_map/time_gradient/pallas_call | solution.py:339
  23.4 4.6 %all-to-all-start.1 = ((f32[16,8,256]{2,1,0:T(8,128)}), f32[16,8,256]{2,1,0:T(8,128)S(1)}, u32[]{:S(2)}, u32[]{:S(2)}) async-start(f32[16,8,256]{2,1,0:T(8,128)} %get-tuple-element.31), calls=%async_computation.1 | async-start | bytes 262144 | tf_op jit(solution)/shard_map/all_to_all | solution.py:331
  28.1 1.3 %collective-permute-start.3 = (f32[8,4096]{1,0:T(8,128)S(1)}, f32[8,4096]{1,0:T(8,128)S(1)}, u32[]{:S(2)}, u32[]{:S(2)}) collective-permute-start(f32[8,4096]{1,0:T(8,128)S(1)} %get-tuple-element.32.scaled), channel_id=1, source_target_pairs={{0,2},{1,3},{4,6},{5,7},{8,10},{9,11},{12,14},{13,15},{16,18},{17,... | collective-permute-start | bytes 393224 | tf_op jit(solution)/shard_map/ppermute | solution.py:320
  29.4 3.5 %all-to-all-done.1.grads = f32[16,8,256]{2,1,0:T(8,128)S(1)} async-done(((f32[16,8,256]{2,1,0:T(8,128)}), f32[16,8,256]{2,1,0:T(8,128)S(1)}, u32[]{:S(2)}, u32[]{:S(2)}) %all-to-all-start.1) | async-done | bytes 131104 | tf_op jit(solution)/shard_map/all_to_all | solution.py:331
  32.9 0.1 unit_totals.1.totals
  33.0 1.3 %collective-permute-start.2 = (f32[8,128]{1,0:T(8,128)S(1)}, f32[8,128]{1,0:T(8,128)S(1)}, u32[]{:S(2)}, u32[]{:S(2)}) collective-permute-start(f32[8,128]{1,0:T(8,128)S(1)} %unit_totals.1.totals), channel_id=1, source_target_pairs={{0,2},{1,3},{4,6},{5,7},{8,10},{9,11},{12,14},{13,15},{16,18},{17,... | collective-permute-start | bytes 12296 | tf_op jit(solution)/shard_map/ppermute | solution.py:320
  34.3 0.9 %scale_weights.1 = (f32[8,4096]{1,0:T(8,128)}, f32[8,256]{1,0:T(8,128)}) custom-call(f32[8,128]{1,0:T(8,128)S(1)} %unit_totals.1.totals, f32[8,4096]{1,0:T(8,128)S(1)} %get-tuple-element.32.scaled, f32[16,8,256]{2,1,0:T(8,128)S(1)} %all-to-all-done.1.grads, f32[8,512]{1,0:T(8,128)S(1)} %get-tuple-element.33.lam, ...), custom_call_target="tpu_custom_call" | custom-call | tf_op jit(solution)/shard_map/scale_weights/pallas_call | solution.py:339
  35.2 0.0 collective-permute-done.3.sent_scaled
  35.2 0.4 %collective-permute-done.2.sent_totals = f32[8,128]{1,0:T(8,128)S(1)} collective-permute-done((f32[8,128]{1,0:T(8,128)S(1)}, f32[8,128]{1,0:T(8,128)S(1)}, u32[]{:S(2)}, u32[]{:S(2)}) %collective-permute-start.2) | collective-permute-done | bytes 4128 | tf_op jit(solution)/shard_map/ppermute | solution.py:320
  (1 shorter events, 0.0 us)
Async XLA Ops:
  4.3 12.7 %all-to-all-start = ((f32[8,1,4224]{2,1,0:T(1,128)}), f32[8,1,4224]{2,1,0:T(1,128)S(1)}, u32[]{:S(2)}, u32[]{:S(2)}) async-start(f32[8,1,4224]{2,1,0:T(1,128)} %get-tuple-element.19), calls=%async_computation | async-start | bytes 270336 | tf_op jit(solution)/shard_map/all_to_all | solution.py:336
  12.1 7.5 %collective-permute-start = (f32[8,4096]{1,0:T(8,128)}, f32[8,4096]{1,0:T(8,128)S(1)}, u32[]{:S(2)}, u32[]{:S(2)}) collective-permute-start(f32[8,4096]{1,0:T(8,128)} %get-tuple-element.25), channel_id=1, source_target_pairs={{2,0},{3,1},{6,4},{7,5},{10,8},{11,9},{14,12},{15,13},{18,16},{19,... | collective-permute-start | bytes 393224 | tf_op jit(solution)/shard_map/ppermute | solution.py:387
  13.4 6.2 %collective-permute-start.1 = (f32[8,128]{1,0:T(8,128)S(1)}, f32[8,128]{1,0:T(8,128)S(1)}, u32[]{:S(2)}, u32[]{:S(2)}) collective-permute-start(f32[8,128]{1,0:T(8,128)S(1)} %get-tuple-element.26.refs_0_), channel_id=1, source_target_pairs={{0,1},{1,0},{4,5},{5,4},{8,9},{9,8},{12,13},{13,12},{16,17},{17,16... | collective-permute-start | bytes 12296 | tf_op jit(solution)/shard_map/ppermute | solution.py:409
  23.4 9.5 %all-to-all-start.1 = ((f32[16,8,256]{2,1,0:T(8,128)}), f32[16,8,256]{2,1,0:T(8,128)S(1)}, u32[]{:S(2)}, u32[]{:S(2)}) async-start(f32[16,8,256]{2,1,0:T(8,128)} %get-tuple-element.31), calls=%async_computation.1 | async-start | bytes 262144 | tf_op jit(solution)/shard_map/all_to_all | solution.py:331
  28.1 7.1 %collective-permute-start.3 = (f32[8,4096]{1,0:T(8,128)S(1)}, f32[8,4096]{1,0:T(8,128)S(1)}, u32[]{:S(2)}, u32[]{:S(2)}) collective-permute-start(f32[8,4096]{1,0:T(8,128)S(1)} %get-tuple-element.32.scaled), channel_id=1, source_target_pairs={{0,2},{1,3},{4,6},{5,7},{8,10},{9,11},{12,14},{13,15},{16,18},{17,... | collective-permute-start | bytes 393224 | tf_op jit(solution)/shard_map/ppermute | solution.py:320
  33.0 2.6 %collective-permute-start.2 = (f32[8,128]{1,0:T(8,128)S(1)}, f32[8,128]{1,0:T(8,128)S(1)}, u32[]{:S(2)}, u32[]{:S(2)}) collective-permute-start(f32[8,128]{1,0:T(8,128)S(1)} %unit_totals.1.totals), channel_id=1, source_target_pairs={{0,2},{1,3},{4,6},{5,7},{8,10},{9,11},{12,14},{13,15},{16,18},{17,... | collective-permute-start | bytes 12296 | tf_op jit(solution)/shard_map/ppermute | solution.py:320

commit v20 on v19

--- a/solution.py
+++ b/solution.py
@@ -204,17 +204,22 @@
             pack[:groups, here] = add_terms(product, groups)
             pack[groups:, here] = add_terms(product, groups, 1)
 
-        for here in blocks_of(0, resident):
+        late = resident - 2 * block_rows
+
+        @pl.loop(0, late // block_rows)
+        def _(block):
+            here = pl.ds(pl.multiple_of(block * block_rows, block_rows), block_rows)
             multiply(here, high_ref[here, :], low_ref[here, :])
+
         wait_all(copies)
         label = lax.broadcasted_iota(jnp.int32, raised_units.shape, 0)
         raised_units[...] = jnp.where(held_cohort[...] > label, jnp.exp(held_logit[...]), 0.0)
-        for here in blocks_of(resident, unit_rows - resident):
-            there = pl.ds(here.start - resident, block_rows)
-            high, low = split_panel(held[there, :])
-            more_high[there, :] = high
-            more_low[there, :] = low
-            multiply(here, high, low)
+        for there in blocks_of(0, unit_rows - resident):
+            more_high[there, :], more_low[there, :] = split_panel(held[there, :])
+        for here in blocks_of(late, resident - late):
+            multiply(here, high_ref[here, :], low_ref[here, :])
+        for there in blocks_of(0, unit_rows - resident):
+            multiply(pl.ds(resident + there.start, block_rows), more_high[there, :], more_low[there, :])
 
 
 @first_half_only

time: 36.1 us -> 35.9 us (level)
  Pallas kernels: 8.89 us -> 8.28 us
    pallas_call x7, Pallas kernels: 8.89 us -> 8.28 us  [call(): pl.pallas_call(kernel, in_specs=in_specs or [vmem] * len(args), out_specs...]
  transfers between devices with their start and end apart: 6 -> 6, of which waited for: 3 -> 4; matrix products, arithmetic and copies ran while one was open for 0% -> 0% of each run, Pallas kernels for 10% -> 9%
where the time goes in v20:
time: 35.9 us; the launch traced here: 35.5 us
  starting transfers between devices  18.5 us (52%)
  Pallas kernels  8.28 us (23%)
  waiting for transfers between devices  5.81 us (16%)
  blocking collectives  2.2 us (6%)
  between operations  0.7 us (2%)
    pallas_call x7, Pallas kernels, call(): pl.pallas_call(kernel, in_specs=in_specs or [vmem] * len(args), out_specs...  8.28 us
    all_to_all x1, starting transfers between devices, over_units(): lax.all_to_all(value, 'unit', split_axis=0, concat_axis=0, axis_index_gro...  7.83 us
    all_to_all x1, starting transfers between devices, over_first_half(): lax.all_to_all(value, ('unit', 'day'), split_axis=0, concat_axis=0, axis_...  4.88 us
    all_to_all x1, waiting for transfers between devices, over_first_half(): lax.all_to_all(value, ('unit', 'day'), split_axis=0, concat_axis=0, axis_...  3.62 us
    ppermute x2, starting transfers between devices, to_other_half(): return lax.ppermute(value, ('unit', 'day'), pairs)  2.56 us
    all_gather x1, blocking collectives, over_days(): return lax.all_gather(value, 'day', axis_index_groups=halves)  2.2 us
    ppermute x1, starting transfers between devices, local(): time_norms.append(lax.ppermute(time_norm, ('unit', 'day'), pairs))  1.92 us
    all_to_all x1, waiting for transfers between devices, over_units(): lax.all_to_all(value, 'unit', split_axis=0, concat_axis=0, axis_index_gro...  1.61 us
  transfers between devices with their start and end apart: 6, of which 4 were waited for; matrix products, arithmetic and copies ran while one was open for 0% of the time, Pallas kernels for 9%

profile of v20, /device:TPU:0, one launch (start us, length us, event | category | flops | bytes accessed | tf_op | source)
XLA Modules:
  0.0 35.5 jit_solution(12543350017051543278)
XLA Ops:
  0.6 3.7 %first_product.1 = (f32[8,1,4224]{2,1,0:T(1,128)}, f32[8,4096]{1,0:T(8,128)}, f32[8,256]{1,0:T(8,128)S(1)}, f32[8,128]{1,0:T(8,128)S(1)}, f32[8,128]{1,0:T(8,128...) custom-call(f32[4096,256]{1,0:T(8,128)} %panel.1, s32[1,4096]{1,0:T(1,128)} %bitcast.5, ...), custom_call_target="tpu_custom_call" | custom-call | tf_op jit(solution)/shard_map/first_product/pallas_call | solution.py:344
  4.3 7.8 %all-to-all-start = ((f32[8,1,4224]{2,1,0:T(1,128)}), f32[8,1,4224]{2,1,0:T(1,128)S(1)}, u32[]{:S(2)}, u32[]{:S(2)}) async-start(f32[8,1,4224]{2,1,0:T(1,128)} %get-tuple-element.19), calls=%async_computation | async-start | bytes 270336 | tf_op jit(solution)/shard_map/all_to_all | solution.py:341
  12.1 1.3 %collective-permute-start = (f32[8,4096]{1,0:T(8,128)}, f32[8,4096]{1,0:T(8,128)S(1)}, u32[]{:S(2)}, u32[]{:S(2)}) collective-permute-start(f32[8,4096]{1,0:T(8,128)} %get-tuple-element.25), channel_id=1, source_target_pairs={{2,0},{3,1},{6,4},{7,5},{10,8},{11,9},{14,12},{15,13},{18,16},{19,... | collective-permute-start | bytes 393224 | tf_op jit(solution)/shard_map/ppermute | solution.py:392
  13.4 1.9 %collective-permute-start.1 = (f32[8,128]{1,0:T(8,128)S(1)}, f32[8,128]{1,0:T(8,128)S(1)}, u32[]{:S(2)}, u32[]{:S(2)}) collective-permute-start(f32[8,128]{1,0:T(8,128)S(1)} %get-tuple-element.26.refs_0_), channel_id=1, source_target_pairs={{0,1},{1,0},{4,5},{5,4},{8,9},{9,8},{12,13},{13,12},{16,17},{17,16... | collective-permute-start | bytes 12296 | tf_op jit(solution)/shard_map/ppermute | solution.py:414
  15.4 1.6 %all-to-all-done.sums = f32[8,1,4224]{2,1,0:T(1,128)S(1)} async-done(((f32[8,1,4224]{2,1,0:T(1,128)}), f32[8,1,4224]{2,1,0:T(1,128)S(1)}, u32[]{:S(2)}, u32[]{:S(2)}) %all-to-all-start) | async-done | bytes 135200 | tf_op jit(solution)/shard_map/all_to_all | solution.py:341
  17.0 2.0 %unit_gradient.1 = (f32[16,4352]{1,0:T(8,128)S(1)}, f32[8,128]{1,0:T(8,128)S(1)}, f32[8,4096]{1,0:T(8,128)S(1)}, bf16[1024,256]{1,0:T(8,128)(2,1)S(1)}, bf16[1024,256]{1,0:T(8,128)(2,1)S(1)}) custom-call(f32[4096,256]{1,0:T(8,128)} %panel.1, s32[1,4096]{1,0:T(1,128)} %bitcast.6, f32[8,4096]{1,0:T(8,128)} %unit_logit.1, f32[8,1,4224]{2,1,0:T(1,128)S(1)} %all-to-all-done.sums, ...), custom_call_target="tpu_custom_call" | custom-call | tf_op jit(solution)/shard_map/unit_gradient/pallas_call | solution.py:344
  19.0 0.0 collective-permute-done.1.refs_1_
  19.0 0.2 collective-permute-done.post
  19.2 0.1 join_post.1
  19.3 2.2 %all-gather = f32[32,4352]{1,0:T(8,128)S(1)} all-gather(f32[16,4352]{1,0:T(8,128)S(1)} %join_post.1), channel_id=2, replica_groups={{0,1},{2,3},{4,5},{6,7},{8,9},{10,11},{12,13},{14,15},{16,17},{18,19},{..., dimensions={0}, use_global_device_ids=true | all-gather | bytes 835584 | tf_op jit(solution)/shard_map/all_gather | solution.py:329
  21.5 1.5 %time_gradient.1 = (f32[8,4096]{1,0:T(8,128)S(1)}, f32[8,512]{1,0:T(8,128)S(1)}, f32[16,8,256]{2,1,0:T(8,128)}) custom-call(f32[2,16,4352]{2,1,0:T(8,128)S(1)} %bitcast.4, bf16[3072,256]{1,0:T(8,128)(2,1)S(1)} %get-tuple-element.22.high_ref.refs_1_, bf16[3072,256]{1,0:T(8,128)(2,1)S(1)} %get-tuple-element.23.low_ref.refs_2_, ...), custom_call_target="tpu_custom_call" | custom-call | tf_op jit(solution)/shard_map/time_gradient/pallas_call | solution.py:344
  23.0 4.9 %all-to-all-start.1 = ((f32[16,8,256]{2,1,0:T(8,128)}), f32[16,8,256]{2,1,0:T(8,128)S(1)}, u32[]{:S(2)}, u32[]{:S(2)}) async-start(f32[16,8,256]{2,1,0:T(8,128)} %get-tuple-element.31), calls=%async_computation.1 | async-start | bytes 262144 | tf_op jit(solution)/shard_map/all_to_all | solution.py:336
  27.9 1.3 %collective-permute-start.3 = (f32[8,4096]{1,0:T(8,128)S(1)}, f32[8,4096]{1,0:T(8,128)S(1)}, u32[]{:S(2)}, u32[]{:S(2)}) collective-permute-start(f32[8,4096]{1,0:T(8,128)S(1)} %get-tuple-element.32.scaled), channel_id=1, source_target_pairs={{0,2},{1,3},{4,6},{5,7},{8,10},{9,11},{12,14},{13,15},{16,18},{17,... | collective-permute-start | bytes 393224 | tf_op jit(solution)/shard_map/ppermute | solution.py:325
  29.2 3.6 %all-to-all-done.1.grads = f32[16,8,256]{2,1,0:T(8,128)S(1)} async-done(((f32[16,8,256]{2,1,0:T(8,128)}), f32[16,8,256]{2,1,0:T(8,128)S(1)}, u32[]{:S(2)}, u32[]{:S(2)}) %all-to-all-start.1) | async-done | bytes 131104 | tf_op jit(solution)/shard_map/all_to_all | solution.py:336
  32.8 0.1 unit_totals.1.totals
  32.9 1.3 %collective-permute-start.2 = (f32[8,128]{1,0:T(8,128)S(1)}, f32[8,128]{1,0:T(8,128)S(1)}, u32[]{:S(2)}, u32[]{:S(2)}) collective-permute-start(f32[8,128]{1,0:T(8,128)S(1)} %unit_totals.1.totals), channel_id=1, source_target_pairs={{0,2},{1,3},{4,6},{5,7},{8,10},{9,11},{12,14},{13,15},{16,18},{17,... | collective-permute-start | bytes 12296 | tf_op jit(solution)/shard_map/ppermute | solution.py:325
  34.2 0.9 %scale_weights.1 = (f32[8,4096]{1,0:T(8,128)}, f32[8,256]{1,0:T(8,128)}) custom-call(f32[8,128]{1,0:T(8,128)S(1)} %unit_totals.1.totals, f32[8,4096]{1,0:T(8,128)S(1)} %get-tuple-element.32.scaled, f32[16,8,256]{2,1,0:T(8,128)S(1)} %all-to-all-done.1.grads, f32[8,512]{1,0:T(8,128)S(1)} %get-tuple-element.33.lam, ...), custom_call_target="tpu_custom_call" | custom-call | tf_op jit(solution)/shard_map/scale_weights/pallas_call | solution.py:344
  35.1 0.0 collective-permute-done.3.sent_scaled
  35.1 0.4 %collective-permute-done.2.sent_totals = f32[8,128]{1,0:T(8,128)S(1)} collective-permute-done((f32[8,128]{1,0:T(8,128)S(1)}, f32[8,128]{1,0:T(8,128)S(1)}, u32[]{:S(2)}, u32[]{:S(2)}) %collective-permute-start.2) | collective-permute-done | bytes 4128 | tf_op jit(solution)/shard_map/ppermute | solution.py:325
  (1 shorter events, 0.0 us)
Async XLA Ops:
  4.3 12.7 %all-to-all-start = ((f32[8,1,4224]{2,1,0:T(1,128)}), f32[8,1,4224]{2,1,0:T(1,128)S(1)}, u32[]{:S(2)}, u32[]{:S(2)}) async-start(f32[8,1,4224]{2,1,0:T(1,128)} %get-tuple-element.19), calls=%async_computation | async-start | bytes 270336 | tf_op jit(solution)/shard_map/all_to_all | solution.py:341
  12.1 7.1 %collective-permute-start = (f32[8,4096]{1,0:T(8,128)}, f32[8,4096]{1,0:T(8,128)S(1)}, u32[]{:S(2)}, u32[]{:S(2)}) collective-permute-start(f32[8,4096]{1,0:T(8,128)} %get-tuple-element.25), channel_id=1, source_target_pairs={{2,0},{3,1},{6,4},{7,5},{10,8},{11,9},{14,12},{15,13},{18,16},{19,... | collective-permute-start | bytes 393224 | tf_op jit(solution)/shard_map/ppermute | solution.py:392
  13.4 5.6 %collective-permute-start.1 = (f32[8,128]{1,0:T(8,128)S(1)}, f32[8,128]{1,0:T(8,128)S(1)}, u32[]{:S(2)}, u32[]{:S(2)}) collective-permute-start(f32[8,128]{1,0:T(8,128)S(1)} %get-tuple-element.26.refs_0_), channel_id=1, source_target_pairs={{0,1},{1,0},{4,5},{5,4},{8,9},{9,8},{12,13},{13,12},{16,17},{17,16... | collective-permute-start | bytes 12296 | tf_op jit(solution)/shard_map/ppermute | solution.py:414
  23.0 9.8 %all-to-all-start.1 = ((f32[16,8,256]{2,1,0:T(8,128)}), f32[16,8,256]{2,1,0:T(8,128)S(1)}, u32[]{:S(2)}, u32[]{:S(2)}) async-start(f32[16,8,256]{2,1,0:T(8,128)} %get-tuple-element.31), calls=%async_computation.1 | async-start | bytes 262144 | tf_op jit(solution)/shard_map/all_to_all | solution.py:336
  27.9 7.2 %collective-permute-start.3 = (f32[8,4096]{1,0:T(8,128)S(1)}, f32[8,4096]{1,0:T(8,128)S(1)}, u32[]{:S(2)}, u32[]{:S(2)}) collective-permute-start(f32[8,4096]{1,0:T(8,128)S(1)} %get-tuple-element.32.scaled), channel_id=1, source_target_pairs={{0,2},{1,3},{4,6},{5,7},{8,10},{9,11},{12,14},{13,15},{16,18},{17,... | collective-permute-start | bytes 393224 | tf_op jit(solution)/shard_map/ppermute | solution.py:325
  32.9 2.6 %collective-permute-start.2 = (f32[8,128]{1,0:T(8,128)S(1)}, f32[8,128]{1,0:T(8,128)S(1)}, u32[]{:S(2)}, u32[]{:S(2)}) collective-permute-start(f32[8,128]{1,0:T(8,128)S(1)} %unit_totals.1.totals), channel_id=1, source_target_pairs={{0,2},{1,3},{4,6},{5,7},{8,10},{9,11},{12,14},{13,15},{16,18},{17,... | collective-permute-start | bytes 12296 | tf_op jit(solution)/shard_map/ppermute | solution.py:325

commit v21 on v20

--- a/solution.py
+++ b/solution.py
@@ -317,8 +317,10 @@
     assert unit_devices & (unit_devices - 1) == 0
     panel_starts = [0, unit_rows // 4, unit_rows // 8 * 5, unit_rows]
     resident = unit_rows * 3 // 4 // block_rows * block_rows
-    middle = unit_devices // 2 - 1
-    unit_order = [middle] + [unit for unit in reversed(range(unit_devices)) if unit != middle]
+    def meeting_at(first):
+        return [first] + [unit for unit in reversed(range(unit_devices)) if unit != first]
+
+    middle = unit_devices // 2
 
     def to_other_half(value):
         pairs = [(u * day_devices + d, u * day_devices + d + half) for u in range(unit_devices) for d in range(half)]
@@ -330,7 +332,7 @@
 
     def over_first_half(value):
         members = [
-            [unit * day_devices + day for unit in unit_order for day in reversed(days)]
+            [unit * day_devices + day for unit in meeting_at(middle + 1) for day in reversed(days)]
             for days in (range(half), range(half, day_devices))
         ]
         return lax.all_to_all(
@@ -338,7 +340,13 @@
         )
 
     def over_units(value):
-        return lax.all_to_all(value, "unit", split_axis=0, concat_axis=0, axis_index_groups=[unit_order], tiled=True)
+        members = [
+            [unit * day_devices + day for unit in meeting_at(middle - 1 if day < half else middle)]
+            for day in range(day_devices)
+        ]
+        return lax.all_to_all(
+            value, ("unit", "day"), split_axis=0, concat_axis=0, axis_index_groups=members, tiled=True
+        )
 
     def call(kernel, shapes, name, args, in_specs=None, out_specs=None, **more):
         return pl.pallas_call(

time: 35.9 us -> 35.2 us (0.981)
  waiting for transfers between devices: 5.81 us -> 4.92 us
    all_to_all x1, waiting for transfers between devices: 3.62 us -> 2.72 us  [over_first_half(): lax.all_to_all(value, ('unit', 'day'), split_axis=0, concat_axis=0, axis_...]
where the time goes in v21:
time: 35.2 us; the launch traced here: 34.8 us
  starting transfers between devices  18.7 us (53%)
  Pallas kernels  8.28 us (24%)
  waiting for transfers between devices  4.92 us (14%)
  blocking collectives  2.2 us (6%)
  between operations  0.7 us (2%)
    pallas_call x7, Pallas kernels, call(): pl.pallas_call(kernel, in_specs=in_specs or [vmem] * len(args), out_specs...  8.28 us
    all_to_all x1, starting transfers between devices, over_units(): lax.all_to_all(value, ('unit', 'day'), split_axis=0, concat_axis=0, axis_...  7.83 us
    all_to_all x1, starting transfers between devices, over_first_half(): lax.all_to_all(value, ('unit', 'day'), split_axis=0, concat_axis=0, axis_...  5.08 us
    all_to_all x1, waiting for transfers between devices, over_first_half(): lax.all_to_all(value, ('unit', 'day'), split_axis=0, concat_axis=0, axis_...  2.72 us
    ppermute x2, starting transfers between devices, to_other_half(): return lax.ppermute(value, ('unit', 'day'), pairs)  2.56 us
    all_gather x1, blocking collectives, over_days(): return lax.all_gather(value, 'day', axis_index_groups=halves)  2.2 us
    ppermute x1, starting transfers between devices, local(): time_norms.append(lax.ppermute(time_norm, ('unit', 'day'), pairs))  1.92 us
    all_to_all x1, waiting for transfers between devices, over_units(): lax.all_to_all(value, ('unit', 'day'), split_axis=0, concat_axis=0, axis_...  1.61 us
  transfers between devices with their start and end apart: 6, of which 4 were waited for; matrix products, arithmetic and copies ran while one was open for 0% of the time, Pallas kernels for 9%

profile of v21, /device:TPU:0, one launch (start us, length us, event | category | flops | bytes accessed | tf_op | source)
XLA Modules:
  0.0 34.8 jit_solution(537300930207037370)
XLA Ops:
  0.6 3.7 %first_product.1 = (f32[8,1,4224]{2,1,0:T(1,128)}, f32[8,4096]{1,0:T(8,128)}, f32[8,256]{1,0:T(8,128)S(1)}, f32[8,128]{1,0:T(8,128)S(1)}, f32[8,128]{1,0:T(8,128...) custom-call(f32[4096,256]{1,0:T(8,128)} %panel.1, s32[1,4096]{1,0:T(1,128)} %bitcast.5, ...), custom_call_target="tpu_custom_call" | custom-call | tf_op jit(solution)/shard_map/first_product/pallas_call | solution.py:352
  4.3 7.8 %all-to-all-start = ((f32[8,1,4224]{2,1,0:T(1,128)}), f32[8,1,4224]{2,1,0:T(1,128)S(1)}, u32[]{:S(2)}, u32[]{:S(2)}) async-start(f32[8,1,4224]{2,1,0:T(1,128)} %get-tuple-element.19), calls=%async_computation | async-start | bytes 270336 | tf_op jit(solution)/shard_map/all_to_all | solution.py:347
  12.1 1.3 %collective-permute-start = (f32[8,4096]{1,0:T(8,128)}, f32[8,4096]{1,0:T(8,128)S(1)}, u32[]{:S(2)}, u32[]{:S(2)}) collective-permute-start(f32[8,4096]{1,0:T(8,128)} %get-tuple-element.25), channel_id=1, source_target_pairs={{2,0},{3,1},{6,4},{7,5},{10,8},{11,9},{14,12},{15,13},{18,16},{19,... | collective-permute-start | bytes 393224 | tf_op jit(solution)/shard_map/ppermute | solution.py:400
  13.4 1.9 %collective-permute-start.1 = (f32[8,128]{1,0:T(8,128)S(1)}, f32[8,128]{1,0:T(8,128)S(1)}, u32[]{:S(2)}, u32[]{:S(2)}) collective-permute-start(f32[8,128]{1,0:T(8,128)S(1)} %get-tuple-element.26.refs_0_), channel_id=1, source_target_pairs={{0,1},{1,0},{4,5},{5,4},{8,9},{9,8},{12,13},{13,12},{16,17},{17,16... | collective-permute-start | bytes 12296 | tf_op jit(solution)/shard_map/ppermute | solution.py:422
  15.4 1.6 %all-to-all-done.sums = f32[8,1,4224]{2,1,0:T(1,128)S(1)} async-done(((f32[8,1,4224]{2,1,0:T(1,128)}), f32[8,1,4224]{2,1,0:T(1,128)S(1)}, u32[]{:S(2)}, u32[]{:S(2)}) %all-to-all-start) | async-done | bytes 135200 | tf_op jit(solution)/shard_map/all_to_all | solution.py:347
  17.0 2.0 %unit_gradient.1 = (f32[16,4352]{1,0:T(8,128)S(1)}, f32[8,128]{1,0:T(8,128)S(1)}, f32[8,4096]{1,0:T(8,128)S(1)}, bf16[1024,256]{1,0:T(8,128)(2,1)S(1)}, bf16[1024,256]{1,0:T(8,128)(2,1)S(1)}) custom-call(f32[4096,256]{1,0:T(8,128)} %panel.1, s32[1,4096]{1,0:T(1,128)} %bitcast.6, f32[8,4096]{1,0:T(8,128)} %unit_logit.1, f32[8,1,4224]{2,1,0:T(1,128)S(1)} %all-to-all-done.sums, ...), custom_call_target="tpu_custom_call" | custom-call | tf_op jit(solution)/shard_map/unit_gradient/pallas_call | solution.py:352
  19.0 0.0 collective-permute-done.1.refs_1_
  19.0 0.2 collective-permute-done.post
  19.2 0.1 join_post.1
  19.3 2.2 %all-gather = f32[32,4352]{1,0:T(8,128)S(1)} all-gather(f32[16,4352]{1,0:T(8,128)S(1)} %join_post.1), channel_id=2, replica_groups={{0,1},{2,3},{4,5},{6,7},{8,9},{10,11},{12,13},{14,15},{16,17},{18,19},{..., dimensions={0}, use_global_device_ids=true | all-gather | bytes 835584 | tf_op jit(solution)/shard_map/all_gather | solution.py:331
  21.5 1.5 %time_gradient.1 = (f32[8,4096]{1,0:T(8,128)S(1)}, f32[8,512]{1,0:T(8,128)S(1)}, f32[16,8,256]{2,1,0:T(8,128)}) custom-call(f32[2,16,4352]{2,1,0:T(8,128)S(1)} %bitcast.4, bf16[3072,256]{1,0:T(8,128)(2,1)S(1)} %get-tuple-element.22.high_ref.refs_1_, bf16[3072,256]{1,0:T(8,128)(2,1)S(1)} %get-tuple-element.23.low_ref.refs_2_, ...), custom_call_target="tpu_custom_call" | custom-call | tf_op jit(solution)/shard_map/time_gradient/pallas_call | solution.py:352
  23.0 5.1 %all-to-all-start.1 = ((f32[16,8,256]{2,1,0:T(8,128)}), f32[16,8,256]{2,1,0:T(8,128)S(1)}, u32[]{:S(2)}, u32[]{:S(2)}) async-start(f32[16,8,256]{2,1,0:T(8,128)} %get-tuple-element.31), calls=%async_computation.1 | async-start | bytes 262144 | tf_op jit(solution)/shard_map/all_to_all | solution.py:338
  28.1 1.3 %collective-permute-start.3 = (f32[8,4096]{1,0:T(8,128)S(1)}, f32[8,4096]{1,0:T(8,128)S(1)}, u32[]{:S(2)}, u32[]{:S(2)}) collective-permute-start(f32[8,4096]{1,0:T(8,128)S(1)} %get-tuple-element.32.scaled), channel_id=1, source_target_pairs={{0,2},{1,3},{4,6},{5,7},{8,10},{9,11},{12,14},{13,15},{16,18},{17,... | collective-permute-start | bytes 393224 | tf_op jit(solution)/shard_map/ppermute | solution.py:327
  29.4 2.7 %all-to-all-done.1.grads = f32[16,8,256]{2,1,0:T(8,128)S(1)} async-done(((f32[16,8,256]{2,1,0:T(8,128)}), f32[16,8,256]{2,1,0:T(8,128)S(1)}, u32[]{:S(2)}, u32[]{:S(2)}) %all-to-all-start.1) | async-done | bytes 131104 | tf_op jit(solution)/shard_map/all_to_all | solution.py:338
  32.1 0.1 unit_totals.1.totals
  32.2 1.3 %collective-permute-start.2 = (f32[8,128]{1,0:T(8,128)S(1)}, f32[8,128]{1,0:T(8,128)S(1)}, u32[]{:S(2)}, u32[]{:S(2)}) collective-permute-start(f32[8,128]{1,0:T(8,128)S(1)} %unit_totals.1.totals), channel_id=1, source_target_pairs={{0,2},{1,3},{4,6},{5,7},{8,10},{9,11},{12,14},{13,15},{16,18},{17,... | collective-permute-start | bytes 12296 | tf_op jit(solution)/shard_map/ppermute | solution.py:327
  33.5 0.9 %scale_weights.1 = (f32[8,4096]{1,0:T(8,128)}, f32[8,256]{1,0:T(8,128)}) custom-call(f32[8,128]{1,0:T(8,128)S(1)} %unit_totals.1.totals, f32[8,4096]{1,0:T(8,128)S(1)} %get-tuple-element.32.scaled, f32[16,8,256]{2,1,0:T(8,128)S(1)} %all-to-all-done.1.grads, f32[8,512]{1,0:T(8,128)S(1)} %get-tuple-element.33.lam, ...), custom_call_target="tpu_custom_call" | custom-call | tf_op jit(solution)/shard_map/scale_weights/pallas_call | solution.py:352
  34.4 0.0 collective-permute-done.3.sent_scaled
  34.4 0.4 %collective-permute-done.2.sent_totals = f32[8,128]{1,0:T(8,128)S(1)} collective-permute-done((f32[8,128]{1,0:T(8,128)S(1)}, f32[8,128]{1,0:T(8,128)S(1)}, u32[]{:S(2)}, u32[]{:S(2)}) %collective-permute-start.2) | collective-permute-done | bytes 4128 | tf_op jit(solution)/shard_map/ppermute | solution.py:327
  (1 shorter events, 0.0 us)
Async XLA Ops:
  4.3 12.7 %all-to-all-start = ((f32[8,1,4224]{2,1,0:T(1,128)}), f32[8,1,4224]{2,1,0:T(1,128)S(1)}, u32[]{:S(2)}, u32[]{:S(2)}) async-start(f32[8,1,4224]{2,1,0:T(1,128)} %get-tuple-element.19), calls=%async_computation | async-start | bytes 270336 | tf_op jit(solution)/shard_map/all_to_all | solution.py:347
  12.1 7.1 %collective-permute-start = (f32[8,4096]{1,0:T(8,128)}, f32[8,4096]{1,0:T(8,128)S(1)}, u32[]{:S(2)}, u32[]{:S(2)}) collective-permute-start(f32[8,4096]{1,0:T(8,128)} %get-tuple-element.25), channel_id=1, source_target_pairs={{2,0},{3,1},{6,4},{7,5},{10,8},{11,9},{14,12},{15,13},{18,16},{19,... | collective-permute-start | bytes 393224 | tf_op jit(solution)/shard_map/ppermute | solution.py:400
  13.4 5.6 %collective-permute-start.1 = (f32[8,128]{1,0:T(8,128)S(1)}, f32[8,128]{1,0:T(8,128)S(1)}, u32[]{:S(2)}, u32[]{:S(2)}) collective-permute-start(f32[8,128]{1,0:T(8,128)S(1)} %get-tuple-element.26.refs_0_), channel_id=1, source_target_pairs={{0,1},{1,0},{4,5},{5,4},{8,9},{9,8},{12,13},{13,12},{16,17},{17,16... | collective-permute-start | bytes 12296 | tf_op jit(solution)/shard_map/ppermute | solution.py:422
  23.0 9.1 %all-to-all-start.1 = ((f32[16,8,256]{2,1,0:T(8,128)}), f32[16,8,256]{2,1,0:T(8,128)S(1)}, u32[]{:S(2)}, u32[]{:S(2)}) async-start(f32[16,8,256]{2,1,0:T(8,128)} %get-tuple-element.31), calls=%async_computation.1 | async-start | bytes 262144 | tf_op jit(solution)/shard_map/all_to_all | solution.py:338
  28.1 6.3 %collective-permute-start.3 = (f32[8,4096]{1,0:T(8,128)S(1)}, f32[8,4096]{1,0:T(8,128)S(1)}, u32[]{:S(2)}, u32[]{:S(2)}) collective-permute-start(f32[8,4096]{1,0:T(8,128)S(1)} %get-tuple-element.32.scaled), channel_id=1, source_target_pairs={{0,2},{1,3},{4,6},{5,7},{8,10},{9,11},{12,14},{13,15},{16,18},{17,... | collective-permute-start | bytes 393224 | tf_op jit(solution)/shard_map/ppermute | solution.py:327
  32.2 2.6 %collective-permute-start.2 = (f32[8,128]{1,0:T(8,128)S(1)}, f32[8,128]{1,0:T(8,128)S(1)}, u32[]{:S(2)}, u32[]{:S(2)}) collective-permute-start(f32[8,128]{1,0:T(8,128)S(1)} %unit_totals.1.totals), channel_id=1, source_target_pairs={{0,2},{1,3},{4,6},{5,7},{8,10},{9,11},{12,14},{13,15},{16,18},{17,... | collective-permute-start | bytes 12296 | tf_op jit(solution)/shard_map/ppermute | solution.py:327

commit v22 on v21

--- a/solution.py
+++ b/solution.py
@@ -245,7 +245,7 @@
     me = lax.rem(lax.axis_index("day"), half)
     for day in range(half):
         lam[:, day * day_cols : (day + 1) * day_cols] = parts[day][:groups, unit_rows:]
-    time_grad = jnp.zeros((groups, day_cols), f32)
+    time_grad = jnp.zeros((2 * groups, 2 * day_cols), f32)
     new_sum = jnp.zeros((groups, 1), f32)
     for start in range(0, unit_rows, block_rows):
         here = pl.ds(start, block_rows)
@@ -260,7 +260,8 @@
         else:
             there = pl.ds(start - resident, block_rows)
             high, low = more_high[there, :], more_low[there, :]
-        time_grad += add_terms(rows_dot(left, high, low), groups)
+        time_grad += jnp.dot(left, jnp.concatenate([high, low], axis=1), preferred_element_type=f32)
+    time_grad = add_terms(time_grad[:, :day_cols] + time_grad[:, day_cols:], groups)
     lane = lax.broadcasted_iota(jnp.int32, (groups, day_cols), 1)
     spare = (lane == day_cols - 1) & (me == half - 1)
     block[...] = jnp.where(spare, new_sum, time_grad)
@@ -322,8 +323,10 @@
 
     middle = unit_devices // 2
 
-    def to_other_half(value):
-        pairs = [(u * day_devices + d, u * day_devices + d + half) for u in range(unit_devices) for d in range(half)]
+    def to_other_half(value, day_xor=0):
+        pairs = [
+            (u * day_devices + d, u * day_devices + half + (d ^ day_xor)) for u in range(unit_devices) for d in range(half)
+        ]
         return lax.ppermute(value, ("unit", "day"), pairs)
 
     def over_days(value):
@@ -454,7 +457,7 @@
         functools.partial(sixth_kernel, half),
         [((groups, unit_rows), f32)],
         "other_half",
-        (to_other_half(totals), sent_scaled, unit_weights),
+        (to_other_half(totals, half > 1), sent_scaled, unit_weights),
         in_specs=[vmem, vmem, hbm],
         out_specs=[hbm],
         input_output_aliases={2: 0},

time: 35.2 us -> 35.2 us (level)
  no operation moved by 1% of the time
where the time goes in v22:
time: 35.2 us; the launch traced here: 34.8 us
  starting transfers between devices  18.7 us (53%)
  Pallas kernels  8.29 us (24%)
  waiting for transfers between devices  4.92 us (14%)
  blocking collectives  2.2 us (6%)
  between operations  0.7 us (2%)
    pallas_call x7, Pallas kernels, call(): pl.pallas_call(kernel, in_specs=in_specs or [vmem] * len(args), out_specs...  8.29 us
    all_to_all x1, starting transfers between devices, over_units(): lax.all_to_all(value, ('unit', 'day'), split_axis=0, concat_axis=0, axis_...  7.83 us
    all_to_all x1, starting transfers between devices, over_first_half(): lax.all_to_all(value, ('unit', 'day'), split_axis=0, concat_axis=0, axis_...  5.08 us
    all_to_all x1, waiting for transfers between devices, over_first_half(): lax.all_to_all(value, ('unit', 'day'), split_axis=0, concat_axis=0, axis_...  2.72 us
    ppermute x2, starting transfers between devices, to_other_half(): return lax.ppermute(value, ('unit', 'day'), pairs)  2.56 us
    all_gather x1, blocking collectives, over_days(): return lax.all_gather(value, 'day', axis_index_groups=halves)  2.2 us
    ppermute x1, starting transfers between devices, local(): time_norms.append(lax.ppermute(time_norm, ('unit', 'day'), pairs))  1.92 us
    all_to_all x1, waiting for transfers between devices, over_units(): lax.all_to_all(value, ('unit', 'day'), split_axis=0, concat_axis=0, axis_...  1.61 us
  transfers between devices with their start and end apart: 6, of which 4 were waited for; matrix products, arithmetic and copies ran while one was open for 0% of the time, Pallas kernels for 9%

profile of v22, /device:TPU:0, one launch (start us, length us, event | category | flops | bytes accessed | tf_op | source)
XLA Modules:
  0.0 34.8 jit_solution(14684933414503441508)
XLA Ops:
  0.6 3.7 %first_product.1 = (f32[8,1,4224]{2,1,0:T(1,128)}, f32[8,4096]{1,0:T(8,128)}, f32[8,256]{1,0:T(8,128)S(1)}, f32[8,128]{1,0:T(8,128)S(1)}, f32[8,128]{1,0:T(8,128...) custom-call(f32[4096,256]{1,0:T(8,128)} %panel.1, s32[1,4096]{1,0:T(1,128)} %bitcast.5, ...), custom_call_target="tpu_custom_call" | custom-call | tf_op jit(solution)/shard_map/first_product/pallas_call | solution.py:355
  4.3 7.8 %all-to-all-start = ((f32[8,1,4224]{2,1,0:T(1,128)}), f32[8,1,4224]{2,1,0:T(1,128)S(1)}, u32[]{:S(2)}, u32[]{:S(2)}) async-start(f32[8,1,4224]{2,1,0:T(1,128)} %get-tuple-element.19), calls=%async_computation | async-start | bytes 270336 | tf_op jit(solution)/shard_map/all_to_all | solution.py:350
  12.1 1.3 %collective-permute-start = (f32[8,4096]{1,0:T(8,128)}, f32[8,4096]{1,0:T(8,128)S(1)}, u32[]{:S(2)}, u32[]{:S(2)}) collective-permute-start(f32[8,4096]{1,0:T(8,128)} %get-tuple-element.25), channel_id=1, source_target_pairs={{2,0},{3,1},{6,4},{7,5},{10,8},{11,9},{14,12},{15,13},{18,16},{19,... | collective-permute-start | bytes 393224 | tf_op jit(solution)/shard_map/ppermute | solution.py:403
  13.4 1.9 %collective-permute-start.1 = (f32[8,128]{1,0:T(8,128)S(1)}, f32[8,128]{1,0:T(8,128)S(1)}, u32[]{:S(2)}, u32[]{:S(2)}) collective-permute-start(f32[8,128]{1,0:T(8,128)S(1)} %get-tuple-element.26.refs_0_), channel_id=1, source_target_pairs={{0,1},{1,0},{4,5},{5,4},{8,9},{9,8},{12,13},{13,12},{16,17},{17,16... | collective-permute-start | bytes 12296 | tf_op jit(solution)/shard_map/ppermute | solution.py:425
  15.4 1.6 %all-to-all-done.sums = f32[8,1,4224]{2,1,0:T(1,128)S(1)} async-done(((f32[8,1,4224]{2,1,0:T(1,128)}), f32[8,1,4224]{2,1,0:T(1,128)S(1)}, u32[]{:S(2)}, u32[]{:S(2)}) %all-to-all-start) | async-done | bytes 135200 | tf_op jit(solution)/shard_map/all_to_all | solution.py:350
  17.0 2.0 %unit_gradient.1 = (f32[16,4352]{1,0:T(8,128)S(1)}, f32[8,128]{1,0:T(8,128)S(1)}, f32[8,4096]{1,0:T(8,128)S(1)}, bf16[1024,256]{1,0:T(8,128)(2,1)S(1)}, bf16[1024,256]{1,0:T(8,128)(2,1)S(1)}) custom-call(f32[4096,256]{1,0:T(8,128)} %panel.1, s32[1,4096]{1,0:T(1,128)} %bitcast.6, f32[8,4096]{1,0:T(8,128)} %unit_logit.1, f32[8,1,4224]{2,1,0:T(1,128)S(1)} %all-to-all-done.sums, ...), custom_call_target="tpu_custom_call" | custom-call | tf_op jit(solution)/shard_map/unit_gradient/pallas_call | solution.py:355
  19.0 0.0 collective-permute-done.1.refs_1_
  19.0 0.2 collective-permute-done.post
  19.2 0.1 join_post.1
  19.3 2.2 %all-gather = f32[32,4352]{1,0:T(8,128)S(1)} all-gather(f32[16,4352]{1,0:T(8,128)S(1)} %join_post.1), channel_id=2, replica_groups={{0,1},{2,3},{4,5},{6,7},{8,9},{10,11},{12,13},{14,15},{16,17},{18,19},{..., dimensions={0}, use_global_device_ids=true | all-gather | bytes 835584 | tf_op jit(solution)/shard_map/all_gather | solution.py:334
  21.5 1.5 %time_gradient.1 = (f32[8,4096]{1,0:T(8,128)S(1)}, f32[8,512]{1,0:T(8,128)S(1)}, f32[16,8,256]{2,1,0:T(8,128)}) custom-call(f32[2,16,4352]{2,1,0:T(8,128)S(1)} %bitcast.4, bf16[3072,256]{1,0:T(8,128)(2,1)S(1)} %get-tuple-element.22.high_ref.refs_1_, bf16[3072,256]{1,0:T(8,128)(2,1)S(1)} %get-tuple-element.23.low_ref.refs_2_, ...), custom_call_target="tpu_custom_call" | custom-call | tf_op jit(solution)/shard_map/time_gradient/pallas_call | solution.py:355
  23.0 5.1 %all-to-all-start.1 = ((f32[16,8,256]{2,1,0:T(8,128)}), f32[16,8,256]{2,1,0:T(8,128)S(1)}, u32[]{:S(2)}, u32[]{:S(2)}) async-start(f32[16,8,256]{2,1,0:T(8,128)} %get-tuple-element.31), calls=%async_computation.1 | async-start | bytes 262144 | tf_op jit(solution)/shard_map/all_to_all | solution.py:341
  28.1 1.3 %collective-permute-start.3 = (f32[8,4096]{1,0:T(8,128)S(1)}, f32[8,4096]{1,0:T(8,128)S(1)}, u32[]{:S(2)}, u32[]{:S(2)}) collective-permute-start(f32[8,4096]{1,0:T(8,128)S(1)} %get-tuple-element.32.scaled), channel_id=1, source_target_pairs={{0,2},{1,3},{4,6},{5,7},{8,10},{9,11},{12,14},{13,15},{16,18},{17,... | collective-permute-start | bytes 393224 | tf_op jit(solution)/shard_map/ppermute | solution.py:330
  29.4 2.7 %all-to-all-done.1.grads = f32[16,8,256]{2,1,0:T(8,128)S(1)} async-done(((f32[16,8,256]{2,1,0:T(8,128)}), f32[16,8,256]{2,1,0:T(8,128)S(1)}, u32[]{:S(2)}, u32[]{:S(2)}) %all-to-all-start.1) | async-done | bytes 131104 | tf_op jit(solution)/shard_map/all_to_all | solution.py:341
  32.1 0.1 unit_totals.1.totals
  32.2 1.3 %collective-permute-start.2 = (f32[8,128]{1,0:T(8,128)S(1)}, f32[8,128]{1,0:T(8,128)S(1)}, u32[]{:S(2)}, u32[]{:S(2)}) collective-permute-start(f32[8,128]{1,0:T(8,128)S(1)} %unit_totals.1.totals), channel_id=1, source_target_pairs={{0,3},{1,2},{4,7},{5,6},{8,11},{9,10},{12,15},{13,14},{16,19},{17,... | collective-permute-start | bytes 12296 | tf_op jit(solution)/shard_map/ppermute | solution.py:330
  33.5 0.9 %scale_weights.1 = (f32[8,4096]{1,0:T(8,128)}, f32[8,256]{1,0:T(8,128)}) custom-call(f32[8,128]{1,0:T(8,128)S(1)} %unit_totals.1.totals, f32[8,4096]{1,0:T(8,128)S(1)} %get-tuple-element.32.scaled, f32[16,8,256]{2,1,0:T(8,128)S(1)} %all-to-all-done.1.grads, f32[8,512]{1,0:T(8,128)S(1)} %get-tuple-element.33.lam, ...), custom_call_target="tpu_custom_call" | custom-call | tf_op jit(solution)/shard_map/scale_weights/pallas_call | solution.py:355
  34.4 0.0 collective-permute-done.3.sent_scaled
  34.4 0.4 %collective-permute-done.2.sent_totals = f32[8,128]{1,0:T(8,128)S(1)} collective-permute-done((f32[8,128]{1,0:T(8,128)S(1)}, f32[8,128]{1,0:T(8,128)S(1)}, u32[]{:S(2)}, u32[]{:S(2)}) %collective-permute-start.2) | collective-permute-done | bytes 4128 | tf_op jit(solution)/shard_map/ppermute | solution.py:330
  (1 shorter events, 0.0 us)
Async XLA Ops:
  4.3 12.7 %all-to-all-start = ((f32[8,1,4224]{2,1,0:T(1,128)}), f32[8,1,4224]{2,1,0:T(1,128)S(1)}, u32[]{:S(2)}, u32[]{:S(2)}) async-start(f32[8,1,4224]{2,1,0:T(1,128)} %get-tuple-element.19), calls=%async_computation | async-start | bytes 270336 | tf_op jit(solution)/shard_map/all_to_all | solution.py:350
  12.1 7.1 %collective-permute-start = (f32[8,4096]{1,0:T(8,128)}, f32[8,4096]{1,0:T(8,128)S(1)}, u32[]{:S(2)}, u32[]{:S(2)}) collective-permute-start(f32[8,4096]{1,0:T(8,128)} %get-tuple-element.25), channel_id=1, source_target_pairs={{2,0},{3,1},{6,4},{7,5},{10,8},{11,9},{14,12},{15,13},{18,16},{19,... | collective-permute-start | bytes 393224 | tf_op jit(solution)/shard_map/ppermute | solution.py:403
  13.4 5.6 %collective-permute-start.1 = (f32[8,128]{1,0:T(8,128)S(1)}, f32[8,128]{1,0:T(8,128)S(1)}, u32[]{:S(2)}, u32[]{:S(2)}) collective-permute-start(f32[8,128]{1,0:T(8,128)S(1)} %get-tuple-element.26.refs_0_), channel_id=1, source_target_pairs={{0,1},{1,0},{4,5},{5,4},{8,9},{9,8},{12,13},{13,12},{16,17},{17,16... | collective-permute-start | bytes 12296 | tf_op jit(solution)/shard_map/ppermute | solution.py:425
  23.0 9.1 %all-to-all-start.1 = ((f32[16,8,256]{2,1,0:T(8,128)}), f32[16,8,256]{2,1,0:T(8,128)S(1)}, u32[]{:S(2)}, u32[]{:S(2)}) async-start(f32[16,8,256]{2,1,0:T(8,128)} %get-tuple-element.31), calls=%async_computation.1 | async-start | bytes 262144 | tf_op jit(solution)/shard_map/all_to_all | solution.py:341
  28.1 6.3 %collective-permute-start.3 = (f32[8,4096]{1,0:T(8,128)S(1)}, f32[8,4096]{1,0:T(8,128)S(1)}, u32[]{:S(2)}, u32[]{:S(2)}) collective-permute-start(f32[8,4096]{1,0:T(8,128)S(1)} %get-tuple-element.32.scaled), channel_id=1, source_target_pairs={{0,2},{1,3},{4,6},{5,7},{8,10},{9,11},{12,14},{13,15},{16,18},{17,... | collective-permute-start | bytes 393224 | tf_op jit(solution)/shard_map/ppermute | solution.py:330
  32.2 2.6 %collective-permute-start.2 = (f32[8,128]{1,0:T(8,128)S(1)}, f32[8,128]{1,0:T(8,128)S(1)}, u32[]{:S(2)}, u32[]{:S(2)}) collective-permute-start(f32[8,128]{1,0:T(8,128)S(1)} %unit_totals.1.totals), channel_id=1, source_target_pairs={{0,3},{1,2},{4,7},{5,6},{8,11},{9,10},{12,15},{13,14},{16,19},{17,... | collective-permute-start | bytes 12296 | tf_op jit(solution)/shard_map/ppermute | solution.py:330

commit v23 on v22

--- a/solution.py
+++ b/solution.py
@@ -98,14 +98,9 @@
         copy.wait()
 
 
-def repeat_start(block, out, sems):
-    places = [out.at[i] for i in range(out.shape[0])]
-    return fetch([block] * len(places), places, sems)
-
-
 def first_kernel(all_count, half, starts, *refs):
     arguments, refs = refs[:6], refs[6:]
-    out, cross, raised_days, time_norm, ends, high_ref, low_ref, *held, block, left_ref, cross_block, small_sems, panel_sems, out_sems = refs
+    out, cross, raised_days, time_norm, ends, high_ref, low_ref, *held, left_ref, cross_block, small_sems, panel_sems, out_sem = refs
     groups, day_cols = held[5].shape
     unit_rows, resident = held[0].shape[0], high_ref.shape[0]
     (post_copy,) = fetch(arguments[3:4], held[3:4], small_sems)
@@ -130,7 +125,7 @@
         norms = jnp.zeros((groups, lanes), f32)
         for i, count in enumerate(counts):
             norms += jnp.where(lane == i * groups + slot, count, 0.0)
-        block[:, 2 * groups * day_cols :] = jnp.sum(norms, axis=0, keepdims=True)
+        norms = jnp.sum(norms, axis=0, keepdims=True)
         product = jnp.zeros((4 * groups, 2 * day_cols), f32)
         for start, rows, copy in parts:
             copy.wait()
@@ -143,9 +138,10 @@
                 product += jnp.dot(left_ref[:, here], both, preferred_element_type=f32)
         product = product[:, :day_cols] + product[:, day_cols:]
         both_sums = jnp.concatenate([add_terms(product, groups), product[2 * groups :][:groups]], axis=0)
-        for row in range(2 * groups):
-            block[:, row * day_cols : (row + 1) * day_cols] = both_sums[row : row + 1, :]
-        sends = repeat_start(block, out, out_sems)
+        for member in range(out.shape[0]):
+            for row in range(2 * groups):
+                out[member, :, row * day_cols : (row + 1) * day_cols] = both_sums[row : row + 1, :]
+            out[member, :, 2 * groups * day_cols :] = norms
         wait_all(day_copies)
         pre_end = column(pre_row)
         ends[...] = jnp.broadcast_to(pre_end.astype(f32), ends.shape)
@@ -153,7 +149,6 @@
         raised_time = jnp.where(before, jnp.exp(time_logit[...]), 0.0)
         raised_days[...] = raised_time
         time_norm[...] = jnp.broadcast_to(jnp.sum(raised_time, axis=1, keepdims=True), time_norm.shape)
-        wait_all(sends)
 
     @pl.when(me >= half)
     def _():
@@ -164,7 +159,7 @@
             copy.wait()
             for here in blocks_of(start, rows):
                 cross_block[:, here] = add_terms(days_dot(left, *split_panel(panel[here, :])), groups)
-        sends = fetch([cross_block], [cross], out_sems)
+        sends = fetch([cross_block], [cross], out_sem)
         wait_all(day_copies)
         wait_all(sends)
 
@@ -236,7 +231,7 @@
 @first_half_only
 def third_kernel(half, *refs):
     parts, refs = [refs[0].at[day] for day in range(half)], refs[1:]
-    high_ref, low_ref, more_high, more_low, norms, raised_units, ends, scaled, lam, out, block, out_sems = refs
+    high_ref, low_ref, more_high, more_low, norms, raised_units, ends, scaled, lam, out = refs
     groups, unit_rows = raised_units.shape
     resident, day_cols = high_ref.shape
     unit_norm, ctrl_count = norms[:, 0:1], norms[:, 1:2]
@@ -264,8 +259,9 @@
     time_grad = add_terms(time_grad[:, :day_cols] + time_grad[:, day_cols:], groups)
     lane = lax.broadcasted_iota(jnp.int32, (groups, day_cols), 1)
     spare = (lane == day_cols - 1) & (me == half - 1)
-    block[...] = jnp.where(spare, new_sum, time_grad)
-    wait_all(repeat_start(block, out, out_sems))
+    block = jnp.where(spare, new_sum, time_grad)
+    for member in range(out.shape[0]):
+        out[member] = block
 
 
 def time_grad_of(grads, unit_devices, half, day):
@@ -357,7 +353,7 @@
             in_specs=in_specs or [vmem] * len(args),
             out_specs=out_specs or [vmem] * len(shapes),
             out_shape=[
-                shape if isinstance(shape, type(in_hbm)) else jax.ShapeDtypeStruct(*shape) for shape in shapes
+                shape if isinstance(shape, type(in_vmem)) else jax.ShapeDtypeStruct(*shape) for shape in shapes
             ],
             compiler_params=params,
             name=name,
@@ -370,13 +366,12 @@
     small_sems, panel_sems = pltpu.SemaphoreType.DMA((5,)), pltpu.SemaphoreType.DMA((3,))
     panel_terms = [((resident, day_cols), bf16)] * 2
     other_terms = [((unit_rows - resident, day_cols), bf16)] * 2
-    out_sems = pltpu.SemaphoreType.DMA((unit_devices,))
     width = 2 * groups * day_cols + lanes
-    in_hbm = pltpu.HBM((unit_devices, 1, width), f32)
+    in_vmem = pltpu.VMEM((unit_devices, 1, width), f32)
     sums, cross, raised_days, time_norm, ends, high, low = call(
         functools.partial(first_kernel, day_devices * day_cols, half, panel_starts),
         [
-            in_hbm,
+            in_vmem,
             pltpu.HBM((groups, unit_rows), f32),
             ((groups, day_cols), f32),
             ((groups, lanes), f32),
@@ -386,15 +381,14 @@
         "first_product",
         fixed,
         in_specs=[hbm] * 6,
-        out_specs=[hbm, hbm] + [vmem] * 5,
+        out_specs=[vmem, hbm] + [vmem] * 5,
         scratch_shapes=held
         + [
-            pltpu.VMEM((1, width), f32),
             pltpu.VMEM((4 * groups, unit_rows), bf16),
             pltpu.VMEM((groups, unit_rows), f32),
             small_sems,
             panel_sems,
-            out_sems,
+            pltpu.SemaphoreType.DMA((1,)),
         ],
     )
     downward = [
@@ -435,12 +429,10 @@
         [
             ((groups, unit_rows), f32),
             ((groups, half * day_cols), f32),
-            pltpu.HBM((members, groups, day_cols), f32),
+            pltpu.VMEM((members, groups, day_cols), f32),
         ],
         "time_gradient",
         (over_days(pack), high, low, more_high, more_low, norms, raised_units, ends),
-        out_specs=[vmem, vmem, hbm],
-        scratch_shapes=[pltpu.VMEM((groups, day_cols), f32), pltpu.SemaphoreType.DMA((members,))],
     )
     sent_scaled = to_other_half(scaled)
     all_grads = over_first_half(grads)

time: 35.2 us -> 35.2 us (level)
  no operation moved by 1% of the time
where the time goes in v23:
time: 35.2 us; the launch traced here: 34.7 us
  starting transfers between devices  18.7 us (53%)
  Pallas kernels  8.28 us (24%)
  waiting for transfers between devices  4.91 us (14%)
  blocking collectives  2.2 us (6%)
  between operations  0.7 us (2%)
    pallas_call x7, Pallas kernels, call(): pl.pallas_call(kernel, in_specs=in_specs or [vmem] * len(args), out_specs...  8.28 us
    all_to_all x1, starting transfers between devices, over_units(): lax.all_to_all(value, ('unit', 'day'), split_axis=0, concat_axis=0, axis_...  7.83 us
    all_to_all x1, starting transfers between devices, over_first_half(): lax.all_to_all(value, ('unit', 'day'), split_axis=0, concat_axis=0, axis_...  5.07 us
    all_to_all x1, waiting for transfers between devices, over_first_half(): lax.all_to_all(value, ('unit', 'day'), split_axis=0, concat_axis=0, axis_...  2.72 us
    ppermute x2, starting transfers between devices, to_other_half(): return lax.ppermute(value, ('unit', 'day'), pairs)  2.56 us
    all_gather x1, blocking collectives, over_days(): return lax.all_gather(value, 'day', axis_index_groups=halves)  2.2 us
    ppermute x1, starting transfers between devices, local(): time_norms.append(lax.ppermute(time_norm, ('unit', 'day'), pairs))  1.92 us
    all_to_all x1, waiting for transfers between devices, over_units(): lax.all_to_all(value, ('unit', 'day'), split_axis=0, concat_axis=0, axis_...  1.61 us
  transfers between devices with their start and end apart: 6, of which 4 were waited for; matrix products, arithmetic and copies ran while one was open for 0% of the time, Pallas kernels for 9%

profile of v23, /device:TPU:0, one launch (start us, length us, event | category | flops | bytes accessed | tf_op | source)
XLA Modules:
  0.0 34.7 jit_solution(12110500049198205110)
XLA Ops:
  0.6 3.8 %first_product.1 = (f32[8,1,4224]{2,1,0:T(1,128)}, f32[8,4096]{1,0:T(8,128)}, f32[8,256]{1,0:T(8,128)S(1)}, f32[8,128]{1,0:T(8,128)S(1)}, f32[8,128]{1,0:T(8,128...) custom-call(f32[4096,256]{1,0:T(8,128)} %panel.1, s32[1,4096]{1,0:T(1,128)} %bitcast.5, ...), custom_call_target="tpu_custom_call" | custom-call | tf_op jit(solution)/shard_map/first_product/pallas_call | solution.py:351
  4.4 7.8 %all-to-all-start = ((f32[8,1,4224]{2,1,0:T(1,128)}), f32[8,1,4224]{2,1,0:T(1,128)S(1)}, u32[]{:S(2)}, u32[]{:S(2)}) async-start(f32[8,1,4224]{2,1,0:T(1,128)} %get-tuple-element.19), calls=%async_computation | async-start | bytes 270336 | tf_op jit(solution)/shard_map/all_to_all | solution.py:346
  12.3 1.3 %collective-permute-start = (f32[8,4096]{1,0:T(8,128)}, f32[8,4096]{1,0:T(8,128)S(1)}, u32[]{:S(2)}, u32[]{:S(2)}) collective-permute-start(f32[8,4096]{1,0:T(8,128)} %get-tuple-element.25), channel_id=1, source_target_pairs={{2,0},{3,1},{6,4},{7,5},{10,8},{11,9},{14,12},{15,13},{18,16},{19,... | collective-permute-start | bytes 393224 | tf_op jit(solution)/shard_map/ppermute | solution.py:397
  13.6 1.9 %collective-permute-start.1 = (f32[8,128]{1,0:T(8,128)S(1)}, f32[8,128]{1,0:T(8,128)S(1)}, u32[]{:S(2)}, u32[]{:S(2)}) collective-permute-start(f32[8,128]{1,0:T(8,128)S(1)} %get-tuple-element.26.refs_0_), channel_id=1, source_target_pairs={{0,1},{1,0},{4,5},{5,4},{8,9},{9,8},{12,13},{13,12},{16,17},{17,16... | collective-permute-start | bytes 12296 | tf_op jit(solution)/shard_map/ppermute | solution.py:419
  15.5 1.6 %all-to-all-done.sums = f32[8,1,4224]{2,1,0:T(1,128)S(1)} async-done(((f32[8,1,4224]{2,1,0:T(1,128)}), f32[8,1,4224]{2,1,0:T(1,128)S(1)}, u32[]{:S(2)}, u32[]{:S(2)}) %all-to-all-start) | async-done | bytes 135200 | tf_op jit(solution)/shard_map/all_to_all | solution.py:346
  17.1 2.0 %unit_gradient.1 = (f32[16,4352]{1,0:T(8,128)S(1)}, f32[8,128]{1,0:T(8,128)S(1)}, f32[8,4096]{1,0:T(8,128)S(1)}, bf16[1024,256]{1,0:T(8,128)(2,1)S(1)}, bf16[1024,256]{1,0:T(8,128)(2,1)S(1)}) custom-call(f32[4096,256]{1,0:T(8,128)} %panel.1, s32[1,4096]{1,0:T(1,128)} %bitcast.6, f32[8,4096]{1,0:T(8,128)} %unit_logit.1, f32[8,1,4224]{2,1,0:T(1,128)S(1)} %all-to-all-done.sums, ...), custom_call_target="tpu_custom_call" | custom-call | tf_op jit(solution)/shard_map/unit_gradient/pallas_call | solution.py:351
  19.1 0.0 collective-permute-done.1.refs_1_
  19.1 0.2 collective-permute-done.post
  19.3 0.1 join_post.1
  19.4 2.2 %all-gather = f32[32,4352]{1,0:T(8,128)S(1)} all-gather(f32[16,4352]{1,0:T(8,128)S(1)} %join_post.1), channel_id=2, replica_groups={{0,1},{2,3},{4,5},{6,7},{8,9},{10,11},{12,13},{14,15},{16,17},{18,19},{..., dimensions={0}, use_global_device_ids=true | all-gather | bytes 835584 | tf_op jit(solution)/shard_map/all_gather | solution.py:330
  21.6 1.4 %time_gradient.1 = (f32[8,4096]{1,0:T(8,128)S(1)}, f32[8,512]{1,0:T(8,128)S(1)}, f32[16,8,256]{2,1,0:T(8,128)}) custom-call(f32[2,16,4352]{2,1,0:T(8,128)S(1)} %bitcast.4, bf16[3072,256]{1,0:T(8,128)(2,1)S(1)} %get-tuple-element.22.high_ref.refs_1_, bf16[3072,256]{1,0:T(8,128)(2,1)S(1)} %get-tuple-element.23.low_ref.refs_2_, ...), custom_call_target="tpu_custom_call" | custom-call | tf_op jit(solution)/shard_map/time_gradient/pallas_call | solution.py:351
  23.0 5.1 %all-to-all-start.1 = ((f32[16,8,256]{2,1,0:T(8,128)}), f32[16,8,256]{2,1,0:T(8,128)S(1)}, u32[]{:S(2)}, u32[]{:S(2)}) async-start(f32[16,8,256]{2,1,0:T(8,128)} %get-tuple-element.31), calls=%async_computation.1 | async-start | bytes 262144 | tf_op jit(solution)/shard_map/all_to_all | solution.py:337
  28.1 1.3 %collective-permute-start.3 = (f32[8,4096]{1,0:T(8,128)S(1)}, f32[8,4096]{1,0:T(8,128)S(1)}, u32[]{:S(2)}, u32[]{:S(2)}) collective-permute-start(f32[8,4096]{1,0:T(8,128)S(1)} %get-tuple-element.32.scaled), channel_id=1, source_target_pairs={{0,2},{1,3},{4,6},{5,7},{8,10},{9,11},{12,14},{13,15},{16,18},{17,... | collective-permute-start | bytes 393224 | tf_op jit(solution)/shard_map/ppermute | solution.py:326
  29.3 2.7 %all-to-all-done.1.grads = f32[16,8,256]{2,1,0:T(8,128)S(1)} async-done(((f32[16,8,256]{2,1,0:T(8,128)}), f32[16,8,256]{2,1,0:T(8,128)S(1)}, u32[]{:S(2)}, u32[]{:S(2)}) %all-to-all-start.1) | async-done | bytes 131104 | tf_op jit(solution)/shard_map/all_to_all | solution.py:337
  32.1 0.1 unit_totals.1.totals
  32.1 1.3 %collective-permute-start.2 = (f32[8,128]{1,0:T(8,128)S(1)}, f32[8,128]{1,0:T(8,128)S(1)}, u32[]{:S(2)}, u32[]{:S(2)}) collective-permute-start(f32[8,128]{1,0:T(8,128)S(1)} %unit_totals.1.totals), channel_id=1, source_target_pairs={{0,3},{1,2},{4,7},{5,6},{8,11},{9,10},{12,15},{13,14},{16,19},{17,... | collective-permute-start | bytes 12296 | tf_op jit(solution)/shard_map/ppermute | solution.py:326
  33.4 0.9 %scale_weights.1 = (f32[8,4096]{1,0:T(8,128)}, f32[8,256]{1,0:T(8,128)}) custom-call(f32[8,128]{1,0:T(8,128)S(1)} %unit_totals.1.totals, f32[8,4096]{1,0:T(8,128)S(1)} %get-tuple-element.32.scaled, f32[16,8,256]{2,1,0:T(8,128)S(1)} %all-to-all-done.1.grads, f32[8,512]{1,0:T(8,128)S(1)} %get-tuple-element.33.lam, ...), custom_call_target="tpu_custom_call" | custom-call | tf_op jit(solution)/shard_map/scale_weights/pallas_call | solution.py:351
  34.3 0.0 collective-permute-done.3.sent_scaled
  34.3 0.4 %collective-permute-done.2.sent_totals = f32[8,128]{1,0:T(8,128)S(1)} collective-permute-done((f32[8,128]{1,0:T(8,128)S(1)}, f32[8,128]{1,0:T(8,128)S(1)}, u32[]{:S(2)}, u32[]{:S(2)}) %collective-permute-start.2) | collective-permute-done | bytes 4128 | tf_op jit(solution)/shard_map/ppermute | solution.py:326
  (1 shorter events, 0.0 us)
Async XLA Ops:
  4.4 12.7 %all-to-all-start = ((f32[8,1,4224]{2,1,0:T(1,128)}), f32[8,1,4224]{2,1,0:T(1,128)S(1)}, u32[]{:S(2)}, u32[]{:S(2)}) async-start(f32[8,1,4224]{2,1,0:T(1,128)} %get-tuple-element.19), calls=%async_computation | async-start | bytes 270336 | tf_op jit(solution)/shard_map/all_to_all | solution.py:346
  12.3 7.1 %collective-permute-start = (f32[8,4096]{1,0:T(8,128)}, f32[8,4096]{1,0:T(8,128)S(1)}, u32[]{:S(2)}, u32[]{:S(2)}) collective-permute-start(f32[8,4096]{1,0:T(8,128)} %get-tuple-element.25), channel_id=1, source_target_pairs={{2,0},{3,1},{6,4},{7,5},{10,8},{11,9},{14,12},{15,13},{18,16},{19,... | collective-permute-start | bytes 393224 | tf_op jit(solution)/shard_map/ppermute | solution.py:397
  13.6 5.6 %collective-permute-start.1 = (f32[8,128]{1,0:T(8,128)S(1)}, f32[8,128]{1,0:T(8,128)S(1)}, u32[]{:S(2)}, u32[]{:S(2)}) collective-permute-start(f32[8,128]{1,0:T(8,128)S(1)} %get-tuple-element.26.refs_0_), channel_id=1, source_target_pairs={{0,1},{1,0},{4,5},{5,4},{8,9},{9,8},{12,13},{13,12},{16,17},{17,16... | collective-permute-start | bytes 12296 | tf_op jit(solution)/shard_map/ppermute | solution.py:419
  23.0 9.1 %all-to-all-start.1 = ((f32[16,8,256]{2,1,0:T(8,128)}), f32[16,8,256]{2,1,0:T(8,128)S(1)}, u32[]{:S(2)}, u32[]{:S(2)}) async-start(f32[16,8,256]{2,1,0:T(8,128)} %get-tuple-element.31), calls=%async_computation.1 | async-start | bytes 262144 | tf_op jit(solution)/shard_map/all_to_all | solution.py:337
  28.1 6.3 %collective-permute-start.3 = (f32[8,4096]{1,0:T(8,128)S(1)}, f32[8,4096]{1,0:T(8,128)S(1)}, u32[]{:S(2)}, u32[]{:S(2)}) collective-permute-start(f32[8,4096]{1,0:T(8,128)S(1)} %get-tuple-element.32.scaled), channel_id=1, source_target_pairs={{0,2},{1,3},{4,6},{5,7},{8,10},{9,11},{12,14},{13,15},{16,18},{17,... | collective-permute-start | bytes 393224 | tf_op jit(solution)/shard_map/ppermute | solution.py:326
  32.1 2.6 %collective-permute-start.2 = (f32[8,128]{1,0:T(8,128)S(1)}, f32[8,128]{1,0:T(8,128)S(1)}, u32[]{:S(2)}, u32[]{:S(2)}) collective-permute-start(f32[8,128]{1,0:T(8,128)S(1)} %unit_totals.1.totals), channel_id=1, source_target_pairs={{0,3},{1,2},{4,7},{5,6},{8,11},{9,10},{12,15},{13,14},{16,19},{17,... | collective-permute-start | bytes 12296 | tf_op jit(solution)/shard_map/ppermute | solution.py:326

commit v24 on v22

--- a/solution.py
+++ b/solution.py
@@ -131,7 +131,7 @@
         for i, count in enumerate(counts):
             norms += jnp.where(lane == i * groups + slot, count, 0.0)
         block[:, 2 * groups * day_cols :] = jnp.sum(norms, axis=0, keepdims=True)
-        product = jnp.zeros((4 * groups, 2 * day_cols), f32)
+        product = jnp.zeros((4 * groups, day_cols), f32)
         for start, rows, copy in parts:
             copy.wait()
             for here in blocks_of(start, rows):
@@ -139,9 +139,7 @@
                 if here.start < resident:
                     high_ref[here, :] = high
                     low_ref[here, :] = low
-                both = jnp.concatenate([high, low], axis=1)
-                product += jnp.dot(left_ref[:, here], both, preferred_element_type=f32)
-        product = product[:, :day_cols] + product[:, day_cols:]
+                product += rows_dot(left_ref[:, here], high, low)
         both_sums = jnp.concatenate([add_terms(product, groups), product[2 * groups :][:groups]], axis=0)
         for row in range(2 * groups):
             block[:, row * day_cols : (row + 1) * day_cols] = both_sums[row : row + 1, :]
@@ -236,7 +234,7 @@
 @first_half_only
 def third_kernel(half, *refs):
     parts, refs = [refs[0].at[day] for day in range(half)], refs[1:]
-    high_ref, low_ref, more_high, more_low, norms, raised_units, ends, scaled, lam, out, block, out_sems = refs
+    high_ref, low_ref, more_high, more_low, norms, raised_units, ends, scaled, lam, out = refs
     groups, unit_rows = raised_units.shape
     resident, day_cols = high_ref.shape
     unit_norm, ctrl_count = norms[:, 0:1], norms[:, 1:2]
@@ -245,7 +243,7 @@
     me = lax.rem(lax.axis_index("day"), half)
     for day in range(half):
         lam[:, day * day_cols : (day + 1) * day_cols] = parts[day][:groups, unit_rows:]
-    time_grad = jnp.zeros((2 * groups, 2 * day_cols), f32)
+    time_grad = jnp.zeros((groups, day_cols), f32)
     new_sum = jnp.zeros((groups, 1), f32)
     for start in range(0, unit_rows, block_rows):
         here = pl.ds(start, block_rows)
@@ -260,12 +258,12 @@
         else:
             there = pl.ds(start - resident, block_rows)
             high, low = more_high[there, :], more_low[there, :]
-        time_grad += jnp.dot(left, jnp.concatenate([high, low], axis=1), preferred_element_type=f32)
-    time_grad = add_terms(time_grad[:, :day_cols] + time_grad[:, day_cols:], groups)
+        time_grad += add_terms(rows_dot(left, high, low), groups)
     lane = lax.broadcasted_iota(jnp.int32, (groups, day_cols), 1)
     spare = (lane == day_cols - 1) & (me == half - 1)
-    block[...] = jnp.where(spare, new_sum, time_grad)
-    wait_all(repeat_start(block, out, out_sems))
+    block = jnp.where(spare, new_sum, time_grad)
+    for member in range(out.shape[0]):
+        out[member] = block
 
 
 def time_grad_of(grads, unit_devices, half, day):
@@ -316,7 +314,7 @@
     half = day_devices // 2
     assert half * 2 == day_devices and half & (half - 1) == 0
     assert unit_devices & (unit_devices - 1) == 0
-    panel_starts = [0, unit_rows // 4, unit_rows // 8 * 5, unit_rows]
+    panel_starts = [0, unit_rows // 8 * 3, unit_rows // 4 * 3, unit_rows]
     resident = unit_rows * 3 // 4 // block_rows * block_rows
     def meeting_at(first):
         return [first] + [unit for unit in reversed(range(unit_devices)) if unit != first]
@@ -435,12 +433,10 @@
         [
             ((groups, unit_rows), f32),
             ((groups, half * day_cols), f32),
-            pltpu.HBM((members, groups, day_cols), f32),
+            ((members, groups, day_cols), f32),
         ],
         "time_gradient",
         (over_days(pack), high, low, more_high, more_low, norms, raised_units, ends),
-        out_specs=[vmem, vmem, hbm],
-        scratch_shapes=[pltpu.VMEM((groups, day_cols), f32), pltpu.SemaphoreType.DMA((members,))],
     )
     sent_scaled = to_other_half(scaled)
     all_grads = over_first_half(grads)

time: 35.2 us -> 35 us (level)
  no operation moved by 1% of the time
where the time goes in v24:
time: 35 us; the launch traced here: 34.5 us
  starting transfers between devices  18.7 us (53%)
  Pallas kernels  8.05 us (23%)
  waiting for transfers between devices  4.92 us (14%)
  blocking collectives  2.2 us (6%)
  between operations  0.7 us (2%)
    pallas_call x7, Pallas kernels, call(): pl.pallas_call(kernel, in_specs=in_specs or [vmem] * len(args), out_specs...  8.05 us
    all_to_all x1, starting transfers between devices, over_units(): lax.all_to_all(value, ('unit', 'day'), split_axis=0, concat_axis=0, axis_...  7.83 us
    all_to_all x1, starting transfers between devices, over_first_half(): lax.all_to_all(value, ('unit', 'day'), split_axis=0, concat_axis=0, axis_...  5.07 us
    all_to_all x1, waiting for transfers between devices, over_first_half(): lax.all_to_all(value, ('unit', 'day'), split_axis=0, concat_axis=0, axis_...  2.72 us
    ppermute x2, starting transfers between devices, to_other_half(): return lax.ppermute(value, ('unit', 'day'), pairs)  2.56 us
    all_gather x1, blocking collectives, over_days(): return lax.all_gather(value, 'day', axis_index_groups=halves)  2.2 us
    ppermute x1, starting transfers between devices, local(): time_norms.append(lax.ppermute(time_norm, ('unit', 'day'), pairs))  1.92 us
    all_to_all x1, waiting for transfers between devices, over_units(): lax.all_to_all(value, ('unit', 'day'), split_axis=0, concat_axis=0, axis_...  1.61 us
  transfers between devices with their start and end apart: 6, of which 4 were waited for; matrix products, arithmetic and copies ran while one was open for 0% of the time, Pallas kernels for 9%

profile of v24, /device:TPU:0, one launch (start us, length us, event | category | flops | bytes accessed | tf_op | source)
XLA Modules:
  0.0 34.5 jit_solution(15250002049506390214)
XLA Ops:
  0.6 3.6 %first_product.1 = (f32[8,1,4224]{2,1,0:T(1,128)}, f32[8,4096]{1,0:T(8,128)}, f32[8,256]{1,0:T(8,128)S(1)}, f32[8,128]{1,0:T(8,128)S(1)}, f32[8,128]{1,0:T(8,128...) custom-call(f32[4096,256]{1,0:T(8,128)} %panel.1, s32[1,4096]{1,0:T(1,128)} %bitcast.5, ...), custom_call_target="tpu_custom_call" | custom-call | tf_op jit(solution)/shard_map/first_product/pallas_call | solution.py:353
  4.2 7.8 %all-to-all-start = ((f32[8,1,4224]{2,1,0:T(1,128)}), f32[8,1,4224]{2,1,0:T(1,128)S(1)}, u32[]{:S(2)}, u32[]{:S(2)}) async-start(f32[8,1,4224]{2,1,0:T(1,128)} %get-tuple-element.19), calls=%async_computation | async-start | bytes 270336 | tf_op jit(solution)/shard_map/all_to_all | solution.py:348
  12.0 1.3 %collective-permute-start = (f32[8,4096]{1,0:T(8,128)}, f32[8,4096]{1,0:T(8,128)S(1)}, u32[]{:S(2)}, u32[]{:S(2)}) collective-permute-start(f32[8,4096]{1,0:T(8,128)} %get-tuple-element.25), channel_id=1, source_target_pairs={{2,0},{3,1},{6,4},{7,5},{10,8},{11,9},{14,12},{15,13},{18,16},{19,... | collective-permute-start | bytes 393224 | tf_op jit(solution)/shard_map/ppermute | solution.py:401
  13.3 1.9 %collective-permute-start.1 = (f32[8,128]{1,0:T(8,128)S(1)}, f32[8,128]{1,0:T(8,128)S(1)}, u32[]{:S(2)}, u32[]{:S(2)}) collective-permute-start(f32[8,128]{1,0:T(8,128)S(1)} %get-tuple-element.26.refs_0_), channel_id=1, source_target_pairs={{0,1},{1,0},{4,5},{5,4},{8,9},{9,8},{12,13},{13,12},{16,17},{17,16... | collective-permute-start | bytes 12296 | tf_op jit(solution)/shard_map/ppermute | solution.py:423
  15.3 1.6 %all-to-all-done.sums = f32[8,1,4224]{2,1,0:T(1,128)S(1)} async-done(((f32[8,1,4224]{2,1,0:T(1,128)}), f32[8,1,4224]{2,1,0:T(1,128)S(1)}, u32[]{:S(2)}, u32[]{:S(2)}) %all-to-all-start) | async-done | bytes 135200 | tf_op jit(solution)/shard_map/all_to_all | solution.py:348
  16.9 2.0 %unit_gradient.1 = (f32[16,4352]{1,0:T(8,128)S(1)}, f32[8,128]{1,0:T(8,128)S(1)}, f32[8,4096]{1,0:T(8,128)S(1)}, bf16[1024,256]{1,0:T(8,128)(2,1)S(1)}, bf16[1024,256]{1,0:T(8,128)(2,1)S(1)}) custom-call(f32[4096,256]{1,0:T(8,128)} %panel.1, s32[1,4096]{1,0:T(1,128)} %bitcast.6, f32[8,4096]{1,0:T(8,128)} %unit_logit.1, f32[8,1,4224]{2,1,0:T(1,128)S(1)} %all-to-all-done.sums, ...), custom_call_target="tpu_custom_call" | custom-call | tf_op jit(solution)/shard_map/unit_gradient/pallas_call | solution.py:353
  18.9 0.0 collective-permute-done.1.refs_1_
  18.9 0.2 collective-permute-done.post
  19.1 0.1 join_post.1
  19.2 2.2 %all-gather = f32[32,4352]{1,0:T(8,128)S(1)} all-gather(f32[16,4352]{1,0:T(8,128)S(1)} %join_post.1), channel_id=2, replica_groups={{0,1},{2,3},{4,5},{6,7},{8,9},{10,11},{12,13},{14,15},{16,17},{18,19},{..., dimensions={0}, use_global_device_ids=true | all-gather | bytes 835584 | tf_op jit(solution)/shard_map/all_gather | solution.py:332
  21.4 1.4 %time_gradient.1 = (f32[8,4096]{1,0:T(8,128)S(1)}, f32[8,512]{1,0:T(8,128)S(1)}, f32[16,8,256]{2,1,0:T(8,128)}) custom-call(f32[2,16,4352]{2,1,0:T(8,128)S(1)} %bitcast.4, bf16[3072,256]{1,0:T(8,128)(2,1)S(1)} %get-tuple-element.22.high_ref.refs_1_, bf16[3072,256]{1,0:T(8,128)(2,1)S(1)} %get-tuple-element.23.low_ref.refs_2_, ...), custom_call_target="tpu_custom_call" | custom-call | tf_op jit(solution)/shard_map/time_gradient/pallas_call | solution.py:353
  22.8 5.1 %all-to-all-start.1 = ((f32[16,8,256]{2,1,0:T(8,128)}), f32[16,8,256]{2,1,0:T(8,128)S(1)}, u32[]{:S(2)}, u32[]{:S(2)}) async-start(f32[16,8,256]{2,1,0:T(8,128)} %get-tuple-element.31), calls=%async_computation.1 | async-start | bytes 262144 | tf_op jit(solution)/shard_map/all_to_all | solution.py:339
  27.8 1.3 %collective-permute-start.3 = (f32[8,4096]{1,0:T(8,128)S(1)}, f32[8,4096]{1,0:T(8,128)S(1)}, u32[]{:S(2)}, u32[]{:S(2)}) collective-permute-start(f32[8,4096]{1,0:T(8,128)S(1)} %get-tuple-element.32.scaled), channel_id=1, source_target_pairs={{0,2},{1,3},{4,6},{5,7},{8,10},{9,11},{12,14},{13,15},{16,18},{17,... | collective-permute-start | bytes 393224 | tf_op jit(solution)/shard_map/ppermute | solution.py:328
  29.1 2.7 %all-to-all-done.1.grads = f32[16,8,256]{2,1,0:T(8,128)S(1)} async-done(((f32[16,8,256]{2,1,0:T(8,128)}), f32[16,8,256]{2,1,0:T(8,128)S(1)}, u32[]{:S(2)}, u32[]{:S(2)}) %all-to-all-start.1) | async-done | bytes 131104 | tf_op jit(solution)/shard_map/all_to_all | solution.py:339
  31.8 0.1 unit_totals.1.totals
  31.9 1.3 %collective-permute-start.2 = (f32[8,128]{1,0:T(8,128)S(1)}, f32[8,128]{1,0:T(8,128)S(1)}, u32[]{:S(2)}, u32[]{:S(2)}) collective-permute-start(f32[8,128]{1,0:T(8,128)S(1)} %unit_totals.1.totals), channel_id=1, source_target_pairs={{0,3},{1,2},{4,7},{5,6},{8,11},{9,10},{12,15},{13,14},{16,19},{17,... | collective-permute-start | bytes 12296 | tf_op jit(solution)/shard_map/ppermute | solution.py:328
  33.2 0.9 %scale_weights.1 = (f32[8,4096]{1,0:T(8,128)}, f32[8,256]{1,0:T(8,128)}) custom-call(f32[8,128]{1,0:T(8,128)S(1)} %unit_totals.1.totals, f32[8,4096]{1,0:T(8,128)S(1)} %get-tuple-element.32.scaled, f32[16,8,256]{2,1,0:T(8,128)S(1)} %all-to-all-done.1.grads, f32[8,512]{1,0:T(8,128)S(1)} %get-tuple-element.33.lam, ...), custom_call_target="tpu_custom_call" | custom-call | tf_op jit(solution)/shard_map/scale_weights/pallas_call | solution.py:353
  34.1 0.0 collective-permute-done.3.sent_scaled
  34.1 0.4 %collective-permute-done.2.sent_totals = f32[8,128]{1,0:T(8,128)S(1)} collective-permute-done((f32[8,128]{1,0:T(8,128)S(1)}, f32[8,128]{1,0:T(8,128)S(1)}, u32[]{:S(2)}, u32[]{:S(2)}) %collective-permute-start.2) | collective-permute-done | bytes 4128 | tf_op jit(solution)/shard_map/ppermute | solution.py:328
  (1 shorter events, 0.0 us)
Async XLA Ops:
  4.2 12.7 %all-to-all-start = ((f32[8,1,4224]{2,1,0:T(1,128)}), f32[8,1,4224]{2,1,0:T(1,128)S(1)}, u32[]{:S(2)}, u32[]{:S(2)}) async-start(f32[8,1,4224]{2,1,0:T(1,128)} %get-tuple-element.19), calls=%async_computation | async-start | bytes 270336 | tf_op jit(solution)/shard_map/all_to_all | solution.py:348
  12.0 7.1 %collective-permute-start = (f32[8,4096]{1,0:T(8,128)}, f32[8,4096]{1,0:T(8,128)S(1)}, u32[]{:S(2)}, u32[]{:S(2)}) collective-permute-start(f32[8,4096]{1,0:T(8,128)} %get-tuple-element.25), channel_id=1, source_target_pairs={{2,0},{3,1},{6,4},{7,5},{10,8},{11,9},{14,12},{15,13},{18,16},{19,... | collective-permute-start | bytes 393224 | tf_op jit(solution)/shard_map/ppermute | solution.py:401
  13.3 5.6 %collective-permute-start.1 = (f32[8,128]{1,0:T(8,128)S(1)}, f32[8,128]{1,0:T(8,128)S(1)}, u32[]{:S(2)}, u32[]{:S(2)}) collective-permute-start(f32[8,128]{1,0:T(8,128)S(1)} %get-tuple-element.26.refs_0_), channel_id=1, source_target_pairs={{0,1},{1,0},{4,5},{5,4},{8,9},{9,8},{12,13},{13,12},{16,17},{17,16... | collective-permute-start | bytes 12296 | tf_op jit(solution)/shard_map/ppermute | solution.py:423
  22.8 9.1 %all-to-all-start.1 = ((f32[16,8,256]{2,1,0:T(8,128)}), f32[16,8,256]{2,1,0:T(8,128)S(1)}, u32[]{:S(2)}, u32[]{:S(2)}) async-start(f32[16,8,256]{2,1,0:T(8,128)} %get-tuple-element.31), calls=%async_computation.1 | async-start | bytes 262144 | tf_op jit(solution)/shard_map/all_to_all | solution.py:339
  27.8 6.3 %collective-permute-start.3 = (f32[8,4096]{1,0:T(8,128)S(1)}, f32[8,4096]{1,0:T(8,128)S(1)}, u32[]{:S(2)}, u32[]{:S(2)}) collective-permute-start(f32[8,4096]{1,0:T(8,128)S(1)} %get-tuple-element.32.scaled), channel_id=1, source_target_pairs={{0,2},{1,3},{4,6},{5,7},{8,10},{9,11},{12,14},{13,15},{16,18},{17,... | collective-permute-start | bytes 393224 | tf_op jit(solution)/shard_map/ppermute | solution.py:328
  31.9 2.6 %collective-permute-start.2 = (f32[8,128]{1,0:T(8,128)S(1)}, f32[8,128]{1,0:T(8,128)S(1)}, u32[]{:S(2)}, u32[]{:S(2)}) collective-permute-start(f32[8,128]{1,0:T(8,128)S(1)} %unit_totals.1.totals), channel_id=1, source_target_pairs={{0,3},{1,2},{4,7},{5,6},{8,11},{9,10},{12,15},{13,14},{16,19},{17,... | collective-permute-start | bytes 12296 | tf_op jit(solution)/shard_map/ppermute | solution.py:328

commit v25 on v24

--- a/solution.py
+++ b/solution.py
@@ -204,9 +204,9 @@
 
         late = resident - 2 * block_rows
 
-        @pl.loop(0, late // block_rows)
+        @pl.loop(0, late // (2 * block_rows))
         def _(block):
-            here = pl.ds(pl.multiple_of(block * block_rows, block_rows), block_rows)
+            here = pl.ds(pl.multiple_of(block * 2 * block_rows, 2 * block_rows), 2 * block_rows)
             multiply(here, high_ref[here, :], low_ref[here, :])
 
         wait_all(copies)
@@ -315,7 +315,7 @@
     assert half * 2 == day_devices and half & (half - 1) == 0
     assert unit_devices & (unit_devices - 1) == 0
     panel_starts = [0, unit_rows // 8 * 3, unit_rows // 4 * 3, unit_rows]
-    resident = unit_rows * 3 // 4 // block_rows * block_rows
+    resident = unit_rows * 3 // 4 // (2 * block_rows) * (2 * block_rows)
     def meeting_at(first):
         return [first] + [unit for unit in reversed(range(unit_devices)) if unit != first]
 

time: 35 us -> 35 us (level)
  no operation moved by 1% of the time
where the time goes in v25:
time: 35 us; the launch traced here: 34.5 us
  starting transfers between devices  18.7 us (53%)
  Pallas kernels  8.05 us (23%)
  waiting for transfers between devices  4.92 us (14%)
  blocking collectives  2.2 us (6%)
  between operations  0.7 us (2%)
    pallas_call x7, Pallas kernels, call(): pl.pallas_call(kernel, in_specs=in_specs or [vmem] * len(args), out_specs...  8.05 us
    all_to_all x1, starting transfers between devices, over_units(): lax.all_to_all(value, ('unit', 'day'), split_axis=0, concat_axis=0, axis_...  7.83 us
    all_to_all x1, starting transfers between devices, over_first_half(): lax.all_to_all(value, ('unit', 'day'), split_axis=0, concat_axis=0, axis_...  5.07 us
    all_to_all x1, waiting for transfers between devices, over_first_half(): lax.all_to_all(value, ('unit', 'day'), split_axis=0, concat_axis=0, axis_...  2.72 us
    ppermute x2, starting transfers between devices, to_other_half(): return lax.ppermute(value, ('unit', 'day'), pairs)  2.56 us
    all_gather x1, blocking collectives, over_days(): return lax.all_gather(value, 'day', axis_index_groups=halves)  2.2 us
    ppermute x1, starting transfers between devices, local(): time_norms.append(lax.ppermute(time_norm, ('unit', 'day'), pairs))  1.92 us
    all_to_all x1, waiting for transfers between devices, over_units(): lax.all_to_all(value, ('unit', 'day'), split_axis=0, concat_axis=0, axis_...  1.61 us
  transfers between devices with their start and end apart: 6, of which 4 were waited for; matrix products, arithmetic and copies ran while one was open for 0% of the time, Pallas kernels for 9%

profile of v25, /device:TPU:0, one launch (start us, length us, event | category | flops | bytes accessed | tf_op | source)
XLA Modules:
  0.0 34.5 jit_solution(16637833315501677503)
XLA Ops:
  0.6 3.6 %first_product.1 = (f32[8,1,4224]{2,1,0:T(1,128)}, f32[8,4096]{1,0:T(8,128)}, f32[8,256]{1,0:T(8,128)S(1)}, f32[8,128]{1,0:T(8,128)S(1)}, f32[8,128]{1,0:T(8,128...) custom-call(f32[4096,256]{1,0:T(8,128)} %panel.1, s32[1,4096]{1,0:T(1,128)} %bitcast.5, ...), custom_call_target="tpu_custom_call" | custom-call | tf_op jit(solution)/shard_map/first_product/pallas_call | solution.py:353
  4.2 7.8 %all-to-all-start = ((f32[8,1,4224]{2,1,0:T(1,128)}), f32[8,1,4224]{2,1,0:T(1,128)S(1)}, u32[]{:S(2)}, u32[]{:S(2)}) async-start(f32[8,1,4224]{2,1,0:T(1,128)} %get-tuple-element.19), calls=%async_computation | async-start | bytes 270336 | tf_op jit(solution)/shard_map/all_to_all | solution.py:348
  12.0 1.3 %collective-permute-start = (f32[8,4096]{1,0:T(8,128)}, f32[8,4096]{1,0:T(8,128)S(1)}, u32[]{:S(2)}, u32[]{:S(2)}) collective-permute-start(f32[8,4096]{1,0:T(8,128)} %get-tuple-element.25), channel_id=1, source_target_pairs={{2,0},{3,1},{6,4},{7,5},{10,8},{11,9},{14,12},{15,13},{18,16},{19,... | collective-permute-start | bytes 393224 | tf_op jit(solution)/shard_map/ppermute | solution.py:401
  13.3 1.9 %collective-permute-start.1 = (f32[8,128]{1,0:T(8,128)S(1)}, f32[8,128]{1,0:T(8,128)S(1)}, u32[]{:S(2)}, u32[]{:S(2)}) collective-permute-start(f32[8,128]{1,0:T(8,128)S(1)} %get-tuple-element.26.refs_0_), channel_id=1, source_target_pairs={{0,1},{1,0},{4,5},{5,4},{8,9},{9,8},{12,13},{13,12},{16,17},{17,16... | collective-permute-start | bytes 12296 | tf_op jit(solution)/shard_map/ppermute | solution.py:423
  15.3 1.6 %all-to-all-done.sums = f32[8,1,4224]{2,1,0:T(1,128)S(1)} async-done(((f32[8,1,4224]{2,1,0:T(1,128)}), f32[8,1,4224]{2,1,0:T(1,128)S(1)}, u32[]{:S(2)}, u32[]{:S(2)}) %all-to-all-start) | async-done | bytes 135200 | tf_op jit(solution)/shard_map/all_to_all | solution.py:348
  16.9 2.0 %unit_gradient.1 = (f32[16,4352]{1,0:T(8,128)S(1)}, f32[8,128]{1,0:T(8,128)S(1)}, f32[8,4096]{1,0:T(8,128)S(1)}, bf16[1024,256]{1,0:T(8,128)(2,1)S(1)}, bf16[1024,256]{1,0:T(8,128)(2,1)S(1)}) custom-call(f32[4096,256]{1,0:T(8,128)} %panel.1, s32[1,4096]{1,0:T(1,128)} %bitcast.6, f32[8,4096]{1,0:T(8,128)} %unit_logit.1, f32[8,1,4224]{2,1,0:T(1,128)S(1)} %all-to-all-done.sums, ...), custom_call_target="tpu_custom_call" | custom-call | tf_op jit(solution)/shard_map/unit_gradient/pallas_call | solution.py:353
  18.9 0.0 collective-permute-done.1.refs_1_
  18.9 0.2 collective-permute-done.post
  19.1 0.1 join_post.1
  19.2 2.2 %all-gather = f32[32,4352]{1,0:T(8,128)S(1)} all-gather(f32[16,4352]{1,0:T(8,128)S(1)} %join_post.1), channel_id=2, replica_groups={{0,1},{2,3},{4,5},{6,7},{8,9},{10,11},{12,13},{14,15},{16,17},{18,19},{..., dimensions={0}, use_global_device_ids=true | all-gather | bytes 835584 | tf_op jit(solution)/shard_map/all_gather | solution.py:332
  21.4 1.4 %time_gradient.1 = (f32[8,4096]{1,0:T(8,128)S(1)}, f32[8,512]{1,0:T(8,128)S(1)}, f32[16,8,256]{2,1,0:T(8,128)}) custom-call(f32[2,16,4352]{2,1,0:T(8,128)S(1)} %bitcast.4, bf16[3072,256]{1,0:T(8,128)(2,1)S(1)} %get-tuple-element.22.high_ref.refs_1_, bf16[3072,256]{1,0:T(8,128)(2,1)S(1)} %get-tuple-element.23.low_ref.refs_2_, ...), custom_call_target="tpu_custom_call" | custom-call | tf_op jit(solution)/shard_map/time_gradient/pallas_call | solution.py:353
  22.8 5.1 %all-to-all-start.1 = ((f32[16,8,256]{2,1,0:T(8,128)}), f32[16,8,256]{2,1,0:T(8,128)S(1)}, u32[]{:S(2)}, u32[]{:S(2)}) async-start(f32[16,8,256]{2,1,0:T(8,128)} %get-tuple-element.31), calls=%async_computation.1 | async-start | bytes 262144 | tf_op jit(solution)/shard_map/all_to_all | solution.py:339
  27.8 1.3 %collective-permute-start.3 = (f32[8,4096]{1,0:T(8,128)S(1)}, f32[8,4096]{1,0:T(8,128)S(1)}, u32[]{:S(2)}, u32[]{:S(2)}) collective-permute-start(f32[8,4096]{1,0:T(8,128)S(1)} %get-tuple-element.32.scaled), channel_id=1, source_target_pairs={{0,2},{1,3},{4,6},{5,7},{8,10},{9,11},{12,14},{13,15},{16,18},{17,... | collective-permute-start | bytes 393224 | tf_op jit(solution)/shard_map/ppermute | solution.py:328
  29.1 2.7 %all-to-all-done.1.grads = f32[16,8,256]{2,1,0:T(8,128)S(1)} async-done(((f32[16,8,256]{2,1,0:T(8,128)}), f32[16,8,256]{2,1,0:T(8,128)S(1)}, u32[]{:S(2)}, u32[]{:S(2)}) %all-to-all-start.1) | async-done | bytes 131104 | tf_op jit(solution)/shard_map/all_to_all | solution.py:339
  31.8 0.1 unit_totals.1.totals
  31.9 1.3 %collective-permute-start.2 = (f32[8,128]{1,0:T(8,128)S(1)}, f32[8,128]{1,0:T(8,128)S(1)}, u32[]{:S(2)}, u32[]{:S(2)}) collective-permute-start(f32[8,128]{1,0:T(8,128)S(1)} %unit_totals.1.totals), channel_id=1, source_target_pairs={{0,3},{1,2},{4,7},{5,6},{8,11},{9,10},{12,15},{13,14},{16,19},{17,... | collective-permute-start | bytes 12296 | tf_op jit(solution)/shard_map/ppermute | solution.py:328
  33.2 0.9 %scale_weights.1 = (f32[8,4096]{1,0:T(8,128)}, f32[8,256]{1,0:T(8,128)}) custom-call(f32[8,128]{1,0:T(8,128)S(1)} %unit_totals.1.totals, f32[8,4096]{1,0:T(8,128)S(1)} %get-tuple-element.32.scaled, f32[16,8,256]{2,1,0:T(8,128)S(1)} %all-to-all-done.1.grads, f32[8,512]{1,0:T(8,128)S(1)} %get-tuple-element.33.lam, ...), custom_call_target="tpu_custom_call" | custom-call | tf_op jit(solution)/shard_map/scale_weights/pallas_call | solution.py:353
  34.1 0.0 collective-permute-done.3.sent_scaled
  34.1 0.4 %collective-permute-done.2.sent_totals = f32[8,128]{1,0:T(8,128)S(1)} collective-permute-done((f32[8,128]{1,0:T(8,128)S(1)}, f32[8,128]{1,0:T(8,128)S(1)}, u32[]{:S(2)}, u32[]{:S(2)}) %collective-permute-start.2) | collective-permute-done | bytes 4128 | tf_op jit(solution)/shard_map/ppermute | solution.py:328
  (1 shorter events, 0.0 us)
Async XLA Ops:
  4.2 12.7 %all-to-all-start = ((f32[8,1,4224]{2,1,0:T(1,128)}), f32[8,1,4224]{2,1,0:T(1,128)S(1)}, u32[]{:S(2)}, u32[]{:S(2)}) async-start(f32[8,1,4224]{2,1,0:T(1,128)} %get-tuple-element.19), calls=%async_computation | async-start | bytes 270336 | tf_op jit(solution)/shard_map/all_to_all | solution.py:348
  12.0 7.1 %collective-permute-start = (f32[8,4096]{1,0:T(8,128)}, f32[8,4096]{1,0:T(8,128)S(1)}, u32[]{:S(2)}, u32[]{:S(2)}) collective-permute-start(f32[8,4096]{1,0:T(8,128)} %get-tuple-element.25), channel_id=1, source_target_pairs={{2,0},{3,1},{6,4},{7,5},{10,8},{11,9},{14,12},{15,13},{18,16},{19,... | collective-permute-start | bytes 393224 | tf_op jit(solution)/shard_map/ppermute | solution.py:401
  13.3 5.6 %collective-permute-start.1 = (f32[8,128]{1,0:T(8,128)S(1)}, f32[8,128]{1,0:T(8,128)S(1)}, u32[]{:S(2)}, u32[]{:S(2)}) collective-permute-start(f32[8,128]{1,0:T(8,128)S(1)} %get-tuple-element.26.refs_0_), channel_id=1, source_target_pairs={{0,1},{1,0},{4,5},{5,4},{8,9},{9,8},{12,13},{13,12},{16,17},{17,16... | collective-permute-start | bytes 12296 | tf_op jit(solution)/shard_map/ppermute | solution.py:423
  22.8 9.1 %all-to-all-start.1 = ((f32[16,8,256]{2,1,0:T(8,128)}), f32[16,8,256]{2,1,0:T(8,128)S(1)}, u32[]{:S(2)}, u32[]{:S(2)}) async-start(f32[16,8,256]{2,1,0:T(8,128)} %get-tuple-element.31), calls=%async_computation.1 | async-start | bytes 262144 | tf_op jit(solution)/shard_map/all_to_all | solution.py:339
  27.8 6.3 %collective-permute-start.3 = (f32[8,4096]{1,0:T(8,128)S(1)}, f32[8,4096]{1,0:T(8,128)S(1)}, u32[]{:S(2)}, u32[]{:S(2)}) collective-permute-start(f32[8,4096]{1,0:T(8,128)S(1)} %get-tuple-element.32.scaled), channel_id=1, source_target_pairs={{0,2},{1,3},{4,6},{5,7},{8,10},{9,11},{12,14},{13,15},{16,18},{17,... | collective-permute-start | bytes 393224 | tf_op jit(solution)/shard_map/ppermute | solution.py:328
  31.9 2.6 %collective-permute-start.2 = (f32[8,128]{1,0:T(8,128)S(1)}, f32[8,128]{1,0:T(8,128)S(1)}, u32[]{:S(2)}, u32[]{:S(2)}) collective-permute-start(f32[8,128]{1,0:T(8,128)S(1)} %unit_totals.1.totals), channel_id=1, source_target_pairs={{0,3},{1,2},{4,7},{5,6},{8,11},{9,10},{12,15},{13,14},{16,19},{17,... | collective-permute-start | bytes 12296 | tf_op jit(solution)/shard_map/ppermute | solution.py:328

commit v26 on v25

--- a/solution.py
+++ b/solution.py
@@ -119,20 +119,20 @@
 
     @pl.when(me < half)
     def _():
-        label = lax.broadcasted_iota(jnp.int32, (groups, unit_rows), 0)
-        treated = jnp.where(cohort[...] == label, 1.0, 0.0)
-        control = jnp.where(cohort[...] > label, 1.0, 0.0)
-        raised = jnp.exp(unit_logit[...]) * control
-        left_ref[...] = left_of(raised, treated)
-        lane = lax.broadcasted_iota(jnp.int32, (groups, lanes), 1)
-        counts = [jnp.sum(value, axis=1, keepdims=True) for value in (raised, treated, control)]
-        slot = lax.broadcasted_iota(jnp.int32, (groups, lanes), 0)
-        norms = jnp.zeros((groups, lanes), f32)
-        for i, count in enumerate(counts):
-            norms += jnp.where(lane == i * groups + slot, count, 0.0)
-        block[:, 2 * groups * day_cols :] = jnp.sum(norms, axis=0, keepdims=True)
+        counts = []
+
+        def prepare(start, rows):
+            here = pl.ds(start, rows)
+            label = lax.broadcasted_iota(jnp.int32, (groups, rows), 0)
+            treated = jnp.where(cohort[:, here] == label, 1.0, 0.0)
+            control = jnp.where(cohort[:, here] > label, 1.0, 0.0)
+            raised = jnp.exp(unit_logit[:, here]) * control
+            left_ref[:, here] = left_of(raised, treated)
+            counts.append([jnp.sum(value, axis=1, keepdims=True) for value in (raised, treated, control)])
+
         product = jnp.zeros((4 * groups, day_cols), f32)
-        for start, rows, copy in parts:
+        prepare(*parts[0][:2])
+        for part, (start, rows, copy) in enumerate(parts):
             copy.wait()
             for here in blocks_of(start, rows):
                 high, low = split_panel(panel[here, :])
@@ -140,6 +140,14 @@
                     high_ref[here, :] = high
                     low_ref[here, :] = low
                 product += rows_dot(left_ref[:, here], high, low)
+            if part + 1 < len(parts):
+                prepare(*parts[part + 1][:2])
+        lane = lax.broadcasted_iota(jnp.int32, (groups, lanes), 1)
+        slot = lax.broadcasted_iota(jnp.int32, (groups, lanes), 0)
+        norms = jnp.zeros((groups, lanes), f32)
+        for i, count in enumerate(zip(*counts)):
+            norms += jnp.where(lane == i * groups + slot, sum(count), 0.0)
+        block[:, 2 * groups * day_cols :] = jnp.sum(norms, axis=0, keepdims=True)
         both_sums = jnp.concatenate([add_terms(product, groups), product[2 * groups :][:groups]], axis=0)
         for row in range(2 * groups):
             block[:, row * day_cols : (row + 1) * day_cols] = both_sums[row : row + 1, :]

time: 35 us -> 35 us (level)
  no operation moved by 1% of the time
where the time goes in v26:
time: 35 us; the launch traced here: 34.5 us
  starting transfers between devices  18.7 us (53%)
  Pallas kernels  8.06 us (23%)
  waiting for transfers between devices  4.91 us (14%)
  blocking collectives  2.2 us (6%)
  between operations  0.7 us (2%)
    pallas_call x7, Pallas kernels, call(): pl.pallas_call(kernel, in_specs=in_specs or [vmem] * len(args), out_specs...  8.06 us
    all_to_all x1, starting transfers between devices, over_units(): lax.all_to_all(value, ('unit', 'day'), split_axis=0, concat_axis=0, axis_...  7.83 us
    all_to_all x1, starting transfers between devices, over_first_half(): lax.all_to_all(value, ('unit', 'day'), split_axis=0, concat_axis=0, axis_...  5.07 us
    all_to_all x1, waiting for transfers between devices, over_first_half(): lax.all_to_all(value, ('unit', 'day'), split_axis=0, concat_axis=0, axis_...  2.72 us
    ppermute x2, starting transfers between devices, to_other_half(): return lax.ppermute(value, ('unit', 'day'), pairs)  2.56 us
    all_gather x1, blocking collectives, over_days(): return lax.all_gather(value, 'day', axis_index_groups=halves)  2.2 us
    ppermute x1, starting transfers between devices, local(): time_norms.append(lax.ppermute(time_norm, ('unit', 'day'), pairs))  1.92 us
    all_to_all x1, waiting for transfers between devices, over_units(): lax.all_to_all(value, ('unit', 'day'), split_axis=0, concat_axis=0, axis_...  1.61 us
  transfers between devices with their start and end apart: 6, of which 4 were waited for; matrix products, arithmetic and copies ran while one was open for 0% of the time, Pallas kernels for 9%

profile of v26, /device:TPU:0, one launch (start us, length us, event | category | flops | bytes accessed | tf_op | source)
XLA Modules:
  0.0 34.5 jit_solution(13519310441293214092)
XLA Ops:
  0.6 3.6 %first_product.1 = (f32[8,1,4224]{2,1,0:T(1,128)}, f32[8,4096]{1,0:T(8,128)}, f32[8,256]{1,0:T(8,128)S(1)}, f32[8,128]{1,0:T(8,128)S(1)}, f32[8,128]{1,0:T(8,128...) custom-call(f32[4096,256]{1,0:T(8,128)} %panel.1, s32[1,4096]{1,0:T(1,128)} %bitcast.5, ...), custom_call_target="tpu_custom_call" | custom-call | tf_op jit(solution)/shard_map/first_product/pallas_call | solution.py:361
  4.2 7.8 %all-to-all-start = ((f32[8,1,4224]{2,1,0:T(1,128)}), f32[8,1,4224]{2,1,0:T(1,128)S(1)}, u32[]{:S(2)}, u32[]{:S(2)}) async-start(f32[8,1,4224]{2,1,0:T(1,128)} %get-tuple-element.19), calls=%async_computation | async-start | bytes 270336 | tf_op jit(solution)/shard_map/all_to_all | solution.py:356
  12.1 1.3 %collective-permute-start = (f32[8,4096]{1,0:T(8,128)}, f32[8,4096]{1,0:T(8,128)S(1)}, u32[]{:S(2)}, u32[]{:S(2)}) collective-permute-start(f32[8,4096]{1,0:T(8,128)} %get-tuple-element.25), channel_id=1, source_target_pairs={{2,0},{3,1},{6,4},{7,5},{10,8},{11,9},{14,12},{15,13},{18,16},{19,... | collective-permute-start | bytes 393224 | tf_op jit(solution)/shard_map/ppermute | solution.py:409
  13.3 1.9 %collective-permute-start.1 = (f32[8,128]{1,0:T(8,128)S(1)}, f32[8,128]{1,0:T(8,128)S(1)}, u32[]{:S(2)}, u32[]{:S(2)}) collective-permute-start(f32[8,128]{1,0:T(8,128)S(1)} %get-tuple-element.26.refs_0_), channel_id=1, source_target_pairs={{0,1},{1,0},{4,5},{5,4},{8,9},{9,8},{12,13},{13,12},{16,17},{17,16... | collective-permute-start | bytes 12296 | tf_op jit(solution)/shard_map/ppermute | solution.py:431
  15.3 1.6 %all-to-all-done.sums = f32[8,1,4224]{2,1,0:T(1,128)S(1)} async-done(((f32[8,1,4224]{2,1,0:T(1,128)}), f32[8,1,4224]{2,1,0:T(1,128)S(1)}, u32[]{:S(2)}, u32[]{:S(2)}) %all-to-all-start) | async-done | bytes 135200 | tf_op jit(solution)/shard_map/all_to_all | solution.py:356
  16.9 2.0 %unit_gradient.1 = (f32[16,4352]{1,0:T(8,128)S(1)}, f32[8,128]{1,0:T(8,128)S(1)}, f32[8,4096]{1,0:T(8,128)S(1)}, bf16[1024,256]{1,0:T(8,128)(2,1)S(1)}, bf16[1024,256]{1,0:T(8,128)(2,1)S(1)}) custom-call(f32[4096,256]{1,0:T(8,128)} %panel.1, s32[1,4096]{1,0:T(1,128)} %bitcast.6, f32[8,4096]{1,0:T(8,128)} %unit_logit.1, f32[8,1,4224]{2,1,0:T(1,128)S(1)} %all-to-all-done.sums, ...), custom_call_target="tpu_custom_call" | custom-call | tf_op jit(solution)/shard_map/unit_gradient/pallas_call | solution.py:361
  18.9 0.0 collective-permute-done.1.refs_1_
  18.9 0.2 collective-permute-done.post
  19.1 0.1 join_post.1
  19.2 2.2 %all-gather = f32[32,4352]{1,0:T(8,128)S(1)} all-gather(f32[16,4352]{1,0:T(8,128)S(1)} %join_post.1), channel_id=2, replica_groups={{0,1},{2,3},{4,5},{6,7},{8,9},{10,11},{12,13},{14,15},{16,17},{18,19},{..., dimensions={0}, use_global_device_ids=true | all-gather | bytes 835584 | tf_op jit(solution)/shard_map/all_gather | solution.py:340
  21.4 1.4 %time_gradient.1 = (f32[8,4096]{1,0:T(8,128)S(1)}, f32[8,512]{1,0:T(8,128)S(1)}, f32[16,8,256]{2,1,0:T(8,128)}) custom-call(f32[2,16,4352]{2,1,0:T(8,128)S(1)} %bitcast.4, bf16[3072,256]{1,0:T(8,128)(2,1)S(1)} %get-tuple-element.22.high_ref.refs_1_, bf16[3072,256]{1,0:T(8,128)(2,1)S(1)} %get-tuple-element.23.low_ref.refs_2_, ...), custom_call_target="tpu_custom_call" | custom-call | tf_op jit(solution)/shard_map/time_gradient/pallas_call | solution.py:361
  22.8 5.1 %all-to-all-start.1 = ((f32[16,8,256]{2,1,0:T(8,128)}), f32[16,8,256]{2,1,0:T(8,128)S(1)}, u32[]{:S(2)}, u32[]{:S(2)}) async-start(f32[16,8,256]{2,1,0:T(8,128)} %get-tuple-element.31), calls=%async_computation.1 | async-start | bytes 262144 | tf_op jit(solution)/shard_map/all_to_all | solution.py:347
  27.8 1.3 %collective-permute-start.3 = (f32[8,4096]{1,0:T(8,128)S(1)}, f32[8,4096]{1,0:T(8,128)S(1)}, u32[]{:S(2)}, u32[]{:S(2)}) collective-permute-start(f32[8,4096]{1,0:T(8,128)S(1)} %get-tuple-element.32.scaled), channel_id=1, source_target_pairs={{0,2},{1,3},{4,6},{5,7},{8,10},{9,11},{12,14},{13,15},{16,18},{17,... | collective-permute-start | bytes 393224 | tf_op jit(solution)/shard_map/ppermute | solution.py:336
  29.1 2.7 %all-to-all-done.1.grads = f32[16,8,256]{2,1,0:T(8,128)S(1)} async-done(((f32[16,8,256]{2,1,0:T(8,128)}), f32[16,8,256]{2,1,0:T(8,128)S(1)}, u32[]{:S(2)}, u32[]{:S(2)}) %all-to-all-start.1) | async-done | bytes 131104 | tf_op jit(solution)/shard_map/all_to_all | solution.py:347
  31.8 0.1 unit_totals.1.totals
  31.9 1.3 %collective-permute-start.2 = (f32[8,128]{1,0:T(8,128)S(1)}, f32[8,128]{1,0:T(8,128)S(1)}, u32[]{:S(2)}, u32[]{:S(2)}) collective-permute-start(f32[8,128]{1,0:T(8,128)S(1)} %unit_totals.1.totals), channel_id=1, source_target_pairs={{0,3},{1,2},{4,7},{5,6},{8,11},{9,10},{12,15},{13,14},{16,19},{17,... | collective-permute-start | bytes 12296 | tf_op jit(solution)/shard_map/ppermute | solution.py:336
  33.2 0.9 %scale_weights.1 = (f32[8,4096]{1,0:T(8,128)}, f32[8,256]{1,0:T(8,128)}) custom-call(f32[8,128]{1,0:T(8,128)S(1)} %unit_totals.1.totals, f32[8,4096]{1,0:T(8,128)S(1)} %get-tuple-element.32.scaled, f32[16,8,256]{2,1,0:T(8,128)S(1)} %all-to-all-done.1.grads, f32[8,512]{1,0:T(8,128)S(1)} %get-tuple-element.33.lam, ...), custom_call_target="tpu_custom_call" | custom-call | tf_op jit(solution)/shard_map/scale_weights/pallas_call | solution.py:361
  34.1 0.0 collective-permute-done.3.sent_scaled
  34.1 0.4 %collective-permute-done.2.sent_totals = f32[8,128]{1,0:T(8,128)S(1)} collective-permute-done((f32[8,128]{1,0:T(8,128)S(1)}, f32[8,128]{1,0:T(8,128)S(1)}, u32[]{:S(2)}, u32[]{:S(2)}) %collective-permute-start.2) | collective-permute-done | bytes 4128 | tf_op jit(solution)/shard_map/ppermute | solution.py:336
  (1 shorter events, 0.0 us)
Async XLA Ops:
  4.2 12.7 %all-to-all-start = ((f32[8,1,4224]{2,1,0:T(1,128)}), f32[8,1,4224]{2,1,0:T(1,128)S(1)}, u32[]{:S(2)}, u32[]{:S(2)}) async-start(f32[8,1,4224]{2,1,0:T(1,128)} %get-tuple-element.19), calls=%async_computation | async-start | bytes 270336 | tf_op jit(solution)/shard_map/all_to_all | solution.py:356
  12.1 7.1 %collective-permute-start = (f32[8,4096]{1,0:T(8,128)}, f32[8,4096]{1,0:T(8,128)S(1)}, u32[]{:S(2)}, u32[]{:S(2)}) collective-permute-start(f32[8,4096]{1,0:T(8,128)} %get-tuple-element.25), channel_id=1, source_target_pairs={{2,0},{3,1},{6,4},{7,5},{10,8},{11,9},{14,12},{15,13},{18,16},{19,... | collective-permute-start | bytes 393224 | tf_op jit(solution)/shard_map/ppermute | solution.py:409
  13.3 5.6 %collective-permute-start.1 = (f32[8,128]{1,0:T(8,128)S(1)}, f32[8,128]{1,0:T(8,128)S(1)}, u32[]{:S(2)}, u32[]{:S(2)}) collective-permute-start(f32[8,128]{1,0:T(8,128)S(1)} %get-tuple-element.26.refs_0_), channel_id=1, source_target_pairs={{0,1},{1,0},{4,5},{5,4},{8,9},{9,8},{12,13},{13,12},{16,17},{17,16... | collective-permute-start | bytes 12296 | tf_op jit(solution)/shard_map/ppermute | solution.py:431
  22.8 9.1 %all-to-all-start.1 = ((f32[16,8,256]{2,1,0:T(8,128)}), f32[16,8,256]{2,1,0:T(8,128)S(1)}, u32[]{:S(2)}, u32[]{:S(2)}) async-start(f32[16,8,256]{2,1,0:T(8,128)} %get-tuple-element.31), calls=%async_computation.1 | async-start | bytes 262144 | tf_op jit(solution)/shard_map/all_to_all | solution.py:347
  27.8 6.3 %collective-permute-start.3 = (f32[8,4096]{1,0:T(8,128)S(1)}, f32[8,4096]{1,0:T(8,128)S(1)}, u32[]{:S(2)}, u32[]{:S(2)}) collective-permute-start(f32[8,4096]{1,0:T(8,128)S(1)} %get-tuple-element.32.scaled), channel_id=1, source_target_pairs={{0,2},{1,3},{4,6},{5,7},{8,10},{9,11},{12,14},{13,15},{16,18},{17,... | collective-permute-start | bytes 393224 | tf_op jit(solution)/shard_map/ppermute | solution.py:336
  31.9 2.6 %collective-permute-start.2 = (f32[8,128]{1,0:T(8,128)S(1)}, f32[8,128]{1,0:T(8,128)S(1)}, u32[]{:S(2)}, u32[]{:S(2)}) collective-permute-start(f32[8,128]{1,0:T(8,128)S(1)} %unit_totals.1.totals), channel_id=1, source_target_pairs={{0,3},{1,2},{4,7},{5,6},{8,11},{9,10},{12,15},{13,14},{16,19},{17,... | collective-permute-start | bytes 12296 | tf_op jit(solution)/shard_map/ppermute | solution.py:336

commit v27 on v26

--- a/solution.py
+++ b/solution.py
@@ -84,9 +84,9 @@
 
 def fetch_rows(source, target, sems, starts):
     spans = [(start, stop - start) for start, stop in zip(starts, starts[1:])]
-    parts = [pl.ds(*span) for span in spans]
-    copies = fetch([source.at[here] for here in parts], [target.at[here] for here in parts], sems)
-    return [(*span, copy) for span, copy in zip(spans, copies)]
+    blocks = blocks_of(0, source.shape[0])
+    copies = fetch([source.at[here] for here in blocks], [target.at[here] for here in blocks], sems)
+    return [(start, rows, copies[start // block_rows : (start + rows) // block_rows]) for start, rows in spans]
 
 
 def blocks_of(start, rows):
@@ -132,8 +132,8 @@
 
         product = jnp.zeros((4 * groups, day_cols), f32)
         prepare(*parts[0][:2])
-        for part, (start, rows, copy) in enumerate(parts):
-            copy.wait()
+        for part, (start, rows, copies) in enumerate(parts):
+            wait_all(copies)
             for here in blocks_of(start, rows):
                 high, low = split_panel(panel[here, :])
                 if here.start < resident:
@@ -166,8 +166,8 @@
         post_start = column(post_row)
         after = jnp.where(days_of(me, (groups, day_cols)) >= post_start, 1.0, 0.0)
         left = left_of(after / (all_count - post_start).astype(f32))
-        for start, rows, copy in parts:
-            copy.wait()
+        for start, rows, copies in parts:
+            wait_all(copies)
             for here in blocks_of(start, rows):
                 cross_block[:, here] = add_terms(days_dot(left, *split_panel(panel[here, :])), groups)
         sends = fetch([cross_block], [cross], out_sems)
@@ -373,7 +373,7 @@
     arguments = (outcomes, cohort[None, :], pre_end[None, :], post_start[None, :], unit_logit, time_logit)
     fixed = [pltpu.with_memory_space_constraint(argument, pltpu.HBM) for argument in arguments]
     held = [pltpu.VMEM(argument.shape, argument.dtype) for argument in arguments]
-    small_sems, panel_sems = pltpu.SemaphoreType.DMA((5,)), pltpu.SemaphoreType.DMA((3,))
+    small_sems, panel_sems = pltpu.SemaphoreType.DMA((5,)), pltpu.SemaphoreType.DMA((unit_rows // block_rows,))
     panel_terms = [((resident, day_cols), bf16)] * 2
     other_terms = [((unit_rows - resident, day_cols), bf16)] * 2
     out_sems = pltpu.SemaphoreType.DMA((unit_devices,))

time: 35 us -> 35.3 us (level)
  no operation moved by 1% of the time
where the time goes in v27:
time: 35.3 us; the launch traced here: 34.9 us
  starting transfers between devices  18.7 us (53%)
  Pallas kernels  8.39 us (24%)
  waiting for transfers between devices  4.91 us (14%)
  blocking collectives  2.2 us (6%)
  between operations  0.7 us (2%)
    pallas_call x7, Pallas kernels, call(): pl.pallas_call(kernel, in_specs=in_specs or [vmem] * len(args), out_specs...  8.39 us
    all_to_all x1, starting transfers between devices, over_units(): lax.all_to_all(value, ('unit', 'day'), split_axis=0, concat_axis=0, axis_...  7.83 us
    all_to_all x1, starting transfers between devices, over_first_half(): lax.all_to_all(value, ('unit', 'day'), split_axis=0, concat_axis=0, axis_...  5.07 us
    all_to_all x1, waiting for transfers between devices, over_first_half(): lax.all_to_all(value, ('unit', 'day'), split_axis=0, concat_axis=0, axis_...  2.72 us
    ppermute x2, starting transfers between devices, to_other_half(): return lax.ppermute(value, ('unit', 'day'), pairs)  2.56 us
    all_gather x1, blocking collectives, over_days(): return lax.all_gather(value, 'day', axis_index_groups=halves)  2.2 us
    ppermute x1, starting transfers between devices, local(): time_norms.append(lax.ppermute(time_norm, ('unit', 'day'), pairs))  1.92 us
    all_to_all x1, waiting for transfers between devices, over_units(): lax.all_to_all(value, ('unit', 'day'), split_axis=0, concat_axis=0, axis_...  1.61 us
  transfers between devices with their start and end apart: 6, of which 4 were waited for; matrix products, arithmetic and copies ran while one was open for 0% of the time, Pallas kernels for 9%

profile of v27, /device:TPU:0, one launch (start us, length us, event | category | flops | bytes accessed | tf_op | source)
XLA Modules:
  0.0 34.9 jit_solution(13103709385888981729)
XLA Ops:
  0.6 3.9 %first_product.1 = (f32[8,1,4224]{2,1,0:T(1,128)}, f32[8,4096]{1,0:T(8,128)}, f32[8,256]{1,0:T(8,128)S(1)}, f32[8,128]{1,0:T(8,128)S(1)}, f32[8,128]{1,0:T(8,128...) custom-call(f32[4096,256]{1,0:T(8,128)} %panel.1, s32[1,4096]{1,0:T(1,128)} %bitcast.5, ...), custom_call_target="tpu_custom_call" | custom-call | tf_op jit(solution)/shard_map/first_product/pallas_call | solution.py:361
  4.6 7.8 %all-to-all-start = ((f32[8,1,4224]{2,1,0:T(1,128)}), f32[8,1,4224]{2,1,0:T(1,128)S(1)}, u32[]{:S(2)}, u32[]{:S(2)}) async-start(f32[8,1,4224]{2,1,0:T(1,128)} %get-tuple-element.19), calls=%async_computation | async-start | bytes 270336 | tf_op jit(solution)/shard_map/all_to_all | solution.py:356
  12.4 1.3 %collective-permute-start = (f32[8,4096]{1,0:T(8,128)}, f32[8,4096]{1,0:T(8,128)S(1)}, u32[]{:S(2)}, u32[]{:S(2)}) collective-permute-start(f32[8,4096]{1,0:T(8,128)} %get-tuple-element.25), channel_id=1, source_target_pairs={{2,0},{3,1},{6,4},{7,5},{10,8},{11,9},{14,12},{15,13},{18,16},{19,... | collective-permute-start | bytes 393224 | tf_op jit(solution)/shard_map/ppermute | solution.py:409
  13.7 1.9 %collective-permute-start.1 = (f32[8,128]{1,0:T(8,128)S(1)}, f32[8,128]{1,0:T(8,128)S(1)}, u32[]{:S(2)}, u32[]{:S(2)}) collective-permute-start(f32[8,128]{1,0:T(8,128)S(1)} %get-tuple-element.26.refs_0_), channel_id=1, source_target_pairs={{0,1},{1,0},{4,5},{5,4},{8,9},{9,8},{12,13},{13,12},{16,17},{17,16... | collective-permute-start | bytes 12296 | tf_op jit(solution)/shard_map/ppermute | solution.py:431
  15.6 1.6 %all-to-all-done.sums = f32[8,1,4224]{2,1,0:T(1,128)S(1)} async-done(((f32[8,1,4224]{2,1,0:T(1,128)}), f32[8,1,4224]{2,1,0:T(1,128)S(1)}, u32[]{:S(2)}, u32[]{:S(2)}) %all-to-all-start) | async-done | bytes 135200 | tf_op jit(solution)/shard_map/all_to_all | solution.py:356
  17.2 2.0 %unit_gradient.1 = (f32[16,4352]{1,0:T(8,128)S(1)}, f32[8,128]{1,0:T(8,128)S(1)}, f32[8,4096]{1,0:T(8,128)S(1)}, bf16[1024,256]{1,0:T(8,128)(2,1)S(1)}, bf16[1024,256]{1,0:T(8,128)(2,1)S(1)}) custom-call(f32[4096,256]{1,0:T(8,128)} %panel.1, s32[1,4096]{1,0:T(1,128)} %bitcast.6, f32[8,4096]{1,0:T(8,128)} %unit_logit.1, f32[8,1,4224]{2,1,0:T(1,128)S(1)} %all-to-all-done.sums, ...), custom_call_target="tpu_custom_call" | custom-call | tf_op jit(solution)/shard_map/unit_gradient/pallas_call | solution.py:361
  19.3 0.0 collective-permute-done.1.refs_1_
  19.3 0.2 collective-permute-done.post
  19.4 0.1 join_post.1
  19.5 2.2 %all-gather = f32[32,4352]{1,0:T(8,128)S(1)} all-gather(f32[16,4352]{1,0:T(8,128)S(1)} %join_post.1), channel_id=2, replica_groups={{0,1},{2,3},{4,5},{6,7},{8,9},{10,11},{12,13},{14,15},{16,17},{18,19},{..., dimensions={0}, use_global_device_ids=true | all-gather | bytes 835584 | tf_op jit(solution)/shard_map/all_gather | solution.py:340
  21.7 1.4 %time_gradient.1 = (f32[8,4096]{1,0:T(8,128)S(1)}, f32[8,512]{1,0:T(8,128)S(1)}, f32[16,8,256]{2,1,0:T(8,128)}) custom-call(f32[2,16,4352]{2,1,0:T(8,128)S(1)} %bitcast.4, bf16[3072,256]{1,0:T(8,128)(2,1)S(1)} %get-tuple-element.22.high_ref.refs_1_, bf16[3072,256]{1,0:T(8,128)(2,1)S(1)} %get-tuple-element.23.low_ref.refs_2_, ...), custom_call_target="tpu_custom_call" | custom-call | tf_op jit(solution)/shard_map/time_gradient/pallas_call | solution.py:361
  23.1 5.1 %all-to-all-start.1 = ((f32[16,8,256]{2,1,0:T(8,128)}), f32[16,8,256]{2,1,0:T(8,128)S(1)}, u32[]{:S(2)}, u32[]{:S(2)}) async-start(f32[16,8,256]{2,1,0:T(8,128)} %get-tuple-element.31), calls=%async_computation.1 | async-start | bytes 262144 | tf_op jit(solution)/shard_map/all_to_all | solution.py:347
  28.2 1.3 %collective-permute-start.3 = (f32[8,4096]{1,0:T(8,128)S(1)}, f32[8,4096]{1,0:T(8,128)S(1)}, u32[]{:S(2)}, u32[]{:S(2)}) collective-permute-start(f32[8,4096]{1,0:T(8,128)S(1)} %get-tuple-element.32.scaled), channel_id=1, source_target_pairs={{0,2},{1,3},{4,6},{5,7},{8,10},{9,11},{12,14},{13,15},{16,18},{17,... | collective-permute-start | bytes 393224 | tf_op jit(solution)/shard_map/ppermute | solution.py:336
  29.5 2.7 %all-to-all-done.1.grads = f32[16,8,256]{2,1,0:T(8,128)S(1)} async-done(((f32[16,8,256]{2,1,0:T(8,128)}), f32[16,8,256]{2,1,0:T(8,128)S(1)}, u32[]{:S(2)}, u32[]{:S(2)}) %all-to-all-start.1) | async-done | bytes 131104 | tf_op jit(solution)/shard_map/all_to_all | solution.py:347
  32.2 0.1 unit_totals.1.totals
  32.3 1.3 %collective-permute-start.2 = (f32[8,128]{1,0:T(8,128)S(1)}, f32[8,128]{1,0:T(8,128)S(1)}, u32[]{:S(2)}, u32[]{:S(2)}) collective-permute-start(f32[8,128]{1,0:T(8,128)S(1)} %unit_totals.1.totals), channel_id=1, source_target_pairs={{0,3},{1,2},{4,7},{5,6},{8,11},{9,10},{12,15},{13,14},{16,19},{17,... | collective-permute-start | bytes 12296 | tf_op jit(solution)/shard_map/ppermute | solution.py:336
  33.5 0.9 %scale_weights.1 = (f32[8,4096]{1,0:T(8,128)}, f32[8,256]{1,0:T(8,128)}) custom-call(f32[8,128]{1,0:T(8,128)S(1)} %unit_totals.1.totals, f32[8,4096]{1,0:T(8,128)S(1)} %get-tuple-element.32.scaled, f32[16,8,256]{2,1,0:T(8,128)S(1)} %all-to-all-done.1.grads, f32[8,512]{1,0:T(8,128)S(1)} %get-tuple-element.33.lam, ...), custom_call_target="tpu_custom_call" | custom-call | tf_op jit(solution)/shard_map/scale_weights/pallas_call | solution.py:361
  34.5 0.0 collective-permute-done.3.sent_scaled
  34.5 0.4 %collective-permute-done.2.sent_totals = f32[8,128]{1,0:T(8,128)S(1)} collective-permute-done((f32[8,128]{1,0:T(8,128)S(1)}, f32[8,128]{1,0:T(8,128)S(1)}, u32[]{:S(2)}, u32[]{:S(2)}) %collective-permute-start.2) | collective-permute-done | bytes 4128 | tf_op jit(solution)/shard_map/ppermute | solution.py:336
  (1 shorter events, 0.0 us)
Async XLA Ops:
  4.6 12.7 %all-to-all-start = ((f32[8,1,4224]{2,1,0:T(1,128)}), f32[8,1,4224]{2,1,0:T(1,128)S(1)}, u32[]{:S(2)}, u32[]{:S(2)}) async-start(f32[8,1,4224]{2,1,0:T(1,128)} %get-tuple-element.19), calls=%async_computation | async-start | bytes 270336 | tf_op jit(solution)/shard_map/all_to_all | solution.py:356
  12.4 7.1 %collective-permute-start = (f32[8,4096]{1,0:T(8,128)}, f32[8,4096]{1,0:T(8,128)S(1)}, u32[]{:S(2)}, u32[]{:S(2)}) collective-permute-start(f32[8,4096]{1,0:T(8,128)} %get-tuple-element.25), channel_id=1, source_target_pairs={{2,0},{3,1},{6,4},{7,5},{10,8},{11,9},{14,12},{15,13},{18,16},{19,... | collective-permute-start | bytes 393224 | tf_op jit(solution)/shard_map/ppermute | solution.py:409
  13.7 5.6 %collective-permute-start.1 = (f32[8,128]{1,0:T(8,128)S(1)}, f32[8,128]{1,0:T(8,128)S(1)}, u32[]{:S(2)}, u32[]{:S(2)}) collective-permute-start(f32[8,128]{1,0:T(8,128)S(1)} %get-tuple-element.26.refs_0_), channel_id=1, source_target_pairs={{0,1},{1,0},{4,5},{5,4},{8,9},{9,8},{12,13},{13,12},{16,17},{17,16... | collective-permute-start | bytes 12296 | tf_op jit(solution)/shard_map/ppermute | solution.py:431
  23.1 9.1 %all-to-all-start.1 = ((f32[16,8,256]{2,1,0:T(8,128)}), f32[16,8,256]{2,1,0:T(8,128)S(1)}, u32[]{:S(2)}, u32[]{:S(2)}) async-start(f32[16,8,256]{2,1,0:T(8,128)} %get-tuple-element.31), calls=%async_computation.1 | async-start | bytes 262144 | tf_op jit(solution)/shard_map/all_to_all | solution.py:347
  28.2 6.3 %collective-permute-start.3 = (f32[8,4096]{1,0:T(8,128)S(1)}, f32[8,4096]{1,0:T(8,128)S(1)}, u32[]{:S(2)}, u32[]{:S(2)}) collective-permute-start(f32[8,4096]{1,0:T(8,128)S(1)} %get-tuple-element.32.scaled), channel_id=1, source_target_pairs={{0,2},{1,3},{4,6},{5,7},{8,10},{9,11},{12,14},{13,15},{16,18},{17,... | collective-permute-start | bytes 393224 | tf_op jit(solution)/shard_map/ppermute | solution.py:336
  32.3 2.6 %collective-permute-start.2 = (f32[8,128]{1,0:T(8,128)S(1)}, f32[8,128]{1,0:T(8,128)S(1)}, u32[]{:S(2)}, u32[]{:S(2)}) collective-permute-start(f32[8,128]{1,0:T(8,128)S(1)} %unit_totals.1.totals), channel_id=1, source_target_pairs={{0,3},{1,2},{4,7},{5,6},{8,11},{9,10},{12,15},{13,14},{16,19},{17,... | collective-permute-start | bytes 12296 | tf_op jit(solution)/shard_map/ppermute | solution.py:336

commit v28 on v26

--- a/solution.py
+++ b/solution.py
@@ -75,17 +75,25 @@
     return guarded
 
 
-def fetch(sources, targets, sems):
-    copies = [pltpu.make_async_copy(*pair, sems.at[i]) for i, pair in enumerate(zip(sources, targets))]
+def describe(sources, targets, sems):
+    return [pltpu.make_async_copy(*pair, sems.at[i]) for i, pair in enumerate(zip(sources, targets))]
+
+
+def start_all(copies):
     for copy in copies:
         copy.start()
+
+
+def fetch(sources, targets, sems):
+    copies = describe(sources, targets, sems)
+    start_all(copies)
     return copies
 
 
 def fetch_rows(source, target, sems, starts):
     spans = [(start, stop - start) for start, stop in zip(starts, starts[1:])]
     parts = [pl.ds(*span) for span in spans]
-    copies = fetch([source.at[here] for here in parts], [target.at[here] for here in parts], sems)
+    copies = describe([source.at[here] for here in parts], [target.at[here] for here in parts], sems)
     return [(*span, copy) for span, copy in zip(spans, copies)]
 
 
@@ -98,27 +106,34 @@
         copy.wait()
 
 
-def repeat_start(block, out, sems):
-    places = [out.at[i] for i in range(out.shape[0])]
-    return fetch([block] * len(places), places, sems)
-
-
 def first_kernel(all_count, half, starts, *refs):
     arguments, refs = refs[:6], refs[6:]
-    out, cross, raised_days, time_norm, ends, high_ref, low_ref, *held, block, left_ref, cross_block, small_sems, panel_sems, out_sems = refs
+    out, cross, raised_days, time_norm, ends, high_ref, low_ref, *held, block, left_ref, cross_block, small_sems, panel_sems, out_sem = refs
     groups, day_cols = held[5].shape
     unit_rows, resident = held[0].shape[0], high_ref.shape[0]
-    (post_copy,) = fetch(arguments[3:4], held[3:4], small_sems)
-    unit_copies = fetch(arguments[1:5:3], held[1:5:3], small_sems.at[pl.ds(1, 2)])
+    me = lax.axis_index("day")
+    panel, cohort, pre_row, post_row, unit_logit, time_logit = held
+    post_copies = describe(arguments[3:4], held[3:4], small_sems)
+    unit_copies = describe(arguments[1:5:3], held[1:5:3], small_sems.at[pl.ds(1, 2)])
+    day_copies = describe(arguments[2:6:3], held[2:6:3], small_sems.at[pl.ds(3, 2)])
     parts = fetch_rows(arguments[0], held[0], panel_sems, starts)
-    day_copies = fetch(arguments[2:6:3], held[2:6:3], small_sems.at[pl.ds(3, 2)])
-    panel, cohort, pre_row, post_row, unit_logit, time_logit = held
-    post_copy.wait()
-    wait_all(unit_copies)
-    me = lax.axis_index("day")
+    panel_copies = [copy for _, _, copy in parts]
+    start_all(panel_copies[:1])
 
     @pl.when(me < half)
     def _():
+        start_all(unit_copies)
+
+    @pl.when(me >= half)
+    def _():
+        start_all(post_copies)
+
+    start_all(panel_copies[1:])
+
+    @pl.when(me < half)
+    def _():
+        start_all(day_copies)
+        wait_all(unit_copies)
         counts = []
 
         def prepare(start, rows):
@@ -151,7 +166,8 @@
         both_sums = jnp.concatenate([add_terms(product, groups), product[2 * groups :][:groups]], axis=0)
         for row in range(2 * groups):
             block[:, row * day_cols : (row + 1) * day_cols] = both_sums[row : row + 1, :]
-        sends = repeat_start(block, out, out_sems)
+        for member in range(out.shape[0]):
+            out[member] = block[...]
         wait_all(day_copies)
         pre_end = column(pre_row)
         ends[...] = jnp.broadcast_to(pre_end.astype(f32), ends.shape)
@@ -159,10 +175,10 @@
         raised_time = jnp.where(before, jnp.exp(time_logit[...]), 0.0)
         raised_days[...] = raised_time
         time_norm[...] = jnp.broadcast_to(jnp.sum(raised_time, axis=1, keepdims=True), time_norm.shape)
-        wait_all(sends)
 
     @pl.when(me >= half)
     def _():
+        wait_all(post_copies)
         post_start = column(post_row)
         after = jnp.where(days_of(me, (groups, day_cols)) >= post_start, 1.0, 0.0)
         left = left_of(after / (all_count - post_start).astype(f32))
@@ -170,9 +186,7 @@
             copy.wait()
             for here in blocks_of(start, rows):
                 cross_block[:, here] = add_terms(days_dot(left, *split_panel(panel[here, :])), groups)
-        sends = fetch([cross_block], [cross], out_sems)
-        wait_all(day_copies)
-        wait_all(sends)
+        wait_all(fetch([cross_block], [cross], out_sem))
 
 
 @first_half_only
@@ -363,7 +377,7 @@
             in_specs=in_specs or [vmem] * len(args),
             out_specs=out_specs or [vmem] * len(shapes),
             out_shape=[
-                shape if isinstance(shape, type(in_hbm)) else jax.ShapeDtypeStruct(*shape) for shape in shapes
+                shape if isinstance(shape, type(cross_hbm)) else jax.ShapeDtypeStruct(*shape) for shape in shapes
             ],
             compiler_params=params,
             name=name,
@@ -376,14 +390,13 @@
     small_sems, panel_sems = pltpu.SemaphoreType.DMA((5,)), pltpu.SemaphoreType.DMA((3,))
     panel_terms = [((resident, day_cols), bf16)] * 2
     other_terms = [((unit_rows - resident, day_cols), bf16)] * 2
-    out_sems = pltpu.SemaphoreType.DMA((unit_devices,))
     width = 2 * groups * day_cols + lanes
-    in_hbm = pltpu.HBM((unit_devices, 1, width), f32)
+    cross_hbm = pltpu.HBM((groups, unit_rows), f32)
     sums, cross, raised_days, time_norm, ends, high, low = call(
         functools.partial(first_kernel, day_devices * day_cols, half, panel_starts),
         [
-            in_hbm,
-            pltpu.HBM((groups, unit_rows), f32),
+            ((unit_devices, 1, width), f32),
+            cross_hbm,
             ((groups, day_cols), f32),
             ((groups, lanes), f32),
             ((groups, lanes), f32),
@@ -392,7 +405,7 @@
         "first_product",
         fixed,
         in_specs=[hbm] * 6,
-        out_specs=[hbm, hbm] + [vmem] * 5,
+        out_specs=[vmem, hbm] + [vmem] * 5,
         scratch_shapes=held
         + [
             pltpu.VMEM((1, width), f32),
@@ -400,7 +413,7 @@
             pltpu.VMEM((groups, unit_rows), f32),
             small_sems,
             panel_sems,
-            out_sems,
+            pltpu.SemaphoreType.DMA((1,)),
         ],
     )
     downward = [

time: 35 us -> 35.5 us (1.014)
  Pallas kernels: 8.06 us -> 8.59 us
    pallas_call x7, Pallas kernels: 8.06 us -> 8.59 us  [call(): pl.pallas_call(kernel, in_specs=in_specs or [vmem] * len(args), out_specs...]
where the time goes in v28:
time: 35.5 us; the launch traced here: 35.1 us
  starting transfers between devices  18.7 us (53%)
  Pallas kernels  8.59 us (24%)
  waiting for transfers between devices  4.91 us (14%)
  blocking collectives  2.2 us (6%)
  between operations  0.7 us (2%)
    pallas_call x7, Pallas kernels, call(): pl.pallas_call(kernel, in_specs=in_specs or [vmem] * len(args), out_specs...  8.59 us
    all_to_all x1, starting transfers between devices, over_units(): lax.all_to_all(value, ('unit', 'day'), split_axis=0, concat_axis=0, axis_...  7.83 us
    all_to_all x1, starting transfers between devices, over_first_half(): lax.all_to_all(value, ('unit', 'day'), split_axis=0, concat_axis=0, axis_...  5.07 us
    all_to_all x1, waiting for transfers between devices, over_first_half(): lax.all_to_all(value, ('unit', 'day'), split_axis=0, concat_axis=0, axis_...  2.72 us
    ppermute x2, starting transfers between devices, to_other_half(): return lax.ppermute(value, ('unit', 'day'), pairs)  2.56 us
    all_gather x1, blocking collectives, over_days(): return lax.all_gather(value, 'day', axis_index_groups=halves)  2.2 us
    ppermute x1, starting transfers between devices, local(): time_norms.append(lax.ppermute(time_norm, ('unit', 'day'), pairs))  1.92 us
    all_to_all x1, waiting for transfers between devices, over_units(): lax.all_to_all(value, ('unit', 'day'), split_axis=0, concat_axis=0, axis_...  1.61 us
  transfers between devices with their start and end apart: 6, of which 4 were waited for; matrix products, arithmetic and copies ran while one was open for 0% of the time, Pallas kernels for 9%

profile of v28, /device:TPU:0, one launch (start us, length us, event | category | flops | bytes accessed | tf_op | source)
XLA Modules:
  0.0 35.1 jit_solution(1200513653284380722)
XLA Ops:
  0.6 4.1 %first_product.1 = (f32[8,1,4224]{2,1,0:T(1,128)}, f32[8,4096]{1,0:T(8,128)}, f32[8,256]{1,0:T(8,128)S(1)}, f32[8,128]{1,0:T(8,128)S(1)}, f32[8,128]{1,0:T(8,128...) custom-call(f32[4096,256]{1,0:T(8,128)} %panel.1, s32[1,4096]{1,0:T(1,128)} %bitcast.5, ...), custom_call_target="tpu_custom_call" | custom-call | tf_op jit(solution)/shard_map/first_product/pallas_call | solution.py:375
  4.8 7.8 %all-to-all-start = ((f32[8,1,4224]{2,1,0:T(1,128)}), f32[8,1,4224]{2,1,0:T(1,128)S(1)}, u32[]{:S(2)}, u32[]{:S(2)}) async-start(f32[8,1,4224]{2,1,0:T(1,128)} %get-tuple-element.19), calls=%async_computation | async-start | bytes 270336 | tf_op jit(solution)/shard_map/all_to_all | solution.py:370
  12.6 1.3 %collective-permute-start = (f32[8,4096]{1,0:T(8,128)}, f32[8,4096]{1,0:T(8,128)S(1)}, u32[]{:S(2)}, u32[]{:S(2)}) collective-permute-start(f32[8,4096]{1,0:T(8,128)} %get-tuple-element.25), channel_id=1, source_target_pairs={{2,0},{3,1},{6,4},{7,5},{10,8},{11,9},{14,12},{15,13},{18,16},{19,... | collective-permute-start | bytes 393224 | tf_op jit(solution)/shard_map/ppermute | solution.py:422
  13.9 1.9 %collective-permute-start.1 = (f32[8,128]{1,0:T(8,128)S(1)}, f32[8,128]{1,0:T(8,128)S(1)}, u32[]{:S(2)}, u32[]{:S(2)}) collective-permute-start(f32[8,128]{1,0:T(8,128)S(1)} %get-tuple-element.26.refs_0_), channel_id=1, source_target_pairs={{0,1},{1,0},{4,5},{5,4},{8,9},{9,8},{12,13},{13,12},{16,17},{17,16... | collective-permute-start | bytes 12296 | tf_op jit(solution)/shard_map/ppermute | solution.py:444
  15.8 1.6 %all-to-all-done.sums = f32[8,1,4224]{2,1,0:T(1,128)S(1)} async-done(((f32[8,1,4224]{2,1,0:T(1,128)}), f32[8,1,4224]{2,1,0:T(1,128)S(1)}, u32[]{:S(2)}, u32[]{:S(2)}) %all-to-all-start) | async-done | bytes 135200 | tf_op jit(solution)/shard_map/all_to_all | solution.py:370
  17.4 2.0 %unit_gradient.1 = (f32[16,4352]{1,0:T(8,128)S(1)}, f32[8,128]{1,0:T(8,128)S(1)}, f32[8,4096]{1,0:T(8,128)S(1)}, bf16[1024,256]{1,0:T(8,128)(2,1)S(1)}, bf16[1024,256]{1,0:T(8,128)(2,1)S(1)}) custom-call(f32[4096,256]{1,0:T(8,128)} %panel.1, s32[1,4096]{1,0:T(1,128)} %bitcast.6, f32[8,4096]{1,0:T(8,128)} %unit_logit.1, f32[8,1,4224]{2,1,0:T(1,128)S(1)} %all-to-all-done.sums, ...), custom_call_target="tpu_custom_call" | custom-call | tf_op jit(solution)/shard_map/unit_gradient/pallas_call | solution.py:375
  19.5 0.0 collective-permute-done.1.refs_1_
  19.5 0.2 collective-permute-done.post
  19.6 0.1 join_post.1
  19.7 2.2 %all-gather = f32[32,4352]{1,0:T(8,128)S(1)} all-gather(f32[16,4352]{1,0:T(8,128)S(1)} %join_post.1), channel_id=2, replica_groups={{0,1},{2,3},{4,5},{6,7},{8,9},{10,11},{12,13},{14,15},{16,17},{18,19},{..., dimensions={0}, use_global_device_ids=true | all-gather | bytes 835584 | tf_op jit(solution)/shard_map/all_gather | solution.py:354
  21.9 1.4 %time_gradient.1 = (f32[8,4096]{1,0:T(8,128)S(1)}, f32[8,512]{1,0:T(8,128)S(1)}, f32[16,8,256]{2,1,0:T(8,128)}) custom-call(f32[2,16,4352]{2,1,0:T(8,128)S(1)} %bitcast.4, bf16[3072,256]{1,0:T(8,128)(2,1)S(1)} %get-tuple-element.22.high_ref.refs_1_, bf16[3072,256]{1,0:T(8,128)(2,1)S(1)} %get-tuple-element.23.low_ref.refs_2_, ...), custom_call_target="tpu_custom_call" | custom-call | tf_op jit(solution)/shard_map/time_gradient/pallas_call | solution.py:375
  23.3 5.1 %all-to-all-start.1 = ((f32[16,8,256]{2,1,0:T(8,128)}), f32[16,8,256]{2,1,0:T(8,128)S(1)}, u32[]{:S(2)}, u32[]{:S(2)}) async-start(f32[16,8,256]{2,1,0:T(8,128)} %get-tuple-element.31), calls=%async_computation.1 | async-start | bytes 262144 | tf_op jit(solution)/shard_map/all_to_all | solution.py:361
  28.4 1.3 %collective-permute-start.3 = (f32[8,4096]{1,0:T(8,128)S(1)}, f32[8,4096]{1,0:T(8,128)S(1)}, u32[]{:S(2)}, u32[]{:S(2)}) collective-permute-start(f32[8,4096]{1,0:T(8,128)S(1)} %get-tuple-element.32.scaled), channel_id=1, source_target_pairs={{0,2},{1,3},{4,6},{5,7},{8,10},{9,11},{12,14},{13,15},{16,18},{17,... | collective-permute-start | bytes 393224 | tf_op jit(solution)/shard_map/ppermute | solution.py:350
  29.7 2.7 %all-to-all-done.1.grads = f32[16,8,256]{2,1,0:T(8,128)S(1)} async-done(((f32[16,8,256]{2,1,0:T(8,128)}), f32[16,8,256]{2,1,0:T(8,128)S(1)}, u32[]{:S(2)}, u32[]{:S(2)}) %all-to-all-start.1) | async-done | bytes 131104 | tf_op jit(solution)/shard_map/all_to_all | solution.py:361
  32.4 0.1 unit_totals.1.totals
  32.5 1.3 %collective-permute-start.2 = (f32[8,128]{1,0:T(8,128)S(1)}, f32[8,128]{1,0:T(8,128)S(1)}, u32[]{:S(2)}, u32[]{:S(2)}) collective-permute-start(f32[8,128]{1,0:T(8,128)S(1)} %unit_totals.1.totals), channel_id=1, source_target_pairs={{0,3},{1,2},{4,7},{5,6},{8,11},{9,10},{12,15},{13,14},{16,19},{17,... | collective-permute-start | bytes 12296 | tf_op jit(solution)/shard_map/ppermute | solution.py:350
  33.7 0.9 %scale_weights.1 = (f32[8,4096]{1,0:T(8,128)}, f32[8,256]{1,0:T(8,128)}) custom-call(f32[8,128]{1,0:T(8,128)S(1)} %unit_totals.1.totals, f32[8,4096]{1,0:T(8,128)S(1)} %get-tuple-element.32.scaled, f32[16,8,256]{2,1,0:T(8,128)S(1)} %all-to-all-done.1.grads, f32[8,512]{1,0:T(8,128)S(1)} %get-tuple-element.33.lam, ...), custom_call_target="tpu_custom_call" | custom-call | tf_op jit(solution)/shard_map/scale_weights/pallas_call | solution.py:375
  34.7 0.0 collective-permute-done.3.sent_scaled
  34.7 0.4 %collective-permute-done.2.sent_totals = f32[8,128]{1,0:T(8,128)S(1)} collective-permute-done((f32[8,128]{1,0:T(8,128)S(1)}, f32[8,128]{1,0:T(8,128)S(1)}, u32[]{:S(2)}, u32[]{:S(2)}) %collective-permute-start.2) | collective-permute-done | bytes 4128 | tf_op jit(solution)/shard_map/ppermute | solution.py:350
  (1 shorter events, 0.0 us)
Async XLA Ops:
  4.8 12.7 %all-to-all-start = ((f32[8,1,4224]{2,1,0:T(1,128)}), f32[8,1,4224]{2,1,0:T(1,128)S(1)}, u32[]{:S(2)}, u32[]{:S(2)}) async-start(f32[8,1,4224]{2,1,0:T(1,128)} %get-tuple-element.19), calls=%async_computation | async-start | bytes 270336 | tf_op jit(solution)/shard_map/all_to_all | solution.py:370
  12.6 7.1 %collective-permute-start = (f32[8,4096]{1,0:T(8,128)}, f32[8,4096]{1,0:T(8,128)S(1)}, u32[]{:S(2)}, u32[]{:S(2)}) collective-permute-start(f32[8,4096]{1,0:T(8,128)} %get-tuple-element.25), channel_id=1, source_target_pairs={{2,0},{3,1},{6,4},{7,5},{10,8},{11,9},{14,12},{15,13},{18,16},{19,... | collective-permute-start | bytes 393224 | tf_op jit(solution)/shard_map/ppermute | solution.py:422
  13.9 5.6 %collective-permute-start.1 = (f32[8,128]{1,0:T(8,128)S(1)}, f32[8,128]{1,0:T(8,128)S(1)}, u32[]{:S(2)}, u32[]{:S(2)}) collective-permute-start(f32[8,128]{1,0:T(8,128)S(1)} %get-tuple-element.26.refs_0_), channel_id=1, source_target_pairs={{0,1},{1,0},{4,5},{5,4},{8,9},{9,8},{12,13},{13,12},{16,17},{17,16... | collective-permute-start | bytes 12296 | tf_op jit(solution)/shard_map/ppermute | solution.py:444
  23.3 9.1 %all-to-all-start.1 = ((f32[16,8,256]{2,1,0:T(8,128)}), f32[16,8,256]{2,1,0:T(8,128)S(1)}, u32[]{:S(2)}, u32[]{:S(2)}) async-start(f32[16,8,256]{2,1,0:T(8,128)} %get-tuple-element.31), calls=%async_computation.1 | async-start | bytes 262144 | tf_op jit(solution)/shard_map/all_to_all | solution.py:361
  28.4 6.3 %collective-permute-start.3 = (f32[8,4096]{1,0:T(8,128)S(1)}, f32[8,4096]{1,0:T(8,128)S(1)}, u32[]{:S(2)}, u32[]{:S(2)}) collective-permute-start(f32[8,4096]{1,0:T(8,128)S(1)} %get-tuple-element.32.scaled), channel_id=1, source_target_pairs={{0,2},{1,3},{4,6},{5,7},{8,10},{9,11},{12,14},{13,15},{16,18},{17,... | collective-permute-start | bytes 393224 | tf_op jit(solution)/shard_map/ppermute | solution.py:350
  32.5 2.6 %collective-permute-start.2 = (f32[8,128]{1,0:T(8,128)S(1)}, f32[8,128]{1,0:T(8,128)S(1)}, u32[]{:S(2)}, u32[]{:S(2)}) collective-permute-start(f32[8,128]{1,0:T(8,128)S(1)} %unit_totals.1.totals), channel_id=1, source_target_pairs={{0,3},{1,2},{4,7},{5,6},{8,11},{9,10},{12,15},{13,14},{16,19},{17,... | collective-permute-start | bytes 12296 | tf_op jit(solution)/shard_map/ppermute | solution.py:350

commit v29 on v26

--- a/solution.py
+++ b/solution.py
@@ -234,14 +234,18 @@
     groups, unit_rows = post.shape
     over_time = 1.0 / tree_sum(ref[:, 0:1] for ref in norms)
     out[:groups, :unit_rows] = pack[:groups, :unit_rows]
-    out[:groups, unit_rows:] = pack[:groups, unit_rows:] * over_time
     out[groups:, :unit_rows] = pack[groups:, :unit_rows] * over_time - post[...]
-    out[groups:, unit_rows:] = pack[groups:, unit_rows:]
+    out[groups:, unit_rows:] = jnp.zeros((groups, out.shape[1] - unit_rows), f32)
+    own = pack[:groups, unit_rows:] * over_time
+    day_cols = own.shape[1]
+    for day in range(half):
+        start = unit_rows + day * day_cols
+        out[:groups, start : start + day_cols] = jnp.where(lax.axis_index("day") == day, own, 0.0)
 
 
 @first_half_only
 def third_kernel(half, *refs):
-    parts, refs = [refs[0].at[day] for day in range(half)], refs[1:]
+    parts, refs = refs[:1], refs[1:]
     high_ref, low_ref, more_high, more_low, norms, raised_units, ends, scaled, lam, out = refs
     groups, unit_rows = raised_units.shape
     resident, day_cols = high_ref.shape
@@ -249,8 +253,7 @@
     factor = -step_rate / jnp.sqrt(ends[:, 0:1])
     over_unit = 1.0 / unit_norm
     me = lax.rem(lax.axis_index("day"), half)
-    for day in range(half):
-        lam[:, day * day_cols : (day + 1) * day_cols] = parts[day][:groups, unit_rows:]
+    lam[...] = parts[0][:groups, unit_rows:]
     time_grad = jnp.zeros((groups, day_cols), f32)
     new_sum = jnp.zeros((groups, 1), f32)
     for start in range(0, unit_rows, block_rows):
@@ -337,7 +340,7 @@
 
     def over_days(value):
         halves = [list(range(half)), list(range(half, day_devices))]
-        return lax.all_gather(value, "day", axis_index_groups=halves)
+        return lax.psum(value, "day", axis_index_groups=halves)
 
     def over_first_half(value):
         members = [
@@ -431,7 +434,7 @@
         time_norms.append(lax.ppermute(time_norm, ("unit", "day"), pairs))
     (pack,) = call(
         functools.partial(join_kernel, half),
-        [((2 * groups, unit_rows + day_cols), f32)],
+        [((2 * groups, unit_rows + half * day_cols), f32)],
         "join_post",
         (pack, post, *time_norms),
     )

time: 35 us -> 73.2 us (2.09)
  waiting for transfers between devices: 4.91 us -> 19.9 us
  between operations: 0.7 us -> 14.1 us
  local copies, waits for them, and re-layouts: 0 us -> 5.92 us
  starting transfers between devices: 18.7 us -> 23.2 us
  blocking collectives: 2.2 us -> 0 us
  Pallas kernels: 8.06 us -> 9.45 us
    psum x0 -> x1, waiting for transfers between devices: none -> 16.6 us  [over_days(): return lax.psum(value, 'day', axis_index_groups=halves)]
    unnamed x0 -> x14, local copies, waits for them, and re-layouts: none -> 5.92 us
    ppermute x2, starting transfers between devices: 2.56 us -> 5.3 us  [to_other_half(): return lax.ppermute(value, ('unit', 'day'), pairs)]
    all_gather x1 -> x0, blocking collectives: 2.2 us -> none  [over_days(): return lax.all_gather(value, 'day', axis_index_groups=halves)]
    all_to_all x1, starting transfers between devices: 5.07 us -> 6.9 us  [over_first_half(): lax.all_to_all(value, ('unit', 'day'), split_axis=0, concat_axis=0, axis_...]
    all_to_all x1, waiting for transfers between devices: 2.72 us -> 1.26 us  [over_first_half(): lax.all_to_all(value, ('unit', 'day'), split_axis=0, concat_axis=0, axis_...]
    pallas_call x7, Pallas kernels: 8.06 us -> 9.45 us  [call(): pl.pallas_call(kernel, in_specs=in_specs or [vmem] * len(args), out_specs...]
  transfers between devices with their start and end apart: 6 -> 7, of which waited for: 4 -> 4; matrix products, arithmetic and copies ran while one was open for 0% -> 0% of each run, Pallas kernels for 9% -> 4%
where the time goes in v29:
time: 73.2 us; the launch traced here: 72.6 us
  starting transfers between devices  23.2 us (32%)
  waiting for transfers between devices  19.9 us (27%)
  between operations  14.1 us (19%)
  Pallas kernels  9.45 us (13%)
  local copies, waits for them, and re-layouts  5.92 us (8%)
    psum x1, waiting for transfers between devices, over_days(): return lax.psum(value, 'day', axis_index_groups=halves)  16.6 us
    pallas_call x7, Pallas kernels, call(): pl.pallas_call(kernel, in_specs=in_specs or [vmem] * len(args), out_specs...  9.45 us
    all_to_all x1, starting transfers between devices, over_units(): lax.all_to_all(value, ('unit', 'day'), split_axis=0, concat_axis=0, axis_...  7.81 us
    all_to_all x1, starting transfers between devices, over_first_half(): lax.all_to_all(value, ('unit', 'day'), split_axis=0, concat_axis=0, axis_...  6.9 us
    unnamed x14, local copies, waits for them, and re-layouts  5.92 us
    ppermute x2, starting transfers between devices, to_other_half(): return lax.ppermute(value, ('unit', 'day'), pairs)  5.3 us
    ppermute x1, starting transfers between devices, local(): time_norms.append(lax.ppermute(time_norm, ('unit', 'day'), pairs))  1.92 us
    all_to_all x1, waiting for transfers between devices, over_units(): lax.all_to_all(value, ('unit', 'day'), split_axis=0, concat_axis=0, axis_...  1.61 us
  transfers between devices with their start and end apart: 7, of which 4 were waited for; matrix products, arithmetic and copies ran while one was open for 0% of the time, Pallas kernels for 4%

profile of v29, /device:TPU:0, one launch (start us, length us, event | category | flops | bytes accessed | tf_op | source)
XLA Modules:
  0.0 72.6 jit_solution(668138076769697218)
XLA Ops:
  7.2 3.6 %first_product.1 = (f32[8,1,4224]{2,1,0:T(1,128)}, f32[8,4096]{1,0:T(8,128)}, f32[8,256]{1,0:T(8,128)S(1)}, f32[8,128]{1,0:T(8,128)S(1)}, f32[8,128]{1,0:T(8,128...) custom-call(f32[4096,256]{1,0:T(8,128)} %panel.1, s32[1,4096]{1,0:T(1,128)} %bitcast.3, ...), custom_call_target="tpu_custom_call" | custom-call | tf_op jit(solution)/shard_map/first_product/pallas_call | solution.py:364
  10.8 0.0 copy-start.5
  10.8 0.6 copy-done.5
  11.4 7.8 %all-to-all-start = ((f32[8,1,4224]{2,1,0:T(1,128)}), f32[8,1,4224]{2,1,0:T(1,128)S(1)}, u32[]{:S(2)}, u32[]{:S(2)}) async-start(f32[8,1,4224]{2,1,0:T(1,128)} %get-tuple-element.19), calls=%async_computation | async-start | bytes 270336 | tf_op jit(solution)/shard_map/all_to_all | solution.py:359
  19.2 0.0 all-reduce.2.cloned.1.call-start
  19.2 1.3 %collective-permute-start = (f32[8,4096]{1,0:T(8,128)}, f32[8,4096]{1,0:T(8,128)S(1)}, u32[]{:S(2)}, u32[]{:S(2)}) collective-permute-start(f32[8,4096]{1,0:T(8,128)} %get-tuple-element.25), channel_id=1, source_target_pairs={{2,0},{3,1},{6,4},{7,5},{10,8},{11,9},{14,12},{15,13},{18,16},{19,... | collective-permute-start | bytes 393224 | tf_op jit(solution)/shard_map/ppermute | solution.py:412
  20.5 1.9 %collective-permute-start.1 = (f32[8,128]{1,0:T(8,128)S(1)}, f32[8,128]{1,0:T(8,128)}, u32[]{:S(2)}, u32[]{:S(2)}) collective-permute-start(f32[8,128]{1,0:T(8,128)S(1)} %get-tuple-element.26.refs_0_), channel_id=1, source_target_pairs={{0,1},{1,0},{4,5},{5,4},{8,9},{9,8},{12,13},{13,12},{16,17},{17,16... | collective-permute-start | bytes 12296 | tf_op jit(solution)/shard_map/ppermute | solution.py:434
  22.4 1.6 %all-to-all-done.sums = f32[8,1,4224]{2,1,0:T(1,128)S(1)} async-done(((f32[8,1,4224]{2,1,0:T(1,128)}), f32[8,1,4224]{2,1,0:T(1,128)S(1)}, u32[]{:S(2)}, u32[]{:S(2)}) %all-to-all-start) | async-done | bytes 135200 | tf_op jit(solution)/shard_map/all_to_all | solution.py:359
  24.0 0.0 copy-start.6
  24.0 0.7 copy-done.6
  24.7 2.0 %unit_gradient.1 = (f32[16,4352]{1,0:T(8,128)S(1)}, f32[8,128]{1,0:T(8,128)S(1)}, f32[8,4096]{1,0:T(8,128)S(1)}, bf16[1024,256]{1,0:T(8,128)(2,1)S(1)}, bf16[1024,256]{1,0:T(8,128)(2,1)S(1)}) custom-call(f32[4096,256]{1,0:T(8,128)} %panel.1, s32[1,4096]{1,0:T(1,128)} %bitcast.4, f32[8,4096]{1,0:T(8,128)} %unit_logit.1, f32[8,1,4224]{2,1,0:T(1,128)S(1)} %all-to-all-done.sums, ...), custom_call_target="tpu_custom_call" | custom-call | tf_op jit(solution)/shard_map/unit_gradient/pallas_call | solution.py:364
  26.8 0.0 copy-start
  26.8 0.8 %copy-done = bf16[1024,256]{1,0:T(8,128)(2,1)} copy-done((bf16[1024,256]{1,0:T(8,128)(2,1)}, bf16[1024,256]{1,0:T(8,128)(2,1)S(1)}, u32[]{:S(2)}) %copy-start) | copy-done | bytes 524312
  27.6 0.0 copy-start.2
  27.6 0.8 %copy-done.2 = bf16[1024,256]{1,0:T(8,128)(2,1)} copy-done((bf16[1024,256]{1,0:T(8,128)(2,1)}, bf16[1024,256]{1,0:T(8,128)(2,1)S(1)}, u32[]{:S(2)}) %copy-start.2) | copy-done | bytes 524312
  28.3 0.0 collective-permute-done.1.refs_1_
  28.4 0.0 collective-permute-done.post
  28.4 1.5 %join_post.1 = f32[16,4608]{1,0:T(8,128)} custom-call(f32[16,4352]{1,0:T(8,128)S(1)} %get-tuple-element.24.pack, f32[8,4096]{1,0:T(8,128)S(1)} %collective-permute-done.post, f32[8,128]{1,0:T(8,128)S(1)} %get-tuple-element.26.refs_0_, f32[8,128]{1,0:T(8,128)} %collective-permute-done.1.refs_1_), custom_call_target="tpu_custom_call" | custom-call | tf_op jit(solution)/shard_map/join_post/pallas_call | solution.py:364
  29.8 0.0 all-reduce.2.cloned.1.call-update
  29.8 16.6 %all-reduce.2.cloned.1.call-done.refs_0_ = f32[16,4608]{1,0:T(8,128)} async-done(((f32[16,4608]{1,0:T(8,128)}), f32[16,4608]{1,0:T(8,128)}) %all-reduce.2.cloned.1.call-update) | async-done | bytes 294928 | tf_op jit(solution)/shard_map/psum | solution.py:343
  46.5 0.0 copy-start.1
  46.5 1.0 %copy-done.1 = bf16[1024,256]{1,0:T(8,128)(2,1)S(1)} copy-done((bf16[1024,256]{1,0:T(8,128)(2,1)S(1)}, bf16[1024,256]{1,0:T(8,128)(2,1)}, u32[]{:S(2)}) %copy-start.1) | copy-done | bytes 524312
  47.5 0.0 copy-start.3
  47.5 1.0 %copy-done.3 = bf16[1024,256]{1,0:T(8,128)(2,1)S(1)} copy-done((bf16[1024,256]{1,0:T(8,128)(2,1)S(1)}, bf16[1024,256]{1,0:T(8,128)(2,1)}, u32[]{:S(2)}) %copy-start.3) | copy-done | bytes 524312
  48.6 0.0 copy-start.4
  48.6 1.0 %copy-done.4 = f32[16,4608]{1,0:T(8,128)S(1)} copy-done((f32[16,4608]{1,0:T(8,128)S(1)}, f32[16,4608]{1,0:T(8,128)}, u32[]{:S(2)}) %copy-start.4) | copy-done | bytes 294936
  49.5 1.4 %time_gradient.1 = (f32[8,4096]{1,0:T(8,128)S(1)}, f32[8,512]{1,0:T(8,128)S(1)}, f32[16,8,256]{2,1,0:T(8,128)}) custom-call(f32[16,4608]{1,0:T(8,128)S(1)} %copy-done.4, bf16[3072,256]{1,0:T(8,128)(2,1)S(1)} %get-tuple-element.22.high_ref.refs_1_, bf16[3072,256]{1,0:T(8,128)(2,1)S(1)} %get-tuple-element.23.low_ref.refs_2_, bf16[1024,256]{1,0:T(8,128)(2,1)S(1)} %copy-done.1, ...), custom_call_target="tpu_custom_call" | custom-call | tf_op jit(solution)/shard_map/time_gradient/pallas_call | solution.py:364
  50.9 6.9 %all-to-all-start.1 = ((f32[16,8,256]{2,1,0:T(8,128)}), f32[16,8,256]{2,1,0:T(8,128)S(1)}, u32[]{:S(2)}, u32[]{:S(2)}) async-start(f32[16,8,256]{2,1,0:T(8,128)} %get-tuple-element.31), calls=%async_computation.1 | async-start | bytes 262144 | tf_op jit(solution)/shard_map/all_to_all | solution.py:350
  57.8 2.7 %collective-permute-start.3 = (f32[8,4096]{1,0:T(8,128)S(1)}, f32[8,4096]{1,0:T(8,128)S(1)}, u32[]{:S(2)}, u32[]{:S(2)}) collective-permute-start(f32[8,4096]{1,0:T(8,128)S(1)} %get-tuple-element.32.scaled), channel_id=1, source_target_pairs={{0,2},{1,3},{4,6},{5,7},{8,10},{9,11},{12,14},{13,15},{16,18},{17,... | collective-permute-start | bytes 393224 | tf_op jit(solution)/shard_map/ppermute | solution.py:339
  60.5 1.3 %all-to-all-done.1.grads = f32[16,8,256]{2,1,0:T(8,128)S(1)} async-done(((f32[16,8,256]{2,1,0:T(8,128)}), f32[16,8,256]{2,1,0:T(8,128)S(1)}, u32[]{:S(2)}, u32[]{:S(2)}) %all-to-all-start.1) | async-done | bytes 131104 | tf_op jit(solution)/shard_map/all_to_all | solution.py:350
  61.7 0.1 unit_totals.1.totals
  61.8 2.6 %collective-permute-start.2 = (f32[8,128]{1,0:T(8,128)S(1)}, f32[8,128]{1,0:T(8,128)S(1)}, u32[]{:S(2)}, u32[]{:S(2)}) collective-permute-start(f32[8,128]{1,0:T(8,128)S(1)} %unit_totals.1.totals), channel_id=1, source_target_pairs={{0,3},{1,2},{4,7},{5,6},{8,11},{9,10},{12,15},{13,14},{16,19},{17,... | collective-permute-start | bytes 12296 | tf_op jit(solution)/shard_map/ppermute | solution.py:339
  64.4 0.9 %scale_weights.1 = (f32[8,4096]{1,0:T(8,128)}, f32[8,256]{1,0:T(8,128)}) custom-call(f32[8,128]{1,0:T(8,128)S(1)} %unit_totals.1.totals, f32[8,4096]{1,0:T(8,128)S(1)} %get-tuple-element.32.scaled, f32[16,8,256]{2,1,0:T(8,128)S(1)} %all-to-all-done.1.grads, f32[8,512]{1,0:T(8,128)S(1)} %get-tuple-element.33.lam, ...), custom_call_target="tpu_custom_call" | custom-call | tf_op jit(solution)/shard_map/scale_weights/pallas_call | solution.py:364
  65.3 0.0 collective-permute-done.3.sent_scaled
  65.3 0.4 collective-permute-done.2.sent_totals
  (1 shorter events, 0.0 us)
Async XLA Ops:
  10.8 0.6 copy-start.5
  11.4 12.6 %all-to-all-start = ((f32[8,1,4224]{2,1,0:T(1,128)}), f32[8,1,4224]{2,1,0:T(1,128)S(1)}, u32[]{:S(2)}, u32[]{:S(2)}) async-start(f32[8,1,4224]{2,1,0:T(1,128)} %get-tuple-element.19), calls=%async_computation | async-start | bytes 270336 | tf_op jit(solution)/shard_map/all_to_all | solution.py:359
  19.2 27.3 %all-reduce.2.cloned.1.call-start = ((), (), s32[]{:S(2)}) async-start(), calls=%async_computation.2 | async-start | bytes 589824 | tf_op jit(solution)/shard_map/psum | solution.py:343
  19.2 9.2 %collective-permute-start = (f32[8,4096]{1,0:T(8,128)}, f32[8,4096]{1,0:T(8,128)S(1)}, u32[]{:S(2)}, u32[]{:S(2)}) collective-permute-start(f32[8,4096]{1,0:T(8,128)} %get-tuple-element.25), channel_id=1, source_target_pairs={{2,0},{3,1},{6,4},{7,5},{10,8},{11,9},{14,12},{15,13},{18,16},{19,... | collective-permute-start | bytes 393224 | tf_op jit(solution)/shard_map/ppermute | solution.py:412
  20.5 7.9 %collective-permute-start.1 = (f32[8,128]{1,0:T(8,128)S(1)}, f32[8,128]{1,0:T(8,128)}, u32[]{:S(2)}, u32[]{:S(2)}) collective-permute-start(f32[8,128]{1,0:T(8,128)S(1)} %get-tuple-element.26.refs_0_), channel_id=1, source_target_pairs={{0,1},{1,0},{4,5},{5,4},{8,9},{9,8},{12,13},{13,12},{16,17},{17,16... | collective-permute-start | bytes 12296 | tf_op jit(solution)/shard_map/ppermute | solution.py:434
  24.0 0.7 copy-start.6
  26.8 0.8 %copy-start = (bf16[1024,256]{1,0:T(8,128)(2,1)}, bf16[1024,256]{1,0:T(8,128)(2,1)S(1)}, u32[]{:S(2)}) copy-start(bf16[1024,256]{1,0:T(8,128)(2,1)S(1)} %get-tuple-element.27.refs_3_) | copy-start | bytes 1572868
  27.6 0.8 %copy-start.2 = (bf16[1024,256]{1,0:T(8,128)(2,1)}, bf16[1024,256]{1,0:T(8,128)(2,1)S(1)}, u32[]{:S(2)}) copy-start(bf16[1024,256]{1,0:T(8,128)(2,1)S(1)} %get-tuple-element.28.refs_4_) | copy-start | bytes 1572868
  46.5 1.0 %copy-start.1 = (bf16[1024,256]{1,0:T(8,128)(2,1)S(1)}, bf16[1024,256]{1,0:T(8,128)(2,1)}, u32[]{:S(2)}) copy-start(bf16[1024,256]{1,0:T(8,128)(2,1)} %copy-done) | copy-start | bytes 1572868
  47.5 1.0 %copy-start.3 = (bf16[1024,256]{1,0:T(8,128)(2,1)S(1)}, bf16[1024,256]{1,0:T(8,128)(2,1)}, u32[]{:S(2)}) copy-start(bf16[1024,256]{1,0:T(8,128)(2,1)} %copy-done.2) | copy-start | bytes 1572868
  48.6 1.0 %copy-start.4 = (f32[16,4608]{1,0:T(8,128)S(1)}, f32[16,4608]{1,0:T(8,128)}, u32[]{:S(2)}) copy-start(f32[16,4608]{1,0:T(8,128)} %all-reduce.2.cloned.1.call-done.refs_0_) | copy-start | bytes 884740
  50.9 10.8 %all-to-all-start.1 = ((f32[16,8,256]{2,1,0:T(8,128)}), f32[16,8,256]{2,1,0:T(8,128)S(1)}, u32[]{:S(2)}, u32[]{:S(2)}) async-start(f32[16,8,256]{2,1,0:T(8,128)} %get-tuple-element.31), calls=%async_computation.1 | async-start | bytes 262144 | tf_op jit(solution)/shard_map/all_to_all | solution.py:350
  57.8 7.6 %collective-permute-start.3 = (f32[8,4096]{1,0:T(8,128)S(1)}, f32[8,4096]{1,0:T(8,128)S(1)}, u32[]{:S(2)}, u32[]{:S(2)}) collective-permute-start(f32[8,4096]{1,0:T(8,128)S(1)} %get-tuple-element.32.scaled), channel_id=1, source_target_pairs={{0,2},{1,3},{4,6},{5,7},{8,10},{9,11},{12,14},{13,15},{16,18},{17,... | collective-permute-start | bytes 393224 | tf_op jit(solution)/shard_map/ppermute | solution.py:339
  61.8 3.9 %collective-permute-start.2 = (f32[8,128]{1,0:T(8,128)S(1)}, f32[8,128]{1,0:T(8,128)S(1)}, u32[]{:S(2)}, u32[]{:S(2)}) collective-permute-start(f32[8,128]{1,0:T(8,128)S(1)} %unit_totals.1.totals), channel_id=1, source_target_pairs={{0,3},{1,2},{4,7},{5,6},{8,11},{9,10},{12,15},{13,14},{16,19},{17,... | collective-permute-start | bytes 12296 | tf_op jit(solution)/shard_map/ppermute | solution.py:339
Sparse Core Ops, SparseCore 0:
  30.0 16.4 all-reduce.1

commit v30 on v26

--- a/solution.py
+++ b/solution.py
@@ -341,7 +341,7 @@
 
     def over_first_half(value):
         members = [
-            [unit * day_devices + day for unit in meeting_at(middle + 1) for day in reversed(days)]
+            [unit * day_devices + day for unit in meeting_at(unit_devices - 1) for day in reversed(days)]
             for days in (range(half), range(half, day_devices))
         ]
         return lax.all_to_all(

time: 35 us -> 36 us (1.029)
  starting transfers between devices: 18.7 us -> 19.6 us
    all_to_all x1, starting transfers between devices: 5.07 us -> 5.97 us  [over_first_half(): lax.all_to_all(value, ('unit', 'day'), split_axis=0, concat_axis=0, axis_...]
where the time goes in v30:
time: 36 us; the launch traced here: 35.5 us
  starting transfers between devices  19.6 us (54%)
  Pallas kernels  8.06 us (22%)
  waiting for transfers between devices  5 us (14%)
  blocking collectives  2.2 us (6%)
  between operations  0.7 us (2%)
    pallas_call x7, Pallas kernels, call(): pl.pallas_call(kernel, in_specs=in_specs or [vmem] * len(args), out_specs...  8.06 us
    all_to_all x1, starting transfers between devices, over_units(): lax.all_to_all(value, ('unit', 'day'), split_axis=0, concat_axis=0, axis_...  7.83 us
    all_to_all x1, starting transfers between devices, over_first_half(): lax.all_to_all(value, ('unit', 'day'), split_axis=0, concat_axis=0, axis_...  5.97 us
    all_to_all x1, waiting for transfers between devices, over_first_half(): lax.all_to_all(value, ('unit', 'day'), split_axis=0, concat_axis=0, axis_...  2.8 us
    ppermute x2, starting transfers between devices, to_other_half(): return lax.ppermute(value, ('unit', 'day'), pairs)  2.56 us
    all_gather x1, blocking collectives, over_days(): return lax.all_gather(value, 'day', axis_index_groups=halves)  2.2 us
    ppermute x1, starting transfers between devices, local(): time_norms.append(lax.ppermute(time_norm, ('unit', 'day'), pairs))  1.92 us
    all_to_all x1, waiting for transfers between devices, over_units(): lax.all_to_all(value, ('unit', 'day'), split_axis=0, concat_axis=0, axis_...  1.61 us
  transfers between devices with their start and end apart: 6, of which 4 were waited for; matrix products, arithmetic and copies ran while one was open for 0% of the time, Pallas kernels for 9%

profile of v30, /device:TPU:0, one launch (start us, length us, event | category | flops | bytes accessed | tf_op | source)
XLA Modules:
  0.0 35.5 jit_solution(4839952575223209359)
XLA Ops:
  0.6 3.6 %first_product.1 = (f32[8,1,4224]{2,1,0:T(1,128)}, f32[8,4096]{1,0:T(8,128)}, f32[8,256]{1,0:T(8,128)S(1)}, f32[8,128]{1,0:T(8,128)S(1)}, f32[8,128]{1,0:T(8,128...) custom-call(f32[4096,256]{1,0:T(8,128)} %panel.1, s32[1,4096]{1,0:T(1,128)} %bitcast.5, ...), custom_call_target="tpu_custom_call" | custom-call | tf_op jit(solution)/shard_map/first_product/pallas_call | solution.py:361
  4.2 7.8 %all-to-all-start = ((f32[8,1,4224]{2,1,0:T(1,128)}), f32[8,1,4224]{2,1,0:T(1,128)S(1)}, u32[]{:S(2)}, u32[]{:S(2)}) async-start(f32[8,1,4224]{2,1,0:T(1,128)} %get-tuple-element.19), calls=%async_computation | async-start | bytes 270336 | tf_op jit(solution)/shard_map/all_to_all | solution.py:356
  12.1 1.3 %collective-permute-start = (f32[8,4096]{1,0:T(8,128)}, f32[8,4096]{1,0:T(8,128)S(1)}, u32[]{:S(2)}, u32[]{:S(2)}) collective-permute-start(f32[8,4096]{1,0:T(8,128)} %get-tuple-element.25), channel_id=1, source_target_pairs={{2,0},{3,1},{6,4},{7,5},{10,8},{11,9},{14,12},{15,13},{18,16},{19,... | collective-permute-start | bytes 393224 | tf_op jit(solution)/shard_map/ppermute | solution.py:409
  13.3 1.9 %collective-permute-start.1 = (f32[8,128]{1,0:T(8,128)S(1)}, f32[8,128]{1,0:T(8,128)S(1)}, u32[]{:S(2)}, u32[]{:S(2)}) collective-permute-start(f32[8,128]{1,0:T(8,128)S(1)} %get-tuple-element.26.refs_0_), channel_id=1, source_target_pairs={{0,1},{1,0},{4,5},{5,4},{8,9},{9,8},{12,13},{13,12},{16,17},{17,16... | collective-permute-start | bytes 12296 | tf_op jit(solution)/shard_map/ppermute | solution.py:431
  15.3 1.6 %all-to-all-done.sums = f32[8,1,4224]{2,1,0:T(1,128)S(1)} async-done(((f32[8,1,4224]{2,1,0:T(1,128)}), f32[8,1,4224]{2,1,0:T(1,128)S(1)}, u32[]{:S(2)}, u32[]{:S(2)}) %all-to-all-start) | async-done | bytes 135200 | tf_op jit(solution)/shard_map/all_to_all | solution.py:356
  16.9 2.0 %unit_gradient.1 = (f32[16,4352]{1,0:T(8,128)S(1)}, f32[8,128]{1,0:T(8,128)S(1)}, f32[8,4096]{1,0:T(8,128)S(1)}, bf16[1024,256]{1,0:T(8,128)(2,1)S(1)}, bf16[1024,256]{1,0:T(8,128)(2,1)S(1)}) custom-call(f32[4096,256]{1,0:T(8,128)} %panel.1, s32[1,4096]{1,0:T(1,128)} %bitcast.6, f32[8,4096]{1,0:T(8,128)} %unit_logit.1, f32[8,1,4224]{2,1,0:T(1,128)S(1)} %all-to-all-done.sums, ...), custom_call_target="tpu_custom_call" | custom-call | tf_op jit(solution)/shard_map/unit_gradient/pallas_call | solution.py:361
  18.9 0.0 collective-permute-done.1.refs_1_
  18.9 0.2 collective-permute-done.post
  19.1 0.1 join_post.1
  19.2 2.2 %all-gather = f32[32,4352]{1,0:T(8,128)S(1)} all-gather(f32[16,4352]{1,0:T(8,128)S(1)} %join_post.1), channel_id=2, replica_groups={{0,1},{2,3},{4,5},{6,7},{8,9},{10,11},{12,13},{14,15},{16,17},{18,19},{..., dimensions={0}, use_global_device_ids=true | all-gather | bytes 835584 | tf_op jit(solution)/shard_map/all_gather | solution.py:340
  21.4 1.4 %time_gradient.1 = (f32[8,4096]{1,0:T(8,128)S(1)}, f32[8,512]{1,0:T(8,128)S(1)}, f32[16,8,256]{2,1,0:T(8,128)}) custom-call(f32[2,16,4352]{2,1,0:T(8,128)S(1)} %bitcast.4, bf16[3072,256]{1,0:T(8,128)(2,1)S(1)} %get-tuple-element.22.high_ref.refs_1_, bf16[3072,256]{1,0:T(8,128)(2,1)S(1)} %get-tuple-element.23.low_ref.refs_2_, ...), custom_call_target="tpu_custom_call" | custom-call | tf_op jit(solution)/shard_map/time_gradient/pallas_call | solution.py:361
  22.8 6.0 %all-to-all-start.1 = ((f32[16,8,256]{2,1,0:T(8,128)}), f32[16,8,256]{2,1,0:T(8,128)S(1)}, u32[]{:S(2)}, u32[]{:S(2)}) async-start(f32[16,8,256]{2,1,0:T(8,128)} %get-tuple-element.31), calls=%async_computation.1 | async-start | bytes 262144 | tf_op jit(solution)/shard_map/all_to_all | solution.py:347
  28.7 1.3 %collective-permute-start.3 = (f32[8,4096]{1,0:T(8,128)S(1)}, f32[8,4096]{1,0:T(8,128)S(1)}, u32[]{:S(2)}, u32[]{:S(2)}) collective-permute-start(f32[8,4096]{1,0:T(8,128)S(1)} %get-tuple-element.32.scaled), channel_id=1, source_target_pairs={{0,2},{1,3},{4,6},{5,7},{8,10},{9,11},{12,14},{13,15},{16,18},{17,... | collective-permute-start | bytes 393224 | tf_op jit(solution)/shard_map/ppermute | solution.py:336
  30.0 2.8 %all-to-all-done.1.grads = f32[16,8,256]{2,1,0:T(8,128)S(1)} async-done(((f32[16,8,256]{2,1,0:T(8,128)}), f32[16,8,256]{2,1,0:T(8,128)S(1)}, u32[]{:S(2)}, u32[]{:S(2)}) %all-to-all-start.1) | async-done | bytes 131104 | tf_op jit(solution)/shard_map/all_to_all | solution.py:347
  32.8 0.1 unit_totals.1.totals
  32.9 1.3 %collective-permute-start.2 = (f32[8,128]{1,0:T(8,128)S(1)}, f32[8,128]{1,0:T(8,128)S(1)}, u32[]{:S(2)}, u32[]{:S(2)}) collective-permute-start(f32[8,128]{1,0:T(8,128)S(1)} %unit_totals.1.totals), channel_id=1, source_target_pairs={{0,3},{1,2},{4,7},{5,6},{8,11},{9,10},{12,15},{13,14},{16,19},{17,... | collective-permute-start | bytes 12296 | tf_op jit(solution)/shard_map/ppermute | solution.py:336
  34.2 0.9 %scale_weights.1 = (f32[8,4096]{1,0:T(8,128)}, f32[8,256]{1,0:T(8,128)}) custom-call(f32[8,128]{1,0:T(8,128)S(1)} %unit_totals.1.totals, f32[8,4096]{1,0:T(8,128)S(1)} %get-tuple-element.32.scaled, f32[16,8,256]{2,1,0:T(8,128)S(1)} %all-to-all-done.1.grads, f32[8,512]{1,0:T(8,128)S(1)} %get-tuple-element.33.lam, ...), custom_call_target="tpu_custom_call" | custom-call | tf_op jit(solution)/shard_map/scale_weights/pallas_call | solution.py:361
  35.1 0.0 collective-permute-done.3.sent_scaled
  35.1 0.4 %collective-permute-done.2.sent_totals = f32[8,128]{1,0:T(8,128)S(1)} collective-permute-done((f32[8,128]{1,0:T(8,128)S(1)}, f32[8,128]{1,0:T(8,128)S(1)}, u32[]{:S(2)}, u32[]{:S(2)}) %collective-permute-start.2) | collective-permute-done | bytes 4128 | tf_op jit(solution)/shard_map/ppermute | solution.py:336
  (1 shorter events, 0.0 us)
Async XLA Ops:
  4.2 12.7 %all-to-all-start = ((f32[8,1,4224]{2,1,0:T(1,128)}), f32[8,1,4224]{2,1,0:T(1,128)S(1)}, u32[]{:S(2)}, u32[]{:S(2)}) async-start(f32[8,1,4224]{2,1,0:T(1,128)} %get-tuple-element.19), calls=%async_computation | async-start | bytes 270336 | tf_op jit(solution)/shard_map/all_to_all | solution.py:356
  12.1 7.1 %collective-permute-start = (f32[8,4096]{1,0:T(8,128)}, f32[8,4096]{1,0:T(8,128)S(1)}, u32[]{:S(2)}, u32[]{:S(2)}) collective-permute-start(f32[8,4096]{1,0:T(8,128)} %get-tuple-element.25), channel_id=1, source_target_pairs={{2,0},{3,1},{6,4},{7,5},{10,8},{11,9},{14,12},{15,13},{18,16},{19,... | collective-permute-start | bytes 393224 | tf_op jit(solution)/shard_map/ppermute | solution.py:409
  13.3 5.6 %collective-permute-start.1 = (f32[8,128]{1,0:T(8,128)S(1)}, f32[8,128]{1,0:T(8,128)S(1)}, u32[]{:S(2)}, u32[]{:S(2)}) collective-permute-start(f32[8,128]{1,0:T(8,128)S(1)} %get-tuple-element.26.refs_0_), channel_id=1, source_target_pairs={{0,1},{1,0},{4,5},{5,4},{8,9},{9,8},{12,13},{13,12},{16,17},{17,16... | collective-permute-start | bytes 12296 | tf_op jit(solution)/shard_map/ppermute | solution.py:431
  22.8 10.1 %all-to-all-start.1 = ((f32[16,8,256]{2,1,0:T(8,128)}), f32[16,8,256]{2,1,0:T(8,128)S(1)}, u32[]{:S(2)}, u32[]{:S(2)}) async-start(f32[16,8,256]{2,1,0:T(8,128)} %get-tuple-element.31), calls=%async_computation.1 | async-start | bytes 262144 | tf_op jit(solution)/shard_map/all_to_all | solution.py:347
  28.7 6.4 %collective-permute-start.3 = (f32[8,4096]{1,0:T(8,128)S(1)}, f32[8,4096]{1,0:T(8,128)S(1)}, u32[]{:S(2)}, u32[]{:S(2)}) collective-permute-start(f32[8,4096]{1,0:T(8,128)S(1)} %get-tuple-element.32.scaled), channel_id=1, source_target_pairs={{0,2},{1,3},{4,6},{5,7},{8,10},{9,11},{12,14},{13,15},{16,18},{17,... | collective-permute-start | bytes 393224 | tf_op jit(solution)/shard_map/ppermute | solution.py:336
  32.9 2.6 %collective-permute-start.2 = (f32[8,128]{1,0:T(8,128)S(1)}, f32[8,128]{1,0:T(8,128)S(1)}, u32[]{:S(2)}, u32[]{:S(2)}) collective-permute-start(f32[8,128]{1,0:T(8,128)S(1)} %unit_totals.1.totals), channel_id=1, source_target_pairs={{0,3},{1,2},{4,7},{5,6},{8,11},{9,10},{12,15},{13,14},{16,19},{17,... | collective-permute-start | bytes 12296 | tf_op jit(solution)/shard_map/ppermute | solution.py:336

commit v31 on v26

--- a/solution.py
+++ b/solution.py
@@ -210,7 +210,7 @@
             pack[:groups, here] = add_terms(product, groups)
             pack[groups:, here] = add_terms(product, groups, 1)
 
-        late = resident - 2 * block_rows
+        late = resident - 4 * block_rows
 
         @pl.loop(0, late // (2 * block_rows))
         def _(block):

time: 35 us -> 35.4 us (1.011)
  Pallas kernels: 8.06 us -> 8.43 us
    pallas_call x7, Pallas kernels: 8.06 us -> 8.43 us  [call(): pl.pallas_call(kernel, in_specs=in_specs or [vmem] * len(args), out_specs...]
  transfers between devices with their start and end apart: 6 -> 6, of which waited for: 4 -> 3; matrix products, arithmetic and copies ran while one was open for 0% -> 0% of each run, Pallas kernels for 9% -> 10%
where the time goes in v31:
time: 35.4 us; the launch traced here: 34.9 us
  starting transfers between devices  18.8 us (53%)
  Pallas kernels  8.43 us (24%)
  waiting for transfers between devices  4.73 us (13%)
  blocking collectives  2.2 us (6%)
  between operations  0.7 us (2%)
    pallas_call x7, Pallas kernels, call(): pl.pallas_call(kernel, in_specs=in_specs or [vmem] * len(args), out_specs...  8.43 us
    all_to_all x1, starting transfers between devices, over_units(): lax.all_to_all(value, ('unit', 'day'), split_axis=0, concat_axis=0, axis_...  7.83 us
    all_to_all x1, starting transfers between devices, over_first_half(): lax.all_to_all(value, ('unit', 'day'), split_axis=0, concat_axis=0, axis_...  5.24 us
    all_to_all x1, waiting for transfers between devices, over_first_half(): lax.all_to_all(value, ('unit', 'day'), split_axis=0, concat_axis=0, axis_...  2.72 us
    ppermute x2, starting transfers between devices, to_other_half(): return lax.ppermute(value, ('unit', 'day'), pairs)  2.56 us
    all_gather x1, blocking collectives, over_days(): return lax.all_gather(value, 'day', axis_index_groups=halves)  2.2 us
    ppermute x1, starting transfers between devices, local(): time_norms.append(lax.ppermute(time_norm, ('unit', 'day'), pairs))  1.92 us
    all_to_all x1, waiting for transfers between devices, over_units(): lax.all_to_all(value, ('unit', 'day'), split_axis=0, concat_axis=0, axis_...  1.61 us
  transfers between devices with their start and end apart: 6, of which 3 were waited for; matrix products, arithmetic and copies ran while one was open for 0% of the time, Pallas kernels for 10%

profile of v31, /device:TPU:0, one launch (start us, length us, event | category | flops | bytes accessed | tf_op | source)
XLA Modules:
  0.0 34.9 jit_solution(602891127348693555)
XLA Ops:
  0.6 3.6 %first_product.1 = (f32[8,1,4224]{2,1,0:T(1,128)}, f32[8,4096]{1,0:T(8,128)}, f32[8,256]{1,0:T(8,128)S(1)}, f32[8,128]{1,0:T(8,128)S(1)}, f32[8,128]{1,0:T(8,128...) custom-call(f32[4096,256]{1,0:T(8,128)} %panel.1, s32[1,4096]{1,0:T(1,128)} %bitcast.5, ...), custom_call_target="tpu_custom_call" | custom-call | tf_op jit(solution)/shard_map/first_product/pallas_call | solution.py:361
  4.2 7.8 %all-to-all-start = ((f32[8,1,4224]{2,1,0:T(1,128)}), f32[8,1,4224]{2,1,0:T(1,128)S(1)}, u32[]{:S(2)}, u32[]{:S(2)}) async-start(f32[8,1,4224]{2,1,0:T(1,128)} %get-tuple-element.19), calls=%async_computation | async-start | bytes 270336 | tf_op jit(solution)/shard_map/all_to_all | solution.py:356
  12.1 1.3 %collective-permute-start = (f32[8,4096]{1,0:T(8,128)}, f32[8,4096]{1,0:T(8,128)S(1)}, u32[]{:S(2)}, u32[]{:S(2)}) collective-permute-start(f32[8,4096]{1,0:T(8,128)} %get-tuple-element.25), channel_id=1, source_target_pairs={{2,0},{3,1},{6,4},{7,5},{10,8},{11,9},{14,12},{15,13},{18,16},{19,... | collective-permute-start | bytes 393224 | tf_op jit(solution)/shard_map/ppermute | solution.py:409
  13.3 1.9 %collective-permute-start.1 = (f32[8,128]{1,0:T(8,128)S(1)}, f32[8,128]{1,0:T(8,128)S(1)}, u32[]{:S(2)}, u32[]{:S(2)}) collective-permute-start(f32[8,128]{1,0:T(8,128)S(1)} %get-tuple-element.26.refs_0_), channel_id=1, source_target_pairs={{0,1},{1,0},{4,5},{5,4},{8,9},{9,8},{12,13},{13,12},{16,17},{17,16... | collective-permute-start | bytes 12296 | tf_op jit(solution)/shard_map/ppermute | solution.py:431
  15.3 1.6 %all-to-all-done.sums = f32[8,1,4224]{2,1,0:T(1,128)S(1)} async-done(((f32[8,1,4224]{2,1,0:T(1,128)}), f32[8,1,4224]{2,1,0:T(1,128)S(1)}, u32[]{:S(2)}, u32[]{:S(2)}) %all-to-all-start) | async-done | bytes 135200 | tf_op jit(solution)/shard_map/all_to_all | solution.py:356
  16.9 2.4 %unit_gradient.1 = (f32[16,4352]{1,0:T(8,128)S(1)}, f32[8,128]{1,0:T(8,128)S(1)}, f32[8,4096]{1,0:T(8,128)S(1)}, bf16[1024,256]{1,0:T(8,128)(2,1)S(1)}, bf16[1024,256]{1,0:T(8,128)(2,1)S(1)}) custom-call(f32[4096,256]{1,0:T(8,128)} %panel.1, s32[1,4096]{1,0:T(1,128)} %bitcast.6, f32[8,4096]{1,0:T(8,128)} %unit_logit.1, f32[8,1,4224]{2,1,0:T(1,128)S(1)} %all-to-all-done.sums, ...), custom_call_target="tpu_custom_call" | custom-call | tf_op jit(solution)/shard_map/unit_gradient/pallas_call | solution.py:361
  19.3 0.0 collective-permute-done.1.refs_1_
  19.3 0.0 collective-permute-done.post
  19.3 0.1 join_post.1
  19.4 2.2 %all-gather = f32[32,4352]{1,0:T(8,128)S(1)} all-gather(f32[16,4352]{1,0:T(8,128)S(1)} %join_post.1), channel_id=2, replica_groups={{0,1},{2,3},{4,5},{6,7},{8,9},{10,11},{12,13},{14,15},{16,17},{18,19},{..., dimensions={0}, use_global_device_ids=true | all-gather | bytes 835584 | tf_op jit(solution)/shard_map/all_gather | solution.py:340
  21.6 1.4 %time_gradient.1 = (f32[8,4096]{1,0:T(8,128)S(1)}, f32[8,512]{1,0:T(8,128)S(1)}, f32[16,8,256]{2,1,0:T(8,128)}) custom-call(f32[2,16,4352]{2,1,0:T(8,128)S(1)} %bitcast.4, bf16[3072,256]{1,0:T(8,128)(2,1)S(1)} %get-tuple-element.22.high_ref.refs_1_, bf16[3072,256]{1,0:T(8,128)(2,1)S(1)} %get-tuple-element.23.low_ref.refs_2_, ...), custom_call_target="tpu_custom_call" | custom-call | tf_op jit(solution)/shard_map/time_gradient/pallas_call | solution.py:361
  23.0 5.2 %all-to-all-start.1 = ((f32[16,8,256]{2,1,0:T(8,128)}), f32[16,8,256]{2,1,0:T(8,128)S(1)}, u32[]{:S(2)}, u32[]{:S(2)}) async-start(f32[16,8,256]{2,1,0:T(8,128)} %get-tuple-element.31), calls=%async_computation.1 | async-start | bytes 262144 | tf_op jit(solution)/shard_map/all_to_all | solution.py:347
  28.2 1.3 %collective-permute-start.3 = (f32[8,4096]{1,0:T(8,128)S(1)}, f32[8,4096]{1,0:T(8,128)S(1)}, u32[]{:S(2)}, u32[]{:S(2)}) collective-permute-start(f32[8,4096]{1,0:T(8,128)S(1)} %get-tuple-element.32.scaled), channel_id=1, source_target_pairs={{0,2},{1,3},{4,6},{5,7},{8,10},{9,11},{12,14},{13,15},{16,18},{17,... | collective-permute-start | bytes 393224 | tf_op jit(solution)/shard_map/ppermute | solution.py:336
  29.5 2.7 %all-to-all-done.1.grads = f32[16,8,256]{2,1,0:T(8,128)S(1)} async-done(((f32[16,8,256]{2,1,0:T(8,128)}), f32[16,8,256]{2,1,0:T(8,128)S(1)}, u32[]{:S(2)}, u32[]{:S(2)}) %all-to-all-start.1) | async-done | bytes 131104 | tf_op jit(solution)/shard_map/all_to_all | solution.py:347
  32.2 0.1 unit_totals.1.totals
  32.3 1.3 %collective-permute-start.2 = (f32[8,128]{1,0:T(8,128)S(1)}, f32[8,128]{1,0:T(8,128)S(1)}, u32[]{:S(2)}, u32[]{:S(2)}) collective-permute-start(f32[8,128]{1,0:T(8,128)S(1)} %unit_totals.1.totals), channel_id=1, source_target_pairs={{0,3},{1,2},{4,7},{5,6},{8,11},{9,10},{12,15},{13,14},{16,19},{17,... | collective-permute-start | bytes 12296 | tf_op jit(solution)/shard_map/ppermute | solution.py:336
  33.6 0.9 %scale_weights.1 = (f32[8,4096]{1,0:T(8,128)}, f32[8,256]{1,0:T(8,128)}) custom-call(f32[8,128]{1,0:T(8,128)S(1)} %unit_totals.1.totals, f32[8,4096]{1,0:T(8,128)S(1)} %get-tuple-element.32.scaled, f32[16,8,256]{2,1,0:T(8,128)S(1)} %all-to-all-done.1.grads, f32[8,512]{1,0:T(8,128)S(1)} %get-tuple-element.33.lam, ...), custom_call_target="tpu_custom_call" | custom-call | tf_op jit(solution)/shard_map/scale_weights/pallas_call | solution.py:361
  34.5 0.0 collective-permute-done.3.sent_scaled
  34.5 0.4 %collective-permute-done.2.sent_totals = f32[8,128]{1,0:T(8,128)S(1)} collective-permute-done((f32[8,128]{1,0:T(8,128)S(1)}, f32[8,128]{1,0:T(8,128)S(1)}, u32[]{:S(2)}, u32[]{:S(2)}) %collective-permute-start.2) | collective-permute-done | bytes 4128 | tf_op jit(solution)/shard_map/ppermute | solution.py:336
  (1 shorter events, 0.0 us)
Async XLA Ops:
  4.2 12.7 %all-to-all-start = ((f32[8,1,4224]{2,1,0:T(1,128)}), f32[8,1,4224]{2,1,0:T(1,128)S(1)}, u32[]{:S(2)}, u32[]{:S(2)}) async-start(f32[8,1,4224]{2,1,0:T(1,128)} %get-tuple-element.19), calls=%async_computation | async-start | bytes 270336 | tf_op jit(solution)/shard_map/all_to_all | solution.py:356
  12.1 7.2 %collective-permute-start = (f32[8,4096]{1,0:T(8,128)}, f32[8,4096]{1,0:T(8,128)S(1)}, u32[]{:S(2)}, u32[]{:S(2)}) collective-permute-start(f32[8,4096]{1,0:T(8,128)} %get-tuple-element.25), channel_id=1, source_target_pairs={{2,0},{3,1},{6,4},{7,5},{10,8},{11,9},{14,12},{15,13},{18,16},{19,... | collective-permute-start | bytes 393224 | tf_op jit(solution)/shard_map/ppermute | solution.py:409
  13.3 5.9 %collective-permute-start.1 = (f32[8,128]{1,0:T(8,128)S(1)}, f32[8,128]{1,0:T(8,128)S(1)}, u32[]{:S(2)}, u32[]{:S(2)}) collective-permute-start(f32[8,128]{1,0:T(8,128)S(1)} %get-tuple-element.26.refs_0_), channel_id=1, source_target_pairs={{0,1},{1,0},{4,5},{5,4},{8,9},{9,8},{12,13},{13,12},{16,17},{17,16... | collective-permute-start | bytes 12296 | tf_op jit(solution)/shard_map/ppermute | solution.py:431
  23.0 9.2 %all-to-all-start.1 = ((f32[16,8,256]{2,1,0:T(8,128)}), f32[16,8,256]{2,1,0:T(8,128)S(1)}, u32[]{:S(2)}, u32[]{:S(2)}) async-start(f32[16,8,256]{2,1,0:T(8,128)} %get-tuple-element.31), calls=%async_computation.1 | async-start | bytes 262144 | tf_op jit(solution)/shard_map/all_to_all | solution.py:347
  28.2 6.3 %collective-permute-start.3 = (f32[8,4096]{1,0:T(8,128)S(1)}, f32[8,4096]{1,0:T(8,128)S(1)}, u32[]{:S(2)}, u32[]{:S(2)}) collective-permute-start(f32[8,4096]{1,0:T(8,128)S(1)} %get-tuple-element.32.scaled), channel_id=1, source_target_pairs={{0,2},{1,3},{4,6},{5,7},{8,10},{9,11},{12,14},{13,15},{16,18},{17,... | collective-permute-start | bytes 393224 | tf_op jit(solution)/shard_map/ppermute | solution.py:336
  32.3 2.6 %collective-permute-start.2 = (f32[8,128]{1,0:T(8,128)S(1)}, f32[8,128]{1,0:T(8,128)S(1)}, u32[]{:S(2)}, u32[]{:S(2)}) collective-permute-start(f32[8,128]{1,0:T(8,128)S(1)} %unit_totals.1.totals), channel_id=1, source_target_pairs={{0,3},{1,2},{4,7},{5,6},{8,11},{9,10},{12,15},{13,14},{16,19},{17,... | collective-permute-start | bytes 12296 | tf_op jit(solution)/shard_map/ppermute | solution.py:336

commit v32 on v31

--- a/solution.py
+++ b/solution.py
@@ -210,11 +210,11 @@
             pack[:groups, here] = add_terms(product, groups)
             pack[groups:, here] = add_terms(product, groups, 1)
 
-        late = resident - 4 * block_rows
-
-        @pl.loop(0, late // (2 * block_rows))
+        late = resident - block_rows
+
+        @pl.loop(0, late // block_rows)
         def _(block):
-            here = pl.ds(pl.multiple_of(block * 2 * block_rows, 2 * block_rows), 2 * block_rows)
+            here = pl.ds(pl.multiple_of(block * block_rows, block_rows), block_rows)
             multiply(here, high_ref[here, :], low_ref[here, :])
 
         wait_all(copies)

time: 35.4 us -> 35 us (0.989)
  transfers between devices with their start and end apart: 6 -> 6, of which waited for: 3 -> 4; matrix products, arithmetic and copies ran while one was open for 0% -> 0% of each run, Pallas kernels for 10% -> 9%
where the time goes in v32:
time: 35 us; the launch traced here: 34.6 us
  starting transfers between devices  18.7 us (53%)
  Pallas kernels  8.12 us (23%)
  waiting for transfers between devices  4.85 us (14%)
  blocking collectives  2.2 us (6%)
  between operations  0.7 us (2%)
    pallas_call x7, Pallas kernels, call(): pl.pallas_call(kernel, in_specs=in_specs or [vmem] * len(args), out_specs...  8.12 us
    all_to_all x1, starting transfers between devices, over_units(): lax.all_to_all(value, ('unit', 'day'), split_axis=0, concat_axis=0, axis_...  7.83 us
    all_to_all x1, starting transfers between devices, over_first_half(): lax.all_to_all(value, ('unit', 'day'), split_axis=0, concat_axis=0, axis_...  5.13 us
    all_to_all x1, waiting for transfers between devices, over_first_half(): lax.all_to_all(value, ('unit', 'day'), split_axis=0, concat_axis=0, axis_...  2.72 us
    ppermute x2, starting transfers between devices, to_other_half(): return lax.ppermute(value, ('unit', 'day'), pairs)  2.56 us
    all_gather x1, blocking collectives, over_days(): return lax.all_gather(value, 'day', axis_index_groups=halves)  2.2 us
    ppermute x1, starting transfers between devices, local(): time_norms.append(lax.ppermute(time_norm, ('unit', 'day'), pairs))  1.92 us
    all_to_all x1, waiting for transfers between devices, over_units(): lax.all_to_all(value, ('unit', 'day'), split_axis=0, concat_axis=0, axis_...  1.61 us
  transfers between devices with their start and end apart: 6, of which 4 were waited for; matrix products, arithmetic and copies ran while one was open for 0% of the time, Pallas kernels for 9%

profile of v32, /device:TPU:0, one launch (start us, length us, event | category | flops | bytes accessed | tf_op | source)
XLA Modules:
  0.0 34.6 jit_solution(5898320682995046892)
XLA Ops:
  0.6 3.6 %first_product.1 = (f32[8,1,4224]{2,1,0:T(1,128)}, f32[8,4096]{1,0:T(8,128)}, f32[8,256]{1,0:T(8,128)S(1)}, f32[8,128]{1,0:T(8,128)S(1)}, f32[8,128]{1,0:T(8,128...) custom-call(f32[4096,256]{1,0:T(8,128)} %panel.1, s32[1,4096]{1,0:T(1,128)} %bitcast.5, ...), custom_call_target="tpu_custom_call" | custom-call | tf_op jit(solution)/shard_map/first_product/pallas_call | solution.py:361
  4.2 7.8 %all-to-all-start = ((f32[8,1,4224]{2,1,0:T(1,128)}), f32[8,1,4224]{2,1,0:T(1,128)S(1)}, u32[]{:S(2)}, u32[]{:S(2)}) async-start(f32[8,1,4224]{2,1,0:T(1,128)} %get-tuple-element.19), calls=%async_computation | async-start | bytes 270336 | tf_op jit(solution)/shard_map/all_to_all | solution.py:356
  12.1 1.3 %collective-permute-start = (f32[8,4096]{1,0:T(8,128)}, f32[8,4096]{1,0:T(8,128)S(1)}, u32[]{:S(2)}, u32[]{:S(2)}) collective-permute-start(f32[8,4096]{1,0:T(8,128)} %get-tuple-element.25), channel_id=1, source_target_pairs={{2,0},{3,1},{6,4},{7,5},{10,8},{11,9},{14,12},{15,13},{18,16},{19,... | collective-permute-start | bytes 393224 | tf_op jit(solution)/shard_map/ppermute | solution.py:409
  13.3 1.9 %collective-permute-start.1 = (f32[8,128]{1,0:T(8,128)S(1)}, f32[8,128]{1,0:T(8,128)S(1)}, u32[]{:S(2)}, u32[]{:S(2)}) collective-permute-start(f32[8,128]{1,0:T(8,128)S(1)} %get-tuple-element.26.refs_0_), channel_id=1, source_target_pairs={{0,1},{1,0},{4,5},{5,4},{8,9},{9,8},{12,13},{13,12},{16,17},{17,16... | collective-permute-start | bytes 12296 | tf_op jit(solution)/shard_map/ppermute | solution.py:431
  15.3 1.6 %all-to-all-done.sums = f32[8,1,4224]{2,1,0:T(1,128)S(1)} async-done(((f32[8,1,4224]{2,1,0:T(1,128)}), f32[8,1,4224]{2,1,0:T(1,128)S(1)}, u32[]{:S(2)}, u32[]{:S(2)}) %all-to-all-start) | async-done | bytes 135200 | tf_op jit(solution)/shard_map/all_to_all | solution.py:356
  16.9 2.1 %unit_gradient.1 = (f32[16,4352]{1,0:T(8,128)S(1)}, f32[8,128]{1,0:T(8,128)S(1)}, f32[8,4096]{1,0:T(8,128)S(1)}, bf16[1024,256]{1,0:T(8,128)(2,1)S(1)}, bf16[1024,256]{1,0:T(8,128)(2,1)S(1)}) custom-call(f32[4096,256]{1,0:T(8,128)} %panel.1, s32[1,4096]{1,0:T(1,128)} %bitcast.6, f32[8,4096]{1,0:T(8,128)} %unit_logit.1, f32[8,1,4224]{2,1,0:T(1,128)S(1)} %all-to-all-done.sums, ...), custom_call_target="tpu_custom_call" | custom-call | tf_op jit(solution)/shard_map/unit_gradient/pallas_call | solution.py:361
  19.0 0.0 collective-permute-done.1.refs_1_
  19.0 0.1 collective-permute-done.post
  19.1 0.1 join_post.1
  19.2 2.2 %all-gather = f32[32,4352]{1,0:T(8,128)S(1)} all-gather(f32[16,4352]{1,0:T(8,128)S(1)} %join_post.1), channel_id=2, replica_groups={{0,1},{2,3},{4,5},{6,7},{8,9},{10,11},{12,13},{14,15},{16,17},{18,19},{..., dimensions={0}, use_global_device_ids=true | all-gather | bytes 835584 | tf_op jit(solution)/shard_map/all_gather | solution.py:340
  21.4 1.4 %time_gradient.1 = (f32[8,4096]{1,0:T(8,128)S(1)}, f32[8,512]{1,0:T(8,128)S(1)}, f32[16,8,256]{2,1,0:T(8,128)}) custom-call(f32[2,16,4352]{2,1,0:T(8,128)S(1)} %bitcast.4, bf16[3072,256]{1,0:T(8,128)(2,1)S(1)} %get-tuple-element.22.high_ref.refs_1_, bf16[3072,256]{1,0:T(8,128)(2,1)S(1)} %get-tuple-element.23.low_ref.refs_2_, ...), custom_call_target="tpu_custom_call" | custom-call | tf_op jit(solution)/shard_map/time_gradient/pallas_call | solution.py:361
  22.8 5.1 %all-to-all-start.1 = ((f32[16,8,256]{2,1,0:T(8,128)}), f32[16,8,256]{2,1,0:T(8,128)S(1)}, u32[]{:S(2)}, u32[]{:S(2)}) async-start(f32[16,8,256]{2,1,0:T(8,128)} %get-tuple-element.31), calls=%async_computation.1 | async-start | bytes 262144 | tf_op jit(solution)/shard_map/all_to_all | solution.py:347
  27.9 1.3 %collective-permute-start.3 = (f32[8,4096]{1,0:T(8,128)S(1)}, f32[8,4096]{1,0:T(8,128)S(1)}, u32[]{:S(2)}, u32[]{:S(2)}) collective-permute-start(f32[8,4096]{1,0:T(8,128)S(1)} %get-tuple-element.32.scaled), channel_id=1, source_target_pairs={{0,2},{1,3},{4,6},{5,7},{8,10},{9,11},{12,14},{13,15},{16,18},{17,... | collective-permute-start | bytes 393224 | tf_op jit(solution)/shard_map/ppermute | solution.py:336
  29.2 2.7 %all-to-all-done.1.grads = f32[16,8,256]{2,1,0:T(8,128)S(1)} async-done(((f32[16,8,256]{2,1,0:T(8,128)}), f32[16,8,256]{2,1,0:T(8,128)S(1)}, u32[]{:S(2)}, u32[]{:S(2)}) %all-to-all-start.1) | async-done | bytes 131104 | tf_op jit(solution)/shard_map/all_to_all | solution.py:347
  31.9 0.1 unit_totals.1.totals
  32.0 1.3 %collective-permute-start.2 = (f32[8,128]{1,0:T(8,128)S(1)}, f32[8,128]{1,0:T(8,128)S(1)}, u32[]{:S(2)}, u32[]{:S(2)}) collective-permute-start(f32[8,128]{1,0:T(8,128)S(1)} %unit_totals.1.totals), channel_id=1, source_target_pairs={{0,3},{1,2},{4,7},{5,6},{8,11},{9,10},{12,15},{13,14},{16,19},{17,... | collective-permute-start | bytes 12296 | tf_op jit(solution)/shard_map/ppermute | solution.py:336
  33.3 0.9 %scale_weights.1 = (f32[8,4096]{1,0:T(8,128)}, f32[8,256]{1,0:T(8,128)}) custom-call(f32[8,128]{1,0:T(8,128)S(1)} %unit_totals.1.totals, f32[8,4096]{1,0:T(8,128)S(1)} %get-tuple-element.32.scaled, f32[16,8,256]{2,1,0:T(8,128)S(1)} %all-to-all-done.1.grads, f32[8,512]{1,0:T(8,128)S(1)} %get-tuple-element.33.lam, ...), custom_call_target="tpu_custom_call" | custom-call | tf_op jit(solution)/shard_map/scale_weights/pallas_call | solution.py:361
  34.2 0.0 collective-permute-done.3.sent_scaled
  34.2 0.4 %collective-permute-done.2.sent_totals = f32[8,128]{1,0:T(8,128)S(1)} collective-permute-done((f32[8,128]{1,0:T(8,128)S(1)}, f32[8,128]{1,0:T(8,128)S(1)}, u32[]{:S(2)}, u32[]{:S(2)}) %collective-permute-start.2) | collective-permute-done | bytes 4128 | tf_op jit(solution)/shard_map/ppermute | solution.py:336
  (1 shorter events, 0.0 us)
Async XLA Ops:
  4.2 12.7 %all-to-all-start = ((f32[8,1,4224]{2,1,0:T(1,128)}), f32[8,1,4224]{2,1,0:T(1,128)S(1)}, u32[]{:S(2)}, u32[]{:S(2)}) async-start(f32[8,1,4224]{2,1,0:T(1,128)} %get-tuple-element.19), calls=%async_computation | async-start | bytes 270336 | tf_op jit(solution)/shard_map/all_to_all | solution.py:356
  12.1 7.1 %collective-permute-start = (f32[8,4096]{1,0:T(8,128)}, f32[8,4096]{1,0:T(8,128)S(1)}, u32[]{:S(2)}, u32[]{:S(2)}) collective-permute-start(f32[8,4096]{1,0:T(8,128)} %get-tuple-element.25), channel_id=1, source_target_pairs={{2,0},{3,1},{6,4},{7,5},{10,8},{11,9},{14,12},{15,13},{18,16},{19,... | collective-permute-start | bytes 393224 | tf_op jit(solution)/shard_map/ppermute | solution.py:409
  13.3 5.6 %collective-permute-start.1 = (f32[8,128]{1,0:T(8,128)S(1)}, f32[8,128]{1,0:T(8,128)S(1)}, u32[]{:S(2)}, u32[]{:S(2)}) collective-permute-start(f32[8,128]{1,0:T(8,128)S(1)} %get-tuple-element.26.refs_0_), channel_id=1, source_target_pairs={{0,1},{1,0},{4,5},{5,4},{8,9},{9,8},{12,13},{13,12},{16,17},{17,16... | collective-permute-start | bytes 12296 | tf_op jit(solution)/shard_map/ppermute | solution.py:431
  22.8 9.1 %all-to-all-start.1 = ((f32[16,8,256]{2,1,0:T(8,128)}), f32[16,8,256]{2,1,0:T(8,128)S(1)}, u32[]{:S(2)}, u32[]{:S(2)}) async-start(f32[16,8,256]{2,1,0:T(8,128)} %get-tuple-element.31), calls=%async_computation.1 | async-start | bytes 262144 | tf_op jit(solution)/shard_map/all_to_all | solution.py:347
  27.9 6.3 %collective-permute-start.3 = (f32[8,4096]{1,0:T(8,128)S(1)}, f32[8,4096]{1,0:T(8,128)S(1)}, u32[]{:S(2)}, u32[]{:S(2)}) collective-permute-start(f32[8,4096]{1,0:T(8,128)S(1)} %get-tuple-element.32.scaled), channel_id=1, source_target_pairs={{0,2},{1,3},{4,6},{5,7},{8,10},{9,11},{12,14},{13,15},{16,18},{17,... | collective-permute-start | bytes 393224 | tf_op jit(solution)/shard_map/ppermute | solution.py:336
  32.0 2.6 %collective-permute-start.2 = (f32[8,128]{1,0:T(8,128)S(1)}, f32[8,128]{1,0:T(8,128)S(1)}, u32[]{:S(2)}, u32[]{:S(2)}) collective-permute-start(f32[8,128]{1,0:T(8,128)S(1)} %unit_totals.1.totals), channel_id=1, source_target_pairs={{0,3},{1,2},{4,7},{5,6},{8,11},{9,10},{12,15},{13,14},{16,19},{17,... | collective-permute-start | bytes 12296 | tf_op jit(solution)/shard_map/ppermute | solution.py:336

commit v33 on v26

--- a/solution.py
+++ b/solution.py
@@ -322,7 +322,7 @@
     half = day_devices // 2
     assert half * 2 == day_devices and half & (half - 1) == 0
     assert unit_devices & (unit_devices - 1) == 0
-    panel_starts = [0, unit_rows // 8 * 3, unit_rows // 4 * 3, unit_rows]
+    panel_starts = [0, unit_rows // 2, unit_rows // 8 * 7, unit_rows]
     resident = unit_rows * 3 // 4 // (2 * block_rows) * (2 * block_rows)
     def meeting_at(first):
         return [first] + [unit for unit in reversed(range(unit_devices)) if unit != first]

time: 35 us -> 35.3 us (level)
  no operation moved by 1% of the time
where the time goes in v33:
time: 35.3 us; the launch traced here: 34.8 us
  starting transfers between devices  18.7 us (53%)
  Pallas kernels  8.35 us (24%)
  waiting for transfers between devices  4.91 us (14%)
  blocking collectives  2.2 us (6%)
  between operations  0.7 us (2%)
    pallas_call x7, Pallas kernels, call(): pl.pallas_call(kernel, in_specs=in_specs or [vmem] * len(args), out_specs...  8.35 us
    all_to_all x1, starting transfers between devices, over_units(): lax.all_to_all(value, ('unit', 'day'), split_axis=0, concat_axis=0, axis_...  7.83 us
    all_to_all x1, starting transfers between devices, over_first_half(): lax.all_to_all(value, ('unit', 'day'), split_axis=0, concat_axis=0, axis_...  5.07 us
    all_to_all x1, waiting for transfers between devices, over_first_half(): lax.all_to_all(value, ('unit', 'day'), split_axis=0, concat_axis=0, axis_...  2.72 us
    ppermute x2, starting transfers between devices, to_other_half(): return lax.ppermute(value, ('unit', 'day'), pairs)  2.56 us
    all_gather x1, blocking collectives, over_days(): return lax.all_gather(value, 'day', axis_index_groups=halves)  2.2 us
    ppermute x1, starting transfers between devices, local(): time_norms.append(lax.ppermute(time_norm, ('unit', 'day'), pairs))  1.92 us
    all_to_all x1, waiting for transfers between devices, over_units(): lax.all_to_all(value, ('unit', 'day'), split_axis=0, concat_axis=0, axis_...  1.61 us
  transfers between devices with their start and end apart: 6, of which 4 were waited for; matrix products, arithmetic and copies ran while one was open for 0% of the time, Pallas kernels for 9%

profile of v33, /device:TPU:0, one launch (start us, length us, event | category | flops | bytes accessed | tf_op | source)
XLA Modules:
  0.0 34.8 jit_solution(10723527794227110106)
XLA Ops:
  0.6 3.9 %first_product.1 = (f32[8,1,4224]{2,1,0:T(1,128)}, f32[8,4096]{1,0:T(8,128)}, f32[8,256]{1,0:T(8,128)S(1)}, f32[8,128]{1,0:T(8,128)S(1)}, f32[8,128]{1,0:T(8,128...) custom-call(f32[4096,256]{1,0:T(8,128)} %panel.1, s32[1,4096]{1,0:T(1,128)} %bitcast.5, ...), custom_call_target="tpu_custom_call" | custom-call | tf_op jit(solution)/shard_map/first_product/pallas_call | solution.py:361
  4.5 7.8 %all-to-all-start = ((f32[8,1,4224]{2,1,0:T(1,128)}), f32[8,1,4224]{2,1,0:T(1,128)S(1)}, u32[]{:S(2)}, u32[]{:S(2)}) async-start(f32[8,1,4224]{2,1,0:T(1,128)} %get-tuple-element.19), calls=%async_computation | async-start | bytes 270336 | tf_op jit(solution)/shard_map/all_to_all | solution.py:356
  12.3 1.3 %collective-permute-start = (f32[8,4096]{1,0:T(8,128)}, f32[8,4096]{1,0:T(8,128)S(1)}, u32[]{:S(2)}, u32[]{:S(2)}) collective-permute-start(f32[8,4096]{1,0:T(8,128)} %get-tuple-element.25), channel_id=1, source_target_pairs={{2,0},{3,1},{6,4},{7,5},{10,8},{11,9},{14,12},{15,13},{18,16},{19,... | collective-permute-start | bytes 393224 | tf_op jit(solution)/shard_map/ppermute | solution.py:409
  13.6 1.9 %collective-permute-start.1 = (f32[8,128]{1,0:T(8,128)S(1)}, f32[8,128]{1,0:T(8,128)S(1)}, u32[]{:S(2)}, u32[]{:S(2)}) collective-permute-start(f32[8,128]{1,0:T(8,128)S(1)} %get-tuple-element.26.refs_0_), channel_id=1, source_target_pairs={{0,1},{1,0},{4,5},{5,4},{8,9},{9,8},{12,13},{13,12},{16,17},{17,16... | collective-permute-start | bytes 12296 | tf_op jit(solution)/shard_map/ppermute | solution.py:431
  15.6 1.6 %all-to-all-done.sums = f32[8,1,4224]{2,1,0:T(1,128)S(1)} async-done(((f32[8,1,4224]{2,1,0:T(1,128)}), f32[8,1,4224]{2,1,0:T(1,128)S(1)}, u32[]{:S(2)}, u32[]{:S(2)}) %all-to-all-start) | async-done | bytes 135200 | tf_op jit(solution)/shard_map/all_to_all | solution.py:356
  17.2 2.0 %unit_gradient.1 = (f32[16,4352]{1,0:T(8,128)S(1)}, f32[8,128]{1,0:T(8,128)S(1)}, f32[8,4096]{1,0:T(8,128)S(1)}, bf16[1024,256]{1,0:T(8,128)(2,1)S(1)}, bf16[1024,256]{1,0:T(8,128)(2,1)S(1)}) custom-call(f32[4096,256]{1,0:T(8,128)} %panel.1, s32[1,4096]{1,0:T(1,128)} %bitcast.6, f32[8,4096]{1,0:T(8,128)} %unit_logit.1, f32[8,1,4224]{2,1,0:T(1,128)S(1)} %all-to-all-done.sums, ...), custom_call_target="tpu_custom_call" | custom-call | tf_op jit(solution)/shard_map/unit_gradient/pallas_call | solution.py:361
  19.2 0.0 collective-permute-done.1.refs_1_
  19.2 0.2 collective-permute-done.post
  19.4 0.1 join_post.1
  19.5 2.2 %all-gather = f32[32,4352]{1,0:T(8,128)S(1)} all-gather(f32[16,4352]{1,0:T(8,128)S(1)} %join_post.1), channel_id=2, replica_groups={{0,1},{2,3},{4,5},{6,7},{8,9},{10,11},{12,13},{14,15},{16,17},{18,19},{..., dimensions={0}, use_global_device_ids=true | all-gather | bytes 835584 | tf_op jit(solution)/shard_map/all_gather | solution.py:340
  21.7 1.4 %time_gradient.1 = (f32[8,4096]{1,0:T(8,128)S(1)}, f32[8,512]{1,0:T(8,128)S(1)}, f32[16,8,256]{2,1,0:T(8,128)}) custom-call(f32[2,16,4352]{2,1,0:T(8,128)S(1)} %bitcast.4, bf16[3072,256]{1,0:T(8,128)(2,1)S(1)} %get-tuple-element.22.high_ref.refs_1_, bf16[3072,256]{1,0:T(8,128)(2,1)S(1)} %get-tuple-element.23.low_ref.refs_2_, ...), custom_call_target="tpu_custom_call" | custom-call | tf_op jit(solution)/shard_map/time_gradient/pallas_call | solution.py:361
  23.1 5.1 %all-to-all-start.1 = ((f32[16,8,256]{2,1,0:T(8,128)}), f32[16,8,256]{2,1,0:T(8,128)S(1)}, u32[]{:S(2)}, u32[]{:S(2)}) async-start(f32[16,8,256]{2,1,0:T(8,128)} %get-tuple-element.31), calls=%async_computation.1 | async-start | bytes 262144 | tf_op jit(solution)/shard_map/all_to_all | solution.py:347
  28.1 1.3 %collective-permute-start.3 = (f32[8,4096]{1,0:T(8,128)S(1)}, f32[8,4096]{1,0:T(8,128)S(1)}, u32[]{:S(2)}, u32[]{:S(2)}) collective-permute-start(f32[8,4096]{1,0:T(8,128)S(1)} %get-tuple-element.32.scaled), channel_id=1, source_target_pairs={{0,2},{1,3},{4,6},{5,7},{8,10},{9,11},{12,14},{13,15},{16,18},{17,... | collective-permute-start | bytes 393224 | tf_op jit(solution)/shard_map/ppermute | solution.py:336
  29.4 2.7 %all-to-all-done.1.grads = f32[16,8,256]{2,1,0:T(8,128)S(1)} async-done(((f32[16,8,256]{2,1,0:T(8,128)}), f32[16,8,256]{2,1,0:T(8,128)S(1)}, u32[]{:S(2)}, u32[]{:S(2)}) %all-to-all-start.1) | async-done | bytes 131104 | tf_op jit(solution)/shard_map/all_to_all | solution.py:347
  32.1 0.1 unit_totals.1.totals
  32.2 1.3 %collective-permute-start.2 = (f32[8,128]{1,0:T(8,128)S(1)}, f32[8,128]{1,0:T(8,128)S(1)}, u32[]{:S(2)}, u32[]{:S(2)}) collective-permute-start(f32[8,128]{1,0:T(8,128)S(1)} %unit_totals.1.totals), channel_id=1, source_target_pairs={{0,3},{1,2},{4,7},{5,6},{8,11},{9,10},{12,15},{13,14},{16,19},{17,... | collective-permute-start | bytes 12296 | tf_op jit(solution)/shard_map/ppermute | solution.py:336
  33.5 0.9 %scale_weights.1 = (f32[8,4096]{1,0:T(8,128)}, f32[8,256]{1,0:T(8,128)}) custom-call(f32[8,128]{1,0:T(8,128)S(1)} %unit_totals.1.totals, f32[8,4096]{1,0:T(8,128)S(1)} %get-tuple-element.32.scaled, f32[16,8,256]{2,1,0:T(8,128)S(1)} %all-to-all-done.1.grads, f32[8,512]{1,0:T(8,128)S(1)} %get-tuple-element.33.lam, ...), custom_call_target="tpu_custom_call" | custom-call | tf_op jit(solution)/shard_map/scale_weights/pallas_call | solution.py:361
  34.4 0.0 collective-permute-done.3.sent_scaled
  34.4 0.4 %collective-permute-done.2.sent_totals = f32[8,128]{1,0:T(8,128)S(1)} collective-permute-done((f32[8,128]{1,0:T(8,128)S(1)}, f32[8,128]{1,0:T(8,128)S(1)}, u32[]{:S(2)}, u32[]{:S(2)}) %collective-permute-start.2) | collective-permute-done | bytes 4128 | tf_op jit(solution)/shard_map/ppermute | solution.py:336
  (1 shorter events, 0.0 us)
Async XLA Ops:
  4.5 12.7 %all-to-all-start = ((f32[8,1,4224]{2,1,0:T(1,128)}), f32[8,1,4224]{2,1,0:T(1,128)S(1)}, u32[]{:S(2)}, u32[]{:S(2)}) async-start(f32[8,1,4224]{2,1,0:T(1,128)} %get-tuple-element.19), calls=%async_computation | async-start | bytes 270336 | tf_op jit(solution)/shard_map/all_to_all | solution.py:356
  12.3 7.1 %collective-permute-start = (f32[8,4096]{1,0:T(8,128)}, f32[8,4096]{1,0:T(8,128)S(1)}, u32[]{:S(2)}, u32[]{:S(2)}) collective-permute-start(f32[8,4096]{1,0:T(8,128)} %get-tuple-element.25), channel_id=1, source_target_pairs={{2,0},{3,1},{6,4},{7,5},{10,8},{11,9},{14,12},{15,13},{18,16},{19,... | collective-permute-start | bytes 393224 | tf_op jit(solution)/shard_map/ppermute | solution.py:409
  13.6 5.6 %collective-permute-start.1 = (f32[8,128]{1,0:T(8,128)S(1)}, f32[8,128]{1,0:T(8,128)S(1)}, u32[]{:S(2)}, u32[]{:S(2)}) collective-permute-start(f32[8,128]{1,0:T(8,128)S(1)} %get-tuple-element.26.refs_0_), channel_id=1, source_target_pairs={{0,1},{1,0},{4,5},{5,4},{8,9},{9,8},{12,13},{13,12},{16,17},{17,16... | collective-permute-start | bytes 12296 | tf_op jit(solution)/shard_map/ppermute | solution.py:431
  23.1 9.1 %all-to-all-start.1 = ((f32[16,8,256]{2,1,0:T(8,128)}), f32[16,8,256]{2,1,0:T(8,128)S(1)}, u32[]{:S(2)}, u32[]{:S(2)}) async-start(f32[16,8,256]{2,1,0:T(8,128)} %get-tuple-element.31), calls=%async_computation.1 | async-start | bytes 262144 | tf_op jit(solution)/shard_map/all_to_all | solution.py:347
  28.1 6.3 %collective-permute-start.3 = (f32[8,4096]{1,0:T(8,128)S(1)}, f32[8,4096]{1,0:T(8,128)S(1)}, u32[]{:S(2)}, u32[]{:S(2)}) collective-permute-start(f32[8,4096]{1,0:T(8,128)S(1)} %get-tuple-element.32.scaled), channel_id=1, source_target_pairs={{0,2},{1,3},{4,6},{5,7},{8,10},{9,11},{12,14},{13,15},{16,18},{17,... | collective-permute-start | bytes 393224 | tf_op jit(solution)/shard_map/ppermute | solution.py:336
  32.2 2.6 %collective-permute-start.2 = (f32[8,128]{1,0:T(8,128)S(1)}, f32[8,128]{1,0:T(8,128)S(1)}, u32[]{:S(2)}, u32[]{:S(2)}) collective-permute-start(f32[8,128]{1,0:T(8,128)S(1)} %unit_totals.1.totals), channel_id=1, source_target_pairs={{0,3},{1,2},{4,7},{5,6},{8,11},{9,10},{12,15},{13,14},{16,19},{17,... | collective-permute-start | bytes 12296 | tf_op jit(solution)/shard_map/ppermute | solution.py:336
